TPU v7x, 32 devices: a whole 2x2x4 slice. The times are simulated.
32 devices in a mesh: parts: 2 (over x), grp: 16 (over z, y, core).
Axes of the slice: x: 2, y: 2, z: 4, core: 2. Of those that a mesh axis runs over, the one named last changes fastest.
Arguments:
- features: bfloat16 [64, 16, 1024], P(('parts', 'grp')), parts along dimension 0, may hold values from -6 to 6
- counts: int32 [64], P(('parts', 'grp')), parts along dimension 0, may hold values from 1 to 16, as said below
- pick_owner: int32 [32, 8], P(('parts', 'grp')), parts along dimension 0, may hold values from 0 to 15, all different within a row
- pick_local: int32 [32, 8], P(('parts', 'grp')), parts along dimension 0, may hold values from 0 to 1
- adjacency: bfloat16 [32, 128, 128], P(('parts', 'grp')), parts along dimension 0, may hold values from 0 to 2
- cotangent: bfloat16 [32, 128, 1024], P(('parts', 'grp')), parts along dimension 0, may hold values from -6 to 6
- w_first: bfloat16 [1024, 1024], replicated, may hold values from -0.1875 to 0.1875
- w_second: bfloat16 [1024, 1024], replicated, may hold values from -0.1875 to 0.1875
Outputs:
- output: bfloat16 [32, 128, 1024], P(('parts', 'grp')), parts along dimension 0
- grad_first: float32 [2048, 1024], P(('parts', 'grp')), parts along dimension 0
- grad_second: float32 [2048, 1024], P(('parts', 'grp')), parts along dimension 0
There are 2 independent parts, one for each index of `parts`. A program takes and returns all parts, laid end to end along the dimension named above; an argument that names none is the same for every part. Nothing has to cross between parts.
Inputs may be any that keep to these rules, and one draw needn't show every extreme that they name: `counts`: each cluster has 1 to 16 live nodes; some cluster has exactly 16. `pick_owner`: within one row the 8 holders differ; every device holds some picked cluster.
All inputs are finite; a program needn't handle non-finite values.
Results may differ from a plain program's by a relative error of at most 0.0062.
Values may be sent and summed in bfloat16 or wider, within the bound.
No kernel may reach another device: no remote copies, remote signals or barrier semaphores. Data moves between devices by JAX's collectives and lax.ppermute only.
A program may use at most 64 MiB of HBM per device.

v0:
```python
import jax
import jax.numpy as jnp
from jax import lax
from jax.sharding import PartitionSpec as P


def body(features, counts, pick_owner, pick_local, adjacency, cotangent, w_first, w_second):
    owners = pick_owner[0]
    picks = pick_local[0]
    width = w_first.shape[0]
    slots = features.shape[1]
    count_picks = owners.shape[0]
    wanted = owners * features.shape[0] + picks
    blank = (
        jnp.zeros((count_picks, slots, width), jnp.bfloat16),
        jnp.zeros((count_picks,), jnp.int32),
    )
    feat_piece = lax.all_gather(features, "grp", axis=0, tiled=True)
    count_piece = lax.all_gather(counts, "grp", axis=0, tiled=True)
    inside = (wanted >= 0) & (wanted < feat_piece.shape[0])
    where_at = jnp.clip(wanted, 0, feat_piece.shape[0] - 1)
    taken = jnp.take(feat_piece, where_at, axis=0)
    taken_count = jnp.take(count_piece, where_at, axis=0)
    chosen = jnp.where(inside[:, None, None], taken, blank[0])
    live = jnp.where(inside, taken_count, blank[1])
    rows = count_picks * slots
    inputs = chosen.reshape(rows, width)
    mask = (jnp.arange(slots)[None, :] < live[:, None]).reshape(rows, 1).astype(jnp.bfloat16)
    inputs = inputs * mask
    maskf = mask.astype(jnp.float32)
    adj = adjacency[0]
    agg_first = jnp.dot(adj, inputs, preferred_element_type=jnp.float32).astype(jnp.bfloat16)
    pre = jnp.dot(agg_first, w_first, preferred_element_type=jnp.float32)
    hidden = (maskf * jax.nn.silu(pre)).astype(jnp.bfloat16)
    agg_second = jnp.dot(adj, hidden, preferred_element_type=jnp.float32).astype(jnp.bfloat16)
    output = (maskf * jnp.dot(agg_second, w_second, preferred_element_type=jnp.float32)).astype(
        jnp.bfloat16
    )
    dout = cotangent[0] * mask
    columns = dout
    grad_second = lax.psum_scatter(
        lax.dot_general(
            columns, agg_second, (((0,), (0,)), ((), ())), preferred_element_type=jnp.float32
        ),
        "grp",
        scatter_dimension=0,
        tiled=True,
    )
    dagg = lax.dot_general(
        dout, w_second, (((1,), (1,)), ((), ())), preferred_element_type=jnp.float32
    ).astype(jnp.bfloat16)
    back = lax.dot_general(adj, dagg, (((0,), (0,)), ((), ())), preferred_element_type=jnp.float32)
    sig = jax.nn.sigmoid(pre)
    dpre = (maskf * back * sig * (1.0 + pre * (1.0 - sig))).astype(jnp.bfloat16)
    columns = dpre
    grad_first = lax.psum_scatter(
        lax.dot_general(
            columns, agg_first, (((0,), (0,)), ((), ())), preferred_element_type=jnp.float32
        ),
        "grp",
        scatter_dimension=0,
        tiled=True,
    )
    return (output.reshape(1, rows, width), grad_first, grad_second)


def solution(mesh):
    in_specs = (
        P(("parts", "grp"), None, None),
        P(("parts", "grp")),
        P(("parts", "grp"), None),
        P(("parts", "grp"), None),
        P(("parts", "grp"), None, None),
        P(("parts", "grp"), None, None),
        P(),
        P(),
    )
    out_specs = (
        P(("parts", "grp"), None, None),
        P(("parts", "grp"), None),
        P(("parts", "grp"), None),
    )
    return jax.shard_map(body, mesh=mesh, in_specs=in_specs, out_specs=out_specs, check_vma=False)
```

profile of v0, /device:TPU:0, one launch (start us, length us, event | category | flops | bytes accessed | tf_op | source)
XLA Modules:
  0.0 214.1 jit_solution(11854577070770387302)
XLA Ops:
  7.2 0.0 copy-start
  7.2 0.0 all-gather.2.cloned.1.call-start
  7.2 0.7 all-gather.2.cloned.1.call-update
  7.9 0.0 reduce-scatter.3.cloned.1.call-start
  8.0 1.2 dynamic-slice
  9.9 0.9 dynamic-update-slice
  10.7 13.7 %all-reduce = s32[32]{0:T(128)S(1)} all-reduce(s32[32]{0:T(128)S(1)} %dynamic-update-slice), channel_id=1, replica_groups=mesh['parts'=2,'grp'=16] {'grp'}, use_global_device_ids=true, to_apply=%add | all-reduce | flops 32 | bytes 256
  24.5 0.7 fusion.14
  25.1 0.6 gather_fusion
  25.8 0.7 select_select_fusion
  26.5 0.1 fusion.13
  26.6 0.1 reshape.204
  26.6 24.2 %all-gather.2.cloned.1.call-done = bf16[32,16,1024]{2,1,0:T(8,128)(2,1)} async-done(((bf16[2,16,1024]{2,1,0:T(8,128)(2,1)}), bf16[32,16,1024]{2,1,0:T(8,128)(2,1)}) %all-gather.2.cloned.1.call-update) | async-done | bytes 1048592 | tf_op jit(solution)/shard_map/all_gather | solution.py:18
  50.8 1.8 gather_fusion.1
  52.6 0.0 copy-start.1
  52.7 0.0 copy-start.2
  52.7 0.1 select_multiply_fusion
  52.8 1.0 convolution_convert_fusion.2
  53.8 2.1 fusion.16
  55.9 0.0 copy-done
  55.9 0.0 copy-done.1
  55.9 0.0 copy-done.2
  55.9 1.0 fusion.3
  56.9 2.7 %fusion.17 = f32[1024,1024]{1,0:T(8,128)} fusion(bf16[128,1024]{1,0:T(8,128)(2,1)S(1)} %fusion.3, bf16[1024,128]{1,0:T(8,128)(2,1)S(1)} %convolution_convert_fusion.2), kind=kOutput, calls=%fused_computation.35 | convolution fusion | flops 268435456 | bytes 4718592 | tf_op jit(solution)/shard_map/dot_general | solution.py:57
  59.6 0.0 reduce-scatter.3.cloned.1.call-update
  59.6 0.0 reduce-scatter.5.cloned.1.call-start
  59.7 0.3 convolution_convert_fusion.1
  60.0 2.8 %fusion.6 = f32[1024,1024]{1,0:T(8,128)} fusion(bf16[1024,128]{1,0:T(8,128)(2,1)S(1)} %convolution_convert_fusion.1, bf16[1,128,1024]{2,1,0:T(8,128)(2,1)S(1)} %copy-done.1, bf16[128]{0:T(256)(128)(2,1)S(1)} %reshape.204), kind=kOutput, calls=%fused_computation.17 | convolution fusion | flops 268566528 | bytes 4718848 | tf_op jit(solution)/shard_map/dot_general | solution.py:42
  62.8 0.0 reduce-scatter.5.cloned.1.call-update
  62.9 1.2 fusion.5
  64.0 67.0 %reduce-scatter.3.cloned.1.call-done = f32[64,1024]{1,0:T(8,128)} async-done(((f32[1024,1024]{1,0:T(8,128)}), f32[64,1024]{1,0:T(8,128)}) %reduce-scatter.3.cloned.1.call-update) | async-done | bytes 262160 | tf_op jit(solution)/shard_map/reduce_scatter | solution.py:56
  131.0 76.5 %reduce-scatter.5.cloned.1.call-done = f32[64,1024]{1,0:T(8,128)} async-done(((f32[1024,1024]{1,0:T(8,128)}), f32[64,1024]{1,0:T(8,128)}) %reduce-scatter.5.cloned.1.call-update) | async-done | bytes 262160 | tf_op jit(solution)/shard_map/reduce_scatter | solution.py:41
  (3 shorter events, 0.0 us)
Async XLA Ops:
  7.2 48.7 %copy-start = (bf16[1024,1024]{1,0:T(8,128)(2,1)S(1)}, bf16[1024,1024]{1,0:T(8,128)(2,1)}, u32[]{:S(2)}) copy-start(bf16[1024,1024]{1,0:T(8,128)(2,1)} %param.15) | copy-start | bytes 6291460
  7.2 43.7 %all-gather.2.cloned.1.call-start = ((), (), s32[]{:S(2)}) async-start(), calls=%async_computation.2 | async-start | bytes 1114112 | tf_op jit(solution)/shard_map/all_gather | solution.py:18
  7.9 123.1 %reduce-scatter.3.cloned.1.call-start = ((), (), s32[]{:S(2)}) async-start(), calls=%async_computation.3 | async-start | bytes 4456448 | tf_op jit(solution)/shard_map/reduce_scatter | solution.py:56
  52.6 3.2 %copy-start.1 = (bf16[1,128,1024]{2,1,0:T(8,128)(2,1)S(1)}, bf16[1,128,1024]{2,1,0:T(8,128)(2,1)}, u32[]{:S(2)}) copy-start(bf16[1,128,1024]{2,1,0:T(8,128)(2,1)} %param.13) | copy-start | bytes 786436
  52.7 3.2 %copy-start.2 = (bf16[1,128,128]{2,1,0:T(8,128)(2,1)S(1)}, bf16[1,128,128]{2,1,0:T(8,128)(2,1)}, u32[]{:S(2)}) copy-start(bf16[1,128,128]{2,1,0:T(8,128)(2,1)} %param.12) | copy-start | bytes 98308
  59.6 147.9 %reduce-scatter.5.cloned.1.call-start = ((), (), s32[]{:S(2)}) async-start(), calls=%async_computation.4 | async-start | bytes 4456448 | tf_op jit(solution)/shard_map/reduce_scatter | solution.py:41
Sparse Core Ops, SparseCore 0:
  10.2 40.6 all-gather.1
  59.8 71.2 reduce-scatter.2
  136.0 71.5 reduce-scatter.4
where the time goes:
time: 214 us
  waiting for transfers between devices  168 us (79%)
  between operations  14.5 us (7%)
  blocking collectives  13.7 us (6%)
  matrix products  11.1 us (5%)
  local copies, waits for them, and re-layouts  4.64 us (2%)
    reduce_scatter x1, waiting for transfers between devices, body(): lax.psum_scatter(lax.dot_general(columns, agg_second, (((0,), (0,)), ((),...  76.5 us
    reduce_scatter x1, waiting for transfers between devices, body(): lax.psum_scatter(lax.dot_general(columns, agg_first, (((0,), (0,)), ((),...  67 us
    all_gather x1, waiting for transfers between devices, body(): feat_piece = lax.all_gather(features, 'grp', axis=0, tiled=True)  24.2 us
    unnamed x1, blocking collectives  13.7 us
  transfers between devices with their start and end apart: 3, of which 3 were waited for; matrix products, arithmetic and copies ran while one was open for 4% of the time, Pallas kernels for 0%

commit v1 on v0

v1 whole, which is shorter than its diff:
```python
import functools

import jax
import jax.numpy as jnp
from jax import lax
from jax.experimental import pallas as pl
from jax.experimental.pallas import tpu as pltpu
from jax.sharding import PartitionSpec as P

F32 = jnp.float32
BF16 = jnp.bfloat16
VMEM = pl.BlockSpec(memory_space=pltpu.VMEM)
SMEM = pl.BlockSpec(memory_space=pltpu.SMEM)
LANES = 128
META = 16


def nn(a, b):
    return jnp.dot(a, b, preferred_element_type=F32)


def nt(a, b):
    return lax.dot_general(a, b, (((1,), (1,)), ((), ())), preferred_element_type=F32)


def pack_kernel(counts, owner, local, features, adjacency, out):
    own, slots, width = features.shape
    rows = adjacency.shape[1]
    held = own * slots
    slot = lax.broadcasted_iota(jnp.int32, (slots, LANES), 0)
    for i in range(own):
        live = slot < counts[i]
        for b in range(width // LANES):
            block = features[i, :, b * LANES : (b + 1) * LANES]
            at = b * held + i * slots
            out[at : at + slots, :] = jnp.where(live, block, jnp.zeros_like(block))
    at = held * (width // LANES)
    out[at : at + rows, :] = adjacency[0]
    at += rows
    line = lax.broadcasted_iota(jnp.int32, (META, LANES), 0)
    pick = lax.broadcasted_iota(jnp.int32, (META, LANES), 1) // slots
    meta = jnp.zeros((META, LANES), jnp.int32)
    for k in range(owner.shape[1]):
        wanted = owner[0, k] * own + local[0, k]
        meta = jnp.where((line == 0) & (pick == k), wanted, meta)
    for i in range(own):
        meta = jnp.where(line == 1 + i, counts[i], meta)
    out[at : at + META, :] = meta.astype(F32).astype(BF16)


def columns_kernel(cotangent, w_second, out):
    n, both, _ = out.shape
    each = both // 2
    cot = cotangent[0]
    for d in range(n):
        part = cot[:, d * each : (d + 1) * each]
        out[d, :each, :] = part.astype(F32).T.astype(BF16)
    for d in range(n):
        out[d, each:, :] = nt(w_second[d * each : (d + 1) * each, :], cot).astype(BF16)


def step_kernel(n, own, slots, me, *refs):
    packs = refs[:n]
    columns, w_first, w_piece, w_second = refs[n : n + 4]
    output, grad_first, grad_second = refs[n + 4 : n + 7]
    feat, adj, lifted, total = refs[n + 7 :]
    width = w_first.shape[0]
    held = own * slots
    rows = adj.shape[1]
    each = grad_first.shape[0]
    clusters = n * own
    place = me[0]

    for s in range(n):
        for b in range(width // LANES):
            feat[s * held : (s + 1) * held, b * LANES : (b + 1) * LANES] = packs[s][
                b * held : (b + 1) * held, :
            ]
        at = held * (width // LANES)
        adj[s] = packs[s][at : at + rows, :]
    at = held * (width // LANES) + rows
    metas = [packs[s][at : at + META, :].astype(F32) for s in range(n)]
    picks = jnp.concatenate([m[0:1] for m in metas], axis=0).astype(jnp.int32)
    lane = lax.broadcasted_iota(jnp.int32, (n, LANES), 1) % slots
    count = jnp.zeros((n, LANES), jnp.int32)
    for s in range(n):
        for i in range(own):
            cluster = (place ^ s) * own + i
            count = jnp.where(picks == cluster, metas[s][1 + i : 2 + i].astype(jnp.int32), count)
    masks = (lane < count).astype(F32)
    wanted = picks * slots + lane
    code = lax.broadcasted_iota(jnp.int32, (clusters * slots, LANES), 0) ^ (place * held)

    lifted[...] = nn(feat[...], w_first[...]).astype(BF16)
    lifted_piece = nt(w_piece[...], feat[...]).astype(BF16)
    total[...] = jnp.zeros_like(total)

    moved = jnp.zeros((each, clusters * slots), F32)
    for j in range(n):
        chosen = jnp.where(code == wanted[j : j + 1], 1.0, 0.0).astype(BF16)
        spread = nt(adj[j], chosen).astype(BF16)
        pre = nn(spread, lifted[...])
        hidden = (pre / (1.0 + jnp.exp(-pre))).astype(BF16)
        mask = masks[j : j + 1]
        source = columns[place ^ j]
        back = nn((source.astype(F32) * mask).astype(BF16), adj[j]) * mask
        total[...] += nn(back[:each].astype(BF16), hidden)
        pre_piece = nt(lifted_piece, spread)
        sig = 1.0 / (1.0 + jnp.exp(-pre_piece))
        dpre = (back[each:] * sig * (1.0 + pre_piece * (1.0 - sig))).astype(BF16)
        moved += nn(dpre, spread)
        if j == 0:
            live = jnp.broadcast_to(mask, (rows, LANES)).T[:, :1]
            agg = nn(adj[0], (hidden.astype(F32) * live).astype(BF16)).astype(BF16)
            output[0] = (nn(agg, w_second[...]) * live).astype(BF16)
    grad_second[...] = total[...]
    grad_first[...] = nn(moved.astype(BF16), feat[...])


def gather_pieces(piece, n):
    def swap(x, s):
        return lax.ppermute(x, "grp", [(i, i ^ s) for i in range(n)])

    got = {0: piece}
    for s in range(4, n, 4):
        got[s] = swap(piece, s)
    for s in range(0, n, 4):
        if n > 2:
            got[s + 2] = swap(got[s], 2)
    for s in range(0, n, 2):
        if n > 1:
            got[s + 1] = swap(got[s], 1)
    return [got[s] for s in range(n)]


def whole_body(n, features, counts, pick_owner, pick_local, adjacency, cotangent, w_first, w_second):
    own, slots, width = features.shape
    rows = adjacency.shape[1]
    held = own * slots
    each = width // n
    piece_rows = held * (width // LANES) + rows + META
    piece = pl.pallas_call(
        pack_kernel,
        out_shape=jax.ShapeDtypeStruct((piece_rows, LANES), BF16),
        in_specs=[SMEM, SMEM, SMEM, VMEM, VMEM],
        out_specs=VMEM,
    )(counts, pick_owner, pick_local, features, adjacency)
    pieces = gather_pieces(piece, n)
    columns = pl.pallas_call(
        columns_kernel,
        out_shape=jax.ShapeDtypeStruct((n, 2 * each, rows), BF16),
        in_specs=[VMEM, VMEM],
        out_specs=VMEM,
        compiler_params=pltpu.CompilerParams(vmem_limit_bytes=32 * 2**20),
        cost_estimate=pl.CostEstimate(
            flops=2 * rows * width * width, bytes_accessed=3 * 2**20, transcendentals=0
        ),
    )(cotangent, w_second)
    columns = lax.all_to_all(columns, "grp", 0, 0, tiled=True)
    me = lax.axis_index("grp")
    w_piece = lax.dynamic_slice_in_dim(w_first, me * each, each, axis=1).T
    total_rows = n * held
    return pl.pallas_call(
        functools.partial(step_kernel, n, own, slots),
        out_shape=(
            jax.ShapeDtypeStruct((1, rows, width), BF16),
            jax.ShapeDtypeStruct((each, width), F32),
            jax.ShapeDtypeStruct((each, width), F32),
        ),
        in_specs=[SMEM] + [VMEM] * (n + 4),
        out_specs=(VMEM, VMEM, VMEM),
        scratch_shapes=[
            pltpu.VMEM((total_rows, width), BF16),
            pltpu.VMEM((n, rows, rows), BF16),
            pltpu.VMEM((total_rows, width), BF16),
            pltpu.VMEM((each, width), F32),
        ],
        compiler_params=pltpu.CompilerParams(vmem_limit_bytes=48 * 2**20),
        cost_estimate=pl.CostEstimate(
            flops=6 * 10**9, bytes_accessed=10 * 2**20, transcendentals=2 * 10**6
        ),
    )(me.reshape(1).astype(jnp.int32), *pieces, columns, w_first, w_piece, w_second)


def split_body(features, counts, pick_owner, pick_local, adjacency, cotangent, w_first, w_second):
    owners = pick_owner[0]
    picks = pick_local[0]
    width = w_first.shape[0]
    slots = features.shape[1]
    count_picks = owners.shape[0]
    wanted = owners * features.shape[0] + picks
    feat_piece = lax.all_gather(features, "grp", axis=0, tiled=True)
    count_piece = lax.all_gather(counts, "grp", axis=0, tiled=True)
    live = jnp.take(count_piece, wanted, axis=0)
    rows = count_picks * slots
    inputs = jnp.take(feat_piece, wanted, axis=0).reshape(rows, width)
    mask = (jnp.arange(slots)[None, :] < live[:, None]).reshape(rows, 1).astype(BF16)
    inputs = inputs * mask
    maskf = mask.astype(F32)
    adj = adjacency[0]
    agg_first = nn(adj, inputs).astype(BF16)
    pre = nn(agg_first, w_first)
    hidden = (maskf * jax.nn.silu(pre)).astype(BF16)
    agg_second = nn(adj, hidden).astype(BF16)
    output = (maskf * nn(agg_second, w_second)).astype(BF16)
    dout = cotangent[0] * mask

    def summed(a, b):
        part = lax.dot_general(a, b, (((0,), (0,)), ((), ())), preferred_element_type=F32)
        return lax.psum_scatter(part, "grp", scatter_dimension=0, tiled=True)

    grad_second = summed(dout, agg_second)
    dagg = nt(dout, w_second).astype(BF16)
    back = lax.dot_general(adj, dagg, (((0,), (0,)), ((), ())), preferred_element_type=F32)
    sig = jax.nn.sigmoid(pre)
    dpre = (maskf * back * sig * (1.0 + pre * (1.0 - sig))).astype(BF16)
    grad_first = summed(dpre, agg_first)
    return (output.reshape(1, rows, width), grad_first, grad_second)


def solution(mesh):
    n = mesh.shape["grp"]

    def body(*args):
        rows = args[4].shape[1]
        small = n & (n - 1) == 0 and rows == LANES and n * rows <= 4096
        return whole_body(n, *args) if small else split_body(*args)

    in_specs = (
        P(("parts", "grp"), None, None),
        P(("parts", "grp")),
        P(("parts", "grp"), None),
        P(("parts", "grp"), None),
        P(("parts", "grp"), None, None),
        P(("parts", "grp"), None, None),
        P(),
        P(),
    )
    out_specs = (
        P(("parts", "grp"), None, None),
        P(("parts", "grp"), None),
        P(("parts", "grp"), None),
    )
    return jax.shard_map(body, mesh=mesh, in_specs=in_specs, out_specs=out_specs, check_vma=False)
```

time: 214 us -> 64 us (0.30)
  waiting for transfers between devices: 168 us -> 18.4 us
  Pallas kernels: 0 us -> 19.1 us
  starting transfers between devices: 0.12 us -> 18.4 us
  between operations: 14.5 us -> 0.73 us
  blocking collectives: 13.7 us -> 0 us
  matrix products: 11.1 us -> 0 us
  local copies, waits for them, and re-layouts: 4.64 us -> 6.88 us
    reduce_scatter x2 -> x0, waiting for transfers between devices: 144 us -> none  [the longest x1 76.5 us: body(): lax.psum_scatter(lax.dot_general(columns, agg_second, (((0,), (0,)), ((),...]
    all_gather x1 -> x0, waiting for transfers between devices: 24.2 us -> none  [body(): feat_piece = lax.all_gather(features, 'grp', axis=0, tiled=True)]
    pallas_call x0 -> x3, Pallas kernels: none -> 19.1 us  [the longest x1 15.2 us: whole_body(): pl.pallas_call(functools.partial(step_kernel, n, own, slots), out_shape=(...]
    ppermute x0 -> x15, waiting for transfers between devices: none -> 18.4 us  [swap(): return lax.ppermute(x, 'grp', [(i, i ^ s) for i in range(n)])]
    unnamed x1 -> x0, blocking collectives: 13.7 us -> none
    dot_general x7 -> x0, matrix products: 11.1 us -> none  [the longest x1 2.78 us: body(): lax.dot_general(columns, agg_second, (((0,), (0,)), ((), ())), preferred_...]
    ppermute x0 -> x15, starting transfers between devices: none -> 11.1 us  [swap(): return lax.ppermute(x, 'grp', [(i, i ^ s) for i in range(n)])]
    all_to_all x0 -> x1, starting transfers between devices: none -> 7.38 us  [whole_body(): columns = lax.all_to_all(columns, 'grp', 0, 0, tiled=True)]
  transfers between devices with their start and end apart: 3 -> 16, of which waited for: 3 -> 4; matrix products, arithmetic and copies ran while one was open for 4% -> 3% of each run, Pallas kernels for 0% -> 2%
where the time goes in v1:
time: 64 us; the launch traced here: 63.5 us
  Pallas kernels  19.1 us (30%)
  starting transfers between devices  18.4 us (29%)
  waiting for transfers between devices  18.4 us (29%)
  local copies, waits for them, and re-layouts  6.88 us (11%)
  between operations  0.73 us (1%)
    ppermute x15, waiting for transfers between devices, swap(): return lax.ppermute(x, 'grp', [(i, i ^ s) for i in range(n)])  18.4 us
    pallas_call x1, Pallas kernels, whole_body(): pl.pallas_call(functools.partial(step_kernel, n, own, slots), out_shape=(...  15.2 us
    ppermute x15, starting transfers between devices, swap(): return lax.ppermute(x, 'grp', [(i, i ^ s) for i in range(n)])  11.1 us
    all_to_all x1, starting transfers between devices, whole_body(): columns = lax.all_to_all(columns, 'grp', 0, 0, tiled=True)  7.38 us
    unnamed x13, local copies, waits for them, and re-layouts  6.03 us
    pallas_call x1, Pallas kernels, whole_body(): pl.pallas_call(columns_kernel, out_shape=jax.ShapeDtypeStruct((n, 2 * eac...  2.38 us
    pallas_call x1, Pallas kernels, whole_body(): pl.pallas_call(pack_kernel, out_shape=jax.ShapeDtypeStruct((piece_rows, L...  1.53 us
  transfers between devices with their start and end apart: 16, of which 4 were waited for; matrix products, arithmetic and copies ran while one was open for 3% of the time, Pallas kernels for 2%

profile of v1, /device:TPU:0, one launch (start us, length us, event | category | flops | bytes accessed | tf_op | source)
XLA Modules:
  0.0 63.5 jit_solution(8061515908280989115)
XLA Ops:
  0.6 0.0 copy-start
  0.6 1.6 %copy-done = bf16[1024,1024]{1,0:T(8,128)(2,1)S(1)} copy-done((bf16[1024,1024]{1,0:T(8,128)(2,1)S(1)}, bf16[1024,1024]{1,0:T(8,128)(2,1)}, u32[]{:S(2)}) %copy-start) | copy-done | bytes 2097176
  2.2 0.0 copy-start.1
  2.2 0.9 %copy-done.1 = bf16[1,128,1024]{2,1,0:T(8,128)(2,1)S(1)} copy-done((bf16[1,128,1024]{2,1,0:T(8,128)(2,1)S(1)}, bf16[1,128,1024]{2,1,0:T(8,128)(2,1)}, u32[]{:S(2)}) %copy-start.1) | copy-done | bytes 262168
  3.2 0.0 copy-start.3
  3.2 2.4 %shard_map.104 = bf16[16,128,128]{2,1,0:T(8,128)(2,1)} custom-call(bf16[1,128,1024]{2,1,0:T(8,128)(2,1)S(1)} %copy-done.1, bf16[1024,1024]{1,0:T(8,128)(2,1)S(1)} %copy-done), custom_call_target="tpu_custom_call" | custom-call | flops 268435456 | bytes 3145728 | tf_op jit(solution)/shard_map/pallas_call | solution.py:149
  5.6 7.4 %all-to-all-start = ((bf16[16,128,128]{2,1,0:T(8,128)(2,1)}), bf16[16,128,128]{2,1,0:T(8,128)(2,1)S(1)}, u32[]{:S(2)}, u32[]{:S(2)}) async-start(bf16[16,128,128]{2,1,0:T(8,128)(2,1)} %shard_map.104), calls=%async_computation | async-start | bytes 1048576 | tf_op jit(solution)/shard_map/all_to_all | solution.py:159
  12.9 1.5 %shard_map.103.refs_0_ = bf16[400,128]{1,0:T(8,128)(2,1)} custom-call(s32[2]{0:T(128)} %counts.1, s32[1,8]{1,0:T(1,128)} %owner.1, s32[1,8]{1,0:T(1,128)} %local.1, bf16[2,16,1024]{2,1,0:T(8,128)(2,1)} %features.1, bf16[1,128,128]{2,1,0:T(8,128)(2,1)} %adjacency.1), custom_call_target="tpu_custom_call" | custom-call | tf_op jit(solution)/shard_map/pallas_call | solution.py:142
  14.5 3.7 %collective-permute-start.11 = (bf16[400,128]{1,0:T(8,128)(2,1)}, bf16[400,128]{1,0:T(8,128)(2,1)S(1)}, u32[]{:S(2)}, u32[]{:S(2)}) collective-permute-start(bf16[400,128]{1,0:T(8,128)(2,1)} %shard_map.103.refs_0_), channel_id=1, source_target_pairs={{0,12},{1,13},{2,14},{3,15},{4,8},{5,9},{6,10},{7,11},{8,4},{9,5},... | collective-permute-start | bytes 307208 | tf_op jit(solution)/shard_map/ppermute | solution.py:122
  18.2 0.0 collective-permute-start.7
  18.2 0.7 %collective-permute-start.3 = (bf16[400,128]{1,0:T(8,128)(2,1)}, bf16[400,128]{1,0:T(8,128)(2,1)S(1)}, u32[]{:S(2)}, u32[]{:S(2)}) collective-permute-start(bf16[400,128]{1,0:T(8,128)(2,1)} %shard_map.103.refs_0_), channel_id=1, source_target_pairs={{0,4},{1,5},{2,6},{3,7},{4,0},{5,1},{6,2},{7,3},{8,12},{9,13},{10,... | collective-permute-start | bytes 307208 | tf_op jit(solution)/shard_map/ppermute | solution.py:122
  18.9 1.9 %collective-permute-start.1 = (bf16[400,128]{1,0:T(8,128)(2,1)}, bf16[400,128]{1,0:T(8,128)(2,1)S(1)}, u32[]{:S(2)}, u32[]{:S(2)}) collective-permute-start(bf16[400,128]{1,0:T(8,128)(2,1)} %shard_map.103.refs_0_), channel_id=1, source_target_pairs={{0,2},{1,3},{2,0},{3,1},{4,6},{5,7},{6,4},{7,5},{8,10},{9,11},{10,... | collective-permute-start | bytes 307208 | tf_op jit(solution)/shard_map/ppermute | solution.py:122
  20.8 0.0 collective-permute-start
  20.8 8.4 %collective-permute-done.11.refs_12_ = bf16[400,128]{1,0:T(8,128)(2,1)S(1)} collective-permute-done((bf16[400,128]{1,0:T(8,128)(2,1)}, bf16[400,128]{1,0:T(8,128)(2,1)S(1)}, u32[]{:S(2)}, u32[]{:S(2)}) %collective-permute-start.11) | collective-permute-done | bytes 102432 | tf_op jit(solution)/shard_map/ppermute | solution.py:122
  29.2 1.5 %collective-permute-start.13 = (bf16[400,128]{1,0:T(8,128)(2,1)S(1)}, bf16[400,128]{1,0:T(8,128)(2,1)S(1)}, u32[]{:S(2)}, u32[]{:S(2)}) collective-permute-start(bf16[400,128]{1,0:T(8,128)(2,1)S(1)} %collective-permute-done.11.refs_12_), channel_id=1, source_target_pairs={{0,2},{1,3},{2,0},{3,1},{4,6},{5,7},{6,4},{7,5},{8,10},{9,11},{10,... | collective-permute-start | bytes 307208 | tf_op jit(solution)/shard_map/ppermute | solution.py:122
  30.6 6.4 %collective-permute-done.7.refs_8_ = bf16[400,128]{1,0:T(8,128)(2,1)S(1)} collective-permute-done((bf16[400,128]{1,0:T(8,128)(2,1)}, bf16[400,128]{1,0:T(8,128)(2,1)S(1)}, u32[]{:S(2)}, u32[]{:S(2)}) %collective-permute-start.7) | collective-permute-done | bytes 102432 | tf_op jit(solution)/shard_map/ppermute | solution.py:122
  37.0 0.0 collective-permute-start.12
  37.0 0.0 collective-permute-done.3.refs_4_
  37.0 1.5 %collective-permute-start.9 = (bf16[400,128]{1,0:T(8,128)(2,1)S(1)}, bf16[400,128]{1,0:T(8,128)(2,1)}, u32[]{:S(2)}, u32[]{:S(2)}) collective-permute-start(bf16[400,128]{1,0:T(8,128)(2,1)S(1)} %collective-permute-done.7.refs_8_), channel_id=1, source_target_pairs={{0,2},{1,3},{2,0},{3,1},{4,6},{5,7},{6,4},{7,5},{8,10},{9,11},{10,... | collective-permute-start | bytes 307208 | tf_op jit(solution)/shard_map/ppermute | solution.py:122
  38.5 0.0 collective-permute-done.1.refs_2_
  38.5 0.2 collective-permute-start.8
  38.7 0.0 collective-permute-done.refs_1_
  38.7 0.6 collective-permute-start.5
  39.3 0.0 collective-permute-done.13.refs_14_
  39.3 0.0 collective-permute-start.4
  39.3 0.0 collective-permute-done.12.refs_13_
  39.3 0.5 collective-permute-start.2
  39.8 3.0 %collective-permute-done.9.refs_10_ = bf16[400,128]{1,0:T(8,128)(2,1)} collective-permute-done((bf16[400,128]{1,0:T(8,128)(2,1)S(1)}, bf16[400,128]{1,0:T(8,128)(2,1)}, u32[]{:S(2)}, u32[]{:S(2)}) %collective-permute-start.9) | collective-permute-done | bytes 102432 | tf_op jit(solution)/shard_map/ppermute | solution.py:122
  42.8 0.0 collective-permute-start.14
  42.8 0.0 collective-permute-done.8.refs_9_
  42.8 0.0 copy-start.4
  42.8 0.6 %copy-done.4 = bf16[400,128]{1,0:T(8,128)(2,1)} copy-done((bf16[400,128]{1,0:T(8,128)(2,1)}, bf16[400,128]{1,0:T(8,128)(2,1)S(1)}, u32[]{:S(2)}) %copy-start.4) | copy-done | bytes 102424
  43.5 0.5 collective-permute-start.10
  44.0 0.7 %collective-permute-done.5.refs_6_ = bf16[400,128]{1,0:T(8,128)(2,1)} collective-permute-done((bf16[400,128]{1,0:T(8,128)(2,1)S(1)}, bf16[400,128]{1,0:T(8,128)(2,1)}, u32[]{:S(2)}, u32[]{:S(2)}) %collective-permute-start.5) | collective-permute-done | bytes 102432 | tf_op jit(solution)/shard_map/ppermute | solution.py:122
  44.6 0.0 collective-permute-start.6
  44.6 0.0 copy-done.3
  44.6 0.8 %constant_dynamic-slice_fusion = bf16[1024,64]{1,0:T(8,128)(2,1)} fusion(bf16[1024,1024]{1,0:T(8,128)(2,1)S(1)} %copy-done.3, s32[]{:T(128)S(6)} %select_n.3), kind=kLoop, calls=%fused_computation | loop fusion | bytes 262148 | tf_op jit(solution)/shard_map/dynamic_slice | solution.py:161
  45.5 1.1 %copy.12 = bf16[1024,64]{0,1:T(8,128)(2,1)S(1)} copy(bf16[1024,64]{1,0:T(8,128)(2,1)} %constant_dynamic-slice_fusion) | data formatting | bytes 262144
  46.5 0.0 collective-permute-done.4.refs_5_
  46.5 0.0 collective-permute-done.2.refs_3_
  46.6 0.0 collective-permute-done.14.refs_15_
  46.6 0.0 collective-permute-done.10.refs_11_
  46.6 0.0 collective-permute-done.6.refs_7_
  46.6 0.0 all-to-all-done.refs_16_
  46.6 0.0 copy-start.2
  46.6 0.9 %copy-done.2 = bf16[400,128]{1,0:T(8,128)(2,1)S(1)} copy-done((bf16[400,128]{1,0:T(8,128)(2,1)S(1)}, bf16[400,128]{1,0:T(8,128)(2,1)}, u32[]{:S(2)}) %copy-start.2) | copy-done | bytes 102424
  47.5 0.0 copy-start.5
  47.5 0.9 %copy-done.5 = bf16[400,128]{1,0:T(8,128)(2,1)S(1)} copy-done((bf16[400,128]{1,0:T(8,128)(2,1)S(1)}, bf16[400,128]{1,0:T(8,128)(2,1)}, u32[]{:S(2)}) %copy-start.5) | copy-done | bytes 102424
  48.4 15.2 %shard_map.105 = (bf16[1,128,1024]{2,1,0:T(8,128)(2,1)}, f32[64,1024]{1,0:T(8,128)}, f32[64,1024]{1,0:T(8,128)}) custom-call(s32[1]{0:T(128)} %bitcast.me, bf16[400,128]{1,0:T(8,128)(2,1)S(1)} %copy-done.2, bf16[400,128]{1,0:T(8,128)(2,1)S(1)} %collective-permute-done.refs_1_, bf16[400,128]{1,0:T(8,128)(2,1)S(1)} %collective-permute-done.1.refs_2_, ...), custom_call_target="tpu_custom_call" | custom-call | flops 6000000000 | bytes 10485760 | tf_op jit(solution)/shard_map/pallas_call | solution.py:163
Async XLA Ops:
  0.6 1.6 %copy-start = (bf16[1024,1024]{1,0:T(8,128)(2,1)S(1)}, bf16[1024,1024]{1,0:T(8,128)(2,1)}, u32[]{:S(2)}) copy-start(bf16[1024,1024]{1,0:T(8,128)(2,1)} %refs_19_.1) | copy-start | bytes 6291460
  2.2 0.9 %copy-start.1 = (bf16[1,128,1024]{2,1,0:T(8,128)(2,1)S(1)}, bf16[1,128,1024]{2,1,0:T(8,128)(2,1)}, u32[]{:S(2)}) copy-start(bf16[1,128,1024]{2,1,0:T(8,128)(2,1)} %cotangent.1) | copy-start | bytes 786436
  3.2 41.4 %copy-start.3 = (bf16[1024,1024]{1,0:T(8,128)(2,1)S(1)}, bf16[1024,1024]{1,0:T(8,128)(2,1)}, u32[]{:S(2)}) copy-start(bf16[1024,1024]{1,0:T(8,128)(2,1)} %refs_17_.1) | copy-start | bytes 6291460
  5.6 41.0 %all-to-all-start = ((bf16[16,128,128]{2,1,0:T(8,128)(2,1)}), bf16[16,128,128]{2,1,0:T(8,128)(2,1)S(1)}, u32[]{:S(2)}, u32[]{:S(2)}) async-start(bf16[16,128,128]{2,1,0:T(8,128)(2,1)} %shard_map.104), calls=%async_computation | async-start | bytes 1048576 | tf_op jit(solution)/shard_map/all_to_all | solution.py:159
  14.5 14.7 %collective-permute-start.11 = (bf16[400,128]{1,0:T(8,128)(2,1)}, bf16[400,128]{1,0:T(8,128)(2,1)S(1)}, u32[]{:S(2)}, u32[]{:S(2)}) collective-permute-start(bf16[400,128]{1,0:T(8,128)(2,1)} %shard_map.103.refs_0_), channel_id=1, source_target_pairs={{0,12},{1,13},{2,14},{3,15},{4,8},{5,9},{6,10},{7,11},{8,4},{9,5},... | collective-permute-start | bytes 307208 | tf_op jit(solution)/shard_map/ppermute | solution.py:122
  18.2 18.8 %collective-permute-start.7 = (bf16[400,128]{1,0:T(8,128)(2,1)}, bf16[400,128]{1,0:T(8,128)(2,1)S(1)}, u32[]{:S(2)}, u32[]{:S(2)}) collective-permute-start(bf16[400,128]{1,0:T(8,128)(2,1)} %shard_map.103.refs_0_), channel_id=1, source_target_pairs={{0,8},{1,9},{2,10},{3,11},{4,12},{5,13},{6,14},{7,15},{8,0},{9,1},... | collective-permute-start | bytes 307208 | tf_op jit(solution)/shard_map/ppermute | solution.py:122
  18.2 18.8 %collective-permute-start.3 = (bf16[400,128]{1,0:T(8,128)(2,1)}, bf16[400,128]{1,0:T(8,128)(2,1)S(1)}, u32[]{:S(2)}, u32[]{:S(2)}) collective-permute-start(bf16[400,128]{1,0:T(8,128)(2,1)} %shard_map.103.refs_0_), channel_id=1, source_target_pairs={{0,4},{1,5},{2,6},{3,7},{4,0},{5,1},{6,2},{7,3},{8,12},{9,13},{10,... | collective-permute-start | bytes 307208 | tf_op jit(solution)/shard_map/ppermute | solution.py:122
  18.9 19.6 %collective-permute-start.1 = (bf16[400,128]{1,0:T(8,128)(2,1)}, bf16[400,128]{1,0:T(8,128)(2,1)S(1)}, u32[]{:S(2)}, u32[]{:S(2)}) collective-permute-start(bf16[400,128]{1,0:T(8,128)(2,1)} %shard_map.103.refs_0_), channel_id=1, source_target_pairs={{0,2},{1,3},{2,0},{3,1},{4,6},{5,7},{6,4},{7,5},{8,10},{9,11},{10,... | collective-permute-start | bytes 307208 | tf_op jit(solution)/shard_map/ppermute | solution.py:122
  20.8 17.9 %collective-permute-start = (bf16[400,128]{1,0:T(8,128)(2,1)}, bf16[400,128]{1,0:T(8,128)(2,1)S(1)}, u32[]{:S(2)}, u32[]{:S(2)}) collective-permute-start(bf16[400,128]{1,0:T(8,128)(2,1)} %shard_map.103.refs_0_), channel_id=1, source_target_pairs={{0,1},{1,0},{2,3},{3,2},{4,5},{5,4},{6,7},{7,6},{8,9},{9,8},{10,11... | collective-permute-start | bytes 307208 | tf_op jit(solution)/shard_map/ppermute | solution.py:122
  29.2 10.1 %collective-permute-start.13 = (bf16[400,128]{1,0:T(8,128)(2,1)S(1)}, bf16[400,128]{1,0:T(8,128)(2,1)S(1)}, u32[]{:S(2)}, u32[]{:S(2)}) collective-permute-start(bf16[400,128]{1,0:T(8,128)(2,1)S(1)} %collective-permute-done.11.refs_12_), channel_id=1, source_target_pairs={{0,2},{1,3},{2,0},{3,1},{4,6},{5,7},{6,4},{7,5},{8,10},{9,11},{10,... | collective-permute-start | bytes 307208 | tf_op jit(solution)/shard_map/ppermute | solution.py:122
  37.0 2.3 %collective-permute-start.12 = (bf16[400,128]{1,0:T(8,128)(2,1)S(1)}, bf16[400,128]{1,0:T(8,128)(2,1)S(1)}, u32[]{:S(2)}, u32[]{:S(2)}) collective-permute-start(bf16[400,128]{1,0:T(8,128)(2,1)S(1)} %collective-permute-done.11.refs_12_), channel_id=1, source_target_pairs={{0,1},{1,0},{2,3},{3,2},{4,5},{5,4},{6,7},{7,6},{8,9},{9,8},{10,11... | collective-permute-start | bytes 307208 | tf_op jit(solution)/shard_map/ppermute | solution.py:122
  37.0 5.8 %collective-permute-start.9 = (bf16[400,128]{1,0:T(8,128)(2,1)S(1)}, bf16[400,128]{1,0:T(8,128)(2,1)}, u32[]{:S(2)}, u32[]{:S(2)}) collective-permute-start(bf16[400,128]{1,0:T(8,128)(2,1)S(1)} %collective-permute-done.7.refs_8_), channel_id=1, source_target_pairs={{0,2},{1,3},{2,0},{3,1},{4,6},{5,7},{6,4},{7,5},{8,10},{9,11},{10,... | collective-permute-start | bytes 307208 | tf_op jit(solution)/shard_map/ppermute | solution.py:122
  38.5 4.3 %collective-permute-start.8 = (bf16[400,128]{1,0:T(8,128)(2,1)S(1)}, bf16[400,128]{1,0:T(8,128)(2,1)S(1)}, u32[]{:S(2)}, u32[]{:S(2)}) collective-permute-start(bf16[400,128]{1,0:T(8,128)(2,1)S(1)} %collective-permute-done.7.refs_8_), channel_id=1, source_target_pairs={{0,1},{1,0},{2,3},{3,2},{4,5},{5,4},{6,7},{7,6},{8,9},{9,8},{10,11... | collective-permute-start | bytes 307208 | tf_op jit(solution)/shard_map/ppermute | solution.py:122
  38.7 5.9 %collective-permute-start.5 = (bf16[400,128]{1,0:T(8,128)(2,1)S(1)}, bf16[400,128]{1,0:T(8,128)(2,1)}, u32[]{:S(2)}, u32[]{:S(2)}) collective-permute-start(bf16[400,128]{1,0:T(8,128)(2,1)S(1)} %collective-permute-done.3.refs_4_), channel_id=1, source_target_pairs={{0,2},{1,3},{2,0},{3,1},{4,6},{5,7},{6,4},{7,5},{8,10},{9,11},{10,... | collective-permute-start | bytes 307208 | tf_op jit(solution)/shard_map/ppermute | solution.py:122
  39.3 7.3 %collective-permute-start.4 = (bf16[400,128]{1,0:T(8,128)(2,1)S(1)}, bf16[400,128]{1,0:T(8,128)(2,1)}, u32[]{:S(2)}, u32[]{:S(2)}) collective-permute-start(bf16[400,128]{1,0:T(8,128)(2,1)S(1)} %collective-permute-done.3.refs_4_), channel_id=1, source_target_pairs={{0,1},{1,0},{2,3},{3,2},{4,5},{5,4},{6,7},{7,6},{8,9},{9,8},{10,11... | collective-permute-start | bytes 307208 | tf_op jit(solution)/shard_map/ppermute | solution.py:122
  39.3 7.3 %collective-permute-start.2 = (bf16[400,128]{1,0:T(8,128)(2,1)S(1)}, bf16[400,128]{1,0:T(8,128)(2,1)}, u32[]{:S(2)}, u32[]{:S(2)}) collective-permute-start(bf16[400,128]{1,0:T(8,128)(2,1)S(1)} %collective-permute-done.1.refs_2_), channel_id=1, source_target_pairs={{0,1},{1,0},{2,3},{3,2},{4,5},{5,4},{6,7},{7,6},{8,9},{9,8},{10,11... | collective-permute-start | bytes 307208 | tf_op jit(solution)/shard_map/ppermute | solution.py:122
  42.8 3.8 %collective-permute-start.14 = (bf16[400,128]{1,0:T(8,128)(2,1)S(1)}, bf16[400,128]{1,0:T(8,128)(2,1)}, u32[]{:S(2)}, u32[]{:S(2)}) collective-permute-start(bf16[400,128]{1,0:T(8,128)(2,1)S(1)} %collective-permute-done.13.refs_14_), channel_id=1, source_target_pairs={{0,1},{1,0},{2,3},{3,2},{4,5},{5,4},{6,7},{7,6},{8,9},{9,8},{10,11... | collective-permute-start | bytes 307208 | tf_op jit(solution)/shard_map/ppermute | solution.py:122
  42.8 0.6 %copy-start.4 = (bf16[400,128]{1,0:T(8,128)(2,1)}, bf16[400,128]{1,0:T(8,128)(2,1)S(1)}, u32[]{:S(2)}) copy-start(bf16[400,128]{1,0:T(8,128)(2,1)S(1)} %collective-permute-done.8.refs_9_) | copy-start | bytes 307204
  43.5 3.1 %collective-permute-start.10 = (bf16[400,128]{1,0:T(8,128)(2,1)}, bf16[400,128]{1,0:T(8,128)(2,1)}, u32[]{:S(2)}, u32[]{:S(2)}) collective-permute-start(bf16[400,128]{1,0:T(8,128)(2,1)} %collective-permute-done.9.refs_10_), channel_id=1, source_target_pairs={{0,1},{1,0},{2,3},{3,2},{4,5},{5,4},{6,7},{7,6},{8,9},{9,8},{10,11... | collective-permute-start | bytes 307208 | tf_op jit(solution)/shard_map/ppermute | solution.py:122
  44.6 2.0 %collective-permute-start.6 = (bf16[400,128]{1,0:T(8,128)(2,1)}, bf16[400,128]{1,0:T(8,128)(2,1)}, u32[]{:S(2)}, u32[]{:S(2)}) collective-permute-start(bf16[400,128]{1,0:T(8,128)(2,1)} %collective-permute-done.5.refs_6_), channel_id=1, source_target_pairs={{0,1},{1,0},{2,3},{3,2},{4,5},{5,4},{6,7},{7,6},{8,9},{9,8},{10,11... | collective-permute-start | bytes 307208 | tf_op jit(solution)/shard_map/ppermute | solution.py:122
  46.6 0.9 %copy-start.2 = (bf16[400,128]{1,0:T(8,128)(2,1)S(1)}, bf16[400,128]{1,0:T(8,128)(2,1)}, u32[]{:S(2)}) copy-start(bf16[400,128]{1,0:T(8,128)(2,1)} %shard_map.103.refs_0_) | copy-start | bytes 307204
  47.5 0.9 %copy-start.5 = (bf16[400,128]{1,0:T(8,128)(2,1)S(1)}, bf16[400,128]{1,0:T(8,128)(2,1)}, u32[]{:S(2)}) copy-start(bf16[400,128]{1,0:T(8,128)(2,1)} %copy-done.4) | copy-start | bytes 307204

commit v2 on v1

--- a/solution.py
+++ b/solution.py
@@ -48,7 +48,7 @@
     out[at : at + META, :] = meta.astype(F32).astype(BF16)
 
 
-def columns_kernel(cotangent, w_second, out):
+def columns_kernel(me, cotangent, w_second, w_first, out, w_piece):
     n, both, _ = out.shape
     each = both // 2
     cot = cotangent[0]
@@ -57,17 +57,24 @@
         out[d, :each, :] = part.astype(F32).T.astype(BF16)
     for d in range(n):
         out[d, each:, :] = nt(w_second[d * each : (d + 1) * each, :], cot).astype(BF16)
-
-
-def step_kernel(n, own, slots, me, *refs):
+    wide = max(each, LANES)
+    per = wide // each
+    start = pl.multiple_of((me[0] // per) * wide, wide)
+    block = w_first[:, pl.ds(start, wide)].astype(F32).T
+    part = block[:each]
+    for q in range(1, per):
+        part = jnp.where(me[0] % per == q, block[q * each : (q + 1) * each], part)
+    w_piece[...] = part.astype(BF16)
+
+
+def forward_kernel(n, own, slots, me, *refs):
     packs = refs[:n]
-    columns, w_first, w_piece, w_second = refs[n : n + 4]
-    output, grad_first, grad_second = refs[n + 4 : n + 7]
-    feat, adj, lifted, total = refs[n + 7 :]
+    w_first, w_piece, w_second = refs[n : n + 3]
+    output, hidden, spread, feat, adj, masks, pre_piece = refs[n + 3 : n + 10]
+    lifted = refs[n + 10]
     width = w_first.shape[0]
     held = own * slots
     rows = adj.shape[1]
-    each = grad_first.shape[0]
     clusters = n * own
     place = me[0]
 
@@ -87,33 +94,40 @@
         for i in range(own):
             cluster = (place ^ s) * own + i
             count = jnp.where(picks == cluster, metas[s][1 + i : 2 + i].astype(jnp.int32), count)
-    masks = (lane < count).astype(F32)
+    masks[...] = (lane < count).astype(F32)
     wanted = picks * slots + lane
     code = lax.broadcasted_iota(jnp.int32, (clusters * slots, LANES), 0) ^ (place * held)
 
     lifted[...] = nn(feat[...], w_first[...]).astype(BF16)
     lifted_piece = nt(w_piece[...], feat[...]).astype(BF16)
-    total[...] = jnp.zeros_like(total)
-
-    moved = jnp.zeros((each, clusters * slots), F32)
     for j in range(n):
         chosen = jnp.where(code == wanted[j : j + 1], 1.0, 0.0).astype(BF16)
-        spread = nt(adj[j], chosen).astype(BF16)
-        pre = nn(spread, lifted[...])
-        hidden = (pre / (1.0 + jnp.exp(-pre))).astype(BF16)
-        mask = masks[j : j + 1]
-        source = columns[place ^ j]
-        back = nn((source.astype(F32) * mask).astype(BF16), adj[j]) * mask
-        total[...] += nn(back[:each].astype(BF16), hidden)
-        pre_piece = nt(lifted_piece, spread)
-        sig = 1.0 / (1.0 + jnp.exp(-pre_piece))
-        dpre = (back[each:] * sig * (1.0 + pre_piece * (1.0 - sig))).astype(BF16)
-        moved += nn(dpre, spread)
-        if j == 0:
-            live = jnp.broadcast_to(mask, (rows, LANES)).T[:, :1]
-            agg = nn(adj[0], (hidden.astype(F32) * live).astype(BF16)).astype(BF16)
-            output[0] = (nn(agg, w_second[...]) * live).astype(BF16)
-    grad_second[...] = total[...]
+        spread[j * rows : (j + 1) * rows, :] = nt(adj[j], chosen).astype(BF16)
+    step = min(width, 2 * LANES)
+    for c in range(0, width, step):
+        half = 0.5 * nn(spread[...], lifted[:, c : c + step])
+        hidden[:, c : c + step] = (half + half * jnp.tanh(half)).astype(BF16)
+    pre_piece[...] = nt(lifted_piece, spread[...])
+    live = jnp.broadcast_to(masks[0:1, :], (rows, LANES)).T[:, :1]
+    agg = nn(adj[0], (hidden[:rows, :].astype(F32) * live).astype(BF16)).astype(BF16)
+    output[0] = (nn(agg, w_second[...]) * live).astype(BF16)
+
+
+def gradient_kernel(n, me, columns, hidden, spread, feat, adj, masks, pre_piece, grad_first, grad_second, dout, dpre):
+    each = grad_first.shape[0]
+    rows = adj.shape[1]
+    place = me[0]
+    for j in range(n):
+        mask = masks[j : j + 1, :]
+        span = slice(j * rows, (j + 1) * rows)
+        source = columns[place ^ j].astype(F32) * mask
+        back = nn(source.astype(BF16), adj[j]) * mask
+        dout[:, span] = back[:each].astype(BF16)
+        pre = pre_piece[:, span]
+        sig = 0.5 + 0.5 * jnp.tanh(0.5 * pre)
+        dpre[:, span] = (back[each:] * sig * (1.0 + pre * (1.0 - sig))).astype(BF16)
+    grad_second[...] = nn(dout[...], hidden[...])
+    moved = nn(dpre[...], spread[...])
     grad_first[...] = nn(moved.astype(BF16), feat[...])
 
 
@@ -146,40 +160,55 @@
         out_specs=VMEM,
     )(counts, pick_owner, pick_local, features, adjacency)
     pieces = gather_pieces(piece, n)
-    columns = pl.pallas_call(
+    me = lax.axis_index("grp").reshape(1).astype(jnp.int32)
+    limit = pltpu.CompilerParams(vmem_limit_bytes=24 * 2**20)
+    cotangent, _ = lax.optimization_barrier((cotangent, piece))
+    columns, w_piece = pl.pallas_call(
         columns_kernel,
-        out_shape=jax.ShapeDtypeStruct((n, 2 * each, rows), BF16),
-        in_specs=[VMEM, VMEM],
-        out_specs=VMEM,
-        compiler_params=pltpu.CompilerParams(vmem_limit_bytes=32 * 2**20),
+        out_shape=(
+            jax.ShapeDtypeStruct((n, 2 * each, rows), BF16),
+            jax.ShapeDtypeStruct((each, width), BF16),
+        ),
+        in_specs=[SMEM, VMEM, VMEM, VMEM],
+        out_specs=(VMEM, VMEM),
+        compiler_params=limit,
         cost_estimate=pl.CostEstimate(
-            flops=2 * rows * width * width, bytes_accessed=3 * 2**20, transcendentals=0
-        ),
-    )(cotangent, w_second)
+            flops=2 * rows * width * width, bytes_accessed=5 * 2**20, transcendentals=0
+        ),
+    )(me, cotangent, w_second, w_first)
     columns = lax.all_to_all(columns, "grp", 0, 0, tiled=True)
-    me = lax.axis_index("grp")
-    w_piece = lax.dynamic_slice_in_dim(w_first, me * each, each, axis=1).T
     total_rows = n * held
-    return pl.pallas_call(
-        functools.partial(step_kernel, n, own, slots),
+    output, *kept = pl.pallas_call(
+        functools.partial(forward_kernel, n, own, slots),
         out_shape=(
             jax.ShapeDtypeStruct((1, rows, width), BF16),
-            jax.ShapeDtypeStruct((each, width), F32),
-            jax.ShapeDtypeStruct((each, width), F32),
-        ),
-        in_specs=[SMEM] + [VMEM] * (n + 4),
-        out_specs=(VMEM, VMEM, VMEM),
-        scratch_shapes=[
-            pltpu.VMEM((total_rows, width), BF16),
-            pltpu.VMEM((n, rows, rows), BF16),
-            pltpu.VMEM((total_rows, width), BF16),
-            pltpu.VMEM((each, width), F32),
-        ],
-        compiler_params=pltpu.CompilerParams(vmem_limit_bytes=48 * 2**20),
+            jax.ShapeDtypeStruct((n * rows, width), BF16),
+            jax.ShapeDtypeStruct((n * rows, total_rows), BF16),
+            jax.ShapeDtypeStruct((total_rows, width), BF16),
+            jax.ShapeDtypeStruct((n, rows, rows), BF16),
+            jax.ShapeDtypeStruct((n, LANES), F32),
+            jax.ShapeDtypeStruct((each, n * rows), F32),
+        ),
+        in_specs=[SMEM] + [VMEM] * (n + 3),
+        out_specs=(VMEM,) * 7,
+        scratch_shapes=[pltpu.VMEM((total_rows, width), BF16)],
+        compiler_params=limit,
         cost_estimate=pl.CostEstimate(
-            flops=6 * 10**9, bytes_accessed=10 * 2**20, transcendentals=2 * 10**6
-        ),
-    )(me.reshape(1).astype(jnp.int32), *pieces, columns, w_first, w_piece, w_second)
+            flops=4 * 10**9, bytes_accessed=10 * 2**20, transcendentals=2 * 10**6
+        ),
+    )(me, *pieces, w_first, w_piece, w_second)
+    grad_first, grad_second = pl.pallas_call(
+        functools.partial(gradient_kernel, n),
+        out_shape=(jax.ShapeDtypeStruct((each, width), F32),) * 2,
+        in_specs=[SMEM] + [VMEM] * 7,
+        out_specs=(VMEM,) * 2,
+        scratch_shapes=[pltpu.VMEM((each, n * rows), BF16)] * 2,
+        compiler_params=limit,
+        cost_estimate=pl.CostEstimate(
+            flops=10**9, bytes_accessed=8 * 2**20, transcendentals=10**5
+        ),
+    )(me, columns, *kept)
+    return output, grad_first, grad_second
 
 
 def split_body(features, counts, pick_owner, pick_local, adjacency, cotangent, w_first, w_second):

time: 64 us -> 71.3 us (1.11)
  local copies, waits for them, and re-layouts: 6.88 us -> 16.9 us
  Pallas kernels: 19.1 us -> 13 us
  waiting for transfers between devices: 18.4 us -> 21.7 us
    unnamed x13 -> x28, local copies, waits for them, and re-layouts: 6.03 us -> 16.9 us
    pallas_call x2 -> x3, Pallas kernels: 17.5 us -> 11.4 us  [the longest x1 6.52 us: whole_body(): pl.pallas_call(functools.partial(forward_kernel, n, own, slots), out_shap...]
    ppermute x15, waiting for transfers between devices: 18.4 us -> 21.7 us  [swap(): return lax.ppermute(x, 'grp', [(i, i ^ s) for i in range(n)])]
    dynamic_slice x1 -> x0, local copies, waits for them, and re-layouts: 0.85 us -> none  [whole_body(): w_piece = lax.dynamic_slice_in_dim(w_first, me * each, each, axis=1).T]
  transfers between devices with their start and end apart: 16 -> 16, of which waited for: 4 -> 5; matrix products, arithmetic and copies ran while one was open for 3% -> 0% of each run, Pallas kernels for 2% -> 9%
where the time goes in v2:
time: 71.3 us; the launch traced here: 70.8 us
  waiting for transfers between devices  21.7 us (30%)
  starting transfers between devices  18.5 us (26%)
  local copies, waits for them, and re-layouts  16.9 us (24%)
  Pallas kernels  13 us (18%)
    ppermute x15, waiting for transfers between devices, swap(): return lax.ppermute(x, 'grp', [(i, i ^ s) for i in range(n)])  21.7 us
    unnamed x28, local copies, waits for them, and re-layouts  16.9 us
    ppermute x15, starting transfers between devices, swap(): return lax.ppermute(x, 'grp', [(i, i ^ s) for i in range(n)])  11.1 us
    all_to_all x1, starting transfers between devices, whole_body(): columns = lax.all_to_all(columns, 'grp', 0, 0, tiled=True)  7.38 us
    pallas_call x1, Pallas kernels, whole_body(): pl.pallas_call(functools.partial(forward_kernel, n, own, slots), out_shap...  6.52 us
    pallas_call x1, Pallas kernels, whole_body(): pl.pallas_call(functools.partial(gradient_kernel, n), out_shape=(jax.Shap...  2.51 us
    pallas_call x1, Pallas kernels, whole_body(): pl.pallas_call(columns_kernel, out_shape=(jax.ShapeDtypeStruct((n, 2 * ea...  2.39 us
    pallas_call x1, Pallas kernels, whole_body(): pl.pallas_call(pack_kernel, out_shape=jax.ShapeDtypeStruct((piece_rows, L...  1.53 us
  transfers between devices with their start and end apart: 16, of which 5 were waited for; matrix products, arithmetic and copies ran while one was open for 0% of the time, Pallas kernels for 9%

profile of v2, /device:TPU:0, one launch (start us, length us, event | category | flops | bytes accessed | tf_op | source)
XLA Modules:
  0.0 70.8 jit_solution(6771012707760701868)
XLA Ops:
  0.6 1.5 %shard_map.103.refs_0_ = bf16[400,128]{1,0:T(8,128)(2,1)} custom-call(s32[2]{0:T(128)} %counts.1, s32[1,8]{1,0:T(1,128)} %owner.1, s32[1,8]{1,0:T(1,128)} %local.1, bf16[2,16,1024]{2,1,0:T(8,128)(2,1)} %features.1, bf16[1,128,128]{2,1,0:T(8,128)(2,1)} %adjacency.1), custom_call_target="tpu_custom_call" | custom-call | tf_op jit(solution)/shard_map/pallas_call | solution.py:156
  2.2 0.0 copy-start.2
  2.2 1.6 %copy-done.2 = bf16[1024,1024]{1,0:T(8,128)(2,1)S(1)} copy-done((bf16[1024,1024]{1,0:T(8,128)(2,1)S(1)}, bf16[1024,1024]{1,0:T(8,128)(2,1)}, u32[]{:S(2)}) %copy-start.2) | copy-done | bytes 2097176
  3.8 0.0 copy-start.4
  3.8 1.6 %copy-done.4 = bf16[1024,1024]{1,0:T(8,128)(2,1)S(1)} copy-done((bf16[1024,1024]{1,0:T(8,128)(2,1)S(1)}, bf16[1024,1024]{1,0:T(8,128)(2,1)}, u32[]{:S(2)}) %copy-start.4) | copy-done | bytes 2097176
  5.3 0.0 copy-start.12
  5.3 0.9 %copy-done.12 = bf16[1,128,1024]{2,1,0:T(8,128)(2,1)S(1)} copy-done((bf16[1,128,1024]{2,1,0:T(8,128)(2,1)S(1)}, bf16[1,128,1024]{2,1,0:T(8,128)(2,1)}, u32[]{:S(2)}) %copy-start.12) | copy-done | bytes 262168
  6.3 0.0 copy-start.13
  6.3 0.0 copy-start.3
  6.3 2.4 %shard_map.104 = (bf16[16,128,128]{2,1,0:T(8,128)(2,1)}, bf16[64,1024]{1,0:T(8,128)(2,1)S(1)}) custom-call(s32[1]{0:T(128)} %bitcast.me, bf16[1,128,1024]{2,1,0:T(8,128)(2,1)S(1)} %copy-done.12, bf16[1024,1024]{1,0:T(8,128)(2,1)S(1)} %copy-done.4, bf16[1024,1024]{1,0:T(8,128)(2,1)S(1)} %copy-done.2), custom_call_target="tpu_custom_call" | custom-call | flops 268435456 | bytes 5242880 | tf_op jit(solution)/shard_map/pallas_call | solution.py:166
  8.7 7.4 %all-to-all-start = ((bf16[16,128,128]{2,1,0:T(8,128)(2,1)}), bf16[16,128,128]{2,1,0:T(8,128)(2,1)S(1)}, u32[]{:S(2)}, u32[]{:S(2)}) async-start(bf16[16,128,128]{2,1,0:T(8,128)(2,1)} %get-tuple-element.18), calls=%async_computation | async-start | bytes 1048576 | tf_op jit(solution)/shard_map/all_to_all | solution.py:179
  16.1 0.0 copy-done.13
  16.1 3.8 %collective-permute-start.11 = (bf16[400,128]{1,0:T(8,128)(2,1)S(1)}, bf16[400,128]{1,0:T(8,128)(2,1)S(1)}, u32[]{:S(2)}, u32[]{:S(2)}) collective-permute-start(bf16[400,128]{1,0:T(8,128)(2,1)S(1)} %copy-done.13), channel_id=1, source_target_pairs={{0,12},{1,13},{2,14},{3,15},{4,8},{5,9},{6,10},{7,11},{8,4},{9,5},... | collective-permute-start | bytes 307208 | tf_op jit(solution)/shard_map/ppermute | solution.py:136
  19.9 0.0 collective-permute-start.7
  19.9 0.7 collective-permute-start.3
  20.5 1.9 %collective-permute-start.1 = (bf16[400,128]{1,0:T(8,128)(2,1)S(1)}, bf16[400,128]{1,0:T(8,128)(2,1)S(1)}, u32[]{:S(2)}, u32[]{:S(2)}) collective-permute-start(bf16[400,128]{1,0:T(8,128)(2,1)S(1)} %copy-done.13), channel_id=1, source_target_pairs={{0,2},{1,3},{2,0},{3,1},{4,6},{5,7},{6,4},{7,5},{8,10},{9,11},{10,... | collective-permute-start | bytes 307208 | tf_op jit(solution)/shard_map/ppermute | solution.py:136
  22.5 0.0 collective-permute-start
  22.5 9.8 %collective-permute-done.11.refs_12_ = bf16[400,128]{1,0:T(8,128)(2,1)S(1)} collective-permute-done((bf16[400,128]{1,0:T(8,128)(2,1)S(1)}, bf16[400,128]{1,0:T(8,128)(2,1)S(1)}, u32[]{:S(2)}, u32[]{:S(2)}) %collective-permute-start.11) | collective-permute-done | bytes 102432 | tf_op jit(solution)/shard_map/ppermute | solution.py:136
  32.3 1.5 %collective-permute-start.13 = (bf16[400,128]{1,0:T(8,128)(2,1)S(1)}, bf16[400,128]{1,0:T(8,128)(2,1)S(1)}, u32[]{:S(2)}, u32[]{:S(2)}) collective-permute-start(bf16[400,128]{1,0:T(8,128)(2,1)S(1)} %collective-permute-done.11.refs_12_), channel_id=1, source_target_pairs={{0,2},{1,3},{2,0},{3,1},{4,6},{5,7},{6,4},{7,5},{8,10},{9,11},{10,... | collective-permute-start | bytes 307208 | tf_op jit(solution)/shard_map/ppermute | solution.py:136
  33.8 6.4 %collective-permute-done.7.refs_8_ = bf16[400,128]{1,0:T(8,128)(2,1)S(1)} collective-permute-done((bf16[400,128]{1,0:T(8,128)(2,1)S(1)}, bf16[400,128]{1,0:T(8,128)(2,1)S(1)}, u32[]{:S(2)}, u32[]{:S(2)}) %collective-permute-start.7) | collective-permute-done | bytes 102432 | tf_op jit(solution)/shard_map/ppermute | solution.py:136
  40.1 0.0 collective-permute-start.12
  40.1 0.0 collective-permute-done.3.refs_4_
  40.2 1.5 %collective-permute-start.9 = (bf16[400,128]{1,0:T(8,128)(2,1)S(1)}, bf16[400,128]{1,0:T(8,128)(2,1)S(1)}, u32[]{:S(2)}, u32[]{:S(2)}) collective-permute-start(bf16[400,128]{1,0:T(8,128)(2,1)S(1)} %collective-permute-done.7.refs_8_), channel_id=1, source_target_pairs={{0,2},{1,3},{2,0},{3,1},{4,6},{5,7},{6,4},{7,5},{8,10},{9,11},{10,... | collective-permute-start | bytes 307208 | tf_op jit(solution)/shard_map/ppermute | solution.py:136
  41.6 0.0 collective-permute-done.1.refs_2_
  41.6 0.2 collective-permute-start.8
  41.8 0.0 collective-permute-done.refs_1_
  41.9 0.6 collective-permute-start.5
  42.4 0.0 collective-permute-done.13.refs_14_
  42.4 0.0 collective-permute-start.4
  42.4 0.0 collective-permute-done.12.refs_13_
  42.4 0.5 collective-permute-start.2
  42.9 2.9 %collective-permute-done.9.refs_10_ = bf16[400,128]{1,0:T(8,128)(2,1)S(1)} collective-permute-done((bf16[400,128]{1,0:T(8,128)(2,1)S(1)}, bf16[400,128]{1,0:T(8,128)(2,1)S(1)}, u32[]{:S(2)}, u32[]{:S(2)}) %collective-permute-start.9) | collective-permute-done | bytes 102432 | tf_op jit(solution)/shard_map/ppermute | solution.py:136
  45.8 0.0 collective-permute-start.14
  45.8 0.0 collective-permute-done.8.refs_9_
  45.8 0.5 collective-permute-start.10
  46.3 1.3 %collective-permute-done.5.refs_6_ = bf16[400,128]{1,0:T(8,128)(2,1)S(1)} collective-permute-done((bf16[400,128]{1,0:T(8,128)(2,1)S(1)}, bf16[400,128]{1,0:T(8,128)(2,1)S(1)}, u32[]{:S(2)}, u32[]{:S(2)}) %collective-permute-start.5) | collective-permute-done | bytes 102432 | tf_op jit(solution)/shard_map/ppermute | solution.py:136
  47.6 0.0 collective-permute-start.6
  47.6 0.0 collective-permute-done.4.refs_5_
  47.6 0.0 collective-permute-done.2.refs_3_
  47.7 0.0 collective-permute-done.14.refs_15_
  47.7 0.0 collective-permute-done.10.refs_11_
  47.7 1.3 %collective-permute-done.6.refs_7_ = bf16[400,128]{1,0:T(8,128)(2,1)S(1)} collective-permute-done((bf16[400,128]{1,0:T(8,128)(2,1)S(1)}, bf16[400,128]{1,0:T(8,128)(2,1)S(1)}, u32[]{:S(2)}, u32[]{:S(2)}) %collective-permute-start.6) | collective-permute-done | bytes 102432 | tf_op jit(solution)/shard_map/ppermute | solution.py:136
  48.9 0.0 copy-done.3
  49.0 0.0 copy-start.5
  49.0 1.6 %copy-done.5 = bf16[1024,1024]{1,0:T(8,128)(2,1)S(1)} copy-done((bf16[1024,1024]{1,0:T(8,128)(2,1)S(1)}, bf16[1024,1024]{1,0:T(8,128)(2,1)}, u32[]{:S(2)}) %copy-start.5) | copy-done | bytes 2097176
  50.5 6.5 %shard_map.105 = (bf16[1,128,1024]{2,1,0:T(8,128)(2,1)}, bf16[2048,1024]{1,0:T(8,128)(2,1)S(1)}, bf16[2048,512]{1,0:T(8,128)(2,1)S(1)}, bf16[512,1024]{1,0:T(8,1...) custom-call(s32[1]{0:T(128)} %bitcast.me, ...), custom_call_target="tpu_custom_call" | custom-call | flops 4000000000 | bytes 10485760 | tf_op jit(solution)/shard_map/pallas_call | solution.py:181
  57.1 0.0 copy-start
  57.1 2.0 %copy-done = bf16[2048,1024]{1,0:T(8,128)(2,1)} copy-done((bf16[2048,1024]{1,0:T(8,128)(2,1)}, bf16[2048,1024]{1,0:T(8,128)(2,1)S(1)}, u32[]{:S(2)}) %copy-start) | copy-done | bytes 4194328
  59.0 0.0 copy-start.6
  59.0 1.4 %copy-done.6 = bf16[2048,512]{1,0:T(8,128)(2,1)} copy-done((bf16[2048,512]{1,0:T(8,128)(2,1)}, bf16[2048,512]{1,0:T(8,128)(2,1)S(1)}, u32[]{:S(2)}) %copy-start.6) | copy-done | bytes 2097176
  60.4 0.0 copy-start.8
  60.4 1.0 %copy-done.8 = bf16[512,1024]{1,0:T(8,128)(2,1)} copy-done((bf16[512,1024]{1,0:T(8,128)(2,1)}, bf16[512,1024]{1,0:T(8,128)(2,1)S(1)}, u32[]{:S(2)}) %copy-start.8) | copy-done | bytes 1048600
  61.4 0.0 copy-start.10
  61.4 0.8 %copy-done.10 = f32[64,2048]{1,0:T(8,128)} copy-done((f32[64,2048]{1,0:T(8,128)}, f32[64,2048]{1,0:T(8,128)S(1)}, u32[]{:S(2)}) %copy-start.10) | copy-done | bytes 524312
  62.2 0.0 all-to-all-done.columns
  62.2 0.0 copy-start.1
  62.2 2.2 %copy-done.1 = bf16[2048,1024]{1,0:T(8,128)(2,1)S(1)} copy-done((bf16[2048,1024]{1,0:T(8,128)(2,1)S(1)}, bf16[2048,1024]{1,0:T(8,128)(2,1)}, u32[]{:S(2)}) %copy-start.1) | copy-done | bytes 4194328
  64.4 0.0 copy-start.7
  64.4 1.6 %copy-done.7 = bf16[2048,512]{1,0:T(8,128)(2,1)S(1)} copy-done((bf16[2048,512]{1,0:T(8,128)(2,1)S(1)}, bf16[2048,512]{1,0:T(8,128)(2,1)}, u32[]{:S(2)}) %copy-start.7) | copy-done | bytes 2097176
  66.0 0.0 copy-start.9
  66.0 1.2 %copy-done.9 = bf16[512,1024]{1,0:T(8,128)(2,1)S(1)} copy-done((bf16[512,1024]{1,0:T(8,128)(2,1)S(1)}, bf16[512,1024]{1,0:T(8,128)(2,1)}, u32[]{:S(2)}) %copy-start.9) | copy-done | bytes 1048600
  67.2 0.0 copy-start.11
  67.2 1.0 %copy-done.11 = f32[64,2048]{1,0:T(8,128)S(1)} copy-done((f32[64,2048]{1,0:T(8,128)S(1)}, f32[64,2048]{1,0:T(8,128)}, u32[]{:S(2)}) %copy-start.11) | copy-done | bytes 524312
  68.3 2.5 %shard_map.106 = (f32[64,1024]{1,0:T(8,128)}, f32[64,1024]{1,0:T(8,128)}) custom-call(s32[1]{0:T(128)} %bitcast.me, bf16[16,128,128]{2,1,0:T(8,128)(2,1)S(1)} %all-to-all-done.columns, bf16[2048,1024]{1,0:T(8,128)(2,1)S(1)} %copy-done.1, bf16[2048,512]{1,0:T(8,128)(2,1)S(1)} %copy-done.7, bf16[512,1024]{1,0:T(8,128)(2,1)S(1)} %copy-done.9, ...), custom_call_target="tpu_custom_call" | custom-call | flops 1000000000 | bytes 8388608 | tf_op jit(solution)/shard_map/pallas_call | solution.py:200
Async XLA Ops:
  2.2 1.6 %copy-start.2 = (bf16[1024,1024]{1,0:T(8,128)(2,1)S(1)}, bf16[1024,1024]{1,0:T(8,128)(2,1)}, u32[]{:S(2)}) copy-start(bf16[1024,1024]{1,0:T(8,128)(2,1)} %refs_16_.1) | copy-start | bytes 6291460
  3.8 1.6 %copy-start.4 = (bf16[1024,1024]{1,0:T(8,128)(2,1)S(1)}, bf16[1024,1024]{1,0:T(8,128)(2,1)}, u32[]{:S(2)}) copy-start(bf16[1024,1024]{1,0:T(8,128)(2,1)} %refs_18_.1) | copy-start | bytes 6291460
  5.3 0.9 %copy-start.12 = (bf16[1,128,1024]{2,1,0:T(8,128)(2,1)S(1)}, bf16[1,128,1024]{2,1,0:T(8,128)(2,1)}, u32[]{:S(2)}) copy-start(bf16[1,128,1024]{2,1,0:T(8,128)(2,1)} %cotangent) | copy-start | bytes 786436
  6.3 9.8 %copy-start.13 = (bf16[400,128]{1,0:T(8,128)(2,1)S(1)}, bf16[400,128]{1,0:T(8,128)(2,1)}, u32[]{:S(2)}) copy-start(bf16[400,128]{1,0:T(8,128)(2,1)} %shard_map.103.refs_0_) | copy-start | bytes 307204
  6.3 42.7 %copy-start.3 = (bf16[1024,1024]{1,0:T(8,128)(2,1)S(1)}, bf16[1024,1024]{1,0:T(8,128)(2,1)}, u32[]{:S(2)}) copy-start(bf16[1024,1024]{1,0:T(8,128)(2,1)} %refs_16_.1) | copy-start | bytes 6291460
  8.7 53.5 %all-to-all-start = ((bf16[16,128,128]{2,1,0:T(8,128)(2,1)}), bf16[16,128,128]{2,1,0:T(8,128)(2,1)S(1)}, u32[]{:S(2)}, u32[]{:S(2)}) async-start(bf16[16,128,128]{2,1,0:T(8,128)(2,1)} %get-tuple-element.18), calls=%async_computation | async-start | bytes 1048576 | tf_op jit(solution)/shard_map/all_to_all | solution.py:179
  16.1 16.2 %collective-permute-start.11 = (bf16[400,128]{1,0:T(8,128)(2,1)S(1)}, bf16[400,128]{1,0:T(8,128)(2,1)S(1)}, u32[]{:S(2)}, u32[]{:S(2)}) collective-permute-start(bf16[400,128]{1,0:T(8,128)(2,1)S(1)} %copy-done.13), channel_id=1, source_target_pairs={{0,12},{1,13},{2,14},{3,15},{4,8},{5,9},{6,10},{7,11},{8,4},{9,5},... | collective-permute-start | bytes 307208 | tf_op jit(solution)/shard_map/ppermute | solution.py:136
  19.9 20.3 %collective-permute-start.7 = (bf16[400,128]{1,0:T(8,128)(2,1)S(1)}, bf16[400,128]{1,0:T(8,128)(2,1)S(1)}, u32[]{:S(2)}, u32[]{:S(2)}) collective-permute-start(bf16[400,128]{1,0:T(8,128)(2,1)S(1)} %copy-done.13), channel_id=1, source_target_pairs={{0,8},{1,9},{2,10},{3,11},{4,12},{5,13},{6,14},{7,15},{8,0},{9,1},... | collective-permute-start | bytes 307208 | tf_op jit(solution)/shard_map/ppermute | solution.py:136
  19.9 20.3 %collective-permute-start.3 = (bf16[400,128]{1,0:T(8,128)(2,1)S(1)}, bf16[400,128]{1,0:T(8,128)(2,1)S(1)}, u32[]{:S(2)}, u32[]{:S(2)}) collective-permute-start(bf16[400,128]{1,0:T(8,128)(2,1)S(1)} %copy-done.13), channel_id=1, source_target_pairs={{0,4},{1,5},{2,6},{3,7},{4,0},{5,1},{6,2},{7,3},{8,12},{9,13},{10,... | collective-permute-start | bytes 307208 | tf_op jit(solution)/shard_map/ppermute | solution.py:136
  20.5 21.1 %collective-permute-start.1 = (bf16[400,128]{1,0:T(8,128)(2,1)S(1)}, bf16[400,128]{1,0:T(8,128)(2,1)S(1)}, u32[]{:S(2)}, u32[]{:S(2)}) collective-permute-start(bf16[400,128]{1,0:T(8,128)(2,1)S(1)} %copy-done.13), channel_id=1, source_target_pairs={{0,2},{1,3},{2,0},{3,1},{4,6},{5,7},{6,4},{7,5},{8,10},{9,11},{10,... | collective-permute-start | bytes 307208 | tf_op jit(solution)/shard_map/ppermute | solution.py:136
  22.5 19.4 %collective-permute-start = (bf16[400,128]{1,0:T(8,128)(2,1)S(1)}, bf16[400,128]{1,0:T(8,128)(2,1)S(1)}, u32[]{:S(2)}, u32[]{:S(2)}) collective-permute-start(bf16[400,128]{1,0:T(8,128)(2,1)S(1)} %copy-done.13), channel_id=1, source_target_pairs={{0,1},{1,0},{2,3},{3,2},{4,5},{5,4},{6,7},{7,6},{8,9},{9,8},{10,11... | collective-permute-start | bytes 307208 | tf_op jit(solution)/shard_map/ppermute | solution.py:136
  32.3 10.1 %collective-permute-start.13 = (bf16[400,128]{1,0:T(8,128)(2,1)S(1)}, bf16[400,128]{1,0:T(8,128)(2,1)S(1)}, u32[]{:S(2)}, u32[]{:S(2)}) collective-permute-start(bf16[400,128]{1,0:T(8,128)(2,1)S(1)} %collective-permute-done.11.refs_12_), channel_id=1, source_target_pairs={{0,2},{1,3},{2,0},{3,1},{4,6},{5,7},{6,4},{7,5},{8,10},{9,11},{10,... | collective-permute-start | bytes 307208 | tf_op jit(solution)/shard_map/ppermute | solution.py:136
  40.1 2.3 %collective-permute-start.12 = (bf16[400,128]{1,0:T(8,128)(2,1)S(1)}, bf16[400,128]{1,0:T(8,128)(2,1)S(1)}, u32[]{:S(2)}, u32[]{:S(2)}) collective-permute-start(bf16[400,128]{1,0:T(8,128)(2,1)S(1)} %collective-permute-done.11.refs_12_), channel_id=1, source_target_pairs={{0,1},{1,0},{2,3},{3,2},{4,5},{5,4},{6,7},{7,6},{8,9},{9,8},{10,11... | collective-permute-start | bytes 307208 | tf_op jit(solution)/shard_map/ppermute | solution.py:136
  40.2 5.7 %collective-permute-start.9 = (bf16[400,128]{1,0:T(8,128)(2,1)S(1)}, bf16[400,128]{1,0:T(8,128)(2,1)S(1)}, u32[]{:S(2)}, u32[]{:S(2)}) collective-permute-start(bf16[400,128]{1,0:T(8,128)(2,1)S(1)} %collective-permute-done.7.refs_8_), channel_id=1, source_target_pairs={{0,2},{1,3},{2,0},{3,1},{4,6},{5,7},{6,4},{7,5},{8,10},{9,11},{10,... | collective-permute-start | bytes 307208 | tf_op jit(solution)/shard_map/ppermute | solution.py:136
  41.6 4.2 %collective-permute-start.8 = (bf16[400,128]{1,0:T(8,128)(2,1)S(1)}, bf16[400,128]{1,0:T(8,128)(2,1)S(1)}, u32[]{:S(2)}, u32[]{:S(2)}) collective-permute-start(bf16[400,128]{1,0:T(8,128)(2,1)S(1)} %collective-permute-done.7.refs_8_), channel_id=1, source_target_pairs={{0,1},{1,0},{2,3},{3,2},{4,5},{5,4},{6,7},{7,6},{8,9},{9,8},{10,11... | collective-permute-start | bytes 307208 | tf_op jit(solution)/shard_map/ppermute | solution.py:136
  41.9 5.8 %collective-permute-start.5 = (bf16[400,128]{1,0:T(8,128)(2,1)S(1)}, bf16[400,128]{1,0:T(8,128)(2,1)S(1)}, u32[]{:S(2)}, u32[]{:S(2)}) collective-permute-start(bf16[400,128]{1,0:T(8,128)(2,1)S(1)} %collective-permute-done.3.refs_4_), channel_id=1, source_target_pairs={{0,2},{1,3},{2,0},{3,1},{4,6},{5,7},{6,4},{7,5},{8,10},{9,11},{10,... | collective-permute-start | bytes 307208 | tf_op jit(solution)/shard_map/ppermute | solution.py:136
  42.4 5.2 %collective-permute-start.4 = (bf16[400,128]{1,0:T(8,128)(2,1)S(1)}, bf16[400,128]{1,0:T(8,128)(2,1)S(1)}, u32[]{:S(2)}, u32[]{:S(2)}) collective-permute-start(bf16[400,128]{1,0:T(8,128)(2,1)S(1)} %collective-permute-done.3.refs_4_), channel_id=1, source_target_pairs={{0,1},{1,0},{2,3},{3,2},{4,5},{5,4},{6,7},{7,6},{8,9},{9,8},{10,11... | collective-permute-start | bytes 307208 | tf_op jit(solution)/shard_map/ppermute | solution.py:136
  42.4 5.2 %collective-permute-start.2 = (bf16[400,128]{1,0:T(8,128)(2,1)S(1)}, bf16[400,128]{1,0:T(8,128)(2,1)S(1)}, u32[]{:S(2)}, u32[]{:S(2)}) collective-permute-start(bf16[400,128]{1,0:T(8,128)(2,1)S(1)} %collective-permute-done.1.refs_2_), channel_id=1, source_target_pairs={{0,1},{1,0},{2,3},{3,2},{4,5},{5,4},{6,7},{7,6},{8,9},{9,8},{10,11... | collective-permute-start | bytes 307208 | tf_op jit(solution)/shard_map/ppermute | solution.py:136
  45.8 1.8 %collective-permute-start.14 = (bf16[400,128]{1,0:T(8,128)(2,1)S(1)}, bf16[400,128]{1,0:T(8,128)(2,1)S(1)}, u32[]{:S(2)}, u32[]{:S(2)}) collective-permute-start(bf16[400,128]{1,0:T(8,128)(2,1)S(1)} %collective-permute-done.13.refs_14_), channel_id=1, source_target_pairs={{0,1},{1,0},{2,3},{3,2},{4,5},{5,4},{6,7},{7,6},{8,9},{9,8},{10,11... | collective-permute-start | bytes 307208 | tf_op jit(solution)/shard_map/ppermute | solution.py:136
  45.8 1.8 %collective-permute-start.10 = (bf16[400,128]{1,0:T(8,128)(2,1)S(1)}, bf16[400,128]{1,0:T(8,128)(2,1)S(1)}, u32[]{:S(2)}, u32[]{:S(2)}) collective-permute-start(bf16[400,128]{1,0:T(8,128)(2,1)S(1)} %collective-permute-done.9.refs_10_), channel_id=1, source_target_pairs={{0,1},{1,0},{2,3},{3,2},{4,5},{5,4},{6,7},{7,6},{8,9},{9,8},{10,11... | collective-permute-start | bytes 307208 | tf_op jit(solution)/shard_map/ppermute | solution.py:136
  47.6 1.3 %collective-permute-start.6 = (bf16[400,128]{1,0:T(8,128)(2,1)S(1)}, bf16[400,128]{1,0:T(8,128)(2,1)S(1)}, u32[]{:S(2)}, u32[]{:S(2)}) collective-permute-start(bf16[400,128]{1,0:T(8,128)(2,1)S(1)} %collective-permute-done.5.refs_6_), channel_id=1, source_target_pairs={{0,1},{1,0},{2,3},{3,2},{4,5},{5,4},{6,7},{7,6},{8,9},{9,8},{10,11... | collective-permute-start | bytes 307208 | tf_op jit(solution)/shard_map/ppermute | solution.py:136
  49.0 1.6 %copy-start.5 = (bf16[1024,1024]{1,0:T(8,128)(2,1)S(1)}, bf16[1024,1024]{1,0:T(8,128)(2,1)}, u32[]{:S(2)}) copy-start(bf16[1024,1024]{1,0:T(8,128)(2,1)} %refs_18_.1) | copy-start | bytes 6291460
  57.1 2.0 %copy-start = (bf16[2048,1024]{1,0:T(8,128)(2,1)}, bf16[2048,1024]{1,0:T(8,128)(2,1)S(1)}, u32[]{:S(2)}) copy-start(bf16[2048,1024]{1,0:T(8,128)(2,1)S(1)} %get-tuple-element.19.hidden) | copy-start | bytes 12582916
  59.0 1.4 %copy-start.6 = (bf16[2048,512]{1,0:T(8,128)(2,1)}, bf16[2048,512]{1,0:T(8,128)(2,1)S(1)}, u32[]{:S(2)}) copy-start(bf16[2048,512]{1,0:T(8,128)(2,1)S(1)} %get-tuple-element.20.spread) | copy-start | bytes 6291460
  60.4 1.0 %copy-start.8 = (bf16[512,1024]{1,0:T(8,128)(2,1)}, bf16[512,1024]{1,0:T(8,128)(2,1)S(1)}, u32[]{:S(2)}) copy-start(bf16[512,1024]{1,0:T(8,128)(2,1)S(1)} %get-tuple-element.21.feat) | copy-start | bytes 3145732
  61.4 0.9 %copy-start.10 = (f32[64,2048]{1,0:T(8,128)}, f32[64,2048]{1,0:T(8,128)S(1)}, u32[]{:S(2)}) copy-start(f32[64,2048]{1,0:T(8,128)S(1)} %get-tuple-element.24.pre_piece) | copy-start | bytes 1572868
  62.2 2.2 %copy-start.1 = (bf16[2048,1024]{1,0:T(8,128)(2,1)S(1)}, bf16[2048,1024]{1,0:T(8,128)(2,1)}, u32[]{:S(2)}) copy-start(bf16[2048,1024]{1,0:T(8,128)(2,1)} %copy-done) | copy-start | bytes 12582916
  64.4 1.6 %copy-start.7 = (bf16[2048,512]{1,0:T(8,128)(2,1)S(1)}, bf16[2048,512]{1,0:T(8,128)(2,1)}, u32[]{:S(2)}) copy-start(bf16[2048,512]{1,0:T(8,128)(2,1)} %copy-done.6) | copy-start | bytes 6291460
  66.0 1.2 %copy-start.9 = (bf16[512,1024]{1,0:T(8,128)(2,1)S(1)}, bf16[512,1024]{1,0:T(8,128)(2,1)}, u32[]{:S(2)}) copy-start(bf16[512,1024]{1,0:T(8,128)(2,1)} %copy-done.8) | copy-start | bytes 3145732
  67.2 1.0 %copy-start.11 = (f32[64,2048]{1,0:T(8,128)S(1)}, f32[64,2048]{1,0:T(8,128)}, u32[]{:S(2)}) copy-start(f32[64,2048]{1,0:T(8,128)} %copy-done.10) | copy-start | bytes 1572868

commit v3 on v2

--- a/solution.py
+++ b/solution.py
@@ -11,6 +11,8 @@
 BF16 = jnp.bfloat16
 VMEM = pl.BlockSpec(memory_space=pltpu.VMEM)
 SMEM = pl.BlockSpec(memory_space=pltpu.SMEM)
+HBM = pl.BlockSpec(memory_space=pltpu.HBM)
+PLANE = 4
 LANES = 128
 META = 16
 
@@ -48,45 +50,71 @@
     out[at : at + META, :] = meta.astype(F32).astype(BF16)
 
 
-def columns_kernel(me, cotangent, w_second, w_first, out, w_piece):
-    n, both, _ = out.shape
-    each = both // 2
-    cot = cotangent[0]
-    for d in range(n):
-        part = cot[:, d * each : (d + 1) * each]
-        out[d, :each, :] = part.astype(F32).T.astype(BF16)
-    for d in range(n):
-        out[d, each:, :] = nt(w_second[d * each : (d + 1) * each, :], cot).astype(BF16)
-    wide = max(each, LANES)
+def columns_kernel(me, cotangent, w_second, w_first, *refs):
+    *outs, w_piece, turned, back, second, strip, sems = refs
+    each = w_piece.shape[0]
+    wide = strip.shape[1]
     per = wide // each
     start = pl.multiple_of((me[0] // per) * wide, wide)
-    block = w_first[:, pl.ds(start, wide)].astype(F32).T
+    weights = pltpu.make_async_copy(w_second, second, sems.at[0])
+    weights.start()
+    columns = pltpu.make_async_copy(w_first.at[:, pl.ds(start, wide)], strip, sems.at[1])
+    columns.start()
+    cot = cotangent[0]
+    turned[...] = cot.astype(F32).T.astype(BF16)
+    weights.wait()
+    back[...] = nt(second[...], cot).astype(BF16)
+    for q, out in enumerate(outs):
+        for s in range(out.shape[0] // (2 * each)):
+            span = pl.ds(pl.multiple_of((me[0] ^ (PLANE * s + q)) * each, each), each)
+            at = s * 2 * each
+            out[at : at + each, :] = turned[span, :]
+            out[at + each : at + 2 * each, :] = back[span, :]
+    columns.wait()
+    block = strip[...].astype(F32).T
     part = block[:each]
     for q in range(1, per):
         part = jnp.where(me[0] % per == q, block[q * each : (q + 1) * each], part)
     w_piece[...] = part.astype(BF16)
 
 
+def regroup_kernel(parts, *refs):
+    pieces, columns = refs[:parts], refs[parts : parts + PLANE]
+    stack, *sent = refs[parts + PLANE :]
+    rows = pieces[0].shape[0]
+    for i, ref in enumerate(pieces):
+        stack[i * rows : (i + 1) * rows, :] = ref[...]
+    rows = sent[0].shape[0] // PLANE
+    for s, out in enumerate(sent, 1):
+        for q, ref in enumerate(columns):
+            out[q * rows : (q + 1) * rows, :] = ref[s * rows : (s + 1) * rows, :]
+
+
 def forward_kernel(n, own, slots, me, *refs):
-    packs = refs[:n]
-    w_first, w_piece, w_second = refs[n : n + 3]
-    output, hidden, spread, feat, adj, masks, pre_piece = refs[n + 3 : n + 10]
-    lifted = refs[n + 10]
+    packs = refs[:PLANE]
+    w_first, w_piece, w_second = refs[PLANE : PLANE + 3]
+    output, hidden, spread, feat, adj, masks, pre_piece = refs[PLANE + 3 : PLANE + 10]
+    lifted, first, second, sems = refs[PLANE + 10 :]
+    first_copy = pltpu.make_async_copy(w_first, first, sems.at[0])
+    first_copy.start()
+    second_copy = pltpu.make_async_copy(w_second, second, sems.at[1])
+    second_copy.start()
     width = w_first.shape[0]
     held = own * slots
     rows = adj.shape[1]
     clusters = n * own
     place = me[0]
-
+    deep = held * (width // LANES) + rows + META
+
+    metas = []
     for s in range(n):
+        pack, at = packs[s % PLANE], (s // PLANE) * deep
         for b in range(width // LANES):
-            feat[s * held : (s + 1) * held, b * LANES : (b + 1) * LANES] = packs[s][
-                b * held : (b + 1) * held, :
-            ]
-        at = held * (width // LANES)
-        adj[s] = packs[s][at : at + rows, :]
-    at = held * (width // LANES) + rows
-    metas = [packs[s][at : at + META, :].astype(F32) for s in range(n)]
+            feat[s * held : (s + 1) * held, b * LANES : (b + 1) * LANES] = pack[at : at + held, :]
+            at += held
+        adj[s] = pack[at : at + rows, :]
+        at += rows
+        metas.append(pack[at : at + META, :].astype(F32))
     picks = jnp.concatenate([m[0:1] for m in metas], axis=0).astype(jnp.int32)
     lane = lax.broadcasted_iota(jnp.int32, (n, LANES), 1) % slots
     count = jnp.zeros((n, LANES), jnp.int32)
@@ -98,11 +126,12 @@
     wanted = picks * slots + lane
     code = lax.broadcasted_iota(jnp.int32, (clusters * slots, LANES), 0) ^ (place * held)
 
-    lifted[...] = nn(feat[...], w_first[...]).astype(BF16)
-    lifted_piece = nt(w_piece[...], feat[...]).astype(BF16)
     for j in range(n):
         chosen = jnp.where(code == wanted[j : j + 1], 1.0, 0.0).astype(BF16)
         spread[j * rows : (j + 1) * rows, :] = nt(adj[j], chosen).astype(BF16)
+    first_copy.wait()
+    lifted[...] = nn(feat[...], first[...]).astype(BF16)
+    lifted_piece = nt(w_piece[...], feat[...]).astype(BF16)
     step = min(width, 2 * LANES)
     for c in range(0, width, step):
         half = 0.5 * nn(spread[...], lifted[:, c : c + step])
@@ -110,18 +139,22 @@
     pre_piece[...] = nt(lifted_piece, spread[...])
     live = jnp.broadcast_to(masks[0:1, :], (rows, LANES)).T[:, :1]
     agg = nn(adj[0], (hidden[:rows, :].astype(F32) * live).astype(BF16)).astype(BF16)
-    output[0] = (nn(agg, w_second[...]) * live).astype(BF16)
-
-
-def gradient_kernel(n, me, columns, hidden, spread, feat, adj, masks, pre_piece, grad_first, grad_second, dout, dpre):
+    second_copy.wait()
+    output[0] = (nn(agg, second[...]) * live).astype(BF16)
+
+
+def gradient_kernel(n, *refs):
+    mine, sent = refs[:PLANE], refs[PLANE : PLANE + n // PLANE - 1]
+    hidden, spread, feat, adj, masks, pre_piece = refs[PLANE + len(sent) :][:6]
+    grad_first, grad_second, dout, dpre = refs[PLANE + len(sent) + 6 :]
     each = grad_first.shape[0]
     rows = adj.shape[1]
-    place = me[0]
     for j in range(n):
         mask = masks[j : j + 1, :]
         span = slice(j * rows, (j + 1) * rows)
-        source = columns[place ^ j].astype(F32) * mask
-        back = nn(source.astype(BF16), adj[j]) * mask
+        s, q = divmod(j, PLANE)
+        source = sent[s - 1][q * 2 * each : (q + 1) * 2 * each, :] if s else mine[q][: 2 * each, :]
+        back = nn((source.astype(F32) * mask).astype(BF16), adj[j]) * mask
         dout[:, span] = back[:each].astype(BF16)
         pre = pre_piece[:, span]
         sig = 0.5 + 0.5 * jnp.tanh(0.5 * pre)
@@ -131,53 +164,60 @@
     grad_first[...] = nn(moved.astype(BF16), feat[...])
 
 
-def gather_pieces(piece, n):
-    def swap(x, s):
-        return lax.ppermute(x, "grp", [(i, i ^ s) for i in range(n)])
-
-    got = {0: piece}
-    for s in range(4, n, 4):
-        got[s] = swap(piece, s)
-    for s in range(0, n, 4):
-        if n > 2:
-            got[s + 2] = swap(got[s], 2)
-    for s in range(0, n, 2):
-        if n > 1:
-            got[s + 1] = swap(got[s], 1)
-    return [got[s] for s in range(n)]
-
-
 def whole_body(n, features, counts, pick_owner, pick_local, adjacency, cotangent, w_first, w_second):
     own, slots, width = features.shape
     rows = adjacency.shape[1]
     held = own * slots
     each = width // n
+    total_rows = n * held
     piece_rows = held * (width // LANES) + rows + META
+    limit = pltpu.CompilerParams(vmem_limit_bytes=24 * 2**20)
+    me = lax.axis_index("grp").reshape(1).astype(jnp.int32)
+
+    def swap(x, s):
+        return lax.ppermute(x, "grp", [(i, i ^ s) for i in range(n)])
+
     piece = pl.pallas_call(
         pack_kernel,
         out_shape=jax.ShapeDtypeStruct((piece_rows, LANES), BF16),
         in_specs=[SMEM, SMEM, SMEM, VMEM, VMEM],
         out_specs=VMEM,
     )(counts, pick_owner, pick_local, features, adjacency)
-    pieces = gather_pieces(piece, n)
-    me = lax.axis_index("grp").reshape(1).astype(jnp.int32)
-    limit = pltpu.CompilerParams(vmem_limit_bytes=24 * 2**20)
+
+    far = range(PLANE, n, PLANE)
+    along = [swap(piece, s) for s in far]
     cotangent, _ = lax.optimization_barrier((cotangent, piece))
-    columns, w_piece = pl.pallas_call(
+    *columns, w_piece = pl.pallas_call(
         columns_kernel,
-        out_shape=(
-            jax.ShapeDtypeStruct((n, 2 * each, rows), BF16),
-            jax.ShapeDtypeStruct((each, width), BF16),
-        ),
-        in_specs=[SMEM, VMEM, VMEM, VMEM],
-        out_specs=(VMEM, VMEM),
+        out_shape=(jax.ShapeDtypeStruct((n // PLANE * 2 * each, rows), BF16),) * PLANE
+        + (jax.ShapeDtypeStruct((each, width), BF16),),
+        in_specs=[SMEM, VMEM, HBM, HBM],
+        out_specs=(VMEM,) * (PLANE + 1),
+        scratch_shapes=[
+            pltpu.VMEM((width, rows), BF16),
+            pltpu.VMEM((width, rows), BF16),
+            pltpu.VMEM((width, width), BF16),
+            pltpu.VMEM((width, max(each, LANES)), BF16),
+            pltpu.SemaphoreType.DMA((2,)),
+        ],
         compiler_params=limit,
         cost_estimate=pl.CostEstimate(
-            flops=2 * rows * width * width, bytes_accessed=5 * 2**20, transcendentals=0
+            flops=2 * rows * width * width, bytes_accessed=3 * 2**20, transcendentals=0
         ),
     )(me, cotangent, w_second, w_first)
-    columns = lax.all_to_all(columns, "grp", 0, 0, tiled=True)
-    total_rows = n * held
+    columns = [columns[0]] + [swap(columns[q], q) for q in range(1, PLANE)]
+    stack, *sent = pl.pallas_call(
+        functools.partial(regroup_kernel, n // PLANE),
+        out_shape=(jax.ShapeDtypeStruct((n // PLANE * piece_rows, LANES), BF16),)
+        + (jax.ShapeDtypeStruct((PLANE * 2 * each, rows), BF16),) * len(far),
+        in_specs=[VMEM] * (n // PLANE + PLANE),
+        out_specs=(VMEM,) * (1 + len(far)),
+        compiler_params=limit,
+    )(piece, *along, *columns)
+    across = swap(stack, 2)
+    pieces = [stack, swap(stack, 1), across, swap(across, 1)]
+    sent = [swap(x, s) for x, s in zip(sent, far)]
+
     output, *kept = pl.pallas_call(
         functools.partial(forward_kernel, n, own, slots),
         out_shape=(
@@ -189,9 +229,14 @@
             jax.ShapeDtypeStruct((n, LANES), F32),
             jax.ShapeDtypeStruct((each, n * rows), F32),
         ),
-        in_specs=[SMEM] + [VMEM] * (n + 3),
+        in_specs=[SMEM] + [VMEM] * PLANE + [HBM, VMEM, HBM],
         out_specs=(VMEM,) * 7,
-        scratch_shapes=[pltpu.VMEM((total_rows, width), BF16)],
+        scratch_shapes=[
+            pltpu.VMEM((total_rows, width), BF16),
+            pltpu.VMEM((width, width), BF16),
+            pltpu.VMEM((width, width), BF16),
+            pltpu.SemaphoreType.DMA((2,)),
+        ],
         compiler_params=limit,
         cost_estimate=pl.CostEstimate(
             flops=4 * 10**9, bytes_accessed=10 * 2**20, transcendentals=2 * 10**6
@@ -200,14 +245,14 @@
     grad_first, grad_second = pl.pallas_call(
         functools.partial(gradient_kernel, n),
         out_shape=(jax.ShapeDtypeStruct((each, width), F32),) * 2,
-        in_specs=[SMEM] + [VMEM] * 7,
+        in_specs=[VMEM] * (PLANE + len(far) + 6),
         out_specs=(VMEM,) * 2,
         scratch_shapes=[pltpu.VMEM((each, n * rows), BF16)] * 2,
         compiler_params=limit,
         cost_estimate=pl.CostEstimate(
             flops=10**9, bytes_accessed=8 * 2**20, transcendentals=10**5
         ),
-    )(me, columns, *kept)
+    )(*columns, *sent, *kept)
     return output, grad_first, grad_second
 
 
@@ -252,7 +297,7 @@
 
     def body(*args):
         rows = args[4].shape[1]
-        small = n & (n - 1) == 0 and rows == LANES and n * rows <= 4096
+        small = n & (n - 1) == 0 and n > PLANE and rows == LANES and n * rows <= 4096
         return whole_body(n, *args) if small else split_body(*args)
 
     in_specs = (

time: 71.3 us -> 49.1 us (0.69)
  local copies, waits for them, and re-layouts: 16.9 us -> 4.14 us
  starting transfers between devices: 18.5 us -> 13.5 us
  waiting for transfers between devices: 21.7 us -> 17.7 us
    unnamed x28 -> x12, local copies, waits for them, and re-layouts: 16.9 us -> 4.14 us
    all_to_all x1 -> x0, starting transfers between devices: 7.38 us -> none  [whole_body(): columns = lax.all_to_all(columns, 'grp', 0, 0, tiled=True)]
    ppermute x15 -> x12, waiting for transfers between devices: 21.7 us -> 17.7 us  [swap(): return lax.ppermute(x, 'grp', [(i, i ^ s) for i in range(n)])]
    ppermute x15 -> x12, starting transfers between devices: 11.1 us -> 13.5 us  [swap(): return lax.ppermute(x, 'grp', [(i, i ^ s) for i in range(n)])]
    pallas_call x1 -> x2, Pallas kernels: 2.39 us -> 1.29 us  [the longest x1 1.23 us: whole_body(): pl.pallas_call(columns_kernel, out_shape=(jax.ShapeDtypeStruct((n // PLAN...]
    pallas_call x1, Pallas kernels: 6.52 us -> 7.46 us  [whole_body(): pl.pallas_call(functools.partial(forward_kernel, n, own, slots), out_shap...]
  transfers between devices with their start and end apart: 16 -> 12, of which waited for: 5 -> 4; matrix products, arithmetic and copies ran while one was open for 0% -> 0% of each run, Pallas kernels for 9% -> 18%
where the time goes in v3:
time: 49.1 us; the launch traced here: 48.8 us
  waiting for transfers between devices  17.7 us (36%)
  starting transfers between devices  13.5 us (27%)
  Pallas kernels  12.8 us (26%)
  local copies, waits for them, and re-layouts  4.14 us (8%)
  between operations  0.71 us (1%)
    ppermute x12, waiting for transfers between devices, swap(): return lax.ppermute(x, 'grp', [(i, i ^ s) for i in range(n)])  17.7 us
    ppermute x12, starting transfers between devices, swap(): return lax.ppermute(x, 'grp', [(i, i ^ s) for i in range(n)])  13.5 us
    pallas_call x1, Pallas kernels, whole_body(): pl.pallas_call(functools.partial(forward_kernel, n, own, slots), out_shap...  7.46 us
    unnamed x12, local copies, waits for them, and re-layouts  4.14 us
    pallas_call x1, Pallas kernels, whole_body(): pl.pallas_call(functools.partial(gradient_kernel, n), out_shape=(jax.Shap...  2.48 us
    pallas_call x1, Pallas kernels, whole_body(): pl.pallas_call(pack_kernel, out_shape=jax.ShapeDtypeStruct((piece_rows, L...  1.53 us
    pallas_call x1, Pallas kernels, whole_body(): pl.pallas_call(columns_kernel, out_shape=(jax.ShapeDtypeStruct((n // PLAN...  1.23 us
  transfers between devices with their start and end apart: 12, of which 4 were waited for; matrix products, arithmetic and copies ran while one was open for 0% of the time, Pallas kernels for 18%

profile of v3, /device:TPU:0, one launch (start us, length us, event | category | flops | bytes accessed | tf_op | source)
XLA Modules:
  0.0 48.8 jit_solution(6080547270286182781)
XLA Ops:
  0.6 1.5 %shard_map.103.refs_0_ = bf16[400,128]{1,0:T(8,128)(2,1)} custom-call(s32[2]{0:T(128)} %counts.1, s32[1,8]{1,0:T(1,128)} %owner.1, s32[1,8]{1,0:T(1,128)} %local.1, bf16[2,16,1024]{2,1,0:T(8,128)(2,1)} %features.1, bf16[1,128,128]{2,1,0:T(8,128)(2,1)} %adjacency.1), custom_call_target="tpu_custom_call" | custom-call | tf_op jit(solution)/shard_map/pallas_call | solution.py:180
  2.2 5.0 %collective-permute-start.2 = (bf16[400,128]{1,0:T(8,128)(2,1)}, bf16[400,128]{1,0:T(8,128)(2,1)S(1)}, u32[]{:S(2)}, u32[]{:S(2)}) collective-permute-start(bf16[400,128]{1,0:T(8,128)(2,1)} %shard_map.103.refs_0_), channel_id=1, source_target_pairs={{0,12},{1,13},{2,14},{3,15},{4,8},{5,9},{6,10},{7,11},{8,4},{9,5},... | collective-permute-start | bytes 307208 | tf_op jit(solution)/shard_map/ppermute | solution.py:178
  7.2 0.0 copy-start
  7.2 1.6 %copy-done = bf16[1024,1024]{1,0:T(8,128)(2,1)S(1)} copy-done((bf16[1024,1024]{1,0:T(8,128)(2,1)S(1)}, bf16[1024,1024]{1,0:T(8,128)(2,1)}, u32[]{:S(2)}) %copy-start) | copy-done | bytes 2097176
  8.8 0.0 copy-start.2
  8.8 1.6 %copy-done.2 = bf16[1024,1024]{1,0:T(8,128)(2,1)S(1)} copy-done((bf16[1024,1024]{1,0:T(8,128)(2,1)S(1)}, bf16[1024,1024]{1,0:T(8,128)(2,1)}, u32[]{:S(2)}) %copy-start.2) | copy-done | bytes 2097176
  10.4 0.0 copy-start.5
  10.4 0.9 %copy-done.5 = bf16[1,128,1024]{2,1,0:T(8,128)(2,1)S(1)} copy-done((bf16[1,128,1024]{2,1,0:T(8,128)(2,1)S(1)}, bf16[1,128,1024]{2,1,0:T(8,128)(2,1)}, u32[]{:S(2)}) %copy-start.5) | copy-done | bytes 262168
  11.3 0.0 copy-start.4
  11.3 0.0 copy-start.1
  11.3 0.0 copy-start.3
  11.3 1.2 %shard_map.104 = (bf16[512,128]{1,0:T(8,128)(2,1)S(1)}, bf16[512,128]{1,0:T(8,128)(2,1)S(1)}, bf16[512,128]{1,0:T(8,128)(2,1)S(1)}, bf16[512,128]{1,0:T(8,128)(2,1)S(1)}, bf16[64,1024]{1,0:T(8,128)(2,1)S(1)}) custom-call(s32[1]{0:T(128)} %bitcast.me, bf16[1,128,1024]{2,1,0:T(8,128)(2,1)S(1)} %copy-done.5, bf16[1024,1024]{1,0:T(8,128)(2,1)S(1)} %copy-done, ...), custom_call_target="tpu_custom_call" | custom-call | flops 268435456 | bytes 3145728 | tf_op jit(solution)/shard_map/pallas_call | solution.py:190
  12.6 0.1 collective-permute-start.3
  12.7 1.6 %collective-permute-start.4 = (bf16[512,128]{1,0:T(8,128)(2,1)S(1)}, bf16[512,128]{1,0:T(8,128)(2,1)S(1)}, u32[]{:S(2)}, u32[]{:S(2)}) collective-permute-start(bf16[512,128]{1,0:T(8,128)(2,1)S(1)} %get-tuple-element.25), channel_id=1, source_target_pairs={{0,2},{1,3},{2,0},{3,1},{4,6},{5,7},{6,4},{7,5},{8,10},{9,11},{10,... | collective-permute-start | bytes 393224 | tf_op jit(solution)/shard_map/ppermute | solution.py:178
  14.2 0.3 collective-permute-start.5
  14.5 0.0 copy-done.4
  14.5 0.0 collective-permute-start.1
  14.5 0.0 collective-permute-done.2.refs_3_
  14.5 0.6 %collective-permute-start = (bf16[400,128]{1,0:T(8,128)(2,1)S(1)}, bf16[400,128]{1,0:T(8,128)(2,1)S(1)}, u32[]{:S(2)}, u32[]{:S(2)}) collective-permute-start(bf16[400,128]{1,0:T(8,128)(2,1)S(1)} %copy-done.4), channel_id=1, source_target_pairs={{0,4},{1,5},{2,6},{3,7},{4,0},{5,1},{6,2},{7,3},{8,12},{9,13},{10,... | collective-permute-start | bytes 307208 | tf_op jit(solution)/shard_map/ppermute | solution.py:178
  15.1 6.7 %collective-permute-done.1.refs_2_ = bf16[400,128]{1,0:T(8,128)(2,1)S(1)} collective-permute-done((bf16[400,128]{1,0:T(8,128)(2,1)S(1)}, bf16[400,128]{1,0:T(8,128)(2,1)S(1)}, u32[]{:S(2)}, u32[]{:S(2)}) %collective-permute-start.1) | collective-permute-done | bytes 102432 | tf_op jit(solution)/shard_map/ppermute | solution.py:178
  21.9 0.1 collective-permute-done.refs_1_
  21.9 0.0 collective-permute-done.3.refs_5_.refs_1_
  21.9 0.0 collective-permute-done.4.refs_6_.refs_2_
  21.9 0.0 collective-permute-done.5.refs_7_.refs_3_
  21.9 0.1 shard_map.105
  22.0 1.6 %collective-permute-start.7 = (bf16[1600,128]{1,0:T(8,128)(2,1)S(1)}, bf16[1600,128]{1,0:T(8,128)(2,1)S(1)}, u32[]{:S(2)}, u32[]{:S(2)}) collective-permute-start(bf16[1600,128]{1,0:T(8,128)(2,1)S(1)} %get-tuple-element.27.refs_0_), channel_id=1, source_target_pairs={{0,2},{1,3},{2,0},{3,1},{4,6},{5,7},{6,4},{7,5},{8,10},{9,11},{10,... | collective-permute-start | bytes 1228808 | tf_op jit(solution)/shard_map/ppermute | solution.py:178
  23.6 0.0 collective-permute-start.6
  23.6 9.8 %collective-permute-done.7.refs_2_ = bf16[1600,128]{1,0:T(8,128)(2,1)S(1)} collective-permute-done((bf16[1600,128]{1,0:T(8,128)(2,1)S(1)}, bf16[1600,128]{1,0:T(8,128)(2,1)S(1)}, u32[]{:S(2)}, u32[]{:S(2)}) %collective-permute-start.7) | collective-permute-done | bytes 409632 | tf_op jit(solution)/shard_map/ppermute | solution.py:178
  33.4 0.0 collective-permute-start.8
  33.4 0.1 collective-permute-start.9
  33.5 0.9 %collective-permute-start.10 = (bf16[512,128]{1,0:T(8,128)(2,1)S(1)}, bf16[512,128]{1,0:T(8,128)(2,1)S(1)}, u32[]{:S(2)}, u32[]{:S(2)}) collective-permute-start(bf16[512,128]{1,0:T(8,128)(2,1)S(1)} %get-tuple-element.31), channel_id=1, source_target_pairs={{0,8},{1,9},{2,10},{3,11},{4,12},{5,13},{6,14},{7,15},{8,0},{9,1},... | collective-permute-start | bytes 393224 | tf_op jit(solution)/shard_map/ppermute | solution.py:178
  34.4 3.4 %collective-permute-start.11 = (bf16[512,128]{1,0:T(8,128)(2,1)S(1)}, bf16[512,128]{1,0:T(8,128)(2,1)S(1)}, u32[]{:S(2)}, u32[]{:S(2)}) collective-permute-start(bf16[512,128]{1,0:T(8,128)(2,1)S(1)} %get-tuple-element.32), channel_id=1, source_target_pairs={{0,12},{1,13},{2,14},{3,15},{4,8},{5,9},{6,10},{7,11},{8,4},{9,5},... | collective-permute-start | bytes 393224 | tf_op jit(solution)/shard_map/ppermute | solution.py:178
  37.8 0.0 collective-permute-done.6.refs_1_
  37.8 0.0 collective-permute-done.8.refs_3_
  37.8 0.0 copy-done.1
  37.8 0.0 copy-done.3
  37.8 7.5 %shard_map.106 = (bf16[1,128,1024]{2,1,0:T(8,128)(2,1)}, bf16[2048,1024]{1,0:T(8,128)(2,1)S(1)}, bf16[2048,512]{1,0:T(8,128)(2,1)S(1)}, bf16[512,1024]{1,0:T(8,1...) custom-call(s32[1]{0:T(128)} %bitcast.me, ...), custom_call_target="tpu_custom_call" | custom-call | flops 4000000000 | bytes 10485760 | tf_op jit(solution)/shard_map/pallas_call | solution.py:221
  45.3 0.0 collective-permute-done.9.refs_4_
  45.3 1.1 %collective-permute-done.10.refs_5_ = bf16[512,128]{1,0:T(8,128)(2,1)S(1)} collective-permute-done((bf16[512,128]{1,0:T(8,128)(2,1)S(1)}, bf16[512,128]{1,0:T(8,128)(2,1)S(1)}, u32[]{:S(2)}, u32[]{:S(2)}) %collective-permute-start.10) | collective-permute-done | bytes 131104 | tf_op jit(solution)/shard_map/ppermute | solution.py:178
  46.3 0.0 collective-permute-done.11.refs_6_
  46.3 2.5 %shard_map.107 = (f32[64,1024]{1,0:T(8,128)}, f32[64,1024]{1,0:T(8,128)}) custom-call(bf16[512,128]{1,0:T(8,128)(2,1)S(1)} %get-tuple-element.23.refs_4_.refs_0_, bf16[512,128]{1,0:T(8,128)(2,1)S(1)} %collective-permute-done.3.refs_5_.refs_1_, bf16[512,128]{1,0:T(8,128)(2,1)S(1)} %collective-permute-done.4.refs_6_.refs_2_, ...), custom_call_target="tpu_custom_call" | custom-call | flops 1000000000 | bytes 8388608 | tf_op jit(solution)/shard_map/pallas_call | solution.py:245
Async XLA Ops:
  2.2 12.4 %collective-permute-start.2 = (bf16[400,128]{1,0:T(8,128)(2,1)}, bf16[400,128]{1,0:T(8,128)(2,1)S(1)}, u32[]{:S(2)}, u32[]{:S(2)}) collective-permute-start(bf16[400,128]{1,0:T(8,128)(2,1)} %shard_map.103.refs_0_), channel_id=1, source_target_pairs={{0,12},{1,13},{2,14},{3,15},{4,8},{5,9},{6,10},{7,11},{8,4},{9,5},... | collective-permute-start | bytes 307208 | tf_op jit(solution)/shard_map/ppermute | solution.py:178
  7.2 1.6 %copy-start = (bf16[1024,1024]{1,0:T(8,128)(2,1)S(1)}, bf16[1024,1024]{1,0:T(8,128)(2,1)}, u32[]{:S(2)}) copy-start(bf16[1024,1024]{1,0:T(8,128)(2,1)} %refs_6_.1) | copy-start | bytes 6291460
  8.8 1.6 %copy-start.2 = (bf16[1024,1024]{1,0:T(8,128)(2,1)S(1)}, bf16[1024,1024]{1,0:T(8,128)(2,1)}, u32[]{:S(2)}) copy-start(bf16[1024,1024]{1,0:T(8,128)(2,1)} %refs_4_.1) | copy-start | bytes 6291460
  10.4 0.9 %copy-start.5 = (bf16[1,128,1024]{2,1,0:T(8,128)(2,1)S(1)}, bf16[1,128,1024]{2,1,0:T(8,128)(2,1)}, u32[]{:S(2)}) copy-start(bf16[1,128,1024]{2,1,0:T(8,128)(2,1)} %cotangent) | copy-start | bytes 786436
  11.3 3.2 %copy-start.4 = (bf16[400,128]{1,0:T(8,128)(2,1)S(1)}, bf16[400,128]{1,0:T(8,128)(2,1)}, u32[]{:S(2)}) copy-start(bf16[400,128]{1,0:T(8,128)(2,1)} %shard_map.103.refs_0_) | copy-start | bytes 307204
  11.3 26.4 %copy-start.1 = (bf16[1024,1024]{1,0:T(8,128)(2,1)S(1)}, bf16[1024,1024]{1,0:T(8,128)(2,1)}, u32[]{:S(2)}) copy-start(bf16[1024,1024]{1,0:T(8,128)(2,1)} %refs_6_.1) | copy-start | bytes 6291460
  11.3 26.4 %copy-start.3 = (bf16[1024,1024]{1,0:T(8,128)(2,1)S(1)}, bf16[1024,1024]{1,0:T(8,128)(2,1)}, u32[]{:S(2)}) copy-start(bf16[1024,1024]{1,0:T(8,128)(2,1)} %refs_4_.1) | copy-start | bytes 6291460
  12.6 9.3 %collective-permute-start.3 = (bf16[512,128]{1,0:T(8,128)(2,1)S(1)}, bf16[512,128]{1,0:T(8,128)(2,1)S(1)}, u32[]{:S(2)}, u32[]{:S(2)}) collective-permute-start(bf16[512,128]{1,0:T(8,128)(2,1)S(1)} %get-tuple-element.24), channel_id=1, source_target_pairs={{0,1},{1,0},{2,3},{3,2},{4,5},{5,4},{6,7},{7,6},{8,9},{9,8},{10,11... | collective-permute-start | bytes 393224 | tf_op jit(solution)/shard_map/ppermute | solution.py:178
  12.7 9.3 %collective-permute-start.4 = (bf16[512,128]{1,0:T(8,128)(2,1)S(1)}, bf16[512,128]{1,0:T(8,128)(2,1)S(1)}, u32[]{:S(2)}, u32[]{:S(2)}) collective-permute-start(bf16[512,128]{1,0:T(8,128)(2,1)S(1)} %get-tuple-element.25), channel_id=1, source_target_pairs={{0,2},{1,3},{2,0},{3,1},{4,6},{5,7},{6,4},{7,5},{8,10},{9,11},{10,... | collective-permute-start | bytes 393224 | tf_op jit(solution)/shard_map/ppermute | solution.py:178
  14.2 7.7 %collective-permute-start.5 = (bf16[512,128]{1,0:T(8,128)(2,1)S(1)}, bf16[512,128]{1,0:T(8,128)(2,1)S(1)}, u32[]{:S(2)}, u32[]{:S(2)}) collective-permute-start(bf16[512,128]{1,0:T(8,128)(2,1)S(1)} %get-tuple-element.26), channel_id=1, source_target_pairs={{0,3},{1,2},{2,1},{3,0},{4,7},{5,6},{6,5},{7,4},{8,11},{9,10},{10,... | collective-permute-start | bytes 393224 | tf_op jit(solution)/shard_map/ppermute | solution.py:178
  14.5 7.3 %collective-permute-start.1 = (bf16[400,128]{1,0:T(8,128)(2,1)S(1)}, bf16[400,128]{1,0:T(8,128)(2,1)S(1)}, u32[]{:S(2)}, u32[]{:S(2)}) collective-permute-start(bf16[400,128]{1,0:T(8,128)(2,1)S(1)} %copy-done.4), channel_id=1, source_target_pairs={{0,8},{1,9},{2,10},{3,11},{4,12},{5,13},{6,14},{7,15},{8,0},{9,1},... | collective-permute-start | bytes 307208 | tf_op jit(solution)/shard_map/ppermute | solution.py:178
  14.5 7.4 %collective-permute-start = (bf16[400,128]{1,0:T(8,128)(2,1)S(1)}, bf16[400,128]{1,0:T(8,128)(2,1)S(1)}, u32[]{:S(2)}, u32[]{:S(2)}) collective-permute-start(bf16[400,128]{1,0:T(8,128)(2,1)S(1)} %copy-done.4), channel_id=1, source_target_pairs={{0,4},{1,5},{2,6},{3,7},{4,0},{5,1},{6,2},{7,3},{8,12},{9,13},{10,... | collective-permute-start | bytes 307208 | tf_op jit(solution)/shard_map/ppermute | solution.py:178
  22.0 11.4 %collective-permute-start.7 = (bf16[1600,128]{1,0:T(8,128)(2,1)S(1)}, bf16[1600,128]{1,0:T(8,128)(2,1)S(1)}, u32[]{:S(2)}, u32[]{:S(2)}) collective-permute-start(bf16[1600,128]{1,0:T(8,128)(2,1)S(1)} %get-tuple-element.27.refs_0_), channel_id=1, source_target_pairs={{0,2},{1,3},{2,0},{3,1},{4,6},{5,7},{6,4},{7,5},{8,10},{9,11},{10,... | collective-permute-start | bytes 1228808 | tf_op jit(solution)/shard_map/ppermute | solution.py:178
  23.6 14.2 %collective-permute-start.6 = (bf16[1600,128]{1,0:T(8,128)(2,1)S(1)}, bf16[1600,128]{1,0:T(8,128)(2,1)S(1)}, u32[]{:S(2)}, u32[]{:S(2)}) collective-permute-start(bf16[1600,128]{1,0:T(8,128)(2,1)S(1)} %get-tuple-element.27.refs_0_), channel_id=1, source_target_pairs={{0,1},{1,0},{2,3},{3,2},{4,5},{5,4},{6,7},{7,6},{8,9},{9,8},{10,11... | collective-permute-start | bytes 1228808 | tf_op jit(solution)/shard_map/ppermute | solution.py:178
  33.4 4.4 %collective-permute-start.8 = (bf16[1600,128]{1,0:T(8,128)(2,1)S(1)}, bf16[1600,128]{1,0:T(8,128)(2,1)S(1)}, u32[]{:S(2)}, u32[]{:S(2)}) collective-permute-start(bf16[1600,128]{1,0:T(8,128)(2,1)S(1)} %collective-permute-done.7.refs_2_), channel_id=1, source_target_pairs={{0,1},{1,0},{2,3},{3,2},{4,5},{5,4},{6,7},{7,6},{8,9},{9,8},{10,11... | collective-permute-start | bytes 1228808 | tf_op jit(solution)/shard_map/ppermute | solution.py:178
  33.4 11.9 %collective-permute-start.9 = (bf16[512,128]{1,0:T(8,128)(2,1)S(1)}, bf16[512,128]{1,0:T(8,128)(2,1)S(1)}, u32[]{:S(2)}, u32[]{:S(2)}) collective-permute-start(bf16[512,128]{1,0:T(8,128)(2,1)S(1)} %get-tuple-element.30), channel_id=1, source_target_pairs={{0,4},{1,5},{2,6},{3,7},{4,0},{5,1},{6,2},{7,3},{8,12},{9,13},{10,... | collective-permute-start | bytes 393224 | tf_op jit(solution)/shard_map/ppermute | solution.py:178
  33.5 12.9 %collective-permute-start.10 = (bf16[512,128]{1,0:T(8,128)(2,1)S(1)}, bf16[512,128]{1,0:T(8,128)(2,1)S(1)}, u32[]{:S(2)}, u32[]{:S(2)}) collective-permute-start(bf16[512,128]{1,0:T(8,128)(2,1)S(1)} %get-tuple-element.31), channel_id=1, source_target_pairs={{0,8},{1,9},{2,10},{3,11},{4,12},{5,13},{6,14},{7,15},{8,0},{9,1},... | collective-permute-start | bytes 393224 | tf_op jit(solution)/shard_map/ppermute | solution.py:178
  34.4 11.9 %collective-permute-start.11 = (bf16[512,128]{1,0:T(8,128)(2,1)S(1)}, bf16[512,128]{1,0:T(8,128)(2,1)S(1)}, u32[]{:S(2)}, u32[]{:S(2)}) collective-permute-start(bf16[512,128]{1,0:T(8,128)(2,1)S(1)} %get-tuple-element.32), channel_id=1, source_target_pairs={{0,12},{1,13},{2,14},{3,15},{4,8},{5,9},{6,10},{7,11},{8,4},{9,5},... | collective-permute-start | bytes 393224 | tf_op jit(solution)/shard_map/ppermute | solution.py:178

commit v4 on v3

v4 whole, which is shorter than its diff:
```python
import functools

import jax
import jax.numpy as jnp
from jax import lax
from jax.experimental import pallas as pl
from jax.experimental.pallas import tpu as pltpu
from jax.sharding import PartitionSpec as P

F32 = jnp.float32
BF16 = jnp.bfloat16
VMEM = pl.BlockSpec(memory_space=pltpu.VMEM)
SMEM = pl.BlockSpec(memory_space=pltpu.SMEM)
ANY = pl.BlockSpec(memory_space=pl.ANY)
PLANE = 4
LIMIT = 60 * 2**20
SMALL = 8 * 2**20
CHUNKS = 4
LANES = 128
META = 16


def nn(a, b):
    return jnp.dot(a, b, preferred_element_type=F32)


def nt(a, b):
    return lax.dot_general(a, b, (((1,), (1,)), ((), ())), preferred_element_type=F32)


def prepare_kernel(me, counts, owner, local, features, adjacency, cotangent, w_second, w_first, *refs):
    piece, near, across, w_piece, feat, adj, cot, turned, back, second, strip, sems = refs
    own, slots, width = features.shape
    rows = adjacency.shape[1]
    each = w_piece.shape[0]
    wide = strip.shape[1]
    per = wide // each
    start = pl.multiple_of((me[0] // per) * wide, wide)
    moves = [(features, feat), (adjacency, adj), (cotangent, cot)]
    some = width // CHUNKS
    for c in range(CHUNKS):
        moves.append((w_second.at[c * some : (c + 1) * some], second.at[c * some : (c + 1) * some]))
    moves.append((w_first.at[:, pl.ds(start, wide)], strip))
    copies = [pltpu.make_async_copy(a, b, sems.at[i]) for i, (a, b) in enumerate(moves)]
    for copy in copies:
        copy.start()

    held = own * slots
    slot = lax.broadcasted_iota(jnp.int32, (slots, LANES), 0)
    copies[0].wait()
    for i in range(own):
        live = slot < counts[i]
        for b in range(width // LANES):
            block = feat[i, :, b * LANES : (b + 1) * LANES]
            at = b * held + i * slots
            piece[at : at + slots, :] = jnp.where(live, block, jnp.zeros_like(block))
    at = held * (width // LANES)
    copies[1].wait()
    piece[at : at + rows, :] = adj[0]
    at += rows
    line = lax.broadcasted_iota(jnp.int32, (META, LANES), 0)
    pick = lax.broadcasted_iota(jnp.int32, (META, LANES), 1) // slots
    meta = jnp.zeros((META, LANES), jnp.int32)
    for k in range(owner.shape[1]):
        wanted = owner[0, k] * own + local[0, k]
        meta = jnp.where((line == 0) & (pick == k), wanted, meta)
    for i in range(own):
        meta = jnp.where(line == 1 + i, counts[i], meta)
    piece[at : at + META, :] = meta.astype(F32).astype(BF16)

    copies[2].wait()
    turned[...] = cot[0].astype(F32).T.astype(BF16)
    for c in range(CHUNKS):
        copies[3 + c].wait()
        span = slice(c * some, (c + 1) * some)
        back[span, :] = nt(second[span, :], cot[0]).astype(BF16)
    for h, out in enumerate((near, across)):
        for i in range(out.shape[0] // (2 * each)):
            to = PLANE * (i // 2) + 2 * h + i % 2
            span = pl.ds(pl.multiple_of((me[0] ^ to) * each, each), each)
            at = i * 2 * each
            out[at : at + each, :] = turned[span, :]
            out[at + each : at + 2 * each, :] = back[span, :]
    copies[3 + CHUNKS].wait()
    block = strip[...].astype(F32).T
    part = block[:each]
    for q in range(1, per):
        part = jnp.where(me[0] % per == q, block[q * each : (q + 1) * each], part)
    w_piece[...] = part.astype(BF16)


def regroup_kernel(parts, *refs):
    pieces, near, across = refs[:parts], refs[parts], refs[parts + 1]
    stack, *sent = refs[parts + 2 :]
    rows = pieces[0].shape[0]
    for i, ref in enumerate(pieces):
        stack[i * rows : (i + 1) * rows, :] = ref[...]
    half = sent[0].shape[0] // 2
    for s, out in enumerate(sent, 1):
        out[:half, :] = near[s * half : (s + 1) * half, :]
        out[half:, :] = across[s * half : (s + 1) * half, :]


def pair_kernel(parts, across, near, other, *refs):
    sent, out = refs[: parts - 1], refs[parts - 1]
    deep = across.shape[0]
    out[:deep, :] = across[...]
    half = near.shape[0] // parts
    rows = half // 2
    for s in range(parts):
        for h in range(2):
            if s:
                block = sent[s - 1][h * half + rows : (h + 1) * half, :]
            else:
                block = (near, other)[h][rows:half, :]
            at = deep + (2 * s + h) * rows
            out[at : at + rows, :] = block


def step_kernel(n, own, slots, me, *refs):
    parts = n // PLANE
    packs = refs[:PLANE]
    pair = packs[3]
    near, other, *sent = refs[PLANE : PLANE + parts + 1]
    w_first, w_piece, w_second = refs[PLANE + parts + 1 : PLANE + parts + 4]
    output, grad_first, grad_second = refs[PLANE + parts + 4 : PLANE + parts + 7]
    hidden, spread, feat, adj, dout, dpre, lifted, first, second, sems = refs[PLANE + parts + 7 :]
    first_copy = pltpu.make_async_copy(w_first, first, sems.at[0])
    first_copy.start()
    second_copy = pltpu.make_async_copy(w_second, second, sems.at[1])
    second_copy.start()
    width = w_first.shape[0]
    held = own * slots
    rows = adj.shape[1]
    clusters = n * own
    place = me[0]
    deep = held * (width // LANES) + rows + META

    metas = []
    for s in range(n):
        pack, at = packs[s % PLANE], (s // PLANE) * deep
        for b in range(width // LANES):
            feat[s * held : (s + 1) * held, b * LANES : (b + 1) * LANES] = pack[at : at + held, :]
            at += held
        adj[s] = pack[at : at + rows, :]
        at += rows
        metas.append(pack[at : at + META, :].astype(F32))
    picks = jnp.concatenate([m[0:1] for m in metas], axis=0).astype(jnp.int32)
    lane = lax.broadcasted_iota(jnp.int32, (n, LANES), 1) % slots
    count = jnp.zeros((n, LANES), jnp.int32)
    for s in range(n):
        for i in range(own):
            cluster = (place ^ s) * own + i
            count = jnp.where(picks == cluster, metas[s][1 + i : 2 + i].astype(jnp.int32), count)
    masks = (lane < count).astype(F32)
    wanted = picks * slots + lane
    code = lax.broadcasted_iota(jnp.int32, (clusters * slots, LANES), 0) ^ (place * held)

    for j in range(n):
        chosen = jnp.where(code == wanted[j : j + 1], 1.0, 0.0).astype(BF16)
        spread[j * rows : (j + 1) * rows, :] = nt(adj[j], chosen).astype(BF16)
    first_copy.wait()
    lifted[...] = nn(feat[...], first[...]).astype(BF16)
    lifted_piece = nt(w_piece[...], feat[...]).astype(BF16)
    step = min(width, 2 * LANES)
    for c in range(0, width, step):
        half = 0.5 * nn(spread[...], lifted[:, c : c + step])
        hidden[:, c : c + step] = (half + half * jnp.tanh(half)).astype(BF16)
    pre_piece = nt(lifted_piece, spread[...])
    live = jnp.broadcast_to(masks[0:1], (rows, LANES)).T[:, :1]
    agg = nn(adj[0], (hidden[:rows, :].astype(F32) * live).astype(BF16)).astype(BF16)
    second_copy.wait()
    output[0] = (nn(agg, second[...]) * live).astype(BF16)

    each = grad_first.shape[0]
    half = near.shape[0] // parts
    deep *= parts
    for j in range(n):
        mask = masks[j : j + 1]
        span = slice(j * rows, (j + 1) * rows)
        s, h, b = j // PLANE, j % PLANE // 2, j % 2
        if b:
            at = deep + (2 * s + h) * 2 * each
            source = pair[at : at + 2 * each, :]
        elif s:
            source = sent[s - 1][h * half : h * half + 2 * each, :]
        else:
            source = (near, other)[h][: 2 * each, :]
        back = nn((source.astype(F32) * mask).astype(BF16), adj[j]) * mask
        dout[:, span] = back[:each].astype(BF16)
        pre = pre_piece[:, span]
        sig = 0.5 + 0.5 * jnp.tanh(0.5 * pre)
        dpre[:, span] = (back[each:] * sig * (1.0 + pre * (1.0 - sig))).astype(BF16)
    grad_second[...] = nn(dout[...], hidden[...])
    moved = nn(dpre[...], spread[...])
    grad_first[...] = nn(moved.astype(BF16), feat[...])


def whole_body(n, features, counts, pick_owner, pick_local, adjacency, cotangent, w_first, w_second):
    own, slots, width = features.shape
    rows = adjacency.shape[1]
    held = own * slots
    each = width // n
    total_rows = n * held
    piece_rows = held * (width // LANES) + rows + META
    limit = pltpu.CompilerParams(vmem_limit_bytes=LIMIT)
    me = lax.axis_index("grp").reshape(1).astype(jnp.int32)

    def swap(x, s):
        return lax.ppermute(x, "grp", [(i, i ^ s) for i in range(n)])

    piece, near, other, w_piece = pl.pallas_call(
        prepare_kernel,
        out_shape=(
            jax.ShapeDtypeStruct((piece_rows, LANES), BF16),
            jax.ShapeDtypeStruct((n * each, rows), BF16),
            jax.ShapeDtypeStruct((n * each, rows), BF16),
            jax.ShapeDtypeStruct((each, width), BF16),
        ),
        in_specs=[SMEM] * 4 + [ANY] * 5,
        out_specs=(VMEM,) * 4,
        scratch_shapes=[
            pltpu.VMEM(features.shape, BF16),
            pltpu.VMEM(adjacency.shape, BF16),
            pltpu.VMEM(cotangent.shape, BF16),
            pltpu.VMEM((width, rows), BF16),
            pltpu.VMEM((width, rows), BF16),
            pltpu.VMEM((width, width), BF16),
            pltpu.VMEM((width, max(each, LANES)), BF16),
            pltpu.SemaphoreType.DMA((4 + CHUNKS,)),
        ],
        compiler_params=limit,
    )(me, counts, pick_owner, pick_local, features, adjacency, cotangent, w_second, w_first)
    far = range(PLANE, n, PLANE)
    parts = n // PLANE
    along = [swap(piece, s) for s in far]
    other = swap(other, 2)
    stack, *sent = pl.pallas_call(
        functools.partial(regroup_kernel, parts),
        out_shape=(jax.ShapeDtypeStruct((parts * piece_rows, LANES), BF16),)
        + (jax.ShapeDtypeStruct((PLANE * 2 * each, rows), BF16),) * len(far),
        in_specs=[VMEM] * (parts + 2),
        out_specs=(VMEM,) * parts,
        compiler_params=pltpu.CompilerParams(vmem_limit_bytes=SMALL),
    )(piece, *along, near, other)
    sent = [swap(x, s) for x, s in zip(sent, far)]
    beside = swap(stack, 1)
    across = swap(stack, 2)
    pair = pl.pallas_call(
        functools.partial(pair_kernel, parts),
        out_shape=jax.ShapeDtypeStruct((parts * piece_rows + n * each, LANES), BF16),
        in_specs=[VMEM] * (parts + 2),
        out_specs=VMEM,
        compiler_params=pltpu.CompilerParams(vmem_limit_bytes=SMALL),
    )(across, near, other, *sent)
    pair = swap(pair, 1)
    pieces = [stack, beside, across, pair]

    return pl.pallas_call(
        functools.partial(step_kernel, n, own, slots),
        out_shape=(
            jax.ShapeDtypeStruct((1, rows, width), BF16),
            jax.ShapeDtypeStruct((each, width), F32),
            jax.ShapeDtypeStruct((each, width), F32),
        ),
        in_specs=[SMEM] + [VMEM] * (PLANE + parts + 1) + [ANY, VMEM, ANY],
        out_specs=(VMEM,) * 3,
        scratch_shapes=[
            pltpu.VMEM((n * rows, width), BF16),
            pltpu.VMEM((n * rows, total_rows), BF16),
            pltpu.VMEM((total_rows, width), BF16),
            pltpu.VMEM((n, rows, rows), BF16),
            pltpu.VMEM((each, n * rows), BF16),
            pltpu.VMEM((each, n * rows), BF16),
            pltpu.VMEM((total_rows, width), BF16),
            pltpu.VMEM((width, width), BF16),
            pltpu.VMEM((width, width), BF16),
            pltpu.SemaphoreType.DMA((2,)),
        ],
        compiler_params=limit,
    )(me, *pieces, near, other, *sent, w_first, w_piece, w_second)


def split_body(features, counts, pick_owner, pick_local, adjacency, cotangent, w_first, w_second):
    owners = pick_owner[0]
    picks = pick_local[0]
    width = w_first.shape[0]
    slots = features.shape[1]
    count_picks = owners.shape[0]
    wanted = owners * features.shape[0] + picks
    feat_piece = lax.all_gather(features, "grp", axis=0, tiled=True)
    count_piece = lax.all_gather(counts, "grp", axis=0, tiled=True)
    live = jnp.take(count_piece, wanted, axis=0)
    rows = count_picks * slots
    inputs = jnp.take(feat_piece, wanted, axis=0).reshape(rows, width)
    mask = (jnp.arange(slots)[None, :] < live[:, None]).reshape(rows, 1).astype(BF16)
    inputs = inputs * mask
    maskf = mask.astype(F32)
    adj = adjacency[0]
    agg_first = nn(adj, inputs).astype(BF16)
    pre = nn(agg_first, w_first)
    hidden = (maskf * jax.nn.silu(pre)).astype(BF16)
    agg_second = nn(adj, hidden).astype(BF16)
    output = (maskf * nn(agg_second, w_second)).astype(BF16)
    dout = cotangent[0] * mask

    def summed(a, b):
        part = lax.dot_general(a, b, (((0,), (0,)), ((), ())), preferred_element_type=F32)
        return lax.psum_scatter(part, "grp", scatter_dimension=0, tiled=True)

    grad_second = summed(dout, agg_second)
    dagg = nt(dout, w_second).astype(BF16)
    back = lax.dot_general(adj, dagg, (((0,), (0,)), ((), ())), preferred_element_type=F32)
    sig = jax.nn.sigmoid(pre)
    dpre = (maskf * back * sig * (1.0 + pre * (1.0 - sig))).astype(BF16)
    grad_first = summed(dpre, agg_first)
    return (output.reshape(1, rows, width), grad_first, grad_second)


def solution(mesh):
    n = mesh.shape["grp"]

    def body(*args):
        rows = args[4].shape[1]
        small = n & (n - 1) == 0 and n > PLANE and rows == LANES and n * rows <= 4096
        return whole_body(n, *args) if small else split_body(*args)

    in_specs = (
        P(("parts", "grp"), None, None),
        P(("parts", "grp")),
        P(("parts", "grp"), None),
        P(("parts", "grp"), None),
        P(("parts", "grp"), None, None),
        P(("parts", "grp"), None, None),
        P(),
        P(),
    )
    out_specs = (
        P(("parts", "grp"), None, None),
        P(("parts", "grp"), None),
        P(("parts", "grp"), None),
    )
    return jax.shard_map(body, mesh=mesh, in_specs=in_specs, out_specs=out_specs, check_vma=False)
```

time: 49.1 us -> 51.8 us (1.055)
  Pallas kernels: 12.8 us -> 16.1 us
  starting transfers between devices: 13.5 us -> 12.9 us
    pallas_call x5 -> x4, Pallas kernels: 12.8 us -> 16.1 us  [the longest x1 11.5 us: whole_body(): pl.pallas_call(functools.partial(step_kernel, n, own, slots), out_shape=(...]
    ppermute x12 -> x10, starting transfers between devices: 13.5 us -> 12.9 us  [swap(): return lax.ppermute(x, 'grp', [(i, i ^ s) for i in range(n)])]
    unnamed x12 -> x22, local copies, waits for them, and re-layouts: 4.14 us -> 3.95 us
    ppermute x12 -> x10, waiting for transfers between devices: 17.7 us -> 17.8 us  [swap(): return lax.ppermute(x, 'grp', [(i, i ^ s) for i in range(n)])]
  transfers between devices with their start and end apart: 12 -> 10, of which waited for: 4 -> 5; matrix products, arithmetic and copies ran while one was open for 0% -> 0% of each run, Pallas kernels for 18% -> 0%
where the time goes in v4:
time: 51.8 us; the launch traced here: 51.5 us
  waiting for transfers between devices  17.8 us (34%)
  Pallas kernels  16.1 us (31%)
  starting transfers between devices  12.9 us (25%)
  local copies, waits for them, and re-layouts  3.95 us (8%)
  between operations  0.75 us (1%)
    ppermute x10, waiting for transfers between devices, swap(): return lax.ppermute(x, 'grp', [(i, i ^ s) for i in range(n)])  17.8 us
    ppermute x10, starting transfers between devices, swap(): return lax.ppermute(x, 'grp', [(i, i ^ s) for i in range(n)])  12.9 us
    pallas_call x1, Pallas kernels, whole_body(): pl.pallas_call(functools.partial(step_kernel, n, own, slots), out_shape=(...  11.5 us
    pallas_call x1, Pallas kernels, whole_body(): pl.pallas_call(prepare_kernel, out_shape=(jax.ShapeDtypeStruct((piece_row...  4.49 us
    unnamed x22, local copies, waits for them, and re-layouts  3.95 us
  transfers between devices with their start and end apart: 10, of which 5 were waited for; matrix products, arithmetic and copies ran while one was open for 0% of the time, Pallas kernels for 0%

profile of v4, /device:TPU:0, one launch (start us, length us, event | category | flops | bytes accessed | tf_op | source)
XLA Modules:
  0.0 51.5 jit_solution(3527555265083760167)
XLA Ops:
  0.6 4.5 %shard_map.103 = (bf16[400,128]{1,0:T(8,128)(2,1)}, bf16[1024,128]{1,0:T(8,128)(2,1)}, bf16[1024,128]{1,0:T(8,128)(2,1)}, bf16[64,1024]{1,0:T(8,128)(2,1)}) custom-call(s32[1]{0:T(128)} %bitcast.me, s32[2]{0:T(128)} %counts.1, s32[1,8]{1,0:T(1,128)} %owner.1, s32[1,8]{1,0:T(1,128)} %local.1, bf16[2,16,1024]{2,1,0:T(8,128)(2,1)} %features.1, ...), custom_call_target="tpu_custom_call" | custom-call | tf_op jit(solution)/shard_map/pallas_call | solution.py:212
  5.1 3.0 %collective-permute-start.3 = (bf16[1024,128]{1,0:T(8,128)(2,1)}, bf16[1024,128]{1,0:T(8,128)(2,1)S(1)}, u32[]{:S(2)}, u32[]{:S(2)}) collective-permute-start(bf16[1024,128]{1,0:T(8,128)(2,1)} %get-tuple-element.13), channel_id=1, source_target_pairs={{0,2},{1,3},{2,0},{3,1},{4,6},{5,7},{6,4},{7,5},{8,10},{9,11},{10,... | collective-permute-start | bytes 786440 | tf_op jit(solution)/shard_map/ppermute | solution.py:210
  8.2 3.6 %collective-permute-start.2 = (bf16[400,128]{1,0:T(8,128)(2,1)}, bf16[400,128]{1,0:T(8,128)(2,1)S(1)}, u32[]{:S(2)}, u32[]{:S(2)}) collective-permute-start(bf16[400,128]{1,0:T(8,128)(2,1)} %get-tuple-element.11.refs_0_), channel_id=1, source_target_pairs={{0,12},{1,13},{2,14},{3,15},{4,8},{5,9},{6,10},{7,11},{8,4},{9,5},... | collective-permute-start | bytes 307208 | tf_op jit(solution)/shard_map/ppermute | solution.py:210
  11.8 0.0 collective-permute-start.1
  11.8 0.8 %collective-permute-start = (bf16[400,128]{1,0:T(8,128)(2,1)}, bf16[400,128]{1,0:T(8,128)(2,1)S(1)}, u32[]{:S(2)}, u32[]{:S(2)}) collective-permute-start(bf16[400,128]{1,0:T(8,128)(2,1)} %get-tuple-element.11.refs_0_), channel_id=1, source_target_pairs={{0,4},{1,5},{2,6},{3,7},{4,0},{5,1},{6,2},{7,3},{8,12},{9,13},{10,... | collective-permute-start | bytes 307208 | tf_op jit(solution)/shard_map/ppermute | solution.py:210
  12.6 3.4 %collective-permute-done.2.refs_3_ = bf16[400,128]{1,0:T(8,128)(2,1)S(1)} collective-permute-done((bf16[400,128]{1,0:T(8,128)(2,1)}, bf16[400,128]{1,0:T(8,128)(2,1)S(1)}, u32[]{:S(2)}, u32[]{:S(2)}) %collective-permute-start.2) | collective-permute-done | bytes 102432 | tf_op jit(solution)/shard_map/ppermute | solution.py:210
  16.0 4.3 %collective-permute-done.1.refs_2_ = bf16[400,128]{1,0:T(8,128)(2,1)S(1)} collective-permute-done((bf16[400,128]{1,0:T(8,128)(2,1)}, bf16[400,128]{1,0:T(8,128)(2,1)S(1)}, u32[]{:S(2)}, u32[]{:S(2)}) %collective-permute-start.1) | collective-permute-done | bytes 102432 | tf_op jit(solution)/shard_map/ppermute | solution.py:210
  20.3 0.0 collective-permute-done.refs_1_
  20.3 0.0 collective-permute-done.3.refs_5_.other
  20.3 0.0 copy-start.2
  20.3 0.0 copy-start
  20.3 1.0 %copy-done = bf16[1024,128]{1,0:T(8,128)(2,1)S(1)} copy-done((bf16[1024,128]{1,0:T(8,128)(2,1)S(1)}, bf16[1024,128]{1,0:T(8,128)(2,1)}, u32[]{:S(2)}) %copy-start) | copy-done | bytes 262168
  21.4 0.0 copy-start.8
  21.4 0.9 %copy-done.8 = bf16[400,128]{1,0:T(8,128)(2,1)S(1)} copy-done((bf16[400,128]{1,0:T(8,128)(2,1)S(1)}, bf16[400,128]{1,0:T(8,128)(2,1)}, u32[]{:S(2)}) %copy-start.8) | copy-done | bytes 102424
  22.3 0.1 shard_map.104
  22.3 0.0 copy-start.7
  22.3 0.6 %collective-permute-start.5 = (bf16[1600,128]{1,0:T(8,128)(2,1)S(1)}, bf16[1600,128]{1,0:T(8,128)(2,1)S(1)}, u32[]{:S(2)}, u32[]{:S(2)}) collective-permute-start(bf16[1600,128]{1,0:T(8,128)(2,1)S(1)} %get-tuple-element.14.refs_0_), channel_id=1, source_target_pairs={{0,2},{1,3},{2,0},{3,1},{4,6},{5,7},{6,4},{7,5},{8,10},{9,11},{10,... | collective-permute-start | bytes 1228808 | tf_op jit(solution)/shard_map/ppermute | solution.py:210
  22.9 0.4 collective-permute-start.6
  23.3 2.6 %collective-permute-start.7 = (bf16[512,128]{1,0:T(8,128)(2,1)S(1)}, bf16[512,128]{1,0:T(8,128)(2,1)S(1)}, u32[]{:S(2)}, u32[]{:S(2)}) collective-permute-start(bf16[512,128]{1,0:T(8,128)(2,1)S(1)} %get-tuple-element.16), channel_id=1, source_target_pairs={{0,8},{1,9},{2,10},{3,11},{4,12},{5,13},{6,14},{7,15},{8,0},{9,1},... | collective-permute-start | bytes 393224 | tf_op jit(solution)/shard_map/ppermute | solution.py:210
  25.9 1.3 %collective-permute-start.8 = (bf16[512,128]{1,0:T(8,128)(2,1)S(1)}, bf16[512,128]{1,0:T(8,128)(2,1)S(1)}, u32[]{:S(2)}, u32[]{:S(2)}) collective-permute-start(bf16[512,128]{1,0:T(8,128)(2,1)S(1)} %get-tuple-element.17), channel_id=1, source_target_pairs={{0,12},{1,13},{2,14},{3,15},{4,8},{5,9},{6,10},{7,11},{8,4},{9,5},... | collective-permute-start | bytes 393224 | tf_op jit(solution)/shard_map/ppermute | solution.py:210
  27.3 1.5 %collective-permute-done.6.refs_0_.refs_6_ = bf16[512,128]{1,0:T(8,128)(2,1)S(1)} collective-permute-done((bf16[512,128]{1,0:T(8,128)(2,1)S(1)}, bf16[512,128]{1,0:T(8,128)(2,1)S(1)}, u32[]{:S(2)}, u32[]{:S(2)}) %collective-permute-start.6) | collective-permute-done | bytes 131104 | tf_op jit(solution)/shard_map/ppermute | solution.py:210
  28.8 0.0 copy-start.4
  28.8 6.4 %collective-permute-done.7.refs_1_.refs_7_ = bf16[512,128]{1,0:T(8,128)(2,1)S(1)} collective-permute-done((bf16[512,128]{1,0:T(8,128)(2,1)S(1)}, bf16[512,128]{1,0:T(8,128)(2,1)S(1)}, u32[]{:S(2)}, u32[]{:S(2)}) %collective-permute-start.7) | collective-permute-done | bytes 131104 | tf_op jit(solution)/shard_map/ppermute | solution.py:210
  35.1 0.0 copy-start.5
  35.1 0.0 collective-permute-done.8.refs_2_.refs_8_
  35.1 0.0 copy-start.6
  35.1 0.0 collective-permute-done.5.across.refs_2_
  35.1 0.0 copy-start.1
  35.1 1.0 %copy-done.1 = bf16[1024,128]{1,0:T(8,128)(2,1)S(1)} copy-done((bf16[1024,128]{1,0:T(8,128)(2,1)S(1)}, bf16[1024,128]{1,0:T(8,128)(2,1)}, u32[]{:S(2)}) %copy-start.1) | copy-done | bytes 262168
  36.2 0.0 copy-start.3
  36.2 0.1 collective-permute-start.9
  36.3 0.5 collective-permute-start.4
  36.8 2.2 %collective-permute-done.4.refs_1_ = bf16[1600,128]{1,0:T(8,128)(2,1)S(1)} collective-permute-done((bf16[1600,128]{1,0:T(8,128)(2,1)S(1)}, bf16[1600,128]{1,0:T(8,128)(2,1)S(1)}, u32[]{:S(2)}, u32[]{:S(2)}) %collective-permute-start.4) | collective-permute-done | bytes 409632 | tf_op jit(solution)/shard_map/ppermute | solution.py:210
  39.0 0.0 copy-start.10
  39.0 0.0 collective-permute-done.9.refs_3_
  39.0 0.0 copy-start.9
  39.0 0.0 copy-done.2
  39.0 0.0 copy-done.7
  39.0 0.0 copy-done.4
  39.0 0.0 copy-done.5
  39.0 0.0 copy-done.6
  39.1 0.0 copy-done.3
  39.1 0.7 %copy-done.10 = bf16[1600,128]{1,0:T(8,128)(2,1)} copy-done((bf16[1600,128]{1,0:T(8,128)(2,1)}, bf16[1600,128]{1,0:T(8,128)(2,1)S(1)}, u32[]{:S(2)}) %copy-start.10) | copy-done | bytes 409624
  39.8 0.3 copy-done.9
  40.0 11.5 %shard_map.106 = (bf16[1,128,1024]{2,1,0:T(8,128)(2,1)}, f32[64,1024]{1,0:T(8,128)}, f32[64,1024]{1,0:T(8,128)}) custom-call(s32[1]{0:T(128)} %bitcast.me, bf16[1600,128]{1,0:T(8,128)(2,1)} %copy-done.7, bf16[1600,128]{1,0:T(8,128)(2,1)} %copy-done.10, bf16[1600,128]{1,0:T(8,128)(2,1)} %copy-done.3, bf16[2624,128]{1,0:T(8,128)(2,1)} %copy-done.9, ...), custom_call_target="tpu_custom_call" | custom-call | tf_op jit(solution)/shard_map/pallas_call | solution.py:259
  (1 shorter events, 0.0 us)
Async XLA Ops:
  5.1 15.2 %collective-permute-start.3 = (bf16[1024,128]{1,0:T(8,128)(2,1)}, bf16[1024,128]{1,0:T(8,128)(2,1)S(1)}, u32[]{:S(2)}, u32[]{:S(2)}) collective-permute-start(bf16[1024,128]{1,0:T(8,128)(2,1)} %get-tuple-element.13), channel_id=1, source_target_pairs={{0,2},{1,3},{2,0},{3,1},{4,6},{5,7},{6,4},{7,5},{8,10},{9,11},{10,... | collective-permute-start | bytes 786440 | tf_op jit(solution)/shard_map/ppermute | solution.py:210
  8.2 7.8 %collective-permute-start.2 = (bf16[400,128]{1,0:T(8,128)(2,1)}, bf16[400,128]{1,0:T(8,128)(2,1)S(1)}, u32[]{:S(2)}, u32[]{:S(2)}) collective-permute-start(bf16[400,128]{1,0:T(8,128)(2,1)} %get-tuple-element.11.refs_0_), channel_id=1, source_target_pairs={{0,12},{1,13},{2,14},{3,15},{4,8},{5,9},{6,10},{7,11},{8,4},{9,5},... | collective-permute-start | bytes 307208 | tf_op jit(solution)/shard_map/ppermute | solution.py:210
  11.8 8.5 %collective-permute-start.1 = (bf16[400,128]{1,0:T(8,128)(2,1)}, bf16[400,128]{1,0:T(8,128)(2,1)S(1)}, u32[]{:S(2)}, u32[]{:S(2)}) collective-permute-start(bf16[400,128]{1,0:T(8,128)(2,1)} %get-tuple-element.11.refs_0_), channel_id=1, source_target_pairs={{0,8},{1,9},{2,10},{3,11},{4,12},{5,13},{6,14},{7,15},{8,0},{9,1},... | collective-permute-start | bytes 307208 | tf_op jit(solution)/shard_map/ppermute | solution.py:210
  11.8 8.5 %collective-permute-start = (bf16[400,128]{1,0:T(8,128)(2,1)}, bf16[400,128]{1,0:T(8,128)(2,1)S(1)}, u32[]{:S(2)}, u32[]{:S(2)}) collective-permute-start(bf16[400,128]{1,0:T(8,128)(2,1)} %get-tuple-element.11.refs_0_), channel_id=1, source_target_pairs={{0,4},{1,5},{2,6},{3,7},{4,0},{5,1},{6,2},{7,3},{8,12},{9,13},{10,... | collective-permute-start | bytes 307208 | tf_op jit(solution)/shard_map/ppermute | solution.py:210
  20.3 18.7 %copy-start.2 = (bf16[1024,128]{1,0:T(8,128)(2,1)}, bf16[1024,128]{1,0:T(8,128)(2,1)S(1)}, u32[]{:S(2)}) copy-start(bf16[1024,128]{1,0:T(8,128)(2,1)S(1)} %collective-permute-done.3.refs_5_.other) | copy-start | bytes 786436
  20.3 1.0 %copy-start = (bf16[1024,128]{1,0:T(8,128)(2,1)S(1)}, bf16[1024,128]{1,0:T(8,128)(2,1)}, u32[]{:S(2)}) copy-start(bf16[1024,128]{1,0:T(8,128)(2,1)} %get-tuple-element.12.refs_4_.near) | copy-start | bytes 786436
  21.4 0.9 %copy-start.8 = (bf16[400,128]{1,0:T(8,128)(2,1)S(1)}, bf16[400,128]{1,0:T(8,128)(2,1)}, u32[]{:S(2)}) copy-start(bf16[400,128]{1,0:T(8,128)(2,1)} %get-tuple-element.11.refs_0_) | copy-start | bytes 307204
  22.3 16.7 %copy-start.7 = (bf16[1600,128]{1,0:T(8,128)(2,1)}, bf16[1600,128]{1,0:T(8,128)(2,1)S(1)}, u32[]{:S(2)}) copy-start(bf16[1600,128]{1,0:T(8,128)(2,1)S(1)} %get-tuple-element.14.refs_0_) | copy-start | bytes 1228804
  22.3 12.8 %collective-permute-start.5 = (bf16[1600,128]{1,0:T(8,128)(2,1)S(1)}, bf16[1600,128]{1,0:T(8,128)(2,1)S(1)}, u32[]{:S(2)}, u32[]{:S(2)}) collective-permute-start(bf16[1600,128]{1,0:T(8,128)(2,1)S(1)} %get-tuple-element.14.refs_0_), channel_id=1, source_target_pairs={{0,2},{1,3},{2,0},{3,1},{4,6},{5,7},{6,4},{7,5},{8,10},{9,11},{10,... | collective-permute-start | bytes 1228808 | tf_op jit(solution)/shard_map/ppermute | solution.py:210
  22.9 5.8 %collective-permute-start.6 = (bf16[512,128]{1,0:T(8,128)(2,1)S(1)}, bf16[512,128]{1,0:T(8,128)(2,1)S(1)}, u32[]{:S(2)}, u32[]{:S(2)}) collective-permute-start(bf16[512,128]{1,0:T(8,128)(2,1)S(1)} %get-tuple-element.15), channel_id=1, source_target_pairs={{0,4},{1,5},{2,6},{3,7},{4,0},{5,1},{6,2},{7,3},{8,12},{9,13},{10,... | collective-permute-start | bytes 393224 | tf_op jit(solution)/shard_map/ppermute | solution.py:210
  23.3 11.8 %collective-permute-start.7 = (bf16[512,128]{1,0:T(8,128)(2,1)S(1)}, bf16[512,128]{1,0:T(8,128)(2,1)S(1)}, u32[]{:S(2)}, u32[]{:S(2)}) collective-permute-start(bf16[512,128]{1,0:T(8,128)(2,1)S(1)} %get-tuple-element.16), channel_id=1, source_target_pairs={{0,8},{1,9},{2,10},{3,11},{4,12},{5,13},{6,14},{7,15},{8,0},{9,1},... | collective-permute-start | bytes 393224 | tf_op jit(solution)/shard_map/ppermute | solution.py:210
  25.9 9.2 %collective-permute-start.8 = (bf16[512,128]{1,0:T(8,128)(2,1)S(1)}, bf16[512,128]{1,0:T(8,128)(2,1)S(1)}, u32[]{:S(2)}, u32[]{:S(2)}) collective-permute-start(bf16[512,128]{1,0:T(8,128)(2,1)S(1)} %get-tuple-element.17), channel_id=1, source_target_pairs={{0,12},{1,13},{2,14},{3,15},{4,8},{5,9},{6,10},{7,11},{8,4},{9,5},... | collective-permute-start | bytes 393224 | tf_op jit(solution)/shard_map/ppermute | solution.py:210
  28.8 10.3 %copy-start.4 = (bf16[512,128]{1,0:T(8,128)(2,1)}, bf16[512,128]{1,0:T(8,128)(2,1)S(1)}, u32[]{:S(2)}) copy-start(bf16[512,128]{1,0:T(8,128)(2,1)S(1)} %collective-permute-done.6.refs_0_.refs_6_) | copy-start | bytes 393220
  35.1 3.9 %copy-start.5 = (bf16[512,128]{1,0:T(8,128)(2,1)}, bf16[512,128]{1,0:T(8,128)(2,1)S(1)}, u32[]{:S(2)}) copy-start(bf16[512,128]{1,0:T(8,128)(2,1)S(1)} %collective-permute-done.7.refs_1_.refs_7_) | copy-start | bytes 393220
  35.1 3.9 %copy-start.6 = (bf16[512,128]{1,0:T(8,128)(2,1)}, bf16[512,128]{1,0:T(8,128)(2,1)S(1)}, u32[]{:S(2)}) copy-start(bf16[512,128]{1,0:T(8,128)(2,1)S(1)} %collective-permute-done.8.refs_2_.refs_8_) | copy-start | bytes 393220
  35.1 1.0 %copy-start.1 = (bf16[1024,128]{1,0:T(8,128)(2,1)S(1)}, bf16[1024,128]{1,0:T(8,128)(2,1)}, u32[]{:S(2)}) copy-start(bf16[1024,128]{1,0:T(8,128)(2,1)} %get-tuple-element.12.refs_4_.near) | copy-start | bytes 786436
  36.2 2.9 %copy-start.3 = (bf16[1600,128]{1,0:T(8,128)(2,1)}, bf16[1600,128]{1,0:T(8,128)(2,1)S(1)}, u32[]{:S(2)}) copy-start(bf16[1600,128]{1,0:T(8,128)(2,1)S(1)} %collective-permute-done.5.across.refs_2_) | copy-start | bytes 1228804
  36.2 2.8 %collective-permute-start.9 = (bf16[2624,128]{1,0:T(8,128)(2,1)S(1)}, bf16[2624,128]{1,0:T(8,128)(2,1)S(1)}, u32[]{:S(2)}, u32[]{:S(2)}) collective-permute-start(bf16[2624,128]{1,0:T(8,128)(2,1)S(1)} %shard_map.105), channel_id=1, source_target_pairs={{0,1},{1,0},{2,3},{3,2},{4,5},{5,4},{6,7},{7,6},{8,9},{9,8},{10,11... | collective-permute-start | bytes 2015240 | tf_op jit(solution)/shard_map/ppermute | solution.py:210
  36.3 2.7 %collective-permute-start.4 = (bf16[1600,128]{1,0:T(8,128)(2,1)S(1)}, bf16[1600,128]{1,0:T(8,128)(2,1)S(1)}, u32[]{:S(2)}, u32[]{:S(2)}) collective-permute-start(bf16[1600,128]{1,0:T(8,128)(2,1)S(1)} %get-tuple-element.14.refs_0_), channel_id=1, source_target_pairs={{0,1},{1,0},{2,3},{3,2},{4,5},{5,4},{6,7},{7,6},{8,9},{9,8},{10,11... | collective-permute-start | bytes 1228808 | tf_op jit(solution)/shard_map/ppermute | solution.py:210
  39.0 0.8 %copy-start.10 = (bf16[1600,128]{1,0:T(8,128)(2,1)}, bf16[1600,128]{1,0:T(8,128)(2,1)S(1)}, u32[]{:S(2)}) copy-start(bf16[1600,128]{1,0:T(8,128)(2,1)S(1)} %collective-permute-done.4.refs_1_) | copy-start | bytes 1228804
  39.0 1.0 %copy-start.9 = (bf16[2624,128]{1,0:T(8,128)(2,1)}, bf16[2624,128]{1,0:T(8,128)(2,1)S(1)}, u32[]{:S(2)}) copy-start(bf16[2624,128]{1,0:T(8,128)(2,1)S(1)} %collective-permute-done.9.refs_3_) | copy-start | bytes 2015236

commit v5 on v4

v5 whole, which is shorter than its diff:
```python
import functools

import jax
import jax.numpy as jnp
from jax import lax
from jax.experimental import pallas as pl
from jax.experimental.pallas import tpu as pltpu
from jax.sharding import PartitionSpec as P

F32 = jnp.float32
BF16 = jnp.bfloat16
VMEM = pl.BlockSpec(memory_space=pltpu.VMEM)
SMEM = pl.BlockSpec(memory_space=pltpu.SMEM)
PLANE = 4
LIMIT = 24 * 2**20
SMALL = 8 * 2**20
LANES = 128
META = 16


def nn(a, b):
    return jnp.dot(a, b, preferred_element_type=F32)


def nt(a, b):
    return lax.dot_general(a, b, (((1,), (1,)), ((), ())), preferred_element_type=F32)


def pack_kernel(counts, owner, local, features, adjacency, piece):
    own, slots, width = features.shape
    rows = adjacency.shape[1]
    held = own * slots
    slot = lax.broadcasted_iota(jnp.int32, (slots, LANES), 0)
    for i in range(own):
        live = slot < counts[i]
        for b in range(width // LANES):
            block = features[i, :, b * LANES : (b + 1) * LANES]
            at = b * held + i * slots
            piece[at : at + slots, :] = jnp.where(live, block, jnp.zeros_like(block))
    at = held * (width // LANES)
    piece[at : at + rows, :] = adjacency[0]
    at += rows
    line = lax.broadcasted_iota(jnp.int32, (META, LANES), 0)
    pick = lax.broadcasted_iota(jnp.int32, (META, LANES), 1) // slots
    meta = jnp.zeros((META, LANES), jnp.int32)
    for k in range(owner.shape[1]):
        wanted = owner[0, k] * own + local[0, k]
        meta = jnp.where((line == 0) & (pick == k), wanted, meta)
    for i in range(own):
        meta = jnp.where(line == 1 + i, counts[i], meta)
    piece[at : at + META, :] = meta.astype(F32).astype(BF16)


def columns_kernel(n, me, cotangent, w_second, near, across, turned, back):
    each = near.shape[0] // n
    cot = cotangent[0]
    turned[...] = cot.astype(F32).T.astype(BF16)
    back[...] = nt(w_second[...], cot).astype(BF16)
    for h, out in enumerate((near, across)):
        for i in range(out.shape[0] // (2 * each)):
            to = PLANE * (i // 2) + 2 * h + i % 2
            span = pl.ds(pl.multiple_of((me[0] ^ to) * each, each), each)
            at = i * 2 * each
            out[at : at + each, :] = turned[span, :]
            out[at + each : at + 2 * each, :] = back[span, :]


def regroup_kernel(parts, *refs):
    pieces, near, across = refs[:parts], refs[parts], refs[parts + 1]
    stack, *sent = refs[parts + 2 :]
    rows = pieces[0].shape[0]
    for i, ref in enumerate(pieces):
        stack[i * rows : (i + 1) * rows, :] = ref[...]
    half = sent[0].shape[0] // 2
    for s, out in enumerate(sent, 1):
        out[:half, :] = near[s * half : (s + 1) * half, :]
        out[half:, :] = across[s * half : (s + 1) * half, :]


def pair_kernel(parts, across, near, other, *refs):
    sent, out = refs[: parts - 1], refs[parts - 1]
    deep = across.shape[0]
    out[:deep, :] = across[...]
    half = near.shape[0] // parts
    rows = half // 2
    for s in range(parts):
        for h in range(2):
            if s:
                block = sent[s - 1][h * half + rows : (h + 1) * half, :]
            else:
                block = (near, other)[h][rows:half, :]
            at = deep + (2 * s + h) * rows
            out[at : at + rows, :] = block


def lay_out(pack, q, parts, held, rows, width, feat, adj, meta):
    at = 0
    for p in range(q * parts, (q + 1) * parts):
        for b in range(width // LANES):
            feat[p * held : (p + 1) * held, b * LANES : (b + 1) * LANES] = pack[at : at + held, :]
            at += held
        adj[p] = pack[at : at + rows, :]
        at += rows
        meta[p] = pack[at : at + META, :]
        at += META


def spread_of(n, place, held, slots, adj, picks):
    parts = n // PLANE
    line = lax.broadcasted_iota(jnp.int32, (held, LANES), 0)
    lane = lax.broadcasted_iota(jnp.int32, (1, LANES), 1) % slots
    owners = [place ^ (PLANE * (p % parts) + p // parts) for p in range(n)]
    code = jnp.concatenate([line + owner * held for owner in owners], axis=0)
    chosen = jnp.where(code == picks * slots + lane, 1.0, 0.0).astype(BF16)
    return nt(adj, chosen).astype(BF16)


def early_kernel(n, own, slots, me, stack, beside, w_first, feat, lifted, spread, adj, meta, w_piece):
    parts = n // PLANE
    width = w_first.shape[0]
    held = own * slots
    rows = adj.shape[1]
    place = me[0]
    lay_out(stack, 0, parts, held, rows, width, feat, adj, meta)
    lay_out(beside, 1, parts, held, rows, width, feat, adj, meta)
    lifted[...] = nn(feat[...], w_first[...]).astype(BF16)
    for p in range(n // 2):
        picks = meta[p, 0:1, :].astype(F32).astype(jnp.int32)
        spread[p * rows : (p + 1) * rows, :] = spread_of(n, place, held, slots, adj[p], picks)
    each = w_piece.shape[0]
    wide = max(each, LANES)
    per = wide // each
    start = pl.multiple_of((place // per) * wide, wide)
    block = w_first[:, pl.ds(start, wide)].astype(F32).T
    part = block[:each]
    for q in range(1, per):
        part = jnp.where(place % per == q, block[q * each : (q + 1) * each], part)
    w_piece[...] = part.astype(BF16)


def step_kernel(n, own, slots, me, *refs):
    parts = n // PLANE
    across, pair, near, other, *sent = refs[: 3 + parts]
    early_feat, early_lifted, early_spread, early_adj, early_meta, w_piece = refs[3 + parts : 9 + parts]
    w_first, w_second, output, grad_first, grad_second = refs[9 + parts : 14 + parts]
    hidden, spread, feat, adj, meta, dout, dpre, lifted = refs[14 + parts :]
    width = w_first.shape[0]
    held = own * slots
    rows = adj.shape[1]
    place = me[0]
    deep = across.shape[0]
    first = n // 2

    feat[: first * held, :] = early_feat[...]
    lifted[: first * held, :] = early_lifted[...]
    spread[: first * rows, :] = early_spread[...]
    adj[:first] = early_adj[...]
    meta[:first] = early_meta[...]
    lay_out(across, 2, parts, held, rows, width, feat, adj, meta)
    lay_out(pair, 3, parts, held, rows, width, feat, adj, meta)
    metas = [meta[p].astype(F32) for p in range(n)]
    picks = jnp.concatenate([m[0:1] for m in metas], axis=0).astype(jnp.int32)
    lane = lax.broadcasted_iota(jnp.int32, (n, LANES), 1) % slots
    count = jnp.zeros((n, LANES), jnp.int32)
    for p in range(n):
        for i in range(own):
            cluster = (place ^ (PLANE * (p % parts) + p // parts)) * own + i
            count = jnp.where(picks == cluster, metas[p][1 + i : 2 + i].astype(jnp.int32), count)
    masks = (lane < count).astype(F32)

    late = slice(first * held, n * held)
    lifted[late, :] = nn(feat[late, :], w_first[...]).astype(BF16)
    for p in range(first, n):
        span = slice(p * rows, (p + 1) * rows)
        spread[span, :] = spread_of(n, place, held, slots, adj[p], picks[p : p + 1])
    lifted_piece = nt(w_piece[...], feat[...]).astype(BF16)
    step = min(width, 2 * LANES)
    for c in range(0, width, step):
        half = 0.5 * nn(spread[...], lifted[:, c : c + step])
        hidden[:, c : c + step] = (half + half * jnp.tanh(half)).astype(BF16)
    pre_piece = nt(lifted_piece, spread[...])
    live = jnp.broadcast_to(masks[0:1], (rows, LANES)).T[:, :1]
    agg = nn(adj[0], (hidden[:rows, :].astype(F32) * live).astype(BF16)).astype(BF16)
    output[0] = (nn(agg, w_second[...]) * live).astype(BF16)

    each = grad_first.shape[0]
    half = near.shape[0] // parts
    for p in range(n):
        mask = masks[p : p + 1]
        span = slice(p * rows, (p + 1) * rows)
        s, h, b = p % parts, p // parts // 2, p // parts % 2
        if b:
            at = deep + (2 * s + h) * 2 * each
            source = pair[at : at + 2 * each, :]
        elif s:
            source = sent[s - 1][h * half : h * half + 2 * each, :]
        else:
            source = (near, other)[h][: 2 * each, :]
        back = nn((source.astype(F32) * mask).astype(BF16), adj[p]) * mask
        dout[:, span] = back[:each].astype(BF16)
        pre = pre_piece[:, span]
        sig = 0.5 + 0.5 * jnp.tanh(0.5 * pre)
        dpre[:, span] = (back[each:] * sig * (1.0 + pre * (1.0 - sig))).astype(BF16)
    grad_second[...] = nn(dout[...], hidden[...])
    moved = nn(dpre[...], spread[...])
    grad_first[...] = nn(moved.astype(BF16), feat[...])


def whole_body(n, features, counts, pick_owner, pick_local, adjacency, cotangent, w_first, w_second):
    own, slots, width = features.shape
    rows = adjacency.shape[1]
    held = own * slots
    each = width // n
    total_rows = n * held
    piece_rows = held * (width // LANES) + rows + META
    limit = pltpu.CompilerParams(vmem_limit_bytes=LIMIT)
    small = pltpu.CompilerParams(vmem_limit_bytes=SMALL)
    me = lax.axis_index("grp").reshape(1).astype(jnp.int32)

    def swap(x, s):
        return lax.ppermute(x, "grp", [(i, i ^ s) for i in range(n)])

    piece = pl.pallas_call(
        pack_kernel,
        out_shape=jax.ShapeDtypeStruct((piece_rows, LANES), BF16),
        in_specs=[SMEM] * 3 + [VMEM] * 2,
        out_specs=VMEM,
        compiler_params=small,
        cost_estimate=pl.CostEstimate(flops=10**10, bytes_accessed=2**18, transcendentals=0),
    )(counts, pick_owner, pick_local, features, adjacency)
    cotangent, _ = lax.optimization_barrier((cotangent, piece))
    near, other = pl.pallas_call(
        functools.partial(columns_kernel, n),
        out_shape=(jax.ShapeDtypeStruct((n * each, rows), BF16),) * 2,
        in_specs=[SMEM, VMEM, VMEM],
        out_specs=(VMEM,) * 2,
        scratch_shapes=[pltpu.VMEM((width, rows), BF16)] * 2,
        compiler_params=small,
    )(me, cotangent, w_second)
    far = range(PLANE, n, PLANE)
    parts = n // PLANE
    along = [swap(piece, s) for s in far]
    other = swap(other, 2)
    stack, *sent = pl.pallas_call(
        functools.partial(regroup_kernel, parts),
        out_shape=(jax.ShapeDtypeStruct((parts * piece_rows, LANES), BF16),)
        + (jax.ShapeDtypeStruct((PLANE * 2 * each, rows), BF16),) * len(far),
        in_specs=[VMEM] * (parts + 2),
        out_specs=(VMEM,) * parts,
        compiler_params=small,
    )(piece, *along, near, other)
    sent = [swap(x, s) for x, s in zip(sent, far)]
    beside = swap(stack, 1)
    across = swap(stack, 2)
    across, beside = lax.optimization_barrier((across, beside))
    pair = pl.pallas_call(
        functools.partial(pair_kernel, parts),
        out_shape=jax.ShapeDtypeStruct((parts * piece_rows + n * each, LANES), BF16),
        in_specs=[VMEM] * (parts + 2),
        out_specs=VMEM,
        compiler_params=small,
    )(across, near, other, *sent)
    pair = swap(pair, 1)
    early = pl.pallas_call(
        functools.partial(early_kernel, n, own, slots),
        out_shape=(
            jax.ShapeDtypeStruct((total_rows // 2, width), BF16),
            jax.ShapeDtypeStruct((total_rows // 2, width), BF16),
            jax.ShapeDtypeStruct((n // 2 * rows, total_rows), BF16),
            jax.ShapeDtypeStruct((n // 2, rows, rows), BF16),
            jax.ShapeDtypeStruct((n // 2, META, LANES), BF16),
            jax.ShapeDtypeStruct((each, width), BF16),
        ),
        in_specs=[SMEM] + [VMEM] * 3,
        out_specs=(VMEM,) * 6,
        compiler_params=limit,
        cost_estimate=pl.CostEstimate(flops=2 * 10**9, bytes_accessed=2**20, transcendentals=0),
    )(me, stack, beside, w_first)
    return pl.pallas_call(
        functools.partial(step_kernel, n, own, slots),
        out_shape=(
            jax.ShapeDtypeStruct((1, rows, width), BF16),
            jax.ShapeDtypeStruct((each, width), F32),
            jax.ShapeDtypeStruct((each, width), F32),
        ),
        in_specs=[SMEM] + [VMEM] * (parts + 11),
        out_specs=(VMEM,) * 3,
        scratch_shapes=[
            pltpu.VMEM((n * rows, width), BF16),
            pltpu.VMEM((n * rows, total_rows), BF16),
            pltpu.VMEM((total_rows, width), BF16),
            pltpu.VMEM((n, rows, rows), BF16),
            pltpu.VMEM((n, META, LANES), BF16),
            pltpu.VMEM((each, n * rows), BF16),
            pltpu.VMEM((each, n * rows), BF16),
            pltpu.VMEM((total_rows, width), BF16),
        ],
        compiler_params=limit,
    )(me, across, pair, near, other, *sent, *early, w_first, w_second)


def split_body(features, counts, pick_owner, pick_local, adjacency, cotangent, w_first, w_second):
    owners = pick_owner[0]
    picks = pick_local[0]
    width = w_first.shape[0]
    slots = features.shape[1]
    count_picks = owners.shape[0]
    wanted = owners * features.shape[0] + picks
    feat_piece = lax.all_gather(features, "grp", axis=0, tiled=True)
    count_piece = lax.all_gather(counts, "grp", axis=0, tiled=True)
    live = jnp.take(count_piece, wanted, axis=0)
    rows = count_picks * slots
    inputs = jnp.take(feat_piece, wanted, axis=0).reshape(rows, width)
    mask = (jnp.arange(slots)[None, :] < live[:, None]).reshape(rows, 1).astype(BF16)
    inputs = inputs * mask
    maskf = mask.astype(F32)
    adj = adjacency[0]
    agg_first = nn(adj, inputs).astype(BF16)
    pre = nn(agg_first, w_first)
    hidden = (maskf * jax.nn.silu(pre)).astype(BF16)
    agg_second = nn(adj, hidden).astype(BF16)
    output = (maskf * nn(agg_second, w_second)).astype(BF16)
    dout = cotangent[0] * mask

    def summed(a, b):
        part = lax.dot_general(a, b, (((0,), (0,)), ((), ())), preferred_element_type=F32)
        return lax.psum_scatter(part, "grp", scatter_dimension=0, tiled=True)

    grad_second = summed(dout, agg_second)
    dagg = nt(dout, w_second).astype(BF16)
    back = lax.dot_general(adj, dagg, (((0,), (0,)), ((), ())), preferred_element_type=F32)
    sig = jax.nn.sigmoid(pre)
    dpre = (maskf * back * sig * (1.0 + pre * (1.0 - sig))).astype(BF16)
    grad_first = summed(dpre, agg_first)
    return (output.reshape(1, rows, width), grad_first, grad_second)


def solution(mesh):
    n = mesh.shape["grp"]

    def body(*args):
        rows = args[4].shape[1]
        small = n & (n - 1) == 0 and n > PLANE and rows == LANES and n * rows <= 4096
        return whole_body(n, *args) if small else split_body(*args)

    in_specs = (
        P(("parts", "grp"), None, None),
        P(("parts", "grp")),
        P(("parts", "grp"), None),
        P(("parts", "grp"), None),
        P(("parts", "grp"), None, None),
        P(("parts", "grp"), None, None),
        P(),
        P(),
    )
    out_specs = (
        P(("parts", "grp"), None, None),
        P(("parts", "grp"), None),
        P(("parts", "grp"), None),
    )
    return jax.shard_map(body, mesh=mesh, in_specs=in_specs, out_specs=out_specs, check_vma=False)
```

time: 51.8 us -> 47 us (0.907)
  Pallas kernels: 16.1 us -> 10.1 us
  waiting for transfers between devices: 17.8 us -> 18.9 us
  local copies, waits for them, and re-layouts: 3.95 us -> 4.56 us
    pallas_call x1, Pallas kernels: 11.5 us -> 7.71 us  [whole_body(): pl.pallas_call(functools.partial(step_kernel, n, own, slots), out_shape=(...]
    pallas_call x1 -> x3, Pallas kernels: 4.49 us -> 2.3 us  [the longest x1 1 us: whole_body(): pl.pallas_call(functools.partial(early_kernel, n, own, slots), out_shape=...]
    ppermute x10, waiting for transfers between devices: 17.8 us -> 18.9 us  [swap(): return lax.ppermute(x, 'grp', [(i, i ^ s) for i in range(n)])]
    unnamed x22 -> x16, local copies, waits for them, and re-layouts: 3.95 us -> 4.56 us
  transfers between devices with their start and end apart: 10 -> 10, of which waited for: 5 -> 5; matrix products, arithmetic and copies ran while one was open for 0% -> 0% of each run, Pallas kernels for 0% -> 2%
where the time goes in v5:
time: 47 us; the launch traced here: 46.7 us
  waiting for transfers between devices  18.9 us (40%)
  starting transfers between devices  12.5 us (27%)
  Pallas kernels  10.1 us (21%)
  local copies, waits for them, and re-layouts  4.56 us (10%)
  between operations  0.71 us (2%)
    ppermute x10, waiting for transfers between devices, swap(): return lax.ppermute(x, 'grp', [(i, i ^ s) for i in range(n)])  18.9 us
    ppermute x10, starting transfers between devices, swap(): return lax.ppermute(x, 'grp', [(i, i ^ s) for i in range(n)])  12.5 us
    pallas_call x1, Pallas kernels, whole_body(): pl.pallas_call(functools.partial(step_kernel, n, own, slots), out_shape=(...  7.71 us
    unnamed x16, local copies, waits for them, and re-layouts  4.56 us
    pallas_call x1, Pallas kernels, whole_body(): pl.pallas_call(functools.partial(early_kernel, n, own, slots), out_shape=...  1 us
  transfers between devices with their start and end apart: 10, of which 5 were waited for; matrix products, arithmetic and copies ran while one was open for 0% of the time, Pallas kernels for 2%

profile of v5, /device:TPU:0, one launch (start us, length us, event | category | flops | bytes accessed | tf_op | source)
XLA Modules:
  0.0 46.7 jit_solution(4002390576102290037)
XLA Ops:
  0.6 0.0 copy-start.3
  0.6 0.8 %copy-done.3 = bf16[2,16,1024]{2,1,0:T(8,128)(2,1)S(1)} copy-done((bf16[2,16,1024]{2,1,0:T(8,128)(2,1)S(1)}, bf16[2,16,1024]{2,1,0:T(8,128)(2,1)}, u32[]{:S(2)}) %copy-start.3) | copy-done | bytes 65560
  1.5 0.0 copy-start.4
  1.5 0.8 %copy-done.4 = bf16[1,128,128]{2,1,0:T(8,128)(2,1)S(1)} copy-done((bf16[1,128,128]{2,1,0:T(8,128)(2,1)S(1)}, bf16[1,128,128]{2,1,0:T(8,128)(2,1)}, u32[]{:S(2)}) %copy-start.4) | copy-done | bytes 32792
  2.2 0.0 copy-start.5
  2.2 0.7 %copy-done.5 = s32[2]{0:T(128)S(1)} copy-done((s32[2]{0:T(128)S(1)}, s32[2]{0:T(128)}, u32[]{:S(2)}) %copy-start.5) | copy-done | bytes 32
  2.9 0.0 copy-start.6
  2.9 0.7 %copy-done.6 = s32[1,8]{1,0:T(1,128)S(1)} copy-done((s32[1,8]{1,0:T(1,128)S(1)}, s32[1,8]{1,0:T(1,128)}, u32[]{:S(2)}) %copy-start.6) | copy-done | bytes 56
  3.5 0.0 copy-start.7
  3.5 0.7 %copy-done.7 = s32[1,8]{1,0:T(1,128)S(1)} copy-done((s32[1,8]{1,0:T(1,128)S(1)}, s32[1,8]{1,0:T(1,128)}, u32[]{:S(2)}) %copy-start.7) | copy-done | bytes 56
  4.2 0.0 copy-start
  4.2 0.0 copy-start.2
  4.2 0.6 %shard_map.103.refs_0_ = bf16[400,128]{1,0:T(8,128)(2,1)S(1)} custom-call(s32[2]{0:T(128)S(1)} %copy-done.5, s32[1,8]{1,0:T(1,128)S(1)} %copy-done.6, s32[1,8]{1,0:T(1,128)S(1)} %copy-done.7, bf16[2,16,1024]{2,1,0:T(8,128)(2,1)S(1)} %copy-done.3, bf16[1,128,128]{2,1,0:T(8,128)(2,1)S(1)} %copy-done.4), custom_call_target="tpu_custom_call" | custom-call | flops 10000000000 | bytes 262144 | tf_op jit(solution)/shard_map/pallas_call | solution.py:223
  4.8 1.0 %copy-done = bf16[1024,1024]{1,0:T(8,128)(2,1)S(1)} copy-done((bf16[1024,1024]{1,0:T(8,128)(2,1)S(1)}, bf16[1024,1024]{1,0:T(8,128)(2,1)}, u32[]{:S(2)}) %copy-start) | copy-done | bytes 2097176
  5.8 0.0 copy-done.2
  5.8 0.0 copy-start.1
  5.8 0.7 %shard_map.104 = (bf16[1024,128]{1,0:T(8,128)(2,1)S(1)}, bf16[1024,128]{1,0:T(8,128)(2,1)S(1)}) custom-call(s32[1]{0:T(128)} %bitcast.me, bf16[1,128,1024]{2,1,0:T(8,128)(2,1)S(1)} %copy-done.2, bf16[1024,1024]{1,0:T(8,128)(2,1)S(1)} %copy-done), custom_call_target="tpu_custom_call" | custom-call | tf_op jit(solution)/shard_map/pallas_call | solution.py:232
  6.5 3.0 %collective-permute-start.3 = (bf16[1024,128]{1,0:T(8,128)(2,1)S(1)}, bf16[1024,128]{1,0:T(8,128)(2,1)S(1)}, u32[]{:S(2)}, u32[]{:S(2)}) collective-permute-start(bf16[1024,128]{1,0:T(8,128)(2,1)S(1)} %get-tuple-element.20), channel_id=1, source_target_pairs={{0,2},{1,3},{2,0},{3,1},{4,6},{5,7},{6,4},{7,5},{8,10},{9,11},{10,... | collective-permute-start | bytes 786440 | tf_op jit(solution)/shard_map/ppermute | solution.py:221
  9.6 1.6 %collective-permute-start = (bf16[400,128]{1,0:T(8,128)(2,1)S(1)}, bf16[400,128]{1,0:T(8,128)(2,1)S(1)}, u32[]{:S(2)}, u32[]{:S(2)}) collective-permute-start(bf16[400,128]{1,0:T(8,128)(2,1)S(1)} %shard_map.103.refs_0_), channel_id=1, source_target_pairs={{0,4},{1,5},{2,6},{3,7},{4,0},{5,1},{6,2},{7,3},{8,12},{9,13},{10,... | collective-permute-start | bytes 307208 | tf_op jit(solution)/shard_map/ppermute | solution.py:221
  11.1 2.6 %collective-permute-start.1 = (bf16[400,128]{1,0:T(8,128)(2,1)S(1)}, bf16[400,128]{1,0:T(8,128)(2,1)S(1)}, u32[]{:S(2)}, u32[]{:S(2)}) collective-permute-start(bf16[400,128]{1,0:T(8,128)(2,1)S(1)} %shard_map.103.refs_0_), channel_id=1, source_target_pairs={{0,8},{1,9},{2,10},{3,11},{4,12},{5,13},{6,14},{7,15},{8,0},{9,1},... | collective-permute-start | bytes 307208 | tf_op jit(solution)/shard_map/ppermute | solution.py:221
  13.7 0.2 collective-permute-start.2
  13.9 1.3 %collective-permute-done.refs_1_ = bf16[400,128]{1,0:T(8,128)(2,1)S(1)} collective-permute-done((bf16[400,128]{1,0:T(8,128)(2,1)S(1)}, bf16[400,128]{1,0:T(8,128)(2,1)S(1)}, u32[]{:S(2)}, u32[]{:S(2)}) %collective-permute-start) | collective-permute-done | bytes 102432 | tf_op jit(solution)/shard_map/ppermute | solution.py:221
  15.3 6.3 %collective-permute-done.1.refs_2_ = bf16[400,128]{1,0:T(8,128)(2,1)S(1)} collective-permute-done((bf16[400,128]{1,0:T(8,128)(2,1)S(1)}, bf16[400,128]{1,0:T(8,128)(2,1)S(1)}, u32[]{:S(2)}, u32[]{:S(2)}) %collective-permute-start.1) | collective-permute-done | bytes 102432 | tf_op jit(solution)/shard_map/ppermute | solution.py:221
  21.6 0.0 collective-permute-done.2.refs_3_
  21.6 0.0 collective-permute-done.3.refs_5_.other.refs_3_
  21.6 0.1 shard_map.105
  21.7 0.6 %collective-permute-start.4 = (bf16[1600,128]{1,0:T(8,128)(2,1)S(1)}, bf16[1600,128]{1,0:T(8,128)(2,1)S(1)}, u32[]{:S(2)}, u32[]{:S(2)}) collective-permute-start(bf16[1600,128]{1,0:T(8,128)(2,1)S(1)} %get-tuple-element.21.stack), channel_id=1, source_target_pairs={{0,2},{1,3},{2,0},{3,1},{4,6},{5,7},{6,4},{7,5},{8,10},{9,11},{10,... | collective-permute-start | bytes 1228808 | tf_op jit(solution)/shard_map/ppermute | solution.py:221
  22.2 0.0 collective-permute-start.5
  22.2 1.7 %collective-permute-start.6 = (bf16[512,128]{1,0:T(8,128)(2,1)S(1)}, bf16[512,128]{1,0:T(8,128)(2,1)S(1)}, u32[]{:S(2)}, u32[]{:S(2)}) collective-permute-start(bf16[512,128]{1,0:T(8,128)(2,1)S(1)} %get-tuple-element.23), channel_id=1, source_target_pairs={{0,4},{1,5},{2,6},{3,7},{4,0},{5,1},{6,2},{7,3},{8,12},{9,13},{10,... | collective-permute-start | bytes 393224 | tf_op jit(solution)/shard_map/ppermute | solution.py:221
  23.9 1.4 %collective-permute-start.7 = (bf16[512,128]{1,0:T(8,128)(2,1)S(1)}, bf16[512,128]{1,0:T(8,128)(2,1)S(1)}, u32[]{:S(2)}, u32[]{:S(2)}) collective-permute-start(bf16[512,128]{1,0:T(8,128)(2,1)S(1)} %get-tuple-element.24), channel_id=1, source_target_pairs={{0,8},{1,9},{2,10},{3,11},{4,12},{5,13},{6,14},{7,15},{8,0},{9,1},... | collective-permute-start | bytes 393224 | tf_op jit(solution)/shard_map/ppermute | solution.py:221
  25.3 1.3 %collective-permute-start.8 = (bf16[512,128]{1,0:T(8,128)(2,1)S(1)}, bf16[512,128]{1,0:T(8,128)(2,1)S(1)}, u32[]{:S(2)}, u32[]{:S(2)}) collective-permute-start(bf16[512,128]{1,0:T(8,128)(2,1)S(1)} %get-tuple-element.25), channel_id=1, source_target_pairs={{0,12},{1,13},{2,14},{3,15},{4,8},{5,9},{6,10},{7,11},{8,4},{9,5},... | collective-permute-start | bytes 393224 | tf_op jit(solution)/shard_map/ppermute | solution.py:221
  26.6 4.3 %collective-permute-done.4.across.refs_0_ = bf16[1600,128]{1,0:T(8,128)(2,1)S(1)} collective-permute-done((bf16[1600,128]{1,0:T(8,128)(2,1)S(1)}, bf16[1600,128]{1,0:T(8,128)(2,1)S(1)}, u32[]{:S(2)}, u32[]{:S(2)}) %collective-permute-start.4) | collective-permute-done | bytes 409632 | tf_op jit(solution)/shard_map/ppermute | solution.py:221
  30.9 0.0 collective-permute-done.5.beside
  30.9 0.0 collective-permute-done.6.refs_0_.refs_4_
  30.9 5.9 %collective-permute-done.7.refs_1_.refs_5_ = bf16[512,128]{1,0:T(8,128)(2,1)S(1)} collective-permute-done((bf16[512,128]{1,0:T(8,128)(2,1)S(1)}, bf16[512,128]{1,0:T(8,128)(2,1)S(1)}, u32[]{:S(2)}, u32[]{:S(2)}) %collective-permute-start.7) | collective-permute-done | bytes 131104 | tf_op jit(solution)/shard_map/ppermute | solution.py:221
  36.8 0.0 collective-permute-done.8.refs_2_.refs_6_
  36.8 0.1 collective-permute-start.9
  36.9 0.0 copy-done.1
  36.9 1.0 %shard_map.107 = (bf16[256,1024]{1,0:T(8,128)(2,1)S(1)}, bf16[256,1024]{1,0:T(8,128)(2,1)S(1)}, bf16[1024,512]{1,0:T(8,128)(2,1)S(1)}, bf16[8,128,128]{2,1,0:T(8...) custom-call(s32[1]{0:T(128)} %bitcast.me, bf16[1600,128]{1,0:T(8,128)(2,1)S(1)} %get-tuple-element.21.stack, ...), custom_call_target="tpu_custom_call" | custom-call | flops 2000000000 | bytes 1048576 | tf_op jit(solution)/shard_map/pallas_call | solution.py:264
  37.9 1.1 %collective-permute-done.9.refs_1_ = bf16[2624,128]{1,0:T(8,128)(2,1)S(1)} collective-permute-done((bf16[2624,128]{1,0:T(8,128)(2,1)S(1)}, bf16[2624,128]{1,0:T(8,128)(2,1)S(1)}, u32[]{:S(2)}, u32[]{:S(2)}) %collective-permute-start.9) | collective-permute-done | bytes 671776 | tf_op jit(solution)/shard_map/ppermute | solution.py:221
  39.0 7.7 %shard_map.108 = (bf16[1,128,1024]{2,1,0:T(8,128)(2,1)}, f32[64,1024]{1,0:T(8,128)}, f32[64,1024]{1,0:T(8,128)}) custom-call(s32[1]{0:T(128)} %bitcast.me, bf16[1600,128]{1,0:T(8,128)(2,1)S(1)} %collective-permute-done.4.across.refs_0_, bf16[2624,128]{1,0:T(8,128)(2,1)S(1)} %collective-permute-done.9.refs_1_, ...), custom_call_target="tpu_custom_call" | custom-call | tf_op jit(solution)/shard_map/pallas_call | solution.py:279
  (1 shorter events, 0.0 us)
Async XLA Ops:
  0.6 0.8 %copy-start.3 = (bf16[2,16,1024]{2,1,0:T(8,128)(2,1)S(1)}, bf16[2,16,1024]{2,1,0:T(8,128)(2,1)}, u32[]{:S(2)}) copy-start(bf16[2,16,1024]{2,1,0:T(8,128)(2,1)} %features.1) | copy-start | bytes 196612
  1.5 0.8 %copy-start.4 = (bf16[1,128,128]{2,1,0:T(8,128)(2,1)S(1)}, bf16[1,128,128]{2,1,0:T(8,128)(2,1)}, u32[]{:S(2)}) copy-start(bf16[1,128,128]{2,1,0:T(8,128)(2,1)} %adjacency.1) | copy-start | bytes 98308
  2.2 0.7 %copy-start.5 = (s32[2]{0:T(128)S(1)}, s32[2]{0:T(128)}, u32[]{:S(2)}) copy-start(s32[2]{0:T(128)} %counts.1) | copy-start | bytes 28
  2.9 0.7 %copy-start.6 = (s32[1,8]{1,0:T(1,128)S(1)}, s32[1,8]{1,0:T(1,128)}, u32[]{:S(2)}) copy-start(s32[1,8]{1,0:T(1,128)} %owner.1) | copy-start | bytes 100
  3.5 0.7 %copy-start.7 = (s32[1,8]{1,0:T(1,128)S(1)}, s32[1,8]{1,0:T(1,128)}, u32[]{:S(2)}) copy-start(s32[1,8]{1,0:T(1,128)} %local.1) | copy-start | bytes 100
  4.2 1.6 %copy-start = (bf16[1024,1024]{1,0:T(8,128)(2,1)S(1)}, bf16[1024,1024]{1,0:T(8,128)(2,1)}, u32[]{:S(2)}) copy-start(bf16[1024,1024]{1,0:T(8,128)(2,1)} %refs_14_.1) | copy-start | bytes 6291460
  4.2 1.6 %copy-start.2 = (bf16[1,128,1024]{2,1,0:T(8,128)(2,1)S(1)}, bf16[1,128,1024]{2,1,0:T(8,128)(2,1)}, u32[]{:S(2)}) copy-start(bf16[1,128,1024]{2,1,0:T(8,128)(2,1)} %cotangent) | copy-start | bytes 786436
  5.8 31.1 %copy-start.1 = (bf16[1024,1024]{1,0:T(8,128)(2,1)S(1)}, bf16[1024,1024]{1,0:T(8,128)(2,1)}, u32[]{:S(2)}) copy-start(bf16[1024,1024]{1,0:T(8,128)(2,1)} %refs_13_.1) | copy-start | bytes 6291460
  6.5 15.1 %collective-permute-start.3 = (bf16[1024,128]{1,0:T(8,128)(2,1)S(1)}, bf16[1024,128]{1,0:T(8,128)(2,1)S(1)}, u32[]{:S(2)}, u32[]{:S(2)}) collective-permute-start(bf16[1024,128]{1,0:T(8,128)(2,1)S(1)} %get-tuple-element.20), channel_id=1, source_target_pairs={{0,2},{1,3},{2,0},{3,1},{4,6},{5,7},{6,4},{7,5},{8,10},{9,11},{10,... | collective-permute-start | bytes 786440 | tf_op jit(solution)/shard_map/ppermute | solution.py:221
  9.6 5.7 %collective-permute-start = (bf16[400,128]{1,0:T(8,128)(2,1)S(1)}, bf16[400,128]{1,0:T(8,128)(2,1)S(1)}, u32[]{:S(2)}, u32[]{:S(2)}) collective-permute-start(bf16[400,128]{1,0:T(8,128)(2,1)S(1)} %shard_map.103.refs_0_), channel_id=1, source_target_pairs={{0,4},{1,5},{2,6},{3,7},{4,0},{5,1},{6,2},{7,3},{8,12},{9,13},{10,... | collective-permute-start | bytes 307208 | tf_op jit(solution)/shard_map/ppermute | solution.py:221
  11.1 10.5 %collective-permute-start.1 = (bf16[400,128]{1,0:T(8,128)(2,1)S(1)}, bf16[400,128]{1,0:T(8,128)(2,1)S(1)}, u32[]{:S(2)}, u32[]{:S(2)}) collective-permute-start(bf16[400,128]{1,0:T(8,128)(2,1)S(1)} %shard_map.103.refs_0_), channel_id=1, source_target_pairs={{0,8},{1,9},{2,10},{3,11},{4,12},{5,13},{6,14},{7,15},{8,0},{9,1},... | collective-permute-start | bytes 307208 | tf_op jit(solution)/shard_map/ppermute | solution.py:221
  13.7 7.9 %collective-permute-start.2 = (bf16[400,128]{1,0:T(8,128)(2,1)S(1)}, bf16[400,128]{1,0:T(8,128)(2,1)S(1)}, u32[]{:S(2)}, u32[]{:S(2)}) collective-permute-start(bf16[400,128]{1,0:T(8,128)(2,1)S(1)} %shard_map.103.refs_0_), channel_id=1, source_target_pairs={{0,12},{1,13},{2,14},{3,15},{4,8},{5,9},{6,10},{7,11},{8,4},{9,5},... | collective-permute-start | bytes 307208 | tf_op jit(solution)/shard_map/ppermute | solution.py:221
  21.7 9.2 %collective-permute-start.4 = (bf16[1600,128]{1,0:T(8,128)(2,1)S(1)}, bf16[1600,128]{1,0:T(8,128)(2,1)S(1)}, u32[]{:S(2)}, u32[]{:S(2)}) collective-permute-start(bf16[1600,128]{1,0:T(8,128)(2,1)S(1)} %get-tuple-element.21.stack), channel_id=1, source_target_pairs={{0,2},{1,3},{2,0},{3,1},{4,6},{5,7},{6,4},{7,5},{8,10},{9,11},{10,... | collective-permute-start | bytes 1228808 | tf_op jit(solution)/shard_map/ppermute | solution.py:221
  22.2 8.7 %collective-permute-start.5 = (bf16[1600,128]{1,0:T(8,128)(2,1)S(1)}, bf16[1600,128]{1,0:T(8,128)(2,1)S(1)}, u32[]{:S(2)}, u32[]{:S(2)}) collective-permute-start(bf16[1600,128]{1,0:T(8,128)(2,1)S(1)} %get-tuple-element.21.stack), channel_id=1, source_target_pairs={{0,1},{1,0},{2,3},{3,2},{4,5},{5,4},{6,7},{7,6},{8,9},{9,8},{10,11... | collective-permute-start | bytes 1228808 | tf_op jit(solution)/shard_map/ppermute | solution.py:221
  22.2 8.7 %collective-permute-start.6 = (bf16[512,128]{1,0:T(8,128)(2,1)S(1)}, bf16[512,128]{1,0:T(8,128)(2,1)S(1)}, u32[]{:S(2)}, u32[]{:S(2)}) collective-permute-start(bf16[512,128]{1,0:T(8,128)(2,1)S(1)} %get-tuple-element.23), channel_id=1, source_target_pairs={{0,4},{1,5},{2,6},{3,7},{4,0},{5,1},{6,2},{7,3},{8,12},{9,13},{10,... | collective-permute-start | bytes 393224 | tf_op jit(solution)/shard_map/ppermute | solution.py:221
  23.9 12.9 %collective-permute-start.7 = (bf16[512,128]{1,0:T(8,128)(2,1)S(1)}, bf16[512,128]{1,0:T(8,128)(2,1)S(1)}, u32[]{:S(2)}, u32[]{:S(2)}) collective-permute-start(bf16[512,128]{1,0:T(8,128)(2,1)S(1)} %get-tuple-element.24), channel_id=1, source_target_pairs={{0,8},{1,9},{2,10},{3,11},{4,12},{5,13},{6,14},{7,15},{8,0},{9,1},... | collective-permute-start | bytes 393224 | tf_op jit(solution)/shard_map/ppermute | solution.py:221
  25.3 11.5 %collective-permute-start.8 = (bf16[512,128]{1,0:T(8,128)(2,1)S(1)}, bf16[512,128]{1,0:T(8,128)(2,1)S(1)}, u32[]{:S(2)}, u32[]{:S(2)}) collective-permute-start(bf16[512,128]{1,0:T(8,128)(2,1)S(1)} %get-tuple-element.25), channel_id=1, source_target_pairs={{0,12},{1,13},{2,14},{3,15},{4,8},{5,9},{6,10},{7,11},{8,4},{9,5},... | collective-permute-start | bytes 393224 | tf_op jit(solution)/shard_map/ppermute | solution.py:221
  36.8 2.2 %collective-permute-start.9 = (bf16[2624,128]{1,0:T(8,128)(2,1)S(1)}, bf16[2624,128]{1,0:T(8,128)(2,1)S(1)}, u32[]{:S(2)}, u32[]{:S(2)}) collective-permute-start(bf16[2624,128]{1,0:T(8,128)(2,1)S(1)} %shard_map.106), channel_id=1, source_target_pairs={{0,1},{1,0},{2,3},{3,2},{4,5},{5,4},{6,7},{7,6},{8,9},{9,8},{10,11... | collective-permute-start | bytes 2015240 | tf_op jit(solution)/shard_map/ppermute | solution.py:221

commit v6 on v0

v6 whole, which is shorter than its diff:
```python
import functools

import jax
import jax.numpy as jnp
from jax import lax
from jax.experimental import pallas as pl
from jax.experimental.pallas import tpu as pltpu
from jax.sharding import PartitionSpec as P

F32 = jnp.float32
BF16 = jnp.bfloat16
VMEM = pl.BlockSpec(memory_space=pltpu.VMEM)
HBM = pl.BlockSpec(memory_space=pltpu.HBM)
LANES = 128
META = 16
CHUNKS = 4
LIMIT = 24 * 2**20
SMALL = 8 * 2**20
Z2, Z1, Y, CORE = 8, 4, 2, 1
GROUP = 16
FAR = (Z2 | Z1, Z2, Z1)
HALF_A = ((0, Z2, Z1, Z1 | Z2), (Y, Y | Z2, Y | Z1, Y | Z1 | Z2))
HALF_B = ((0, Z2, Y, Y | Z2), (Z1, Z1 | Z2, Z1 | Y, Z1 | Y | Z2))


def nn(a, b):
    return jnp.dot(a, b, preferred_element_type=F32)


def nt(a, b):
    return lax.dot_general(a, b, (((1,), (1,)), ((), ())), preferred_element_type=F32)


def prepare_kernel(counts, owner, local, features, adjacency, cotangent, w_second, *refs):
    piece, near, across, count, own_by, own_at, feat, adj, cot, second, turned, back, sems = refs
    own, slots, width = features.shape
    rows = adjacency.shape[1]
    each = width // GROUP
    place = lax.axis_index("grp")
    moves = [(features, feat), (adjacency, adj), (counts, count), (owner, own_by), (local, own_at)]
    moves.append((cotangent, cot))
    some = width // CHUNKS
    for c in range(CHUNKS):
        span = slice(c * some, (c + 1) * some)
        moves.append((w_second.at[span], second.at[span]))
    copies = [pltpu.make_async_copy(a, b, sems.at[i]) for i, (a, b) in enumerate(moves)]
    for copy in copies:
        copy.start()

    held = own * slots
    slot = lax.broadcasted_iota(jnp.int32, (slots, LANES), 0)
    line = lax.broadcasted_iota(jnp.int32, (META, LANES), 0)
    pick = lax.broadcasted_iota(jnp.int32, (META, LANES), 1) // slots
    meta = jnp.zeros((META, LANES), jnp.int32)
    for copy in copies[:5]:
        copy.wait()
    for i in range(own):
        live = slot < count[i]
        for b in range(width // LANES):
            block = feat[i, :, b * LANES : (b + 1) * LANES]
            at = b * held + i * slots
            piece[at : at + slots, :] = jnp.where(live, block, jnp.zeros_like(block))
        meta = jnp.where(line == 1 + i, count[i], meta)
    for k in range(owner.shape[1]):
        meta = jnp.where((line == 0) & (pick == k), own_by[0, k] * own + own_at[0, k], meta)
    at = held * (width // LANES)
    piece[at : at + rows, :] = adj[0]
    piece[at + rows : at + rows + META, :] = meta.astype(F32).astype(BF16)

    copies[5].wait()
    turned[...] = cot[0].astype(F32).T.astype(BF16)
    for c in range(CHUNKS):
        copies[6 + c].wait()
        span = slice(c * some, (c + 1) * some)
        back[span, :] = nt(second[span, :], cot[0]).astype(BF16)
    for h, out in enumerate((near, across)):
        for i in range(out.shape[0] // (2 * each)):
            to = 4 * (i // 2) + 2 * h + i % 2
            span = pl.ds(pl.multiple_of((place ^ to) * each, each), each)
            at = i * 2 * each
            out[at : at + each, :] = turned[span, :]
            out[at + each : at + 2 * each, :] = back[span, :]


def stack(out, at, *blocks):
    for block in blocks:
        out[at : at + block.shape[0], :] = block[...]
        at += block.shape[0]
    return at


def split_kernel(piece, came, near, across, half_a, half_b, *sent):
    cut = half_a.shape[0] // 2
    stack(half_a, 0, piece.at[:cut], came.at[:cut])
    stack(half_b, 0, piece.at[cut:], came.at[cut:])
    size = sent[0].shape[0] // 2
    for slot, out in zip(FAR + (0,), sent):
        span = slice(slot // 4 * size, (slot // 4 + 1) * size)
        stack(out, 0, near.at[span], across.at[span])


def join_kernel(a, came_a, b, came_b, out_a, out_b):
    stack(out_a, 0, a, came_a)
    stack(out_b, 0, b, came_b)


def pair_kernel(a, far_a, b, far_b, *refs):
    *sent, out = refs
    at = stack(out, 0, a, far_a, b, far_b)
    size = sent[0].shape[0] // 2
    rows = size // 2
    for s in range(GROUP // 4):
        for h in range(2):
            block = sent[(FAR + (0,)).index(4 * s)]
            at = stack(out, at, block.at[h * size + rows : (h + 1) * size])


def place_of(slot):
    return slot // 2 + GROUP // 2 * (slot % 2)


def lay_out(arrays, held, cut, feat, adj, meta):
    rows = adj.shape[1]
    for ref, at, slots in arrays[:2]:
        for slot in slots:
            p = place_of(slot)
            for b in range(cut // held):
                feat[p * held : (p + 1) * held, b * LANES : (b + 1) * LANES] = ref[at : at + held, :]
                at += held
    for ref, at, slots in arrays[2:]:
        for slot in slots:
            p = place_of(slot)
            for b in range(cut // held, feat.shape[1] // LANES):
                feat[p * held : (p + 1) * held, b * LANES : (b + 1) * LANES] = ref[at : at + held, :]
                at += held
            adj[p] = ref[at : at + rows, :]
            at += rows
            meta[p] = ref[at : at + META, :]
            at += META


def spread_of(place, held, slots, adj, picks):
    line = lax.broadcasted_iota(jnp.int32, (held, LANES), 0)
    lane = lax.broadcasted_iota(jnp.int32, (1, LANES), 1) % slots
    owners = [None] * GROUP
    for slot in range(GROUP):
        owners[place_of(slot)] = place ^ slot
    code = jnp.concatenate([line + owner * held for owner in owners], axis=0)
    chosen = jnp.where(code == picks * slots + lane, 1.0, 0.0).astype(BF16)
    return nt(adj, chosen).astype(BF16)


def early_kernel(own, slots, cut, a, far_a, b, far_b, w_first, feat, lifted, spread, adj, meta, w_piece):
    held = own * slots
    rows = adj.shape[1]
    place = lax.axis_index("grp")
    arrays = list(zip((a, far_a, b, far_b), HALF_A + HALF_B))
    lay_out([(ref, 0, at) for ref, at in arrays], held, cut, feat, adj, meta)
    lifted[...] = nn(feat[...], w_first[...]).astype(BF16)
    for p in range(GROUP // 2):
        picks = meta[p, 0:1, :].astype(F32).astype(jnp.int32)
        spread[p * rows : (p + 1) * rows, :] = spread_of(place, held, slots, adj[p], picks)
    each = w_piece.shape[0]
    wide = max(each, LANES)
    per = wide // each
    start = pl.multiple_of((place // per) * wide, wide)
    block = w_first[:, pl.ds(start, wide)].astype(F32).T
    part = block[:each]
    for q in range(1, per):
        part = jnp.where(place % per == q, block[q * each : (q + 1) * each], part)
    w_piece[...] = part.astype(BF16)


def step_kernel(own, slots, cut, rest, pair, *refs):
    sent, refs = refs[: len(FAR) + 1], refs[len(FAR) + 1 :]
    early_feat, early_lifted, early_spread, early_adj, early_meta, w_piece = refs[:6]
    w_first, w_second, output, grad_first, grad_second = refs[6:11]
    hidden, spread, feat, adj, meta, dout, dpre, lifted = refs[11:]
    width = w_first.shape[0]
    held = own * slots
    rows = adj.shape[1]
    place = lax.axis_index("grp")
    first = GROUP // 2

    feat[: first * held, :] = early_feat[...]
    lifted[: first * held, :] = early_lifted[...]
    spread[: first * rows, :] = early_spread[...]
    adj[:first] = early_adj[...]
    meta[:first] = early_meta[...]
    arrays, deep = [], 0
    for size, halves in ((cut, HALF_A), (rest, HALF_B)):
        for group in halves:
            arrays.append((pair, deep, [slot | CORE for slot in group]))
            deep += size * len(group)
    lay_out(arrays, held, cut, feat, adj, meta)
    metas = [meta[p].astype(F32) for p in range(GROUP)]
    picks = jnp.concatenate([m[0:1] for m in metas], axis=0).astype(jnp.int32)
    lane = lax.broadcasted_iota(jnp.int32, (GROUP, LANES), 1) % slots
    count = jnp.zeros((GROUP, LANES), jnp.int32)
    for slot in range(GROUP):
        for i in range(own):
            held_by = metas[place_of(slot)][1 + i : 2 + i].astype(jnp.int32)
            count = jnp.where(picks == (place ^ slot) * own + i, held_by, count)
    masks = (lane < count).astype(F32)

    late = slice(first * held, GROUP * held)
    lifted[late, :] = nn(feat[late, :], w_first[...]).astype(BF16)
    lifted_piece = nt(w_piece[...], feat[...]).astype(BF16)
    for p in range(first, GROUP):
        span = slice(p * rows, (p + 1) * rows)
        spread[span, :] = spread_of(place, held, slots, adj[p], picks[p : p + 1])
    step = min(width, 2 * LANES)
    for c in range(0, width, step):
        half = 0.5 * nn(spread[...], lifted[:, c : c + step])
        hidden[:, c : c + step] = (half + half * jnp.tanh(half)).astype(BF16)
    pre_piece = nt(lifted_piece, spread[...])
    live = jnp.broadcast_to(masks[0:1], (rows, LANES)).T[:, :1]
    agg = nn(adj[0], (hidden[:rows, :].astype(F32) * live).astype(BF16)).astype(BF16)
    output[0] = (nn(agg, w_second[...]) * live).astype(BF16)

    each = grad_first.shape[0]
    size = sent[0].shape[0] // 2
    for slot in range(GROUP):
        p = place_of(slot)
        mask = masks[p : p + 1]
        span = slice(p * rows, (p + 1) * rows)
        s, h = slot // 4, slot // 2 % 2
        if slot % 2:
            at = deep + (2 * s + h) * 2 * each
            source = pair[at : at + 2 * each, :]
        else:
            source = sent[(FAR + (0,)).index(4 * s)][h * size : h * size + 2 * each, :]
        back = nn((source.astype(F32) * mask).astype(BF16), adj[p]) * mask
        dout[:, span] = back[:each].astype(BF16)
        pre = pre_piece[:, span]
        sig = 0.5 + 0.5 * jnp.tanh(0.5 * pre)
        dpre[:, span] = (back[each:] * sig * (1.0 + pre * (1.0 - sig))).astype(BF16)
    grad_second[...] = nn(dout[...], hidden[...])
    moved = nn(dpre[...], spread[...])
    grad_first[...] = nn(moved.astype(BF16), feat[...])


def call(kernel, ins, outs, scratch=(), limit=SMALL, stay=False):
    if stay:
        ins = [pltpu.with_memory_space_constraint(x, pltpu.HBM) for x in ins]
    return pl.pallas_call(
        kernel,
        out_shape=tuple(jax.ShapeDtypeStruct(*out) for out in outs),
        in_specs=[HBM if stay else VMEM] * len(ins),
        out_specs=(VMEM,) * len(outs),
        scratch_shapes=list(scratch),
        compiler_params=pltpu.CompilerParams(vmem_limit_bytes=limit),
    )(*ins)


def whole_body(features, counts, pick_owner, pick_local, adjacency, cotangent, w_first, w_second):
    own, slots, width = features.shape
    rows = adjacency.shape[1]
    held = own * slots
    each = width // GROUP
    total = GROUP * held
    cut = held * (width // LANES * 3 // 4)
    rest = held * (width // LANES) + rows + META - cut
    half = GROUP // 2

    def swap(x, slot):
        return lax.ppermute(x, "grp", [(i, i ^ slot) for i in range(GROUP)])

    piece, near, across = call(
        prepare_kernel,
        (counts, pick_owner, pick_local, features, adjacency, cotangent, w_second),
        [((cut + rest, LANES), BF16)] + [((GROUP * each, rows), BF16)] * 2,
        [pltpu.SMEM(x.shape, jnp.int32) for x in (counts, pick_owner, pick_local)]
        + [pltpu.VMEM(x.shape, BF16) for x in (features, adjacency, cotangent, w_second)]
        + [pltpu.VMEM((width, rows), BF16)] * 2
        + [pltpu.SemaphoreType.DMA((6 + CHUNKS,))],
        stay=True,
    )
    came = swap(piece, Z2)
    across = swap(across, Y)
    a, b, *sent = call(
        split_kernel,
        (piece, came, near, across),
        [((2 * cut, LANES), BF16), ((2 * rest, LANES), BF16)] + [((8 * each, rows), BF16)] * (len(FAR) + 1),
    )
    sent = [swap(x, slot) for x, slot in zip(sent, FAR)] + sent[-1:]
    came_a, came_b = swap(a, Z1), swap(b, Y)
    came_a, came_b, sent[0] = lax.optimization_barrier((came_a, came_b, sent[0]))
    a, b = call(
        join_kernel, (a, came_a, b, came_b), [((4 * cut, LANES), BF16), ((4 * rest, LANES), BF16)]
    )
    far_a, far_b = swap(a, Y), swap(b, Z1)
    (pair,) = call(
        pair_kernel,
        (a, far_a, b, far_b, *sent),
        [((half * (cut + rest) + half * 2 * each, LANES), BF16)],
    )
    pair = swap(pair, CORE)
    early = call(
        functools.partial(early_kernel, own, slots, cut),
        (a, far_a, b, far_b, w_first),
        [
            ((total // 2, width), BF16),
            ((total // 2, width), BF16),
            ((half * rows, total), BF16),
            ((half, rows, rows), BF16),
            ((half, META, LANES), BF16),
            ((each, width), BF16),
        ],
        limit=LIMIT,
    )
    return call(
        functools.partial(step_kernel, own, slots, cut, rest),
        (pair, *sent, *early, w_first, w_second),
        [((1, rows, width), BF16), ((each, width), F32), ((each, width), F32)],
        [
            pltpu.VMEM((GROUP * rows, width), BF16),
            pltpu.VMEM((GROUP * rows, total), BF16),
            pltpu.VMEM((total, width), BF16),
            pltpu.VMEM((GROUP, rows, rows), BF16),
            pltpu.VMEM((GROUP, META, LANES), BF16),
            pltpu.VMEM((each, GROUP * rows), BF16),
            pltpu.VMEM((each, GROUP * rows), BF16),
            pltpu.VMEM((total, width), BF16),
        ],
        LIMIT,
    )


def split_body(features, counts, pick_owner, pick_local, adjacency, cotangent, w_first, w_second):
    owners = pick_owner[0]
    picks = pick_local[0]
    width = w_first.shape[0]
    slots = features.shape[1]
    count_picks = owners.shape[0]
    wanted = owners * features.shape[0] + picks
    feat_piece = lax.all_gather(features, "grp", axis=0, tiled=True)
    count_piece = lax.all_gather(counts, "grp", axis=0, tiled=True)
    live = jnp.take(count_piece, wanted, axis=0)
    rows = count_picks * slots
    inputs = jnp.take(feat_piece, wanted, axis=0).reshape(rows, width)
    mask = (jnp.arange(slots)[None, :] < live[:, None]).reshape(rows, 1).astype(BF16)
    inputs = inputs * mask
    maskf = mask.astype(F32)
    adj = adjacency[0]
    agg_first = nn(adj, inputs).astype(BF16)
    pre = nn(agg_first, w_first)
    hidden = (maskf * jax.nn.silu(pre)).astype(BF16)
    agg_second = nn(adj, hidden).astype(BF16)
    output = (maskf * nn(agg_second, w_second)).astype(BF16)
    dout = cotangent[0] * mask

    def summed(a, b):
        part = lax.dot_general(a, b, (((0,), (0,)), ((), ())), preferred_element_type=F32)
        return lax.psum_scatter(part, "grp", scatter_dimension=0, tiled=True)

    grad_second = summed(dout, agg_second)
    dagg = nt(dout, w_second).astype(BF16)
    back = lax.dot_general(adj, dagg, (((0,), (0,)), ((), ())), preferred_element_type=F32)
    sig = jax.nn.sigmoid(pre)
    dpre = (maskf * back * sig * (1.0 + pre * (1.0 - sig))).astype(BF16)
    grad_first = summed(dpre, agg_first)
    return (output.reshape(1, rows, width), grad_first, grad_second)


def solution(mesh):
    n = mesh.shape["grp"]

    def body(*args):
        rows = args[4].shape[1]
        return whole_body(*args) if n == GROUP and rows == LANES else split_body(*args)

    in_specs = (
        P(("parts", "grp"), None, None),
        P(("parts", "grp")),
        P(("parts", "grp"), None),
        P(("parts", "grp"), None),
        P(("parts", "grp"), None, None),
        P(("parts", "grp"), None, None),
        P(),
        P(),
    )
    out_specs = (
        P(("parts", "grp"), None, None),
        P(("parts", "grp"), None),
        P(("parts", "grp"), None),
    )
    return jax.shard_map(body, mesh=mesh, in_specs=in_specs, out_specs=out_specs, check_vma=False)
```

time: 214 us -> 45.9 us (0.21)
  waiting for transfers between devices: 168 us -> 19.3 us
  starting transfers between devices: 0.12 us -> 14.1 us
  between operations: 14.5 us -> 0.7 us
  blocking collectives: 13.7 us -> 0 us
  Pallas kernels: 0 us -> 11.6 us
  matrix products: 11.1 us -> 0 us
  local copies, waits for them, and re-layouts: 4.64 us -> 0.01 us
    reduce_scatter x2 -> x0, waiting for transfers between devices: 144 us -> none  [the longest x1 76.5 us: body(): lax.psum_scatter(lax.dot_general(columns, agg_second, (((0,), (0,)), ((),...]
    all_gather x1 -> x0, waiting for transfers between devices: 24.2 us -> none  [body(): feat_piece = lax.all_gather(features, 'grp', axis=0, tiled=True)]
    ppermute x0 -> x10, waiting for transfers between devices: none -> 19.3 us  [swap(): return lax.ppermute(x, 'grp', [(i, i ^ slot) for i in range(GROUP)])]
    ppermute x0 -> x10, starting transfers between devices: none -> 14.1 us  [swap(): return lax.ppermute(x, 'grp', [(i, i ^ slot) for i in range(GROUP)])]
    unnamed x1 -> x0, blocking collectives: 13.7 us -> none
    pallas_call x0 -> x6, Pallas kernels: none -> 11.6 us  [call(): pl.pallas_call(kernel, out_shape=tuple((jax.ShapeDtypeStruct(*out) for ou...]
    dot_general x7 -> x0, matrix products: 11.1 us -> none  [the longest x1 2.78 us: body(): lax.dot_general(columns, agg_second, (((0,), (0,)), ((), ())), preferred_...]
    gather x2 -> x0, local copies, waits for them, and re-layouts: 2.43 us -> none  [the longest x1 1.79 us: body(): taken = jnp.take(feat_piece, where_at, axis=0)]
  transfers between devices with their start and end apart: 3 -> 10, of which waited for: 3 -> 5; matrix products, arithmetic and copies ran while one was open for 4% -> 0% of each run, Pallas kernels for 0% -> 2%
where the time goes in v6:
time: 45.9 us; the launch traced here: 45.7 us
  waiting for transfers between devices  19.3 us (42%)
  starting transfers between devices  14.1 us (31%)
  Pallas kernels  11.6 us (25%)
  between operations  0.7 us (2%)
    ppermute x10, waiting for transfers between devices, swap(): return lax.ppermute(x, 'grp', [(i, i ^ slot) for i in range(GROUP)])  19.3 us
    ppermute x10, starting transfers between devices, swap(): return lax.ppermute(x, 'grp', [(i, i ^ slot) for i in range(GROUP)])  14.1 us
    pallas_call x6, Pallas kernels, call(): pl.pallas_call(kernel, out_shape=tuple((jax.ShapeDtypeStruct(*out) for ou...  11.6 us
  transfers between devices with their start and end apart: 10, of which 5 were waited for; matrix products, arithmetic and copies ran while one was open for 0% of the time, Pallas kernels for 2%

profile of v6, /device:TPU:0, one launch (start us, length us, event | category | flops | bytes accessed | tf_op | source)
XLA Modules:
  0.0 45.7 jit_solution(8247442464625463544)
XLA Ops:
  0.6 3.0 %shard_map.103 = (bf16[400,128]{1,0:T(8,128)(2,1)S(1)}, bf16[1024,128]{1,0:T(8,128)(2,1)S(1)}, bf16[1024,128]{1,0:T(8,128)(2,1)S(1)}) custom-call(s32[2]{0:T(128)} %counts.1, s32[1,8]{1,0:T(1,128)} %owner.1, s32[1,8]{1,0:T(1,128)} %local.1, bf16[2,16,1024]{2,1,0:T(8,128)(2,1)} %features.1, bf16[1,128,128]{2,1,0:T(8,128)(2,1)} %adjacency.1, ...), custom_call_target="tpu_custom_call" | custom-call | tf_op jit(solution)/shard_map/pallas_call | solution.py:246
  3.6 0.0 copy-start.1
  3.6 3.0 %collective-permute-start.1 = (bf16[1024,128]{1,0:T(8,128)(2,1)S(1)}, bf16[1024,128]{1,0:T(8,128)(2,1)S(1)}, u32[]{:S(2)}, u32[]{:S(2)}) collective-permute-start(bf16[1024,128]{1,0:T(8,128)(2,1)S(1)} %get-tuple-element.25), channel_id=1, source_target_pairs={{0,2},{1,3},{2,0},{3,1},{4,6},{5,7},{6,4},{7,5},{8,10},{9,11},{10,... | collective-permute-start | bytes 786440 | tf_op jit(solution)/shard_map/ppermute | solution.py:267
  6.7 2.6 %collective-permute-start = (bf16[400,128]{1,0:T(8,128)(2,1)S(1)}, bf16[400,128]{1,0:T(8,128)(2,1)S(1)}, u32[]{:S(2)}, u32[]{:S(2)}) collective-permute-start(bf16[400,128]{1,0:T(8,128)(2,1)S(1)} %get-tuple-element.23.piece), channel_id=1, source_target_pairs={{0,8},{1,9},{2,10},{3,11},{4,12},{5,13},{6,14},{7,15},{8,0},{9,1},... | collective-permute-start | bytes 307208 | tf_op jit(solution)/shard_map/ppermute | solution.py:267
  9.2 4.8 %collective-permute-done.came = bf16[400,128]{1,0:T(8,128)(2,1)S(1)} collective-permute-done((bf16[400,128]{1,0:T(8,128)(2,1)S(1)}, bf16[400,128]{1,0:T(8,128)(2,1)S(1)}, u32[]{:S(2)}, u32[]{:S(2)}) %collective-permute-start) | collective-permute-done | bytes 102432 | tf_op jit(solution)/shard_map/ppermute | solution.py:267
  14.1 0.0 collective-permute-done.1.across
  14.1 0.1 shard_map.104
  14.1 3.6 %collective-permute-start.4 = (bf16[512,128]{1,0:T(8,128)(2,1)S(1)}, bf16[512,128]{1,0:T(8,128)(2,1)S(1)}, u32[]{:S(2)}, u32[]{:S(2)}) collective-permute-start(bf16[512,128]{1,0:T(8,128)(2,1)S(1)} %get-tuple-element.28), channel_id=1, source_target_pairs={{0,12},{1,13},{2,14},{3,15},{4,8},{5,9},{6,10},{7,11},{8,4},{9,5},... | collective-permute-start | bytes 393224 | tf_op jit(solution)/shard_map/ppermute | solution.py:267
  17.7 0.7 %collective-permute-start.3 = (bf16[416,128]{1,0:T(8,128)(2,1)S(1)}, bf16[416,128]{1,0:T(8,128)(2,1)S(1)}, u32[]{:S(2)}, u32[]{:S(2)}) collective-permute-start(bf16[416,128]{1,0:T(8,128)(2,1)S(1)} %get-tuple-element.27.b), channel_id=1, source_target_pairs={{0,2},{1,3},{2,0},{3,1},{4,6},{5,7},{6,4},{7,5},{8,10},{9,11},{10,... | collective-permute-start | bytes 319496 | tf_op jit(solution)/shard_map/ppermute | solution.py:267
  18.4 0.0 collective-permute-start.2
  18.4 4.9 %collective-permute-done.2.came_a = bf16[384,128]{1,0:T(8,128)(2,1)S(1)} collective-permute-done((bf16[384,128]{1,0:T(8,128)(2,1)S(1)}, bf16[384,128]{1,0:T(8,128)(2,1)S(1)}, u32[]{:S(2)}, u32[]{:S(2)}) %collective-permute-start.2) | collective-permute-done | bytes 98336 | tf_op jit(solution)/shard_map/ppermute | solution.py:267
  23.4 0.0 collective-permute-done.3.came_b
  23.4 0.0 collective-permute-done.4.refs_0_
  23.4 1.7 %collective-permute-start.6 = (bf16[832,128]{1,0:T(8,128)(2,1)S(1)}, bf16[832,128]{1,0:T(8,128)(2,1)S(1)}, u32[]{:S(2)}, u32[]{:S(2)}) collective-permute-start(bf16[832,128]{1,0:T(8,128)(2,1)S(1)} %get-tuple-element.32.b), channel_id=1, source_target_pairs={{0,4},{1,5},{2,6},{3,7},{4,0},{5,1},{6,2},{7,3},{8,12},{9,13},{10,... | collective-permute-start | bytes 638984 | tf_op jit(solution)/shard_map/ppermute | solution.py:267
  25.1 0.6 %collective-permute-start.5 = (bf16[768,128]{1,0:T(8,128)(2,1)S(1)}, bf16[768,128]{1,0:T(8,128)(2,1)S(1)}, u32[]{:S(2)}, u32[]{:S(2)}) collective-permute-start(bf16[768,128]{1,0:T(8,128)(2,1)S(1)} %get-tuple-element.31.a), channel_id=1, source_target_pairs={{0,2},{1,3},{2,0},{3,1},{4,6},{5,7},{6,4},{7,5},{8,10},{9,11},{10,... | collective-permute-start | bytes 589832 | tf_op jit(solution)/shard_map/ppermute | solution.py:267
  25.7 1.8 %collective-permute-start.7 = (bf16[512,128]{1,0:T(8,128)(2,1)S(1)}, bf16[512,128]{1,0:T(8,128)(2,1)S(1)}, u32[]{:S(2)}, u32[]{:S(2)}) collective-permute-start(bf16[512,128]{1,0:T(8,128)(2,1)S(1)} %get-tuple-element.34), channel_id=1, source_target_pairs={{0,8},{1,9},{2,10},{3,11},{4,12},{5,13},{6,14},{7,15},{8,0},{9,1},... | collective-permute-start | bytes 393224 | tf_op jit(solution)/shard_map/ppermute | solution.py:267
  27.5 0.1 collective-permute-start.8
  27.6 5.0 %collective-permute-done.7.refs_1_ = bf16[512,128]{1,0:T(8,128)(2,1)S(1)} collective-permute-done((bf16[512,128]{1,0:T(8,128)(2,1)S(1)}, bf16[512,128]{1,0:T(8,128)(2,1)S(1)}, u32[]{:S(2)}, u32[]{:S(2)}) %collective-permute-start.7) | collective-permute-done | bytes 131104 | tf_op jit(solution)/shard_map/ppermute | solution.py:267
  32.6 2.7 %collective-permute-done.8.refs_2_ = bf16[512,128]{1,0:T(8,128)(2,1)S(1)} collective-permute-done((bf16[512,128]{1,0:T(8,128)(2,1)S(1)}, bf16[512,128]{1,0:T(8,128)(2,1)S(1)}, u32[]{:S(2)}, u32[]{:S(2)}) %collective-permute-start.8) | collective-permute-done | bytes 131104 | tf_op jit(solution)/shard_map/ppermute | solution.py:267
  35.3 0.0 collective-permute-done.5.far_a
  35.3 0.0 collective-permute-done.6.far_b
  35.4 0.0 copy-start
  35.4 0.1 shard_map.106
  35.4 0.1 collective-permute-start.9
  35.5 0.0 copy-done.1
  35.5 1.0 %shard_map.107 = (bf16[256,1024]{1,0:T(8,128)(2,1)S(1)}, bf16[256,1024]{1,0:T(8,128)(2,1)S(1)}, bf16[1024,512]{1,0:T(8,128)(2,1)S(1)}, bf16[8,128,128]{2,1,0:T(8...) custom-call(bf16[768,128]{1,0:T(8,128)(2,1)S(1)} %get-tuple-element.31.a, ...), custom_call_target="tpu_custom_call" | custom-call | tf_op jit(solution)/shard_map/pallas_call | solution.py:246
  36.5 1.7 %collective-permute-done.9.pair = bf16[4224,128]{1,0:T(8,128)(2,1)S(1)} collective-permute-done((bf16[4224,128]{1,0:T(8,128)(2,1)S(1)}, bf16[4224,128]{1,0:T(8,128)(2,1)S(1)}, u32[]{:S(2)}, u32[]{:S(2)}) %collective-permute-start.9) | collective-permute-done | bytes 1081376 | tf_op jit(solution)/shard_map/ppermute | solution.py:267
  38.2 0.0 copy-done
  38.2 7.5 %shard_map.108 = (bf16[1,128,1024]{2,1,0:T(8,128)(2,1)}, f32[64,1024]{1,0:T(8,128)}, f32[64,1024]{1,0:T(8,128)}) custom-call(bf16[4224,128]{1,0:T(8,128)(2,1)S(1)} %collective-permute-done.9.pair, bf16[512,128]{1,0:T(8,128)(2,1)S(1)} %collective-permute-done.4.refs_0_, bf16[512,128]{1,0:T(8,128)(2,1)S(1)} %collective-permute-done.7.refs_1_, ...), custom_call_target="tpu_custom_call" | custom-call | tf_op jit(solution)/shard_map/pallas_call | solution.py:246
  (1 shorter events, 0.0 us)
Async XLA Ops:
  3.6 31.9 %copy-start.1 = (bf16[1024,1024]{1,0:T(8,128)(2,1)S(1)}, bf16[1024,1024]{1,0:T(8,128)(2,1)}, u32[]{:S(2)}) copy-start(bf16[1024,1024]{1,0:T(8,128)(2,1)} %refs_10_.1) | copy-start | bytes 6291460
  3.6 10.5 %collective-permute-start.1 = (bf16[1024,128]{1,0:T(8,128)(2,1)S(1)}, bf16[1024,128]{1,0:T(8,128)(2,1)S(1)}, u32[]{:S(2)}, u32[]{:S(2)}) collective-permute-start(bf16[1024,128]{1,0:T(8,128)(2,1)S(1)} %get-tuple-element.25), channel_id=1, source_target_pairs={{0,2},{1,3},{2,0},{3,1},{4,6},{5,7},{6,4},{7,5},{8,10},{9,11},{10,... | collective-permute-start | bytes 786440 | tf_op jit(solution)/shard_map/ppermute | solution.py:267
  6.7 7.4 %collective-permute-start = (bf16[400,128]{1,0:T(8,128)(2,1)S(1)}, bf16[400,128]{1,0:T(8,128)(2,1)S(1)}, u32[]{:S(2)}, u32[]{:S(2)}) collective-permute-start(bf16[400,128]{1,0:T(8,128)(2,1)S(1)} %get-tuple-element.23.piece), channel_id=1, source_target_pairs={{0,8},{1,9},{2,10},{3,11},{4,12},{5,13},{6,14},{7,15},{8,0},{9,1},... | collective-permute-start | bytes 307208 | tf_op jit(solution)/shard_map/ppermute | solution.py:267
  14.1 9.2 %collective-permute-start.4 = (bf16[512,128]{1,0:T(8,128)(2,1)S(1)}, bf16[512,128]{1,0:T(8,128)(2,1)S(1)}, u32[]{:S(2)}, u32[]{:S(2)}) collective-permute-start(bf16[512,128]{1,0:T(8,128)(2,1)S(1)} %get-tuple-element.28), channel_id=1, source_target_pairs={{0,12},{1,13},{2,14},{3,15},{4,8},{5,9},{6,10},{7,11},{8,4},{9,5},... | collective-permute-start | bytes 393224 | tf_op jit(solution)/shard_map/ppermute | solution.py:267
  17.7 5.7 %collective-permute-start.3 = (bf16[416,128]{1,0:T(8,128)(2,1)S(1)}, bf16[416,128]{1,0:T(8,128)(2,1)S(1)}, u32[]{:S(2)}, u32[]{:S(2)}) collective-permute-start(bf16[416,128]{1,0:T(8,128)(2,1)S(1)} %get-tuple-element.27.b), channel_id=1, source_target_pairs={{0,2},{1,3},{2,0},{3,1},{4,6},{5,7},{6,4},{7,5},{8,10},{9,11},{10,... | collective-permute-start | bytes 319496 | tf_op jit(solution)/shard_map/ppermute | solution.py:267
  18.4 4.9 %collective-permute-start.2 = (bf16[384,128]{1,0:T(8,128)(2,1)S(1)}, bf16[384,128]{1,0:T(8,128)(2,1)S(1)}, u32[]{:S(2)}, u32[]{:S(2)}) collective-permute-start(bf16[384,128]{1,0:T(8,128)(2,1)S(1)} %get-tuple-element.26.a), channel_id=1, source_target_pairs={{0,4},{1,5},{2,6},{3,7},{4,0},{5,1},{6,2},{7,3},{8,12},{9,13},{10,... | collective-permute-start | bytes 294920 | tf_op jit(solution)/shard_map/ppermute | solution.py:267
  23.4 12.0 %collective-permute-start.6 = (bf16[832,128]{1,0:T(8,128)(2,1)S(1)}, bf16[832,128]{1,0:T(8,128)(2,1)S(1)}, u32[]{:S(2)}, u32[]{:S(2)}) collective-permute-start(bf16[832,128]{1,0:T(8,128)(2,1)S(1)} %get-tuple-element.32.b), channel_id=1, source_target_pairs={{0,4},{1,5},{2,6},{3,7},{4,0},{5,1},{6,2},{7,3},{8,12},{9,13},{10,... | collective-permute-start | bytes 638984 | tf_op jit(solution)/shard_map/ppermute | solution.py:267
  25.1 10.2 %collective-permute-start.5 = (bf16[768,128]{1,0:T(8,128)(2,1)S(1)}, bf16[768,128]{1,0:T(8,128)(2,1)S(1)}, u32[]{:S(2)}, u32[]{:S(2)}) collective-permute-start(bf16[768,128]{1,0:T(8,128)(2,1)S(1)} %get-tuple-element.31.a), channel_id=1, source_target_pairs={{0,2},{1,3},{2,0},{3,1},{4,6},{5,7},{6,4},{7,5},{8,10},{9,11},{10,... | collective-permute-start | bytes 589832 | tf_op jit(solution)/shard_map/ppermute | solution.py:267
  25.7 7.0 %collective-permute-start.7 = (bf16[512,128]{1,0:T(8,128)(2,1)S(1)}, bf16[512,128]{1,0:T(8,128)(2,1)S(1)}, u32[]{:S(2)}, u32[]{:S(2)}) collective-permute-start(bf16[512,128]{1,0:T(8,128)(2,1)S(1)} %get-tuple-element.34), channel_id=1, source_target_pairs={{0,8},{1,9},{2,10},{3,11},{4,12},{5,13},{6,14},{7,15},{8,0},{9,1},... | collective-permute-start | bytes 393224 | tf_op jit(solution)/shard_map/ppermute | solution.py:267
  27.5 7.8 %collective-permute-start.8 = (bf16[512,128]{1,0:T(8,128)(2,1)S(1)}, bf16[512,128]{1,0:T(8,128)(2,1)S(1)}, u32[]{:S(2)}, u32[]{:S(2)}) collective-permute-start(bf16[512,128]{1,0:T(8,128)(2,1)S(1)} %get-tuple-element.35), channel_id=1, source_target_pairs={{0,4},{1,5},{2,6},{3,7},{4,0},{5,1},{6,2},{7,3},{8,12},{9,13},{10,... | collective-permute-start | bytes 393224 | tf_op jit(solution)/shard_map/ppermute | solution.py:267
  35.4 2.9 %copy-start = (bf16[1024,1024]{1,0:T(8,128)(2,1)S(1)}, bf16[1024,1024]{1,0:T(8,128)(2,1)}, u32[]{:S(2)}) copy-start(bf16[1024,1024]{1,0:T(8,128)(2,1)} %refs_11_.1) | copy-start | bytes 6291460
  35.4 2.8 %collective-permute-start.9 = (bf16[4224,128]{1,0:T(8,128)(2,1)S(1)}, bf16[4224,128]{1,0:T(8,128)(2,1)S(1)}, u32[]{:S(2)}, u32[]{:S(2)}) collective-permute-start(bf16[4224,128]{1,0:T(8,128)(2,1)S(1)} %shard_map.106), channel_id=1, source_target_pairs={{0,1},{1,0},{2,3},{3,2},{4,5},{5,4},{6,7},{7,6},{8,9},{9,8},{10,11... | collective-permute-start | bytes 3244040 | tf_op jit(solution)/shard_map/ppermute | solution.py:267

commit v7 on v6

--- a/solution.py
+++ b/solution.py
@@ -18,7 +18,7 @@
 SMALL = 8 * 2**20
 Z2, Z1, Y, CORE = 8, 4, 2, 1
 GROUP = 16
-FAR = (Z2 | Z1, Z2, Z1)
+FAR = (Z2 | Z1, Z2, 0)
 HALF_A = ((0, Z2, Z1, Z1 | Z2), (Y, Y | Z2, Y | Z1, Y | Z1 | Z2))
 HALF_B = ((0, Z2, Y, Y | Z2), (Z1, Z1 | Z2, Z1 | Y, Z1 | Y | Z2))
 
@@ -89,30 +89,37 @@
     return at
 
 
-def split_kernel(piece, came, near, across, half_a, half_b, *sent):
-    cut = half_a.shape[0] // 2
-    stack(half_a, 0, piece.at[:cut], came.at[:cut])
-    stack(half_b, 0, piece.at[cut:], came.at[cut:])
+def split_kernel(piece, came, near, across, beside, half_b, *sent):
+    cut = beside.shape[0] - sent[0].shape[0]
+    stack(half_b, 0, piece.at[cut // 2 :], came.at[cut // 2 :])
+    at = stack(beside, 0, piece.at[: cut // 2], came.at[: cut // 2])
     size = sent[0].shape[0] // 2
-    for slot, out in zip(FAR + (0,), sent):
+    for slot, (out, at) in {Z1: (beside, at), **{slot: (out, 0) for slot, out in zip(FAR, sent)}}.items():
         span = slice(slot // 4 * size, (slot // 4 + 1) * size)
-        stack(out, 0, near.at[span], across.at[span])
-
-
-def join_kernel(a, came_a, b, came_b, out_a, out_b):
-    stack(out_a, 0, a, came_a)
-    stack(out_b, 0, b, came_b)
-
-
-def pair_kernel(a, far_a, b, far_b, *refs):
+        stack(out, at, near.at[span], across.at[span])
+
+
+def join_kernel(beside, came, half_b, came_b, out_a, out_b, both):
+    cut = out_a.shape[0] // 2
+    stack(out_a, 0, beside.at[:cut], came.at[:cut])
+    stack(out_b, 0, half_b, came_b)
+    stack(both, 0, out_a, out_b)
+
+
+def columns_kernel(came, *refs):
     *sent, out = refs
-    at = stack(out, 0, a, far_a, b, far_b)
-    size = sent[0].shape[0] // 2
-    rows = size // 2
-    for s in range(GROUP // 4):
+    size = sent[0].shape[0]
+    blocks = dict(zip(FAR, sent))
+    blocks[Z1] = came.at[came.shape[0] - size :]
+    rows = size // 4
+    at = 0
+    for slot in range(0, GROUP, 4):
         for h in range(2):
-            block = sent[(FAR + (0,)).index(4 * s)]
-            at = stack(out, at, block.at[h * size + rows : (h + 1) * size])
+            at = stack(out, at, blocks[slot].at[(2 * h + 1) * rows : (2 * h + 2) * rows])
+
+
+def pair_kernel(far_a, far_b, columns, out):
+    stack(out, 0, far_a, far_b, columns)
 
 
 def place_of(slot):
@@ -171,8 +178,8 @@
     w_piece[...] = part.astype(BF16)
 
 
-def step_kernel(own, slots, cut, rest, pair, *refs):
-    sent, refs = refs[: len(FAR) + 1], refs[len(FAR) + 1 :]
+def step_kernel(own, slots, cut, rest, core, pair, came, *refs):
+    sent, refs = dict(zip(FAR, refs)), refs[len(FAR) :]
     early_feat, early_lifted, early_spread, early_adj, early_meta, w_piece = refs[:6]
     w_first, w_second, output, grad_first, grad_second = refs[6:11]
     hidden, spread, feat, adj, meta, dout, dpre, lifted = refs[11:]
@@ -187,11 +194,11 @@
     spread[: first * rows, :] = early_spread[...]
     adj[:first] = early_adj[...]
     meta[:first] = early_meta[...]
-    arrays, deep = [], 0
-    for size, halves in ((cut, HALF_A), (rest, HALF_B)):
-        for group in halves:
-            arrays.append((pair, deep, [slot | CORE for slot in group]))
-            deep += size * len(group)
+    arrays = []
+    for size, start, halves in ((cut, 0, HALF_A), (rest, 4 * cut, HALF_B)):
+        for ref, group in zip((core, pair), halves):
+            arrays.append((ref, start, [slot | CORE for slot in group]))
+    deep = 4 * (cut + rest)
     lay_out(arrays, held, cut, feat, adj, meta)
     metas = [meta[p].astype(F32) for p in range(GROUP)]
     picks = jnp.concatenate([m[0:1] for m in metas], axis=0).astype(jnp.int32)
@@ -219,7 +226,8 @@
     output[0] = (nn(agg, w_second[...]) * live).astype(BF16)
 
     each = grad_first.shape[0]
-    size = sent[0].shape[0] // 2
+    size = sent[0].shape[0]
+    sent[Z1] = came.at[came.shape[0] - size :]
     for slot in range(GROUP):
         p = place_of(slot)
         mask = masks[p : p + 1]
@@ -229,7 +237,7 @@
             at = deep + (2 * s + h) * 2 * each
             source = pair[at : at + 2 * each, :]
         else:
-            source = sent[(FAR + (0,)).index(4 * s)][h * size : h * size + 2 * each, :]
+            source = sent[4 * s][h * size // 2 : h * size // 2 + 2 * each, :]
         back = nn((source.astype(F32) * mask).astype(BF16), adj[p]) * mask
         dout[:, span] = back[:each].astype(BF16)
         pre = pre_piece[:, span]
@@ -240,7 +248,7 @@
     grad_first[...] = nn(moved.astype(BF16), feat[...])
 
 
-def call(kernel, ins, outs, scratch=(), limit=SMALL, stay=False):
+def call(kernel, ins, outs, scratch=(), limit=SMALL, stay=False, flops=0):
     if stay:
         ins = [pltpu.with_memory_space_constraint(x, pltpu.HBM) for x in ins]
     return pl.pallas_call(
@@ -250,6 +258,7 @@
         out_specs=(VMEM,) * len(outs),
         scratch_shapes=list(scratch),
         compiler_params=pltpu.CompilerParams(vmem_limit_bytes=limit),
+        cost_estimate=pl.CostEstimate(flops=flops, bytes_accessed=0, transcendentals=0),
     )(*ins)
 
 
@@ -278,22 +287,28 @@
     )
     came = swap(piece, Z2)
     across = swap(across, Y)
-    a, b, *sent = call(
+    beside, b, *sent = call(
         split_kernel,
         (piece, came, near, across),
-        [((2 * cut, LANES), BF16), ((2 * rest, LANES), BF16)] + [((8 * each, rows), BF16)] * (len(FAR) + 1),
-    )
-    sent = [swap(x, slot) for x, slot in zip(sent, FAR)] + sent[-1:]
-    came_a, came_b = swap(a, Z1), swap(b, Y)
-    came_a, came_b, sent[0] = lax.optimization_barrier((came_a, came_b, sent[0]))
-    a, b = call(
-        join_kernel, (a, came_a, b, came_b), [((4 * cut, LANES), BF16), ((4 * rest, LANES), BF16)]
-    )
-    far_a, far_b = swap(a, Y), swap(b, Z1)
+        [((2 * cut + 8 * each, LANES), BF16), ((2 * rest, LANES), BF16)]
+        + [((8 * each, rows), BF16)] * len(FAR),
+    )
+    came, came_b = swap(beside, Z1), swap(b, Y)
+    sent = [swap(x, slot) if slot else x for x, slot in zip(sent, FAR)]
+    a, b, both = call(
+        join_kernel,
+        (beside, came, b, came_b),
+        [((4 * size, LANES), BF16) for size in (cut, rest, cut + rest)],
+    )
+    far_a, far_b, core = swap(a, Y), swap(b, Z1), swap(both, CORE)
+    (columns,) = call(
+        columns_kernel, (came, *sent), [((half * 2 * each, rows), BF16)], flops=8 * 10**9
+    )
+    far_a, far_b, core = lax.optimization_barrier((far_a, far_b, core))
     (pair,) = call(
         pair_kernel,
-        (a, far_a, b, far_b, *sent),
-        [((half * (cut + rest) + half * 2 * each, LANES), BF16)],
+        (far_a, far_b, columns),
+        [((4 * (cut + rest) + half * 2 * each, LANES), BF16)],
     )
     pair = swap(pair, CORE)
     early = call(
@@ -311,7 +326,7 @@
     )
     return call(
         functools.partial(step_kernel, own, slots, cut, rest),
-        (pair, *sent, *early, w_first, w_second),
+        (core, pair, came, *sent, *early, w_first, w_second),
         [((1, rows, width), BF16), ((each, width), F32), ((each, width), F32)],
         [
             pltpu.VMEM((GROUP * rows, width), BF16),

time: 45.9 us -> 42.5 us (0.926); the launches traced: 45.7 us -> 41.8 us
  waiting for transfers between devices: 19.3 us -> 16.3 us
  starting transfers between devices: 14.1 us -> 13.2 us
    ppermute x10, waiting for transfers between devices: 19.3 us -> 16.3 us  [swap(): return lax.ppermute(x, 'grp', [(i, i ^ slot) for i in range(GROUP)])]
    ppermute x10, starting transfers between devices: 14.1 us -> 13.2 us  [swap(): return lax.ppermute(x, 'grp', [(i, i ^ slot) for i in range(GROUP)])]
    pallas_call x6 -> x7, Pallas kernels: 11.6 us -> 11.6 us  [call(): pl.pallas_call(kernel, out_shape=tuple((jax.ShapeDtypeStruct(*out) for ou...]
  transfers between devices with their start and end apart: 10 -> 10, of which waited for: 5 -> 7; matrix products, arithmetic and copies ran while one was open for 0% -> 0% of each run, Pallas kernels for 2% -> 3%
where the time goes in v7:
time: 42.5 us; the launch traced here: 41.8 us
  waiting for transfers between devices  16.3 us (38%)
  starting transfers between devices  13.2 us (31%)
  Pallas kernels  11.6 us (27%)
  between operations  0.71 us (2%)
    ppermute x10, waiting for transfers between devices, swap(): return lax.ppermute(x, 'grp', [(i, i ^ slot) for i in range(GROUP)])  16.3 us
    ppermute x10, starting transfers between devices, swap(): return lax.ppermute(x, 'grp', [(i, i ^ slot) for i in range(GROUP)])  13.2 us
    pallas_call x7, Pallas kernels, call(): pl.pallas_call(kernel, out_shape=tuple((jax.ShapeDtypeStruct(*out) for ou...  11.6 us
  transfers between devices with their start and end apart: 10, of which 7 were waited for; matrix products, arithmetic and copies ran while one was open for 0% of the time, Pallas kernels for 3%

profile of v7, /device:TPU:0, one launch (start us, length us, event | category | flops | bytes accessed | tf_op | source)
XLA Modules:
  0.0 41.8 jit_solution(9748409051361272474)
XLA Ops:
  0.6 3.0 %shard_map.103 = (bf16[400,128]{1,0:T(8,128)(2,1)S(1)}, bf16[1024,128]{1,0:T(8,128)(2,1)S(1)}, bf16[1024,128]{1,0:T(8,128)(2,1)S(1)}) custom-call(s32[2]{0:T(128)} %counts.1, s32[1,8]{1,0:T(1,128)} %owner.1, s32[1,8]{1,0:T(1,128)} %local.1, bf16[2,16,1024]{2,1,0:T(8,128)(2,1)} %features.1, bf16[1,128,128]{2,1,0:T(8,128)(2,1)} %adjacency.1, ...), custom_call_target="tpu_custom_call" | custom-call | tf_op jit(solution)/shard_map/pallas_call | solution.py:254
  3.6 3.0 %collective-permute-start.1 = (bf16[1024,128]{1,0:T(8,128)(2,1)S(1)}, bf16[1024,128]{1,0:T(8,128)(2,1)S(1)}, u32[]{:S(2)}, u32[]{:S(2)}) collective-permute-start(bf16[1024,128]{1,0:T(8,128)(2,1)S(1)} %get-tuple-element.25), channel_id=1, source_target_pairs={{0,2},{1,3},{2,0},{3,1},{4,6},{5,7},{6,4},{7,5},{8,10},{9,11},{10,... | collective-permute-start | bytes 786440 | tf_op jit(solution)/shard_map/ppermute | solution.py:276
  6.6 2.6 %collective-permute-start = (bf16[400,128]{1,0:T(8,128)(2,1)S(1)}, bf16[400,128]{1,0:T(8,128)(2,1)S(1)}, u32[]{:S(2)}, u32[]{:S(2)}) collective-permute-start(bf16[400,128]{1,0:T(8,128)(2,1)S(1)} %get-tuple-element.23.piece), channel_id=1, source_target_pairs={{0,8},{1,9},{2,10},{3,11},{4,12},{5,13},{6,14},{7,15},{8,0},{9,1},... | collective-permute-start | bytes 307208 | tf_op jit(solution)/shard_map/ppermute | solution.py:276
  9.2 4.8 %collective-permute-done.came = bf16[400,128]{1,0:T(8,128)(2,1)S(1)} collective-permute-done((bf16[400,128]{1,0:T(8,128)(2,1)S(1)}, bf16[400,128]{1,0:T(8,128)(2,1)S(1)}, u32[]{:S(2)}, u32[]{:S(2)}) %collective-permute-start) | collective-permute-done | bytes 102432 | tf_op jit(solution)/shard_map/ppermute | solution.py:276
  14.1 0.0 collective-permute-done.1.across
  14.1 0.1 shard_map.104
  14.1 0.7 %collective-permute-start.2 = (bf16[896,128]{1,0:T(8,128)(2,1)S(1)}, bf16[896,128]{1,0:T(8,128)(2,1)S(1)}, u32[]{:S(2)}, u32[]{:S(2)}) collective-permute-start(bf16[896,128]{1,0:T(8,128)(2,1)S(1)} %get-tuple-element.26.beside), channel_id=1, source_target_pairs={{0,4},{1,5},{2,6},{3,7},{4,0},{5,1},{6,2},{7,3},{8,12},{9,13},{10,... | collective-permute-start | bytes 688136 | tf_op jit(solution)/shard_map/ppermute | solution.py:276
  14.9 2.9 %collective-permute-start.7 = (bf16[512,128]{1,0:T(8,128)(2,1)S(1)}, bf16[512,128]{1,0:T(8,128)(2,1)S(1)}, u32[]{:S(2)}, u32[]{:S(2)}) collective-permute-start(bf16[512,128]{1,0:T(8,128)(2,1)S(1)} %get-tuple-element.34), channel_id=1, source_target_pairs={{0,12},{1,13},{2,14},{3,15},{4,8},{5,9},{6,10},{7,11},{8,4},{9,5},... | collective-permute-start | bytes 393224 | tf_op jit(solution)/shard_map/ppermute | solution.py:276
  17.8 0.5 %collective-permute-start.8 = (bf16[512,128]{1,0:T(8,128)(2,1)S(1)}, bf16[512,128]{1,0:T(8,128)(2,1)S(1)}, u32[]{:S(2)}, u32[]{:S(2)}) collective-permute-start(bf16[512,128]{1,0:T(8,128)(2,1)S(1)} %get-tuple-element.35), channel_id=1, source_target_pairs={{0,8},{1,9},{2,10},{3,11},{4,12},{5,13},{6,14},{7,15},{8,0},{9,1},... | collective-permute-start | bytes 393224 | tf_op jit(solution)/shard_map/ppermute | solution.py:276
  18.3 0.7 %collective-permute-start.3 = (bf16[416,128]{1,0:T(8,128)(2,1)S(1)}, bf16[416,128]{1,0:T(8,128)(2,1)S(1)}, u32[]{:S(2)}, u32[]{:S(2)}) collective-permute-start(bf16[416,128]{1,0:T(8,128)(2,1)S(1)} %get-tuple-element.27.half_b), channel_id=1, source_target_pairs={{0,2},{1,3},{2,0},{3,1},{4,6},{5,7},{6,4},{7,5},{8,10},{9,11},{10,... | collective-permute-start | bytes 319496 | tf_op jit(solution)/shard_map/ppermute | solution.py:276
  19.0 4.0 %collective-permute-done.3.came_b = bf16[416,128]{1,0:T(8,128)(2,1)S(1)} collective-permute-done((bf16[416,128]{1,0:T(8,128)(2,1)S(1)}, bf16[416,128]{1,0:T(8,128)(2,1)S(1)}, u32[]{:S(2)}, u32[]{:S(2)}) %collective-permute-start.3) | collective-permute-done | bytes 106528 | tf_op jit(solution)/shard_map/ppermute | solution.py:276
  23.0 0.0 collective-permute-done.2.came
  23.0 0.1 shard_map.105
  23.0 0.1 collective-permute-start.6
  23.1 1.1 %collective-permute-start.5 = (bf16[832,128]{1,0:T(8,128)(2,1)S(1)}, bf16[832,128]{1,0:T(8,128)(2,1)S(1)}, u32[]{:S(2)}, u32[]{:S(2)}) collective-permute-start(bf16[832,128]{1,0:T(8,128)(2,1)S(1)} %get-tuple-element.29.b), channel_id=1, source_target_pairs={{0,4},{1,5},{2,6},{3,7},{4,0},{5,1},{6,2},{7,3},{8,12},{9,13},{10,... | collective-permute-start | bytes 638984 | tf_op jit(solution)/shard_map/ppermute | solution.py:276
  24.2 1.5 %collective-permute-start.4 = (bf16[768,128]{1,0:T(8,128)(2,1)S(1)}, bf16[768,128]{1,0:T(8,128)(2,1)S(1)}, u32[]{:S(2)}, u32[]{:S(2)}) collective-permute-start(bf16[768,128]{1,0:T(8,128)(2,1)S(1)} %get-tuple-element.28.a), channel_id=1, source_target_pairs={{0,2},{1,3},{2,0},{3,1},{4,6},{5,7},{6,4},{7,5},{8,10},{9,11},{10,... | collective-permute-start | bytes 589832 | tf_op jit(solution)/shard_map/ppermute | solution.py:276
  25.7 1.4 %collective-permute-done.7.refs_0_ = bf16[512,128]{1,0:T(8,128)(2,1)S(1)} collective-permute-done((bf16[512,128]{1,0:T(8,128)(2,1)S(1)}, bf16[512,128]{1,0:T(8,128)(2,1)S(1)}, u32[]{:S(2)}, u32[]{:S(2)}) %collective-permute-start.7) | collective-permute-done | bytes 131104 | tf_op jit(solution)/shard_map/ppermute | solution.py:276
  27.0 2.9 %collective-permute-done.8.refs_1_ = bf16[512,128]{1,0:T(8,128)(2,1)S(1)} collective-permute-done((bf16[512,128]{1,0:T(8,128)(2,1)S(1)}, bf16[512,128]{1,0:T(8,128)(2,1)S(1)}, u32[]{:S(2)}, u32[]{:S(2)}) %collective-permute-start.8) | collective-permute-done | bytes 131104 | tf_op jit(solution)/shard_map/ppermute | solution.py:276
  30.0 0.0 copy-start.1
  30.0 0.0 copy-start
  30.0 1.1 %collective-permute-done.4.far_a = bf16[768,128]{1,0:T(8,128)(2,1)S(1)} collective-permute-done((bf16[768,128]{1,0:T(8,128)(2,1)S(1)}, bf16[768,128]{1,0:T(8,128)(2,1)S(1)}, u32[]{:S(2)}, u32[]{:S(2)}) %collective-permute-start.4) | collective-permute-done | bytes 196640 | tf_op jit(solution)/shard_map/ppermute | solution.py:276
  31.1 0.9 %collective-permute-done.5.far_b = bf16[832,128]{1,0:T(8,128)(2,1)S(1)} collective-permute-done((bf16[832,128]{1,0:T(8,128)(2,1)S(1)}, bf16[832,128]{1,0:T(8,128)(2,1)S(1)}, u32[]{:S(2)}, u32[]{:S(2)}) %collective-permute-start.5) | collective-permute-done | bytes 213024 | tf_op jit(solution)/shard_map/ppermute | solution.py:276
  32.1 0.0 collective-permute-done.6.core
  32.1 0.1 collective-permute-start.9
  32.2 0.0 copy-done.1
  32.2 1.0 %shard_map.108 = (bf16[256,1024]{1,0:T(8,128)(2,1)S(1)}, bf16[256,1024]{1,0:T(8,128)(2,1)S(1)}, bf16[1024,512]{1,0:T(8,128)(2,1)S(1)}, bf16[8,128,128]{2,1,0:T(8...) custom-call(bf16[768,128]{1,0:T(8,128)(2,1)S(1)} %get-tuple-element.28.a, ...), custom_call_target="tpu_custom_call" | custom-call | tf_op jit(solution)/shard_map/pallas_call | solution.py:254
  33.2 1.1 %collective-permute-done.9.pair = bf16[2624,128]{1,0:T(8,128)(2,1)S(1)} collective-permute-done((bf16[2624,128]{1,0:T(8,128)(2,1)S(1)}, bf16[2624,128]{1,0:T(8,128)(2,1)S(1)}, u32[]{:S(2)}, u32[]{:S(2)}) %collective-permute-start.9) | collective-permute-done | bytes 671776 | tf_op jit(solution)/shard_map/ppermute | solution.py:276
  34.3 0.0 copy-done
  34.3 7.5 %shard_map.109 = (bf16[1,128,1024]{2,1,0:T(8,128)(2,1)}, f32[64,1024]{1,0:T(8,128)}, f32[64,1024]{1,0:T(8,128)}) custom-call(bf16[1600,128]{1,0:T(8,128)(2,1)S(1)} %collective-permute-done.6.core, bf16[2624,128]{1,0:T(8,128)(2,1)S(1)} %collective-permute-done.9.pair, bf16[896,128]{1,0:T(8,128)(2,1)S(1)} %collective-permute-done.2.came, ...), custom_call_target="tpu_custom_call" | custom-call | tf_op jit(solution)/shard_map/pallas_call | solution.py:254
  (2 shorter events, 0.1 us)
Async XLA Ops:
  3.6 10.5 %collective-permute-start.1 = (bf16[1024,128]{1,0:T(8,128)(2,1)S(1)}, bf16[1024,128]{1,0:T(8,128)(2,1)S(1)}, u32[]{:S(2)}, u32[]{:S(2)}) collective-permute-start(bf16[1024,128]{1,0:T(8,128)(2,1)S(1)} %get-tuple-element.25), channel_id=1, source_target_pairs={{0,2},{1,3},{2,0},{3,1},{4,6},{5,7},{6,4},{7,5},{8,10},{9,11},{10,... | collective-permute-start | bytes 786440 | tf_op jit(solution)/shard_map/ppermute | solution.py:276
  6.6 7.4 %collective-permute-start = (bf16[400,128]{1,0:T(8,128)(2,1)S(1)}, bf16[400,128]{1,0:T(8,128)(2,1)S(1)}, u32[]{:S(2)}, u32[]{:S(2)}) collective-permute-start(bf16[400,128]{1,0:T(8,128)(2,1)S(1)} %get-tuple-element.23.piece), channel_id=1, source_target_pairs={{0,8},{1,9},{2,10},{3,11},{4,12},{5,13},{6,14},{7,15},{8,0},{9,1},... | collective-permute-start | bytes 307208 | tf_op jit(solution)/shard_map/ppermute | solution.py:276
  14.1 8.8 %collective-permute-start.2 = (bf16[896,128]{1,0:T(8,128)(2,1)S(1)}, bf16[896,128]{1,0:T(8,128)(2,1)S(1)}, u32[]{:S(2)}, u32[]{:S(2)}) collective-permute-start(bf16[896,128]{1,0:T(8,128)(2,1)S(1)} %get-tuple-element.26.beside), channel_id=1, source_target_pairs={{0,4},{1,5},{2,6},{3,7},{4,0},{5,1},{6,2},{7,3},{8,12},{9,13},{10,... | collective-permute-start | bytes 688136 | tf_op jit(solution)/shard_map/ppermute | solution.py:276
  14.9 12.2 %collective-permute-start.7 = (bf16[512,128]{1,0:T(8,128)(2,1)S(1)}, bf16[512,128]{1,0:T(8,128)(2,1)S(1)}, u32[]{:S(2)}, u32[]{:S(2)}) collective-permute-start(bf16[512,128]{1,0:T(8,128)(2,1)S(1)} %get-tuple-element.34), channel_id=1, source_target_pairs={{0,12},{1,13},{2,14},{3,15},{4,8},{5,9},{6,10},{7,11},{8,4},{9,5},... | collective-permute-start | bytes 393224 | tf_op jit(solution)/shard_map/ppermute | solution.py:276
  17.8 12.2 %collective-permute-start.8 = (bf16[512,128]{1,0:T(8,128)(2,1)S(1)}, bf16[512,128]{1,0:T(8,128)(2,1)S(1)}, u32[]{:S(2)}, u32[]{:S(2)}) collective-permute-start(bf16[512,128]{1,0:T(8,128)(2,1)S(1)} %get-tuple-element.35), channel_id=1, source_target_pairs={{0,8},{1,9},{2,10},{3,11},{4,12},{5,13},{6,14},{7,15},{8,0},{9,1},... | collective-permute-start | bytes 393224 | tf_op jit(solution)/shard_map/ppermute | solution.py:276
  18.3 4.7 %collective-permute-start.3 = (bf16[416,128]{1,0:T(8,128)(2,1)S(1)}, bf16[416,128]{1,0:T(8,128)(2,1)S(1)}, u32[]{:S(2)}, u32[]{:S(2)}) collective-permute-start(bf16[416,128]{1,0:T(8,128)(2,1)S(1)} %get-tuple-element.27.half_b), channel_id=1, source_target_pairs={{0,2},{1,3},{2,0},{3,1},{4,6},{5,7},{6,4},{7,5},{8,10},{9,11},{10,... | collective-permute-start | bytes 319496 | tf_op jit(solution)/shard_map/ppermute | solution.py:276
  23.0 9.1 %collective-permute-start.6 = (bf16[1600,128]{1,0:T(8,128)(2,1)S(1)}, bf16[1600,128]{1,0:T(8,128)(2,1)S(1)}, u32[]{:S(2)}, u32[]{:S(2)}) collective-permute-start(bf16[1600,128]{1,0:T(8,128)(2,1)S(1)} %get-tuple-element.30), channel_id=1, source_target_pairs={{0,1},{1,0},{2,3},{3,2},{4,5},{5,4},{6,7},{7,6},{8,9},{9,8},{10,11... | collective-permute-start | bytes 1228808 | tf_op jit(solution)/shard_map/ppermute | solution.py:276
  23.1 9.0 %collective-permute-start.5 = (bf16[832,128]{1,0:T(8,128)(2,1)S(1)}, bf16[832,128]{1,0:T(8,128)(2,1)S(1)}, u32[]{:S(2)}, u32[]{:S(2)}) collective-permute-start(bf16[832,128]{1,0:T(8,128)(2,1)S(1)} %get-tuple-element.29.b), channel_id=1, source_target_pairs={{0,4},{1,5},{2,6},{3,7},{4,0},{5,1},{6,2},{7,3},{8,12},{9,13},{10,... | collective-permute-start | bytes 638984 | tf_op jit(solution)/shard_map/ppermute | solution.py:276
  24.2 7.0 %collective-permute-start.4 = (bf16[768,128]{1,0:T(8,128)(2,1)S(1)}, bf16[768,128]{1,0:T(8,128)(2,1)S(1)}, u32[]{:S(2)}, u32[]{:S(2)}) collective-permute-start(bf16[768,128]{1,0:T(8,128)(2,1)S(1)} %get-tuple-element.28.a), channel_id=1, source_target_pairs={{0,2},{1,3},{2,0},{3,1},{4,6},{5,7},{6,4},{7,5},{8,10},{9,11},{10,... | collective-permute-start | bytes 589832 | tf_op jit(solution)/shard_map/ppermute | solution.py:276
  30.0 2.2 %copy-start.1 = (bf16[1024,1024]{1,0:T(8,128)(2,1)S(1)}, bf16[1024,1024]{1,0:T(8,128)(2,1)}, u32[]{:S(2)}) copy-start(bf16[1024,1024]{1,0:T(8,128)(2,1)} %refs_9_.1) | copy-start | bytes 6291460
  30.0 4.3 %copy-start = (bf16[1024,1024]{1,0:T(8,128)(2,1)S(1)}, bf16[1024,1024]{1,0:T(8,128)(2,1)}, u32[]{:S(2)}) copy-start(bf16[1024,1024]{1,0:T(8,128)(2,1)} %refs_10_.1) | copy-start | bytes 6291460
  32.1 2.2 %collective-permute-start.9 = (bf16[2624,128]{1,0:T(8,128)(2,1)S(1)}, bf16[2624,128]{1,0:T(8,128)(2,1)S(1)}, u32[]{:S(2)}, u32[]{:S(2)}) collective-permute-start(bf16[2624,128]{1,0:T(8,128)(2,1)S(1)} %shard_map.107), channel_id=1, source_target_pairs={{0,1},{1,0},{2,3},{3,2},{4,5},{5,4},{6,7},{7,6},{8,9},{9,8},{10,11... | collective-permute-start | bytes 2015240 | tf_op jit(solution)/shard_map/ppermute | solution.py:276

commit v8 on v7

--- a/solution.py
+++ b/solution.py
@@ -14,11 +14,14 @@
 LANES = 128
 META = 16
 CHUNKS = 4
-LIMIT = 24 * 2**20
+LIMIT = 16 * 2**20
 SMALL = 8 * 2**20
 Z2, Z1, Y, CORE = 8, 4, 2, 1
 GROUP = 16
-FAR = (Z2 | Z1, Z2, 0)
+HINT = (0, 8 * 10**9, 0, 0, 0, 8 * 10**9, 0)
+FAR = (Z2 | Z1, Z2, Z1, 0)
+FIRST = (0, 2, 3)
+LAST = (1,)
 HALF_A = ((0, Z2, Z1, Z1 | Z2), (Y, Y | Z2, Y | Z1, Y | Z1 | Z2))
 HALF_B = ((0, Z2, Y, Y | Z2), (Z1, Z1 | Z2, Z1 | Y, Z1 | Y | Z2))
 
@@ -31,28 +34,24 @@
     return lax.dot_general(a, b, (((1,), (1,)), ((), ())), preferred_element_type=F32)
 
 
-def prepare_kernel(counts, owner, local, features, adjacency, cotangent, w_second, *refs):
-    piece, near, across, count, own_by, own_at, feat, adj, cot, second, turned, back, sems = refs
-    own, slots, width = features.shape
-    rows = adjacency.shape[1]
-    each = width // GROUP
-    place = lax.axis_index("grp")
-    moves = [(features, feat), (adjacency, adj), (counts, count), (owner, own_by), (local, own_at)]
-    moves.append((cotangent, cot))
-    some = width // CHUNKS
-    for c in range(CHUNKS):
-        span = slice(c * some, (c + 1) * some)
-        moves.append((w_second.at[span], second.at[span]))
+def start_all(moves, sems):
     copies = [pltpu.make_async_copy(a, b, sems.at[i]) for i, (a, b) in enumerate(moves)]
     for copy in copies:
         copy.start()
-
+    return copies
+
+
+def pack_kernel(counts, owner, local, features, adjacency, piece, *scratch):
+    count, own_by, own_at, feat, adj, sems = scratch
+    own, slots, width = features.shape
+    rows = adjacency.shape[1]
     held = own * slots
+    copies = start_all(zip((features, adjacency, counts, owner, local), (feat, adj, count, own_by, own_at)), sems)
     slot = lax.broadcasted_iota(jnp.int32, (slots, LANES), 0)
     line = lax.broadcasted_iota(jnp.int32, (META, LANES), 0)
     pick = lax.broadcasted_iota(jnp.int32, (META, LANES), 1) // slots
     meta = jnp.zeros((META, LANES), jnp.int32)
-    for copy in copies[:5]:
+    for copy in copies:
         copy.wait()
     for i in range(own):
         live = slot < count[i]
@@ -67,19 +66,28 @@
     piece[at : at + rows, :] = adj[0]
     piece[at + rows : at + rows + META, :] = meta.astype(F32).astype(BF16)
 
-    copies[5].wait()
+
+def columns_kernel(cotangent, w_second, near, beside, across, *scratch):
+    cot, second, turned, back, sems = scratch
+    width = w_second.shape[0]
+    each = width // GROUP
+    place = lax.axis_index("grp")
+    spans = [slice(c * width // CHUNKS, (c + 1) * width // CHUNKS) for c in range(CHUNKS)]
+    moves = [(cotangent, cot)] + [(w_second.at[span], second.at[span]) for span in spans]
+    copies = start_all(moves, sems)
+    copies[0].wait()
     turned[...] = cot[0].astype(F32).T.astype(BF16)
-    for c in range(CHUNKS):
-        copies[6 + c].wait()
-        span = slice(c * some, (c + 1) * some)
+    for span, copy in zip(spans, copies[1:]):
+        copy.wait()
         back[span, :] = nt(second[span, :], cot[0]).astype(BF16)
-    for h, out in enumerate((near, across)):
-        for i in range(out.shape[0] // (2 * each)):
-            to = 4 * (i // 2) + 2 * h + i % 2
-            span = pl.ds(pl.multiple_of((place ^ to) * each, each), each)
-            at = i * 2 * each
-            out[at : at + each, :] = turned[span, :]
-            out[at + each : at + 2 * each, :] = back[span, :]
+    for out, slots in ((near, (0,)), (beside, (CORE,)), (across, (Y, Y | CORE))):
+        at = 0
+        for first in slots:
+            for slot in range(first, GROUP, 4):
+                span = pl.ds(pl.multiple_of((place ^ slot) * each, each), each)
+                out[at : at + each, :] = turned[span, :]
+                out[at + each : at + 2 * each, :] = back[span, :]
+                at += 2 * each
 
 
 def stack(out, at, *blocks):
@@ -89,37 +97,35 @@
     return at
 
 
-def split_kernel(piece, came, near, across, beside, half_b, *sent):
-    cut = beside.shape[0] - sent[0].shape[0]
-    stack(half_b, 0, piece.at[cut // 2 :], came.at[cut // 2 :])
-    at = stack(beside, 0, piece.at[: cut // 2], came.at[: cut // 2])
-    size = sent[0].shape[0] // 2
-    for slot, (out, at) in {Z1: (beside, at), **{slot: (out, 0) for slot, out in zip(FAR, sent)}}.items():
-        span = slice(slot // 4 * size, (slot // 4 + 1) * size)
-        stack(out, at, near.at[span], across.at[span])
-
-
-def join_kernel(beside, came, half_b, came_b, out_a, out_b, both):
-    cut = out_a.shape[0] // 2
-    stack(out_a, 0, beside.at[:cut], came.at[:cut])
+def split_kernel(piece, came, half_a, half_b):
+    cut = half_a.shape[0] // 2
+    stack(half_a, 0, piece.at[:cut], came.at[:cut])
+    stack(half_b, 0, piece.at[cut:], came.at[cut:])
+
+
+def join_kernel(half_a, came_a, half_b, came_b, out_a, out_b, both):
+    stack(out_a, 0, half_a, came_a)
     stack(out_b, 0, half_b, came_b)
     stack(both, 0, out_a, out_b)
 
 
-def columns_kernel(came, *refs):
-    *sent, out = refs
-    size = sent[0].shape[0]
-    blocks = dict(zip(FAR, sent))
-    blocks[Z1] = came.at[came.shape[0] - size :]
-    rows = size // 4
-    at = 0
-    for slot in range(0, GROUP, 4):
-        for h in range(2):
-            at = stack(out, at, blocks[slot].at[(2 * h + 1) * rows : (2 * h + 2) * rows])
-
-
-def pair_kernel(far_a, far_b, columns, out):
-    stack(out, 0, far_a, far_b, columns)
+def pair_kernel(far_a, far_b, out):
+    stack(out, 0, far_a, far_b)
+
+
+def half_kernel(across, out):
+    stack(out, 0, across.at[across.shape[0] // 2 :])
+
+
+def gather_kernel(*refs):
+    stack(refs[-1], 0, *refs[:-1])
+
+
+def along_kernel(near, beside, across, other, *sent):
+    size = sent[0].shape[0] // 4
+    for slot, out in zip(FAR, sent):
+        span = slice(slot // 4 * size, (slot // 4 + 1) * size)
+        stack(out, 0, *[ref.at[span] for ref in (near, beside, across, other)])
 
 
 def place_of(slot):
@@ -178,11 +184,10 @@
     w_piece[...] = part.astype(BF16)
 
 
-def step_kernel(own, slots, cut, rest, core, pair, came, *refs):
-    sent, refs = dict(zip(FAR, refs)), refs[len(FAR) :]
+def forward_kernel(own, slots, cut, rest, core, pair, *refs):
     early_feat, early_lifted, early_spread, early_adj, early_meta, w_piece = refs[:6]
-    w_first, w_second, output, grad_first, grad_second = refs[6:11]
-    hidden, spread, feat, adj, meta, dout, dpre, lifted = refs[11:]
+    w_first, w_second, output, hidden, spread, feat, adj, keep, pre_piece = refs[6:15]
+    meta, lifted = refs[15:]
     width = w_first.shape[0]
     held = own * slots
     rows = adj.shape[1]
@@ -198,7 +203,6 @@
     for size, start, halves in ((cut, 0, HALF_A), (rest, 4 * cut, HALF_B)):
         for ref, group in zip((core, pair), halves):
             arrays.append((ref, start, [slot | CORE for slot in group]))
-    deep = 4 * (cut + rest)
     lay_out(arrays, held, cut, feat, adj, meta)
     metas = [meta[p].astype(F32) for p in range(GROUP)]
     picks = jnp.concatenate([m[0:1] for m in metas], axis=0).astype(jnp.int32)
@@ -209,6 +213,7 @@
             held_by = metas[place_of(slot)][1 + i : 2 + i].astype(jnp.int32)
             count = jnp.where(picks == (place ^ slot) * own + i, held_by, count)
     masks = (lane < count).astype(F32)
+    keep[...] = masks
 
     late = slice(first * held, GROUP * held)
     lifted[late, :] = nn(feat[late, :], w_first[...]).astype(BF16)
@@ -220,24 +225,26 @@
     for c in range(0, width, step):
         half = 0.5 * nn(spread[...], lifted[:, c : c + step])
         hidden[:, c : c + step] = (half + half * jnp.tanh(half)).astype(BF16)
-    pre_piece = nt(lifted_piece, spread[...])
+    pre_piece[...] = nt(lifted_piece, spread[...])
     live = jnp.broadcast_to(masks[0:1], (rows, LANES)).T[:, :1]
     agg = nn(adj[0], (hidden[:rows, :].astype(F32) * live).astype(BF16)).astype(BF16)
     output[0] = (nn(agg, w_second[...]) * live).astype(BF16)
 
+
+def gradient_kernel(hidden, spread, feat, adj, masks, pre_piece, *refs):
+    far, *last = refs[: 1 + len(LAST)]
+    grad_first, grad_second, dout, dpre = refs[1 + len(LAST) :]
     each = grad_first.shape[0]
-    size = sent[0].shape[0]
-    sent[Z1] = came.at[came.shape[0] - size :]
+    size = 8 * each
+    sent = {FAR[i]: far.at[k * size : (k + 1) * size] for k, i in enumerate(FIRST)}
+    sent.update({FAR[i]: ref for i, ref in zip(LAST, last)})
+    rows = adj.shape[1]
     for slot in range(GROUP):
         p = place_of(slot)
-        mask = masks[p : p + 1]
+        mask = masks[p : p + 1, :]
         span = slice(p * rows, (p + 1) * rows)
-        s, h = slot // 4, slot // 2 % 2
-        if slot % 2:
-            at = deep + (2 * s + h) * 2 * each
-            source = pair[at : at + 2 * each, :]
-        else:
-            source = sent[4 * s][h * size // 2 : h * size // 2 + 2 * each, :]
+        at = slot % 4 * 2 * each
+        source = sent[slot - slot % 4][at : at + 2 * each, :]
         back = nn((source.astype(F32) * mask).astype(BF16), adj[p]) * mask
         dout[:, span] = back[:each].astype(BF16)
         pre = pre_piece[:, span]
@@ -275,42 +282,47 @@
     def swap(x, slot):
         return lax.ppermute(x, "grp", [(i, i ^ slot) for i in range(GROUP)])
 
-    piece, near, across = call(
-        prepare_kernel,
-        (counts, pick_owner, pick_local, features, adjacency, cotangent, w_second),
-        [((cut + rest, LANES), BF16)] + [((GROUP * each, rows), BF16)] * 2,
+    (piece,) = call(
+        pack_kernel,
+        (counts, pick_owner, pick_local, features, adjacency),
+        [((cut + rest, LANES), BF16)],
         [pltpu.SMEM(x.shape, jnp.int32) for x in (counts, pick_owner, pick_local)]
-        + [pltpu.VMEM(x.shape, BF16) for x in (features, adjacency, cotangent, w_second)]
+        + [pltpu.VMEM(x.shape, BF16) for x in (features, adjacency)]
+        + [pltpu.SemaphoreType.DMA((5,))],
+        stay=True,
+    )
+    came = swap(piece, Z2)
+    cotangent, _ = lax.optimization_barrier((cotangent, piece))
+    near, beside, across = call(
+        columns_kernel,
+        (cotangent, w_second),
+        [((8 * each, rows), BF16)] * 2 + [((16 * each, rows), BF16)],
+        [pltpu.VMEM(x.shape, BF16) for x in (cotangent, w_second)]
         + [pltpu.VMEM((width, rows), BF16)] * 2
-        + [pltpu.SemaphoreType.DMA((6 + CHUNKS,))],
+        + [pltpu.SemaphoreType.DMA((1 + CHUNKS,))],
         stay=True,
-    )
-    came = swap(piece, Z2)
+        flops=HINT[0],
+    )
+    came, across = lax.optimization_barrier((came, across))
     across = swap(across, Y)
-    beside, b, *sent = call(
-        split_kernel,
-        (piece, came, near, across),
-        [((2 * cut + 8 * each, LANES), BF16), ((2 * rest, LANES), BF16)]
-        + [((8 * each, rows), BF16)] * len(FAR),
-    )
-    came, came_b = swap(beside, Z1), swap(b, Y)
+    (other,) = call(half_kernel, (across,), [((8 * each, rows), BF16)], flops=HINT[1])
+    beside, other = swap(beside, CORE), swap(other, CORE)
+    sent = call(along_kernel, (near, beside, across, other), [((8 * each, rows), BF16)] * len(FAR), flops=HINT[2])
     sent = [swap(x, slot) if slot else x for x, slot in zip(sent, FAR)]
+
+    a, b = call(split_kernel, (piece, came), [((2 * size, LANES), BF16) for size in (cut, rest)], flops=HINT[3])
+    came_a, came_b = swap(a, Z1), swap(b, Y)
     a, b, both = call(
         join_kernel,
-        (beside, came, b, came_b),
+        (a, came_a, b, came_b),
         [((4 * size, LANES), BF16) for size in (cut, rest, cut + rest)],
+        flops=HINT[4],
     )
     far_a, far_b, core = swap(a, Y), swap(b, Z1), swap(both, CORE)
-    (columns,) = call(
-        columns_kernel, (came, *sent), [((half * 2 * each, rows), BF16)], flops=8 * 10**9
-    )
     far_a, far_b, core = lax.optimization_barrier((far_a, far_b, core))
-    (pair,) = call(
-        pair_kernel,
-        (far_a, far_b, columns),
-        [((4 * (cut + rest) + half * 2 * each, LANES), BF16)],
-    )
+    (pair,) = call(pair_kernel, (far_a, far_b), [((4 * (cut + rest), LANES), BF16)])
     pair = swap(pair, CORE)
+    (far,) = call(gather_kernel, [sent[i] for i in FIRST], [((8 * each * len(FIRST), rows), BF16)], flops=HINT[5])
     early = call(
         functools.partial(early_kernel, own, slots, cut),
         (a, far_a, b, far_b, w_first),
@@ -324,22 +336,31 @@
         ],
         limit=LIMIT,
     )
-    return call(
-        functools.partial(step_kernel, own, slots, cut, rest),
-        (core, pair, came, *sent, *early, w_first, w_second),
-        [((1, rows, width), BF16), ((each, width), F32), ((each, width), F32)],
+    pair, far = lax.optimization_barrier((pair, far))
+    output, *kept = call(
+        functools.partial(forward_kernel, own, slots, cut, rest),
+        (core, pair, *early, w_first, w_second),
         [
-            pltpu.VMEM((GROUP * rows, width), BF16),
-            pltpu.VMEM((GROUP * rows, total), BF16),
-            pltpu.VMEM((total, width), BF16),
-            pltpu.VMEM((GROUP, rows, rows), BF16),
-            pltpu.VMEM((GROUP, META, LANES), BF16),
-            pltpu.VMEM((each, GROUP * rows), BF16),
-            pltpu.VMEM((each, GROUP * rows), BF16),
-            pltpu.VMEM((total, width), BF16),
+            ((1, rows, width), BF16),
+            ((GROUP * rows, width), BF16),
+            ((GROUP * rows, total), BF16),
+            ((total, width), BF16),
+            ((GROUP, rows, rows), BF16),
+            ((GROUP, LANES), F32),
+            ((each, GROUP * rows), F32),
         ],
+        [pltpu.VMEM((GROUP, META, LANES), BF16), pltpu.VMEM((total, width), BF16)],
         LIMIT,
-    )
+        flops=HINT[6],
+    )
+    grad_first, grad_second = call(
+        gradient_kernel,
+        (*kept, far, *[sent[i] for i in LAST]),
+        [((each, width), F32)] * 2,
+        [pltpu.VMEM((each, GROUP * rows), BF16)] * 2,
+        LIMIT,
+    )
+    return output, grad_first, grad_second
 
 
 def split_body(features, counts, pick_owner, pick_local, adjacency, cotangent, w_first, w_second):

time: 42.5 us -> 48.1 us (1.13)
  starting transfers between devices: 13.2 us -> 18 us
  waiting for transfers between devices: 16.3 us -> 14.2 us
  Pallas kernels: 11.6 us -> 13.4 us
  local copies, waits for them, and re-layouts: 0.01 us -> 1.56 us
    ppermute x10 -> x13, starting transfers between devices: 13.2 us -> 18 us  [swap(): return lax.ppermute(x, 'grp', [(i, i ^ slot) for i in range(GROUP)])]
    ppermute x10 -> x13, waiting for transfers between devices: 16.3 us -> 14.2 us  [swap(): return lax.ppermute(x, 'grp', [(i, i ^ slot) for i in range(GROUP)])]
    pallas_call x7 -> x11, Pallas kernels: 11.6 us -> 13.4 us  [call(): pl.pallas_call(kernel, out_shape=tuple((jax.ShapeDtypeStruct(*out) for ou...]
    unnamed x4, local copies, waits for them, and re-layouts: 0.01 us -> 1.56 us
  transfers between devices with their start and end apart: 10 -> 13, of which waited for: 7 -> 6; matrix products, arithmetic and copies ran while one was open for 0% -> 0% of each run, Pallas kernels for 3% -> 21%
where the time goes in v8:
time: 48.1 us; the launch traced here: 47.8 us
  starting transfers between devices  18 us (37%)
  waiting for transfers between devices  14.2 us (30%)
  Pallas kernels  13.4 us (28%)
  local copies, waits for them, and re-layouts  1.56 us (3%)
  between operations  0.74 us (2%)
    ppermute x13, starting transfers between devices, swap(): return lax.ppermute(x, 'grp', [(i, i ^ slot) for i in range(GROUP)])  18 us
    ppermute x13, waiting for transfers between devices, swap(): return lax.ppermute(x, 'grp', [(i, i ^ slot) for i in range(GROUP)])  14.2 us
    pallas_call x11, Pallas kernels, call(): pl.pallas_call(kernel, out_shape=tuple((jax.ShapeDtypeStruct(*out) for ou...  13.4 us
    unnamed x4, local copies, waits for them, and re-layouts  1.56 us
  transfers between devices with their start and end apart: 13, of which 6 were waited for; matrix products, arithmetic and copies ran while one was open for 0% of the time, Pallas kernels for 21%

profile of v8, /device:TPU:0, one launch (start us, length us, event | category | flops | bytes accessed | tf_op | source)
XLA Modules:
  0.0 47.8 jit_solution(14368885099949517429)
XLA Ops:
  0.6 0.9 %shard_map.103.piece = bf16[400,128]{1,0:T(8,128)(2,1)S(1)} custom-call(s32[2]{0:T(128)} %counts.1, s32[1,8]{1,0:T(1,128)} %owner.1, s32[1,8]{1,0:T(1,128)} %local.1, bf16[2,16,1024]{2,1,0:T(8,128)(2,1)} %features.1, bf16[1,128,128]{2,1,0:T(8,128)(2,1)} %adjacency.1), custom_call_target="tpu_custom_call" | custom-call | tf_op jit(solution)/shard_map/pallas_call | solution.py:261
  1.6 4.1 %collective-permute-start = (bf16[400,128]{1,0:T(8,128)(2,1)S(1)}, bf16[400,128]{1,0:T(8,128)(2,1)S(1)}, u32[]{:S(2)}, u32[]{:S(2)}) collective-permute-start(bf16[400,128]{1,0:T(8,128)(2,1)S(1)} %shard_map.103.piece), channel_id=1, source_target_pairs={{0,8},{1,9},{2,10},{3,11},{4,12},{5,13},{6,14},{7,15},{8,0},{9,1},... | collective-permute-start | bytes 307208 | tf_op jit(solution)/shard_map/ppermute | solution.py:283
  5.7 2.9 %shard_map.104 = (bf16[512,128]{1,0:T(8,128)(2,1)S(1)}, bf16[512,128]{1,0:T(8,128)(2,1)S(1)}, bf16[1024,128]{1,0:T(8,128)(2,1)S(1)}) custom-call(bf16[1,128,1024]{2,1,0:T(8,128)(2,1)} %cotangent, bf16[1024,1024]{1,0:T(8,128)(2,1)} %refs_7_.1), custom_call_target="tpu_custom_call" | custom-call | tf_op jit(solution)/shard_map/pallas_call | solution.py:261
  8.6 2.2 %collective-permute-done.came = bf16[400,128]{1,0:T(8,128)(2,1)S(1)} collective-permute-done((bf16[400,128]{1,0:T(8,128)(2,1)S(1)}, bf16[400,128]{1,0:T(8,128)(2,1)S(1)}, u32[]{:S(2)}, u32[]{:S(2)}) %collective-permute-start) | collective-permute-done | bytes 102432 | tf_op jit(solution)/shard_map/ppermute | solution.py:283
  10.8 1.6 %collective-permute-start.8 = (bf16[1024,128]{1,0:T(8,128)(2,1)S(1)}, bf16[1024,128]{1,0:T(8,128)(2,1)S(1)}, u32[]{:S(2)}, u32[]{:S(2)}) collective-permute-start(bf16[1024,128]{1,0:T(8,128)(2,1)S(1)} %get-tuple-element.51), channel_id=1, source_target_pairs={{0,2},{1,3},{2,0},{3,1},{4,6},{5,7},{6,4},{7,5},{8,10},{9,11},{10,... | collective-permute-start | bytes 786440 | tf_op jit(solution)/shard_map/ppermute | solution.py:283
  12.3 0.5 %collective-permute-start.2 = (bf16[416,128]{1,0:T(8,128)(2,1)S(1)}, bf16[416,128]{1,0:T(8,128)(2,1)S(1)}, u32[]{:S(2)}, u32[]{:S(2)}) collective-permute-start(bf16[416,128]{1,0:T(8,128)(2,1)S(1)} %get-tuple-element.42.half_b), channel_id=1, source_target_pairs={{0,2},{1,3},{2,0},{3,1},{4,6},{5,7},{6,4},{7,5},{8,10},{9,11},{10,... | collective-permute-start | bytes 319496 | tf_op jit(solution)/shard_map/ppermute | solution.py:283
  12.9 0.7 %collective-permute-start.1 = (bf16[384,128]{1,0:T(8,128)(2,1)S(1)}, bf16[384,128]{1,0:T(8,128)(2,1)S(1)}, u32[]{:S(2)}, u32[]{:S(2)}) collective-permute-start(bf16[384,128]{1,0:T(8,128)(2,1)S(1)} %get-tuple-element.41.half_a), channel_id=1, source_target_pairs={{0,4},{1,5},{2,6},{3,7},{4,0},{5,1},{6,2},{7,3},{8,12},{9,13},{10,... | collective-permute-start | bytes 294920 | tf_op jit(solution)/shard_map/ppermute | solution.py:283
  13.6 0.0 collective-permute-start.7
  13.6 3.9 %collective-permute-done.1.came_a = bf16[384,128]{1,0:T(8,128)(2,1)S(1)} collective-permute-done((bf16[384,128]{1,0:T(8,128)(2,1)S(1)}, bf16[384,128]{1,0:T(8,128)(2,1)S(1)}, u32[]{:S(2)}, u32[]{:S(2)}) %collective-permute-start.1) | collective-permute-done | bytes 98336 | tf_op jit(solution)/shard_map/ppermute | solution.py:283
  17.5 3.0 %collective-permute-done.2.came_b = bf16[416,128]{1,0:T(8,128)(2,1)S(1)} collective-permute-done((bf16[416,128]{1,0:T(8,128)(2,1)S(1)}, bf16[416,128]{1,0:T(8,128)(2,1)S(1)}, u32[]{:S(2)}, u32[]{:S(2)}) %collective-permute-start.2) | collective-permute-done | bytes 106528 | tf_op jit(solution)/shard_map/ppermute | solution.py:283
  20.5 0.1 shard_map.106
  20.6 0.1 collective-permute-start.5
  20.7 0.0 collective-permute-done.8.across
  20.7 0.0 copy-start
  20.7 0.5 %collective-permute-start.9 = (bf16[512,128]{1,0:T(8,128)(2,1)S(1)}, bf16[512,128]{1,0:T(8,128)(2,1)S(1)}, u32[]{:S(2)}, u32[]{:S(2)}) collective-permute-start(bf16[512,128]{1,0:T(8,128)(2,1)S(1)} %shard_map.108), channel_id=1, source_target_pairs={{0,1},{1,0},{2,3},{3,2},{4,5},{5,4},{6,7},{7,6},{8,9},{9,8},{10,11... | collective-permute-start | bytes 393224 | tf_op jit(solution)/shard_map/ppermute | solution.py:283
  21.3 1.5 %collective-permute-start.4 = (bf16[832,128]{1,0:T(8,128)(2,1)S(1)}, bf16[832,128]{1,0:T(8,128)(2,1)S(1)}, u32[]{:S(2)}, u32[]{:S(2)}) collective-permute-start(bf16[832,128]{1,0:T(8,128)(2,1)S(1)} %get-tuple-element.44.b), channel_id=1, source_target_pairs={{0,4},{1,5},{2,6},{3,7},{4,0},{5,1},{6,2},{7,3},{8,12},{9,13},{10,... | collective-permute-start | bytes 638984 | tf_op jit(solution)/shard_map/ppermute | solution.py:283
  22.7 1.5 %collective-permute-start.3 = (bf16[768,128]{1,0:T(8,128)(2,1)S(1)}, bf16[768,128]{1,0:T(8,128)(2,1)S(1)}, u32[]{:S(2)}, u32[]{:S(2)}) collective-permute-start(bf16[768,128]{1,0:T(8,128)(2,1)S(1)} %get-tuple-element.43.a), channel_id=1, source_target_pairs={{0,2},{1,3},{2,0},{3,1},{4,6},{5,7},{6,4},{7,5},{8,10},{9,11},{10,... | collective-permute-start | bytes 589832 | tf_op jit(solution)/shard_map/ppermute | solution.py:283
  24.2 0.0 collective-permute-done.7.beside
  24.2 0.0 collective-permute-done.9.other
  24.3 2.9 %collective-permute-start.10 = (bf16[512,128]{1,0:T(8,128)(2,1)S(1)}, bf16[512,128]{1,0:T(8,128)(2,1)S(1)}, u32[]{:S(2)}, u32[]{:S(2)}) collective-permute-start(bf16[512,128]{1,0:T(8,128)(2,1)S(1)} %get-tuple-element.52), channel_id=1, source_target_pairs={{0,12},{1,13},{2,14},{3,15},{4,8},{5,9},{6,10},{7,11},{8,4},{9,5},... | collective-permute-start | bytes 393224 | tf_op jit(solution)/shard_map/ppermute | solution.py:283
  27.2 1.1 %collective-permute-start.11 = (bf16[512,128]{1,0:T(8,128)(2,1)S(1)}, bf16[512,128]{1,0:T(8,128)(2,1)S(1)}, u32[]{:S(2)}, u32[]{:S(2)}) collective-permute-start(bf16[512,128]{1,0:T(8,128)(2,1)S(1)} %get-tuple-element.53), channel_id=1, source_target_pairs={{0,4},{1,5},{2,6},{3,7},{4,0},{5,1},{6,2},{7,3},{8,12},{9,13},{10,... | collective-permute-start | bytes 393224 | tf_op jit(solution)/shard_map/ppermute | solution.py:283
  28.3 1.0 %collective-permute-done.3.far_a = bf16[768,128]{1,0:T(8,128)(2,1)S(1)} collective-permute-done((bf16[768,128]{1,0:T(8,128)(2,1)S(1)}, bf16[768,128]{1,0:T(8,128)(2,1)S(1)}, u32[]{:S(2)}, u32[]{:S(2)}) %collective-permute-start.3) | collective-permute-done | bytes 196640 | tf_op jit(solution)/shard_map/ppermute | solution.py:283
  29.3 3.4 %collective-permute-start.12 = (bf16[512,128]{1,0:T(8,128)(2,1)S(1)}, bf16[512,128]{1,0:T(8,128)(2,1)S(1)}, u32[]{:S(2)}, u32[]{:S(2)}) collective-permute-start(bf16[512,128]{1,0:T(8,128)(2,1)S(1)} %get-tuple-element.70), channel_id=1, source_target_pairs={{0,8},{1,9},{2,10},{3,11},{4,12},{5,13},{6,14},{7,15},{8,0},{9,1},... | collective-permute-start | bytes 393224 | tf_op jit(solution)/shard_map/ppermute | solution.py:283
  32.7 0.0 collective-permute-done.4.far_b
  32.7 0.0 collective-permute-done.5.core
  32.7 0.1 collective-permute-start.6
  32.8 0.0 copy-done
  32.8 1.0 %shard_map.111 = (bf16[256,1024]{1,0:T(8,128)(2,1)S(1)}, bf16[256,1024]{1,0:T(8,128)(2,1)S(1)}, bf16[1024,512]{1,0:T(8,128)(2,1)S(1)}, bf16[8,128,128]{2,1,0:T(8...) custom-call(bf16[768,128]{1,0:T(8,128)(2,1)S(1)} %get-tuple-element.43.a, ...), custom_call_target="tpu_custom_call" | custom-call | tf_op jit(solution)/shard_map/pallas_call | solution.py:261
  33.9 0.6 %collective-permute-done.10.refs_0_ = bf16[512,128]{1,0:T(8,128)(2,1)S(1)} collective-permute-done((bf16[512,128]{1,0:T(8,128)(2,1)S(1)}, bf16[512,128]{1,0:T(8,128)(2,1)S(1)}, u32[]{:S(2)}, u32[]{:S(2)}) %collective-permute-start.10) | collective-permute-done | bytes 131104 | tf_op jit(solution)/shard_map/ppermute | solution.py:283
  34.4 3.4 %collective-permute-done.11.refs_1_ = bf16[512,128]{1,0:T(8,128)(2,1)S(1)} collective-permute-done((bf16[512,128]{1,0:T(8,128)(2,1)S(1)}, bf16[512,128]{1,0:T(8,128)(2,1)S(1)}, u32[]{:S(2)}, u32[]{:S(2)}) %collective-permute-start.11) | collective-permute-done | bytes 131104 | tf_op jit(solution)/shard_map/ppermute | solution.py:283
  37.8 0.0 copy-start.1
  37.9 0.0 collective-permute-done.6.pair
  37.9 1.5 %copy-done.1 = bf16[1024,1024]{1,0:T(8,128)(2,1)S(1)} copy-done((bf16[1024,1024]{1,0:T(8,128)(2,1)S(1)}, bf16[1024,1024]{1,0:T(8,128)(2,1)}, u32[]{:S(2)}) %copy-start.1) | copy-done | bytes 2097176
  39.4 5.9 %shard_map.112 = (bf16[1,128,1024]{2,1,0:T(8,128)(2,1)}, bf16[2048,1024]{1,0:T(8,128)(2,1)S(1)}, bf16[2048,512]{1,0:T(8,128)(2,1)S(1)}, bf16[512,1024]{1,0:T(8,1...) custom-call(bf16[1600,128]{1,0:T(8,128)(2,1)S(1)} %collective-permute-done.5.core, ...), custom_call_target="tpu_custom_call" | custom-call | tf_op jit(solution)/shard_map/pallas_call | solution.py:261
  45.3 0.0 collective-permute-done.12.refs_1_
  45.3 2.5 %shard_map.113 = (f32[64,1024]{1,0:T(8,128)}, f32[64,1024]{1,0:T(8,128)}) custom-call(bf16[2048,1024]{1,0:T(8,128)(2,1)S(1)} %get-tuple-element.63.hidden, bf16[2048,512]{1,0:T(8,128)(2,1)S(1)} %get-tuple-element.64.spread, bf16[512,1024]{1,0:T(8,128)(2,1)S(1)} %get-tuple-element.65.feat, bf16[16,128,128]{2,1,0:T(8,128)(2,1)S(1)} %get-tuple-element.66.adj, ...), custom_call_target="tpu_custom_call" | custom-call | tf_op jit(solution)/shard_map/pallas_call | solution.py:261
  (5 shorter events, 0.1 us)
Async XLA Ops:
  1.6 9.2 %collective-permute-start = (bf16[400,128]{1,0:T(8,128)(2,1)S(1)}, bf16[400,128]{1,0:T(8,128)(2,1)S(1)}, u32[]{:S(2)}, u32[]{:S(2)}) collective-permute-start(bf16[400,128]{1,0:T(8,128)(2,1)S(1)} %shard_map.103.piece), channel_id=1, source_target_pairs={{0,8},{1,9},{2,10},{3,11},{4,12},{5,13},{6,14},{7,15},{8,0},{9,1},... | collective-permute-start | bytes 307208 | tf_op jit(solution)/shard_map/ppermute | solution.py:283
  10.8 9.9 %collective-permute-start.8 = (bf16[1024,128]{1,0:T(8,128)(2,1)S(1)}, bf16[1024,128]{1,0:T(8,128)(2,1)S(1)}, u32[]{:S(2)}, u32[]{:S(2)}) collective-permute-start(bf16[1024,128]{1,0:T(8,128)(2,1)S(1)} %get-tuple-element.51), channel_id=1, source_target_pairs={{0,2},{1,3},{2,0},{3,1},{4,6},{5,7},{6,4},{7,5},{8,10},{9,11},{10,... | collective-permute-start | bytes 786440 | tf_op jit(solution)/shard_map/ppermute | solution.py:283
  12.3 8.2 %collective-permute-start.2 = (bf16[416,128]{1,0:T(8,128)(2,1)S(1)}, bf16[416,128]{1,0:T(8,128)(2,1)S(1)}, u32[]{:S(2)}, u32[]{:S(2)}) collective-permute-start(bf16[416,128]{1,0:T(8,128)(2,1)S(1)} %get-tuple-element.42.half_b), channel_id=1, source_target_pairs={{0,2},{1,3},{2,0},{3,1},{4,6},{5,7},{6,4},{7,5},{8,10},{9,11},{10,... | collective-permute-start | bytes 319496 | tf_op jit(solution)/shard_map/ppermute | solution.py:283
  12.9 4.6 %collective-permute-start.1 = (bf16[384,128]{1,0:T(8,128)(2,1)S(1)}, bf16[384,128]{1,0:T(8,128)(2,1)S(1)}, u32[]{:S(2)}, u32[]{:S(2)}) collective-permute-start(bf16[384,128]{1,0:T(8,128)(2,1)S(1)} %get-tuple-element.41.half_a), channel_id=1, source_target_pairs={{0,4},{1,5},{2,6},{3,7},{4,0},{5,1},{6,2},{7,3},{8,12},{9,13},{10,... | collective-permute-start | bytes 294920 | tf_op jit(solution)/shard_map/ppermute | solution.py:283
  13.6 10.6 %collective-permute-start.7 = (bf16[512,128]{1,0:T(8,128)(2,1)S(1)}, bf16[512,128]{1,0:T(8,128)(2,1)S(1)}, u32[]{:S(2)}, u32[]{:S(2)}) collective-permute-start(bf16[512,128]{1,0:T(8,128)(2,1)S(1)} %get-tuple-element.50), channel_id=1, source_target_pairs={{0,1},{1,0},{2,3},{3,2},{4,5},{5,4},{6,7},{7,6},{8,9},{9,8},{10,11... | collective-permute-start | bytes 393224 | tf_op jit(solution)/shard_map/ppermute | solution.py:283
  20.6 12.1 %collective-permute-start.5 = (bf16[1600,128]{1,0:T(8,128)(2,1)S(1)}, bf16[1600,128]{1,0:T(8,128)(2,1)S(1)}, u32[]{:S(2)}, u32[]{:S(2)}) collective-permute-start(bf16[1600,128]{1,0:T(8,128)(2,1)S(1)} %get-tuple-element.45), channel_id=1, source_target_pairs={{0,1},{1,0},{2,3},{3,2},{4,5},{5,4},{6,7},{7,6},{8,9},{9,8},{10,11... | collective-permute-start | bytes 1228808 | tf_op jit(solution)/shard_map/ppermute | solution.py:283
  20.7 12.1 %copy-start = (bf16[1024,1024]{1,0:T(8,128)(2,1)S(1)}, bf16[1024,1024]{1,0:T(8,128)(2,1)}, u32[]{:S(2)}) copy-start(bf16[1024,1024]{1,0:T(8,128)(2,1)} %refs_6_.1) | copy-start | bytes 6291460
  20.7 3.5 %collective-permute-start.9 = (bf16[512,128]{1,0:T(8,128)(2,1)S(1)}, bf16[512,128]{1,0:T(8,128)(2,1)S(1)}, u32[]{:S(2)}, u32[]{:S(2)}) collective-permute-start(bf16[512,128]{1,0:T(8,128)(2,1)S(1)} %shard_map.108), channel_id=1, source_target_pairs={{0,1},{1,0},{2,3},{3,2},{4,5},{5,4},{6,7},{7,6},{8,9},{9,8},{10,11... | collective-permute-start | bytes 393224 | tf_op jit(solution)/shard_map/ppermute | solution.py:283
  21.3 11.4 %collective-permute-start.4 = (bf16[832,128]{1,0:T(8,128)(2,1)S(1)}, bf16[832,128]{1,0:T(8,128)(2,1)S(1)}, u32[]{:S(2)}, u32[]{:S(2)}) collective-permute-start(bf16[832,128]{1,0:T(8,128)(2,1)S(1)} %get-tuple-element.44.b), channel_id=1, source_target_pairs={{0,4},{1,5},{2,6},{3,7},{4,0},{5,1},{6,2},{7,3},{8,12},{9,13},{10,... | collective-permute-start | bytes 638984 | tf_op jit(solution)/shard_map/ppermute | solution.py:283
  22.7 6.6 %collective-permute-start.3 = (bf16[768,128]{1,0:T(8,128)(2,1)S(1)}, bf16[768,128]{1,0:T(8,128)(2,1)S(1)}, u32[]{:S(2)}, u32[]{:S(2)}) collective-permute-start(bf16[768,128]{1,0:T(8,128)(2,1)S(1)} %get-tuple-element.43.a), channel_id=1, source_target_pairs={{0,2},{1,3},{2,0},{3,1},{4,6},{5,7},{6,4},{7,5},{8,10},{9,11},{10,... | collective-permute-start | bytes 589832 | tf_op jit(solution)/shard_map/ppermute | solution.py:283
  24.3 10.2 %collective-permute-start.10 = (bf16[512,128]{1,0:T(8,128)(2,1)S(1)}, bf16[512,128]{1,0:T(8,128)(2,1)S(1)}, u32[]{:S(2)}, u32[]{:S(2)}) collective-permute-start(bf16[512,128]{1,0:T(8,128)(2,1)S(1)} %get-tuple-element.52), channel_id=1, source_target_pairs={{0,12},{1,13},{2,14},{3,15},{4,8},{5,9},{6,10},{7,11},{8,4},{9,5},... | collective-permute-start | bytes 393224 | tf_op jit(solution)/shard_map/ppermute | solution.py:283
  27.2 10.7 %collective-permute-start.11 = (bf16[512,128]{1,0:T(8,128)(2,1)S(1)}, bf16[512,128]{1,0:T(8,128)(2,1)S(1)}, u32[]{:S(2)}, u32[]{:S(2)}) collective-permute-start(bf16[512,128]{1,0:T(8,128)(2,1)S(1)} %get-tuple-element.53), channel_id=1, source_target_pairs={{0,4},{1,5},{2,6},{3,7},{4,0},{5,1},{6,2},{7,3},{8,12},{9,13},{10,... | collective-permute-start | bytes 393224 | tf_op jit(solution)/shard_map/ppermute | solution.py:283
  29.3 16.0 %collective-permute-start.12 = (bf16[512,128]{1,0:T(8,128)(2,1)S(1)}, bf16[512,128]{1,0:T(8,128)(2,1)S(1)}, u32[]{:S(2)}, u32[]{:S(2)}) collective-permute-start(bf16[512,128]{1,0:T(8,128)(2,1)S(1)} %get-tuple-element.70), channel_id=1, source_target_pairs={{0,8},{1,9},{2,10},{3,11},{4,12},{5,13},{6,14},{7,15},{8,0},{9,1},... | collective-permute-start | bytes 393224 | tf_op jit(solution)/shard_map/ppermute | solution.py:283
  32.7 5.1 %collective-permute-start.6 = (bf16[1600,128]{1,0:T(8,128)(2,1)S(1)}, bf16[1600,128]{1,0:T(8,128)(2,1)S(1)}, u32[]{:S(2)}, u32[]{:S(2)}) collective-permute-start(bf16[1600,128]{1,0:T(8,128)(2,1)S(1)} %shard_map.107), channel_id=1, source_target_pairs={{0,1},{1,0},{2,3},{3,2},{4,5},{5,4},{6,7},{7,6},{8,9},{9,8},{10,11... | collective-permute-start | bytes 1228808 | tf_op jit(solution)/shard_map/ppermute | solution.py:283
  37.8 1.6 %copy-start.1 = (bf16[1024,1024]{1,0:T(8,128)(2,1)S(1)}, bf16[1024,1024]{1,0:T(8,128)(2,1)}, u32[]{:S(2)}) copy-start(bf16[1024,1024]{1,0:T(8,128)(2,1)} %refs_7_.1) | copy-start | bytes 6291460

commit v9 on v7

--- a/solution.py
+++ b/solution.py
@@ -13,12 +13,15 @@
 HBM = pl.BlockSpec(memory_space=pltpu.HBM)
 LANES = 128
 META = 16
-CHUNKS = 4
+CHUNKS = 8
 LIMIT = 24 * 2**20
 SMALL = 8 * 2**20
 Z2, Z1, Y, CORE = 8, 4, 2, 1
 GROUP = 16
-FAR = (Z2 | Z1, Z2, 0)
+FAR = (Z2 | Z1, Z2)
+NEAR = tuple(z | c for z in (0, *FAR) for c in (0, CORE))
+ACROSS = tuple(Y | slot for slot in NEAR)
+BESIDE = (Z1, Z1 | CORE, Z1 | Y, Z1 | Y | CORE)
 HALF_A = ((0, Z2, Z1, Z1 | Z2), (Y, Y | Z2, Y | Z1, Y | Z1 | Z2))
 HALF_B = ((0, Z2, Y, Y | Z2), (Z1, Z1 | Z2, Z1 | Y, Z1 | Y | Z2))
 
@@ -32,7 +35,7 @@
 
 
 def prepare_kernel(counts, owner, local, features, adjacency, cotangent, w_second, *refs):
-    piece, near, across, count, own_by, own_at, feat, adj, cot, second, turned, back, sems = refs
+    piece, near, across, beside, count, own_by, own_at, feat, adj, cot, second, turned, back, sems = refs
     own, slots, width = features.shape
     rows = adjacency.shape[1]
     each = width // GROUP
@@ -73,10 +76,9 @@
         copies[6 + c].wait()
         span = slice(c * some, (c + 1) * some)
         back[span, :] = nt(second[span, :], cot[0]).astype(BF16)
-    for h, out in enumerate((near, across)):
-        for i in range(out.shape[0] // (2 * each)):
-            to = 4 * (i // 2) + 2 * h + i % 2
-            span = pl.ds(pl.multiple_of((place ^ to) * each, each), each)
+    for out, slots in ((near, NEAR), (across, ACROSS), (beside, BESIDE)):
+        for i, slot in enumerate(slots):
+            span = pl.ds(pl.multiple_of((place ^ slot) * each, each), each)
             at = i * 2 * each
             out[at : at + each, :] = turned[span, :]
             out[at + each : at + 2 * each, :] = back[span, :]
@@ -89,33 +91,42 @@
     return at
 
 
-def split_kernel(piece, came, near, across, beside, half_b, *sent):
-    cut = beside.shape[0] - sent[0].shape[0]
-    stack(half_b, 0, piece.at[cut // 2 :], came.at[cut // 2 :])
-    at = stack(beside, 0, piece.at[: cut // 2], came.at[: cut // 2])
-    size = sent[0].shape[0] // 2
-    for slot, (out, at) in {Z1: (beside, at), **{slot: (out, 0) for slot, out in zip(FAR, sent)}}.items():
-        span = slice(slot // 4 * size, (slot // 4 + 1) * size)
-        stack(out, at, near.at[span], across.at[span])
-
-
-def join_kernel(beside, came, half_b, came_b, out_a, out_b, both):
-    cut = out_a.shape[0] // 2
-    stack(out_a, 0, beside.at[:cut], came.at[:cut])
-    stack(out_b, 0, half_b, came_b)
+def split_kernel(piece, came, near, across, beside, half_a, turn, keep, *sent):
+    cut = half_a.shape[0] // 2
+    stack(half_a, 0, piece.at[:cut], came.at[:cut])
+    two = beside.shape[0] // 2
+    stack(turn, 0, piece.at[cut:], came.at[cut:], beside.at[two:])
+    stack(keep, 0, near.at[:two], across.at[:two], beside.at[:two])
+    for i, out in enumerate(sent, 1):
+        span = slice(i * two, (i + 1) * two)
+        stack(out, 0, near.at[span], across.at[span])
+
+
+def join_kernel(half_a, came_a, turn, came_b, out_a, out_b, both):
+    size = out_b.shape[0] // 2
+    stack(out_a, 0, half_a, came_a)
+    stack(out_b, 0, turn.at[:size], came_b.at[:size])
     stack(both, 0, out_a, out_b)
 
 
-def columns_kernel(came, *refs):
-    *sent, out = refs
-    size = sent[0].shape[0]
-    blocks = dict(zip(FAR, sent))
-    blocks[Z1] = came.at[came.shape[0] - size :]
-    rows = size // 4
+def block_of(slot, rows, keep, came, *sent):
+    z, h, b = slot - slot % 4, slot // 2 % 2, slot % 2
+    if z in FAR:
+        ref, at = sent[FAR.index(z)], 2 * h + b
+    elif z == 0 or h == 0:
+        ref, at = keep, (4 if z else 2 * h) + b
+    else:
+        ref, at = came, came.shape[0] // rows - 2 + b
+    at = at * rows + ref.shape[0] % rows
+    return ref.at[at : at + rows]
+
+
+def columns_kernel(*refs):
+    *refs, out = refs
+    rows = out.shape[0] * 2 // GROUP
     at = 0
-    for slot in range(0, GROUP, 4):
-        for h in range(2):
-            at = stack(out, at, blocks[slot].at[(2 * h + 1) * rows : (2 * h + 2) * rows])
+    for slot in range(1, GROUP, 2):
+        at = stack(out, at, block_of(slot, rows, *refs))
 
 
 def pair_kernel(far_a, far_b, columns, out):
@@ -178,8 +189,8 @@
     w_piece[...] = part.astype(BF16)
 
 
-def step_kernel(own, slots, cut, rest, core, pair, came, *refs):
-    sent, refs = dict(zip(FAR, refs)), refs[len(FAR) :]
+def step_kernel(own, slots, cut, rest, core, pair, *refs):
+    blocks, refs = refs[: 2 + len(FAR)], refs[2 + len(FAR) :]
     early_feat, early_lifted, early_spread, early_adj, early_meta, w_piece = refs[:6]
     w_first, w_second, output, grad_first, grad_second = refs[6:11]
     hidden, spread, feat, adj, meta, dout, dpre, lifted = refs[11:]
@@ -226,18 +237,15 @@
     output[0] = (nn(agg, w_second[...]) * live).astype(BF16)
 
     each = grad_first.shape[0]
-    size = sent[0].shape[0]
-    sent[Z1] = came.at[came.shape[0] - size :]
     for slot in range(GROUP):
         p = place_of(slot)
         mask = masks[p : p + 1]
         span = slice(p * rows, (p + 1) * rows)
-        s, h = slot // 4, slot // 2 % 2
         if slot % 2:
-            at = deep + (2 * s + h) * 2 * each
+            at = deep + slot // 2 * 2 * each
             source = pair[at : at + 2 * each, :]
         else:
-            source = sent[4 * s][h * size // 2 : h * size // 2 + 2 * each, :]
+            source = block_of(slot, 2 * each, *blocks)[...]
         back = nn((source.astype(F32) * mask).astype(BF16), adj[p]) * mask
         dout[:, span] = back[:each].astype(BF16)
         pre = pre_piece[:, span]
@@ -275,34 +283,34 @@
     def swap(x, slot):
         return lax.ppermute(x, "grp", [(i, i ^ slot) for i in range(GROUP)])
 
-    piece, near, across = call(
+    piece, near, across, beside = call(
         prepare_kernel,
         (counts, pick_owner, pick_local, features, adjacency, cotangent, w_second),
-        [((cut + rest, LANES), BF16)] + [((GROUP * each, rows), BF16)] * 2,
+        [((cut + rest, LANES), BF16)]
+        + [((len(x) * 2 * each, rows), BF16) for x in (NEAR, ACROSS, BESIDE)],
         [pltpu.SMEM(x.shape, jnp.int32) for x in (counts, pick_owner, pick_local)]
         + [pltpu.VMEM(x.shape, BF16) for x in (features, adjacency, cotangent, w_second)]
         + [pltpu.VMEM((width, rows), BF16)] * 2
         + [pltpu.SemaphoreType.DMA((6 + CHUNKS,))],
         stay=True,
     )
-    came = swap(piece, Z2)
-    across = swap(across, Y)
-    beside, b, *sent = call(
+    came, across, beside = swap(piece, Z2), swap(across, Y), swap(beside, Z1)
+    a, turn, keep, *sent = call(
         split_kernel,
-        (piece, came, near, across),
-        [((2 * cut + 8 * each, LANES), BF16), ((2 * rest, LANES), BF16)]
+        (piece, came, near, across, beside),
+        [((x, LANES), BF16) for x in (2 * cut, 2 * rest + 4 * each, 12 * each)]
         + [((8 * each, rows), BF16)] * len(FAR),
     )
-    came, came_b = swap(beside, Z1), swap(b, Y)
-    sent = [swap(x, slot) if slot else x for x, slot in zip(sent, FAR)]
+    came_a, came_b = swap(a, Z1), swap(turn, Y)
+    sent = [swap(x, slot) for x, slot in zip(sent, FAR)]
     a, b, both = call(
         join_kernel,
-        (beside, came, b, came_b),
+        (a, came_a, turn, came_b),
         [((4 * size, LANES), BF16) for size in (cut, rest, cut + rest)],
     )
     far_a, far_b, core = swap(a, Y), swap(b, Z1), swap(both, CORE)
     (columns,) = call(
-        columns_kernel, (came, *sent), [((half * 2 * each, rows), BF16)], flops=8 * 10**9
+        columns_kernel, (keep, came_b, *sent), [((half * 2 * each, rows), BF16)], flops=8 * 10**9
     )
     far_a, far_b, core = lax.optimization_barrier((far_a, far_b, core))
     (pair,) = call(
@@ -326,7 +334,7 @@
     )
     return call(
         functools.partial(step_kernel, own, slots, cut, rest),
-        (core, pair, came, *sent, *early, w_first, w_second),
+        (core, pair, keep, came_b, *sent, *early, w_first, w_second),
         [((1, rows, width), BF16), ((each, width), F32), ((each, width), F32)],
         [
             pltpu.VMEM((GROUP * rows, width), BF16),

time: 42.5 us -> 44 us (1.035); the launches traced: 41.8 us -> 43.8 us
  starting transfers between devices: 13.2 us -> 16.4 us
  waiting for transfers between devices: 16.3 us -> 14.4 us
  Pallas kernels: 11.6 us -> 12.3 us
    ppermute x10 -> x11, starting transfers between devices: 13.2 us -> 16.4 us  [swap(): return lax.ppermute(x, 'grp', [(i, i ^ slot) for i in range(GROUP)])]
    ppermute x10 -> x11, waiting for transfers between devices: 16.3 us -> 14.4 us  [swap(): return lax.ppermute(x, 'grp', [(i, i ^ slot) for i in range(GROUP)])]
    pallas_call x7, Pallas kernels: 11.6 us -> 12.3 us  [call(): pl.pallas_call(kernel, out_shape=tuple((jax.ShapeDtypeStruct(*out) for ou...]
  transfers between devices with their start and end apart: 10 -> 11, of which waited for: 7 -> 5; matrix products, arithmetic and copies ran while one was open for 0% -> 0% of each run, Pallas kernels for 3% -> 3%
where the time goes in v9:
time: 44 us; the launch traced here: 43.8 us
  starting transfers between devices  16.4 us (37%)
  waiting for transfers between devices  14.4 us (33%)
  Pallas kernels  12.3 us (28%)
  between operations  0.71 us (2%)
    ppermute x11, starting transfers between devices, swap(): return lax.ppermute(x, 'grp', [(i, i ^ slot) for i in range(GROUP)])  16.4 us
    ppermute x11, waiting for transfers between devices, swap(): return lax.ppermute(x, 'grp', [(i, i ^ slot) for i in range(GROUP)])  14.4 us
    pallas_call x7, Pallas kernels, call(): pl.pallas_call(kernel, out_shape=tuple((jax.ShapeDtypeStruct(*out) for ou...  12.3 us
  transfers between devices with their start and end apart: 11, of which 5 were waited for; matrix products, arithmetic and copies ran while one was open for 0% of the time, Pallas kernels for 3%

profile of v9, /device:TPU:0, one launch (start us, length us, event | category | flops | bytes accessed | tf_op | source)
XLA Modules:
  0.0 43.8 jit_solution(8814377587604860315)
XLA Ops:
  0.6 3.6 %shard_map.103 = (bf16[400,128]{1,0:T(8,128)(2,1)S(1)}, bf16[768,128]{1,0:T(8,128)(2,1)S(1)}, bf16[768,128]{1,0:T(8,128)(2,1)S(1)}, bf16[512,128]{1,0:T(8,128)(2,1)S(1)}) custom-call(s32[2]{0:T(128)} %counts.1, s32[1,8]{1,0:T(1,128)} %owner.1, s32[1,8]{1,0:T(1,128)} %local.1, bf16[2,16,1024]{2,1,0:T(8,128)(2,1)} %features.1, bf16[1,128,128]{2,1,0:T(8,128)(2,1)} %adjacency.1, ...), custom_call_target="tpu_custom_call" | custom-call | tf_op jit(solution)/shard_map/pallas_call | solution.py:262
  4.2 3.0 %collective-permute-start.1 = (bf16[768,128]{1,0:T(8,128)(2,1)S(1)}, bf16[768,128]{1,0:T(8,128)(2,1)S(1)}, u32[]{:S(2)}, u32[]{:S(2)}) collective-permute-start(bf16[768,128]{1,0:T(8,128)(2,1)S(1)} %get-tuple-element.26), channel_id=1, source_target_pairs={{0,2},{1,3},{2,0},{3,1},{4,6},{5,7},{6,4},{7,5},{8,10},{9,11},{10,... | collective-permute-start | bytes 589832 | tf_op jit(solution)/shard_map/ppermute | solution.py:284
  7.2 1.6 %collective-permute-start.2 = (bf16[512,128]{1,0:T(8,128)(2,1)S(1)}, bf16[512,128]{1,0:T(8,128)(2,1)S(1)}, u32[]{:S(2)}, u32[]{:S(2)}) collective-permute-start(bf16[512,128]{1,0:T(8,128)(2,1)S(1)} %get-tuple-element.27), channel_id=1, source_target_pairs={{0,4},{1,5},{2,6},{3,7},{4,0},{5,1},{6,2},{7,3},{8,12},{9,13},{10,... | collective-permute-start | bytes 393224 | tf_op jit(solution)/shard_map/ppermute | solution.py:284
  8.8 2.6 %collective-permute-start = (bf16[400,128]{1,0:T(8,128)(2,1)S(1)}, bf16[400,128]{1,0:T(8,128)(2,1)S(1)}, u32[]{:S(2)}, u32[]{:S(2)}) collective-permute-start(bf16[400,128]{1,0:T(8,128)(2,1)S(1)} %get-tuple-element.24.piece), channel_id=1, source_target_pairs={{0,8},{1,9},{2,10},{3,11},{4,12},{5,13},{6,14},{7,15},{8,0},{9,1},... | collective-permute-start | bytes 307208 | tf_op jit(solution)/shard_map/ppermute | solution.py:284
  11.4 3.8 %collective-permute-done.came = bf16[400,128]{1,0:T(8,128)(2,1)S(1)} collective-permute-done((bf16[400,128]{1,0:T(8,128)(2,1)S(1)}, bf16[400,128]{1,0:T(8,128)(2,1)S(1)}, u32[]{:S(2)}, u32[]{:S(2)}) %collective-permute-start) | collective-permute-done | bytes 102432 | tf_op jit(solution)/shard_map/ppermute | solution.py:284
  15.2 0.0 collective-permute-done.2.beside
  15.2 0.0 collective-permute-done.1.across
  15.2 0.1 shard_map.104
  15.3 0.6 %collective-permute-start.4 = (bf16[672,128]{1,0:T(8,128)(2,1)S(1)}, bf16[672,128]{1,0:T(8,128)(2,1)S(1)}, u32[]{:S(2)}, u32[]{:S(2)}) collective-permute-start(bf16[672,128]{1,0:T(8,128)(2,1)S(1)} %get-tuple-element.29.turn), channel_id=1, source_target_pairs={{0,2},{1,3},{2,0},{3,1},{4,6},{5,7},{6,4},{7,5},{8,10},{9,11},{10,... | collective-permute-start | bytes 516104 | tf_op jit(solution)/shard_map/ppermute | solution.py:284
  15.9 3.5 %collective-permute-start.8 = (bf16[512,128]{1,0:T(8,128)(2,1)S(1)}, bf16[512,128]{1,0:T(8,128)(2,1)S(1)}, u32[]{:S(2)}, u32[]{:S(2)}) collective-permute-start(bf16[512,128]{1,0:T(8,128)(2,1)S(1)} %get-tuple-element.37), channel_id=1, source_target_pairs={{0,12},{1,13},{2,14},{3,15},{4,8},{5,9},{6,10},{7,11},{8,4},{9,5},... | collective-permute-start | bytes 393224 | tf_op jit(solution)/shard_map/ppermute | solution.py:284
  19.3 0.0 collective-permute-start.9
  19.3 0.9 %collective-permute-start.3 = (bf16[384,128]{1,0:T(8,128)(2,1)S(1)}, bf16[384,128]{1,0:T(8,128)(2,1)S(1)}, u32[]{:S(2)}, u32[]{:S(2)}) collective-permute-start(bf16[384,128]{1,0:T(8,128)(2,1)S(1)} %get-tuple-element.28.half_a), channel_id=1, source_target_pairs={{0,4},{1,5},{2,6},{3,7},{4,0},{5,1},{6,2},{7,3},{8,12},{9,13},{10,... | collective-permute-start | bytes 294920 | tf_op jit(solution)/shard_map/ppermute | solution.py:284
  20.2 4.1 %collective-permute-done.3.came_a = bf16[384,128]{1,0:T(8,128)(2,1)S(1)} collective-permute-done((bf16[384,128]{1,0:T(8,128)(2,1)S(1)}, bf16[384,128]{1,0:T(8,128)(2,1)S(1)}, u32[]{:S(2)}, u32[]{:S(2)}) %collective-permute-start.3) | collective-permute-done | bytes 98336 | tf_op jit(solution)/shard_map/ppermute | solution.py:284
  24.3 0.0 collective-permute-done.4.came_b.refs_1_
  24.3 0.1 shard_map.105
  24.4 0.1 collective-permute-start.7
  24.5 2.5 %collective-permute-start.6 = (bf16[832,128]{1,0:T(8,128)(2,1)S(1)}, bf16[832,128]{1,0:T(8,128)(2,1)S(1)}, u32[]{:S(2)}, u32[]{:S(2)}) collective-permute-start(bf16[832,128]{1,0:T(8,128)(2,1)S(1)} %get-tuple-element.31.b), channel_id=1, source_target_pairs={{0,4},{1,5},{2,6},{3,7},{4,0},{5,1},{6,2},{7,3},{8,12},{9,13},{10,... | collective-permute-start | bytes 638984 | tf_op jit(solution)/shard_map/ppermute | solution.py:284
  27.0 1.5 %collective-permute-start.5 = (bf16[768,128]{1,0:T(8,128)(2,1)S(1)}, bf16[768,128]{1,0:T(8,128)(2,1)S(1)}, u32[]{:S(2)}, u32[]{:S(2)}) collective-permute-start(bf16[768,128]{1,0:T(8,128)(2,1)S(1)} %get-tuple-element.30.a), channel_id=1, source_target_pairs={{0,2},{1,3},{2,0},{3,1},{4,6},{5,7},{6,4},{7,5},{8,10},{9,11},{10,... | collective-permute-start | bytes 589832 | tf_op jit(solution)/shard_map/ppermute | solution.py:284
  28.5 0.0 collective-permute-done.8.refs_2_
  28.5 0.1 collective-permute-done.9.refs_3_
  28.6 0.0 copy-start.1
  28.6 0.0 copy-start
  28.7 5.3 %collective-permute-done.5.far_a = bf16[768,128]{1,0:T(8,128)(2,1)S(1)} collective-permute-done((bf16[768,128]{1,0:T(8,128)(2,1)S(1)}, bf16[768,128]{1,0:T(8,128)(2,1)S(1)}, u32[]{:S(2)}, u32[]{:S(2)}) %collective-permute-start.5) | collective-permute-done | bytes 196640 | tf_op jit(solution)/shard_map/ppermute | solution.py:284
  34.0 0.0 collective-permute-done.6.far_b
  34.0 0.0 collective-permute-done.7.core
  34.0 0.1 collective-permute-start.10
  34.1 0.0 copy-done.1
  34.1 1.0 %shard_map.108 = (bf16[256,1024]{1,0:T(8,128)(2,1)S(1)}, bf16[256,1024]{1,0:T(8,128)(2,1)S(1)}, bf16[1024,512]{1,0:T(8,128)(2,1)S(1)}, bf16[8,128,128]{2,1,0:T(8...) custom-call(bf16[768,128]{1,0:T(8,128)(2,1)S(1)} %get-tuple-element.30.a, ...), custom_call_target="tpu_custom_call" | custom-call | tf_op jit(solution)/shard_map/pallas_call | solution.py:262
  35.2 1.1 %collective-permute-done.10.pair = bf16[2624,128]{1,0:T(8,128)(2,1)S(1)} collective-permute-done((bf16[2624,128]{1,0:T(8,128)(2,1)S(1)}, bf16[2624,128]{1,0:T(8,128)(2,1)S(1)}, u32[]{:S(2)}, u32[]{:S(2)}) %collective-permute-start.10) | collective-permute-done | bytes 671776 | tf_op jit(solution)/shard_map/ppermute | solution.py:284
  36.2 0.0 copy-done
  36.2 7.6 %shard_map.109 = (bf16[1,128,1024]{2,1,0:T(8,128)(2,1)}, f32[64,1024]{1,0:T(8,128)}, f32[64,1024]{1,0:T(8,128)}) custom-call(bf16[1600,128]{1,0:T(8,128)(2,1)S(1)} %collective-permute-done.7.core, bf16[2624,128]{1,0:T(8,128)(2,1)S(1)} %collective-permute-done.10.pair, bf16[768,128]{1,0:T(8,128)(2,1)S(1)} %get-tuple-element.36.refs_0_, ...), custom_call_target="tpu_custom_call" | custom-call | tf_op jit(solution)/shard_map/pallas_call | solution.py:262
  (2 shorter events, 0.1 us)
Async XLA Ops:
  4.2 11.0 %collective-permute-start.1 = (bf16[768,128]{1,0:T(8,128)(2,1)S(1)}, bf16[768,128]{1,0:T(8,128)(2,1)S(1)}, u32[]{:S(2)}, u32[]{:S(2)}) collective-permute-start(bf16[768,128]{1,0:T(8,128)(2,1)S(1)} %get-tuple-element.26), channel_id=1, source_target_pairs={{0,2},{1,3},{2,0},{3,1},{4,6},{5,7},{6,4},{7,5},{8,10},{9,11},{10,... | collective-permute-start | bytes 589832 | tf_op jit(solution)/shard_map/ppermute | solution.py:284
  7.2 8.0 %collective-permute-start.2 = (bf16[512,128]{1,0:T(8,128)(2,1)S(1)}, bf16[512,128]{1,0:T(8,128)(2,1)S(1)}, u32[]{:S(2)}, u32[]{:S(2)}) collective-permute-start(bf16[512,128]{1,0:T(8,128)(2,1)S(1)} %get-tuple-element.27), channel_id=1, source_target_pairs={{0,4},{1,5},{2,6},{3,7},{4,0},{5,1},{6,2},{7,3},{8,12},{9,13},{10,... | collective-permute-start | bytes 393224 | tf_op jit(solution)/shard_map/ppermute | solution.py:284
  8.8 6.4 %collective-permute-start = (bf16[400,128]{1,0:T(8,128)(2,1)S(1)}, bf16[400,128]{1,0:T(8,128)(2,1)S(1)}, u32[]{:S(2)}, u32[]{:S(2)}) collective-permute-start(bf16[400,128]{1,0:T(8,128)(2,1)S(1)} %get-tuple-element.24.piece), channel_id=1, source_target_pairs={{0,8},{1,9},{2,10},{3,11},{4,12},{5,13},{6,14},{7,15},{8,0},{9,1},... | collective-permute-start | bytes 307208 | tf_op jit(solution)/shard_map/ppermute | solution.py:284
  15.3 9.1 %collective-permute-start.4 = (bf16[672,128]{1,0:T(8,128)(2,1)S(1)}, bf16[672,128]{1,0:T(8,128)(2,1)S(1)}, u32[]{:S(2)}, u32[]{:S(2)}) collective-permute-start(bf16[672,128]{1,0:T(8,128)(2,1)S(1)} %get-tuple-element.29.turn), channel_id=1, source_target_pairs={{0,2},{1,3},{2,0},{3,1},{4,6},{5,7},{6,4},{7,5},{8,10},{9,11},{10,... | collective-permute-start | bytes 516104 | tf_op jit(solution)/shard_map/ppermute | solution.py:284
  15.9 12.7 %collective-permute-start.8 = (bf16[512,128]{1,0:T(8,128)(2,1)S(1)}, bf16[512,128]{1,0:T(8,128)(2,1)S(1)}, u32[]{:S(2)}, u32[]{:S(2)}) collective-permute-start(bf16[512,128]{1,0:T(8,128)(2,1)S(1)} %get-tuple-element.37), channel_id=1, source_target_pairs={{0,12},{1,13},{2,14},{3,15},{4,8},{5,9},{6,10},{7,11},{8,4},{9,5},... | collective-permute-start | bytes 393224 | tf_op jit(solution)/shard_map/ppermute | solution.py:284
  19.3 9.3 %collective-permute-start.9 = (bf16[512,128]{1,0:T(8,128)(2,1)S(1)}, bf16[512,128]{1,0:T(8,128)(2,1)S(1)}, u32[]{:S(2)}, u32[]{:S(2)}) collective-permute-start(bf16[512,128]{1,0:T(8,128)(2,1)S(1)} %get-tuple-element.38), channel_id=1, source_target_pairs={{0,8},{1,9},{2,10},{3,11},{4,12},{5,13},{6,14},{7,15},{8,0},{9,1},... | collective-permute-start | bytes 393224 | tf_op jit(solution)/shard_map/ppermute | solution.py:284
  19.3 5.0 %collective-permute-start.3 = (bf16[384,128]{1,0:T(8,128)(2,1)S(1)}, bf16[384,128]{1,0:T(8,128)(2,1)S(1)}, u32[]{:S(2)}, u32[]{:S(2)}) collective-permute-start(bf16[384,128]{1,0:T(8,128)(2,1)S(1)} %get-tuple-element.28.half_a), channel_id=1, source_target_pairs={{0,4},{1,5},{2,6},{3,7},{4,0},{5,1},{6,2},{7,3},{8,12},{9,13},{10,... | collective-permute-start | bytes 294920 | tf_op jit(solution)/shard_map/ppermute | solution.py:284
  24.4 9.6 %collective-permute-start.7 = (bf16[1600,128]{1,0:T(8,128)(2,1)S(1)}, bf16[1600,128]{1,0:T(8,128)(2,1)S(1)}, u32[]{:S(2)}, u32[]{:S(2)}) collective-permute-start(bf16[1600,128]{1,0:T(8,128)(2,1)S(1)} %get-tuple-element.32), channel_id=1, source_target_pairs={{0,1},{1,0},{2,3},{3,2},{4,5},{5,4},{6,7},{7,6},{8,9},{9,8},{10,11... | collective-permute-start | bytes 1228808 | tf_op jit(solution)/shard_map/ppermute | solution.py:284
  24.5 9.5 %collective-permute-start.6 = (bf16[832,128]{1,0:T(8,128)(2,1)S(1)}, bf16[832,128]{1,0:T(8,128)(2,1)S(1)}, u32[]{:S(2)}, u32[]{:S(2)}) collective-permute-start(bf16[832,128]{1,0:T(8,128)(2,1)S(1)} %get-tuple-element.31.b), channel_id=1, source_target_pairs={{0,4},{1,5},{2,6},{3,7},{4,0},{5,1},{6,2},{7,3},{8,12},{9,13},{10,... | collective-permute-start | bytes 638984 | tf_op jit(solution)/shard_map/ppermute | solution.py:284
  27.0 7.0 %collective-permute-start.5 = (bf16[768,128]{1,0:T(8,128)(2,1)S(1)}, bf16[768,128]{1,0:T(8,128)(2,1)S(1)}, u32[]{:S(2)}, u32[]{:S(2)}) collective-permute-start(bf16[768,128]{1,0:T(8,128)(2,1)S(1)} %get-tuple-element.30.a), channel_id=1, source_target_pairs={{0,2},{1,3},{2,0},{3,1},{4,6},{5,7},{6,4},{7,5},{8,10},{9,11},{10,... | collective-permute-start | bytes 589832 | tf_op jit(solution)/shard_map/ppermute | solution.py:284
  28.6 5.5 %copy-start.1 = (bf16[1024,1024]{1,0:T(8,128)(2,1)S(1)}, bf16[1024,1024]{1,0:T(8,128)(2,1)}, u32[]{:S(2)}) copy-start(bf16[1024,1024]{1,0:T(8,128)(2,1)} %refs_10_.1) | copy-start | bytes 6291460
  28.6 7.6 %copy-start = (bf16[1024,1024]{1,0:T(8,128)(2,1)S(1)}, bf16[1024,1024]{1,0:T(8,128)(2,1)}, u32[]{:S(2)}) copy-start(bf16[1024,1024]{1,0:T(8,128)(2,1)} %refs_11_.1) | copy-start | bytes 6291460
  34.0 2.2 %collective-permute-start.10 = (bf16[2624,128]{1,0:T(8,128)(2,1)S(1)}, bf16[2624,128]{1,0:T(8,128)(2,1)S(1)}, u32[]{:S(2)}, u32[]{:S(2)}) collective-permute-start(bf16[2624,128]{1,0:T(8,128)(2,1)S(1)} %shard_map.107), channel_id=1, source_target_pairs={{0,1},{1,0},{2,3},{3,2},{4,5},{5,4},{6,7},{7,6},{8,9},{9,8},{10,11... | collective-permute-start | bytes 2015240 | tf_op jit(solution)/shard_map/ppermute | solution.py:284

commit v10 on v8

--- a/solution.py
+++ b/solution.py
@@ -14,14 +14,12 @@
 LANES = 128
 META = 16
 CHUNKS = 4
-LIMIT = 16 * 2**20
+LIMIT = 24 * 2**20
 SMALL = 8 * 2**20
 Z2, Z1, Y, CORE = 8, 4, 2, 1
 GROUP = 16
-HINT = (0, 8 * 10**9, 0, 0, 0, 8 * 10**9, 0)
-FAR = (Z2 | Z1, Z2, Z1, 0)
-FIRST = (0, 2, 3)
-LAST = (1,)
+HINT = (0, 8 * 10**9)
+PLACES = tuple(range(0, GROUP, 2))
 HALF_A = ((0, Z2, Z1, Z1 | Z2), (Y, Y | Z2, Y | Z1, Y | Z1 | Z2))
 HALF_B = ((0, Z2, Y, Y | Z2), (Z1, Z1 | Z2, Z1 | Y, Z1 | Y | Z2))
 
@@ -67,8 +65,8 @@
     piece[at + rows : at + rows + META, :] = meta.astype(F32).astype(BF16)
 
 
-def columns_kernel(cotangent, w_second, near, beside, across, *scratch):
-    cot, second, turned, back, sems = scratch
+def columns_kernel(cotangent, w_second, *refs):
+    outs, (cot, second, turned, back, sems) = refs[: len(PLACES)], refs[len(PLACES) :]
     width = w_second.shape[0]
     each = width // GROUP
     place = lax.axis_index("grp")
@@ -80,14 +78,12 @@
     for span, copy in zip(spans, copies[1:]):
         copy.wait()
         back[span, :] = nt(second[span, :], cot[0]).astype(BF16)
-    for out, slots in ((near, (0,)), (beside, (CORE,)), (across, (Y, Y | CORE))):
-        at = 0
-        for first in slots:
-            for slot in range(first, GROUP, 4):
-                span = pl.ds(pl.multiple_of((place ^ slot) * each, each), each)
-                out[at : at + each, :] = turned[span, :]
-                out[at + each : at + 2 * each, :] = back[span, :]
-                at += 2 * each
+    for out, slot in zip(outs, PLACES):
+        for core in range(2):
+            span = pl.ds(pl.multiple_of((place ^ (slot | core)) * each, each), each)
+            at = core * 2 * each
+            out[at : at + each, :] = turned[span, :]
+            out[at + each : at + 2 * each, :] = back[span, :]
 
 
 def stack(out, at, *blocks):
@@ -109,23 +105,14 @@
     stack(both, 0, out_a, out_b)
 
 
-def pair_kernel(far_a, far_b, out):
-    stack(out, 0, far_a, far_b)
-
-
-def half_kernel(across, out):
-    stack(out, 0, across.at[across.shape[0] // 2 :])
-
-
-def gather_kernel(*refs):
-    stack(refs[-1], 0, *refs[:-1])
-
-
-def along_kernel(near, beside, across, other, *sent):
-    size = sent[0].shape[0] // 4
-    for slot, out in zip(FAR, sent):
-        span = slice(slot // 4 * size, (slot // 4 + 1) * size)
-        stack(out, 0, *[ref.at[span] for ref in (near, beside, across, other)])
+def other_kernel(*refs):
+    *blocks, out = refs
+    rows = out.shape[0] // len(PLACES)
+    stack(out, 0, *[ref.at[rows:] for ref in blocks])
+
+
+def pair_kernel(far_a, far_b, columns, out):
+    stack(out, 0, far_a, far_b, columns)
 
 
 def place_of(slot):
@@ -184,10 +171,11 @@
     w_piece[...] = part.astype(BF16)
 
 
-def forward_kernel(own, slots, cut, rest, core, pair, *refs):
+def step_kernel(own, slots, cut, rest, core, pair, *refs):
+    blocks, refs = refs[: len(PLACES)], refs[len(PLACES) :]
     early_feat, early_lifted, early_spread, early_adj, early_meta, w_piece = refs[:6]
-    w_first, w_second, output, hidden, spread, feat, adj, keep, pre_piece = refs[6:15]
-    meta, lifted = refs[15:]
+    w_first, w_second, output, grad_first, grad_second = refs[6:11]
+    hidden, spread, feat, adj, meta, dout, dpre, lifted = refs[11:]
     width = w_first.shape[0]
     held = own * slots
     rows = adj.shape[1]
@@ -203,6 +191,7 @@
     for size, start, halves in ((cut, 0, HALF_A), (rest, 4 * cut, HALF_B)):
         for ref, group in zip((core, pair), halves):
             arrays.append((ref, start, [slot | CORE for slot in group]))
+    deep = 4 * (cut + rest)
     lay_out(arrays, held, cut, feat, adj, meta)
     metas = [meta[p].astype(F32) for p in range(GROUP)]
     picks = jnp.concatenate([m[0:1] for m in metas], axis=0).astype(jnp.int32)
@@ -213,7 +202,6 @@
             held_by = metas[place_of(slot)][1 + i : 2 + i].astype(jnp.int32)
             count = jnp.where(picks == (place ^ slot) * own + i, held_by, count)
     masks = (lane < count).astype(F32)
-    keep[...] = masks
 
     late = slice(first * held, GROUP * held)
     lifted[late, :] = nn(feat[late, :], w_first[...]).astype(BF16)
@@ -225,26 +213,21 @@
     for c in range(0, width, step):
         half = 0.5 * nn(spread[...], lifted[:, c : c + step])
         hidden[:, c : c + step] = (half + half * jnp.tanh(half)).astype(BF16)
-    pre_piece[...] = nt(lifted_piece, spread[...])
+    pre_piece = nt(lifted_piece, spread[...])
     live = jnp.broadcast_to(masks[0:1], (rows, LANES)).T[:, :1]
     agg = nn(adj[0], (hidden[:rows, :].astype(F32) * live).astype(BF16)).astype(BF16)
     output[0] = (nn(agg, w_second[...]) * live).astype(BF16)
 
-
-def gradient_kernel(hidden, spread, feat, adj, masks, pre_piece, *refs):
-    far, *last = refs[: 1 + len(LAST)]
-    grad_first, grad_second, dout, dpre = refs[1 + len(LAST) :]
     each = grad_first.shape[0]
-    size = 8 * each
-    sent = {FAR[i]: far.at[k * size : (k + 1) * size] for k, i in enumerate(FIRST)}
-    sent.update({FAR[i]: ref for i, ref in zip(LAST, last)})
-    rows = adj.shape[1]
     for slot in range(GROUP):
         p = place_of(slot)
-        mask = masks[p : p + 1, :]
+        mask = masks[p : p + 1]
         span = slice(p * rows, (p + 1) * rows)
-        at = slot % 4 * 2 * each
-        source = sent[slot - slot % 4][at : at + 2 * each, :]
+        if slot % 2:
+            at = deep + slot // 2 * 2 * each
+            source = pair[at : at + 2 * each, :]
+        else:
+            source = blocks[slot // 2][: 2 * each, :]
         back = nn((source.astype(F32) * mask).astype(BF16), adj[p]) * mask
         dout[:, span] = back[:each].astype(BF16)
         pre = pre_piece[:, span]
@@ -293,36 +276,34 @@
     )
     came = swap(piece, Z2)
     cotangent, _ = lax.optimization_barrier((cotangent, piece))
-    near, beside, across = call(
+    columns = list(call(
         columns_kernel,
         (cotangent, w_second),
-        [((8 * each, rows), BF16)] * 2 + [((16 * each, rows), BF16)],
+        [((4 * each, rows), BF16)] * len(PLACES),
         [pltpu.VMEM(x.shape, BF16) for x in (cotangent, w_second)]
         + [pltpu.VMEM((width, rows), BF16)] * 2
         + [pltpu.SemaphoreType.DMA((1 + CHUNKS,))],
         stay=True,
-        flops=HINT[0],
-    )
-    came, across = lax.optimization_barrier((came, across))
-    across = swap(across, Y)
-    (other,) = call(half_kernel, (across,), [((8 * each, rows), BF16)], flops=HINT[1])
-    beside, other = swap(beside, CORE), swap(other, CORE)
-    sent = call(along_kernel, (near, beside, across, other), [((8 * each, rows), BF16)] * len(FAR), flops=HINT[2])
-    sent = [swap(x, slot) if slot else x for x, slot in zip(sent, FAR)]
-
-    a, b = call(split_kernel, (piece, came), [((2 * size, LANES), BF16) for size in (cut, rest)], flops=HINT[3])
+    ))
+    came, columns[0] = lax.optimization_barrier((came, columns[0]))
+    columns = [swap(x, slot) if slot else x for x, slot in zip(columns, PLACES)]
+    a, b = call(split_kernel, (piece, came), [((2 * size, LANES), BF16) for size in (cut, rest)])
     came_a, came_b = swap(a, Z1), swap(b, Y)
     a, b, both = call(
         join_kernel,
         (a, came_a, b, came_b),
         [((4 * size, LANES), BF16) for size in (cut, rest, cut + rest)],
-        flops=HINT[4],
+        flops=HINT[0],
     )
     far_a, far_b, core = swap(a, Y), swap(b, Z1), swap(both, CORE)
+    (others,) = call(other_kernel, columns, [((half * 2 * each, rows), BF16)], flops=HINT[1])
     far_a, far_b, core = lax.optimization_barrier((far_a, far_b, core))
-    (pair,) = call(pair_kernel, (far_a, far_b), [((4 * (cut + rest), LANES), BF16)])
+    (pair,) = call(
+        pair_kernel,
+        (far_a, far_b, others),
+        [((4 * (cut + rest) + half * 2 * each, LANES), BF16)],
+    )
     pair = swap(pair, CORE)
-    (far,) = call(gather_kernel, [sent[i] for i in FIRST], [((8 * each * len(FIRST), rows), BF16)], flops=HINT[5])
     early = call(
         functools.partial(early_kernel, own, slots, cut),
         (a, far_a, b, far_b, w_first),
@@ -336,31 +317,22 @@
         ],
         limit=LIMIT,
     )
-    pair, far = lax.optimization_barrier((pair, far))
-    output, *kept = call(
-        functools.partial(forward_kernel, own, slots, cut, rest),
-        (core, pair, *early, w_first, w_second),
+    return call(
+        functools.partial(step_kernel, own, slots, cut, rest),
+        (core, pair, *columns, *early, w_first, w_second),
+        [((1, rows, width), BF16), ((each, width), F32), ((each, width), F32)],
         [
-            ((1, rows, width), BF16),
-            ((GROUP * rows, width), BF16),
-            ((GROUP * rows, total), BF16),
-            ((total, width), BF16),
-            ((GROUP, rows, rows), BF16),
-            ((GROUP, LANES), F32),
-            ((each, GROUP * rows), F32),
+            pltpu.VMEM((GROUP * rows, width), BF16),
+            pltpu.VMEM((GROUP * rows, total), BF16),
+            pltpu.VMEM((total, width), BF16),
+            pltpu.VMEM((GROUP, rows, rows), BF16),
+            pltpu.VMEM((GROUP, META, LANES), BF16),
+            pltpu.VMEM((each, GROUP * rows), BF16),
+            pltpu.VMEM((each, GROUP * rows), BF16),
+            pltpu.VMEM((total, width), BF16),
         ],
-        [pltpu.VMEM((GROUP, META, LANES), BF16), pltpu.VMEM((total, width), BF16)],
         LIMIT,
-        flops=HINT[6],
-    )
-    grad_first, grad_second = call(
-        gradient_kernel,
-        (*kept, far, *[sent[i] for i in LAST]),
-        [((each, width), F32)] * 2,
-        [pltpu.VMEM((each, GROUP * rows), BF16)] * 2,
-        LIMIT,
-    )
-    return output, grad_first, grad_second
+    )
 
 
 def split_body(features, counts, pick_owner, pick_local, adjacency, cotangent, w_first, w_second):

time: 48.1 us -> 46 us (0.956)
  starting transfers between devices: 18 us -> 23.8 us
  waiting for transfers between devices: 14.2 us -> 8.87 us
  local copies, waits for them, and re-layouts: 1.56 us -> 0.01 us
  Pallas kernels: 13.4 us -> 12.4 us
    ppermute x13 -> x14, starting transfers between devices: 18 us -> 23.8 us  [swap(): return lax.ppermute(x, 'grp', [(i, i ^ slot) for i in range(GROUP)])]
    ppermute x13 -> x14, waiting for transfers between devices: 14.2 us -> 8.87 us  [swap(): return lax.ppermute(x, 'grp', [(i, i ^ slot) for i in range(GROUP)])]
    unnamed x4, local copies, waits for them, and re-layouts: 1.56 us -> 0.01 us
    pallas_call x11 -> x8, Pallas kernels: 13.4 us -> 12.4 us  [call(): pl.pallas_call(kernel, out_shape=tuple((jax.ShapeDtypeStruct(*out) for ou...]
  transfers between devices with their start and end apart: 13 -> 14, of which waited for: 6 -> 4; matrix products, arithmetic and copies ran while one was open for 0% -> 0% of each run, Pallas kernels for 21% -> 9%
where the time goes in v10:
time: 46 us; the launch traced here: 45.8 us
  starting transfers between devices  23.8 us (52%)
  Pallas kernels  12.4 us (27%)
  waiting for transfers between devices  8.87 us (19%)
  between operations  0.73 us (2%)
    ppermute x14, starting transfers between devices, swap(): return lax.ppermute(x, 'grp', [(i, i ^ slot) for i in range(GROUP)])  23.8 us
    pallas_call x8, Pallas kernels, call(): pl.pallas_call(kernel, out_shape=tuple((jax.ShapeDtypeStruct(*out) for ou...  12.4 us
    ppermute x14, waiting for transfers between devices, swap(): return lax.ppermute(x, 'grp', [(i, i ^ slot) for i in range(GROUP)])  8.87 us
  transfers between devices with their start and end apart: 14, of which 4 were waited for; matrix products, arithmetic and copies ran while one was open for 0% of the time, Pallas kernels for 9%

profile of v10, /device:TPU:0, one launch (start us, length us, event | category | flops | bytes accessed | tf_op | source)
XLA Modules:
  0.0 45.8 jit_solution(14570322404648597405)
XLA Ops:
  0.6 0.9 %shard_map.103.piece = bf16[400,128]{1,0:T(8,128)(2,1)S(1)} custom-call(s32[2]{0:T(128)} %counts.1, s32[1,8]{1,0:T(1,128)} %owner.1, s32[1,8]{1,0:T(1,128)} %local.1, bf16[2,16,1024]{2,1,0:T(8,128)(2,1)} %features.1, bf16[1,128,128]{2,1,0:T(8,128)(2,1)} %adjacency.1), custom_call_target="tpu_custom_call" | custom-call | tf_op jit(solution)/shard_map/pallas_call | solution.py:244
  1.6 4.1 %collective-permute-start = (bf16[400,128]{1,0:T(8,128)(2,1)S(1)}, bf16[400,128]{1,0:T(8,128)(2,1)S(1)}, u32[]{:S(2)}, u32[]{:S(2)}) collective-permute-start(bf16[400,128]{1,0:T(8,128)(2,1)S(1)} %shard_map.103.piece), channel_id=1, source_target_pairs={{0,8},{1,9},{2,10},{3,11},{4,12},{5,13},{6,14},{7,15},{8,0},{9,1},... | collective-permute-start | bytes 307208 | tf_op jit(solution)/shard_map/ppermute | solution.py:266
  5.7 2.9 %shard_map.104 = (bf16[256,128]{1,0:T(8,128)(2,1)S(1)}, bf16[256,128]{1,0:T(8,128)(2,1)S(1)}, bf16[256,128]{1,0:T(8,128)(2,1)S(1)}, bf16[256,128]{1,0:T(8,128)(2...) custom-call(bf16[1,128,1024]{2,1,0:T(8,128)(2,1)} %cotangent, ...), custom_call_target="tpu_custom_call" | custom-call | tf_op jit(solution)/shard_map/pallas_call | solution.py:244
  8.6 2.2 %collective-permute-done.came = bf16[400,128]{1,0:T(8,128)(2,1)S(1)} collective-permute-done((bf16[400,128]{1,0:T(8,128)(2,1)S(1)}, bf16[400,128]{1,0:T(8,128)(2,1)S(1)}, u32[]{:S(2)}, u32[]{:S(2)}) %collective-permute-start) | collective-permute-done | bytes 102432 | tf_op jit(solution)/shard_map/ppermute | solution.py:266
  10.8 1.6 %collective-permute-start.2 = (bf16[416,128]{1,0:T(8,128)(2,1)S(1)}, bf16[416,128]{1,0:T(8,128)(2,1)S(1)}, u32[]{:S(2)}, u32[]{:S(2)}) collective-permute-start(bf16[416,128]{1,0:T(8,128)(2,1)S(1)} %get-tuple-element.32.half_b), channel_id=1, source_target_pairs={{0,2},{1,3},{2,0},{3,1},{4,6},{5,7},{6,4},{7,5},{8,10},{9,11},{10,... | collective-permute-start | bytes 319496 | tf_op jit(solution)/shard_map/ppermute | solution.py:266
  12.4 0.7 %collective-permute-start.1 = (bf16[384,128]{1,0:T(8,128)(2,1)S(1)}, bf16[384,128]{1,0:T(8,128)(2,1)S(1)}, u32[]{:S(2)}, u32[]{:S(2)}) collective-permute-start(bf16[384,128]{1,0:T(8,128)(2,1)S(1)} %get-tuple-element.31.half_a), channel_id=1, source_target_pairs={{0,4},{1,5},{2,6},{3,7},{4,0},{5,1},{6,2},{7,3},{8,12},{9,13},{10,... | collective-permute-start | bytes 294920 | tf_op jit(solution)/shard_map/ppermute | solution.py:266
  13.1 3.3 %collective-permute-start.10 = (bf16[256,128]{1,0:T(8,128)(2,1)S(1)}, bf16[256,128]{1,0:T(8,128)(2,1)S(1)}, u32[]{:S(2)}, u32[]{:S(2)}) collective-permute-start(bf16[256,128]{1,0:T(8,128)(2,1)S(1)} %get-tuple-element.44), channel_id=1, source_target_pairs={{0,10},{1,11},{2,8},{3,9},{4,14},{5,15},{6,12},{7,13},{8,2},{9,3},... | collective-permute-start | bytes 196616 | tf_op jit(solution)/shard_map/ppermute | solution.py:266
  16.4 0.3 collective-permute-start.11
  16.7 4.5 %collective-permute-start.12 = (bf16[256,128]{1,0:T(8,128)(2,1)S(1)}, bf16[256,128]{1,0:T(8,128)(2,1)S(1)}, u32[]{:S(2)}, u32[]{:S(2)}) collective-permute-start(bf16[256,128]{1,0:T(8,128)(2,1)S(1)} %get-tuple-element.46), channel_id=1, source_target_pairs={{0,14},{1,15},{2,12},{3,13},{4,10},{5,11},{6,8},{7,9},{8,6},{9,7},... | collective-permute-start | bytes 196616 | tf_op jit(solution)/shard_map/ppermute | solution.py:266
  21.2 0.0 collective-permute-done.10.refs_5_
  21.2 3.0 %collective-permute-start.6 = (bf16[256,128]{1,0:T(8,128)(2,1)S(1)}, bf16[256,128]{1,0:T(8,128)(2,1)S(1)}, u32[]{:S(2)}, u32[]{:S(2)}) collective-permute-start(bf16[256,128]{1,0:T(8,128)(2,1)S(1)} %get-tuple-element.40), channel_id=1, source_target_pairs={{0,2},{1,3},{2,0},{3,1},{4,6},{5,7},{6,4},{7,5},{8,10},{9,11},{10,... | collective-permute-start | bytes 196616 | tf_op jit(solution)/shard_map/ppermute | solution.py:266
  24.2 0.0 collective-permute-done.11.refs_6_
  24.2 1.2 %collective-permute-start.7 = (bf16[256,128]{1,0:T(8,128)(2,1)S(1)}, bf16[256,128]{1,0:T(8,128)(2,1)S(1)}, u32[]{:S(2)}, u32[]{:S(2)}) collective-permute-start(bf16[256,128]{1,0:T(8,128)(2,1)S(1)} %get-tuple-element.41), channel_id=1, source_target_pairs={{0,4},{1,5},{2,6},{3,7},{4,0},{5,1},{6,2},{7,3},{8,12},{9,13},{10,... | collective-permute-start | bytes 196616 | tf_op jit(solution)/shard_map/ppermute | solution.py:266
  25.4 0.0 collective-permute-done.1.came_a
  25.4 0.3 collective-permute-start.8
  25.7 0.0 collective-permute-done.2.came_b
  25.7 3.1 %collective-permute-start.9 = (bf16[256,128]{1,0:T(8,128)(2,1)S(1)}, bf16[256,128]{1,0:T(8,128)(2,1)S(1)}, u32[]{:S(2)}, u32[]{:S(2)}) collective-permute-start(bf16[256,128]{1,0:T(8,128)(2,1)S(1)} %get-tuple-element.43), channel_id=1, source_target_pairs={{0,8},{1,9},{2,10},{3,11},{4,12},{5,13},{6,14},{7,15},{8,0},{9,1},... | collective-permute-start | bytes 196616 | tf_op jit(solution)/shard_map/ppermute | solution.py:266
  28.7 0.1 shard_map.106
  28.8 0.0 collective-permute-done.12.refs_7_
  28.8 1.6 %collective-permute-start.4 = (bf16[832,128]{1,0:T(8,128)(2,1)S(1)}, bf16[832,128]{1,0:T(8,128)(2,1)S(1)}, u32[]{:S(2)}, u32[]{:S(2)}) collective-permute-start(bf16[832,128]{1,0:T(8,128)(2,1)S(1)} %get-tuple-element.34.b), channel_id=1, source_target_pairs={{0,4},{1,5},{2,6},{3,7},{4,0},{5,1},{6,2},{7,3},{8,12},{9,13},{10,... | collective-permute-start | bytes 638984 | tf_op jit(solution)/shard_map/ppermute | solution.py:266
  30.4 0.0 collective-permute-done.6.refs_1_
  30.4 0.0 collective-permute-start.3
  30.4 0.0 collective-permute-done.7.refs_2_
  30.4 0.1 collective-permute-start.5
  30.5 0.8 %collective-permute-done.8.refs_3_ = bf16[256,128]{1,0:T(8,128)(2,1)S(1)} collective-permute-done((bf16[256,128]{1,0:T(8,128)(2,1)S(1)}, bf16[256,128]{1,0:T(8,128)(2,1)S(1)}, u32[]{:S(2)}, u32[]{:S(2)}) %collective-permute-start.8) | collective-permute-done | bytes 65568 | tf_op jit(solution)/shard_map/ppermute | solution.py:266
  31.3 0.0 collective-permute-done.9.refs_4_
  31.3 0.0 copy-start.1
  31.3 0.0 copy-start
  31.3 4.7 %collective-permute-done.3.far_a = bf16[768,128]{1,0:T(8,128)(2,1)S(1)} collective-permute-done((bf16[768,128]{1,0:T(8,128)(2,1)S(1)}, bf16[768,128]{1,0:T(8,128)(2,1)S(1)}, u32[]{:S(2)}, u32[]{:S(2)}) %collective-permute-start.3) | collective-permute-done | bytes 196640 | tf_op jit(solution)/shard_map/ppermute | solution.py:266
  36.1 0.0 collective-permute-done.4.far_b
  36.1 0.0 collective-permute-done.5.core
  36.1 0.1 collective-permute-start.13
  36.2 0.0 copy-done.1
  36.2 1.0 %shard_map.109 = (bf16[256,1024]{1,0:T(8,128)(2,1)S(1)}, bf16[256,1024]{1,0:T(8,128)(2,1)S(1)}, bf16[1024,512]{1,0:T(8,128)(2,1)S(1)}, bf16[8,128,128]{2,1,0:T(8...) custom-call(bf16[768,128]{1,0:T(8,128)(2,1)S(1)} %get-tuple-element.33.a, ...), custom_call_target="tpu_custom_call" | custom-call | tf_op jit(solution)/shard_map/pallas_call | solution.py:244
  37.2 1.1 %collective-permute-done.13.pair = bf16[2624,128]{1,0:T(8,128)(2,1)S(1)} collective-permute-done((bf16[2624,128]{1,0:T(8,128)(2,1)S(1)}, bf16[2624,128]{1,0:T(8,128)(2,1)S(1)}, u32[]{:S(2)}, u32[]{:S(2)}) %collective-permute-start.13) | collective-permute-done | bytes 671776 | tf_op jit(solution)/shard_map/ppermute | solution.py:266
  38.3 0.0 copy-done
  38.3 7.5 %shard_map.110 = (bf16[1,128,1024]{2,1,0:T(8,128)(2,1)}, f32[64,1024]{1,0:T(8,128)}, f32[64,1024]{1,0:T(8,128)}) custom-call(bf16[1600,128]{1,0:T(8,128)(2,1)S(1)} %collective-permute-done.5.core, bf16[2624,128]{1,0:T(8,128)(2,1)S(1)} %collective-permute-done.13.pair, bf16[256,128]{1,0:T(8,128)(2,1)S(1)} %get-tuple-element.39.refs_0_, ...), custom_call_target="tpu_custom_call" | custom-call | tf_op jit(solution)/shard_map/pallas_call | solution.py:244
  (3 shorter events, 0.1 us)
Async XLA Ops:
  1.6 9.2 %collective-permute-start = (bf16[400,128]{1,0:T(8,128)(2,1)S(1)}, bf16[400,128]{1,0:T(8,128)(2,1)S(1)}, u32[]{:S(2)}, u32[]{:S(2)}) collective-permute-start(bf16[400,128]{1,0:T(8,128)(2,1)S(1)} %shard_map.103.piece), channel_id=1, source_target_pairs={{0,8},{1,9},{2,10},{3,11},{4,12},{5,13},{6,14},{7,15},{8,0},{9,1},... | collective-permute-start | bytes 307208 | tf_op jit(solution)/shard_map/ppermute | solution.py:266
  10.8 14.9 %collective-permute-start.2 = (bf16[416,128]{1,0:T(8,128)(2,1)S(1)}, bf16[416,128]{1,0:T(8,128)(2,1)S(1)}, u32[]{:S(2)}, u32[]{:S(2)}) collective-permute-start(bf16[416,128]{1,0:T(8,128)(2,1)S(1)} %get-tuple-element.32.half_b), channel_id=1, source_target_pairs={{0,2},{1,3},{2,0},{3,1},{4,6},{5,7},{6,4},{7,5},{8,10},{9,11},{10,... | collective-permute-start | bytes 319496 | tf_op jit(solution)/shard_map/ppermute | solution.py:266
  12.4 13.0 %collective-permute-start.1 = (bf16[384,128]{1,0:T(8,128)(2,1)S(1)}, bf16[384,128]{1,0:T(8,128)(2,1)S(1)}, u32[]{:S(2)}, u32[]{:S(2)}) collective-permute-start(bf16[384,128]{1,0:T(8,128)(2,1)S(1)} %get-tuple-element.31.half_a), channel_id=1, source_target_pairs={{0,4},{1,5},{2,6},{3,7},{4,0},{5,1},{6,2},{7,3},{8,12},{9,13},{10,... | collective-permute-start | bytes 294920 | tf_op jit(solution)/shard_map/ppermute | solution.py:266
  13.1 8.1 %collective-permute-start.10 = (bf16[256,128]{1,0:T(8,128)(2,1)S(1)}, bf16[256,128]{1,0:T(8,128)(2,1)S(1)}, u32[]{:S(2)}, u32[]{:S(2)}) collective-permute-start(bf16[256,128]{1,0:T(8,128)(2,1)S(1)} %get-tuple-element.44), channel_id=1, source_target_pairs={{0,10},{1,11},{2,8},{3,9},{4,14},{5,15},{6,12},{7,13},{8,2},{9,3},... | collective-permute-start | bytes 196616 | tf_op jit(solution)/shard_map/ppermute | solution.py:266
  16.4 7.8 %collective-permute-start.11 = (bf16[256,128]{1,0:T(8,128)(2,1)S(1)}, bf16[256,128]{1,0:T(8,128)(2,1)S(1)}, u32[]{:S(2)}, u32[]{:S(2)}) collective-permute-start(bf16[256,128]{1,0:T(8,128)(2,1)S(1)} %get-tuple-element.45), channel_id=1, source_target_pairs={{0,12},{1,13},{2,14},{3,15},{4,8},{5,9},{6,10},{7,11},{8,4},{9,5},... | collective-permute-start | bytes 196616 | tf_op jit(solution)/shard_map/ppermute | solution.py:266
  16.7 12.1 %collective-permute-start.12 = (bf16[256,128]{1,0:T(8,128)(2,1)S(1)}, bf16[256,128]{1,0:T(8,128)(2,1)S(1)}, u32[]{:S(2)}, u32[]{:S(2)}) collective-permute-start(bf16[256,128]{1,0:T(8,128)(2,1)S(1)} %get-tuple-element.46), channel_id=1, source_target_pairs={{0,14},{1,15},{2,12},{3,13},{4,10},{5,11},{6,8},{7,9},{8,6},{9,7},... | collective-permute-start | bytes 196616 | tf_op jit(solution)/shard_map/ppermute | solution.py:266
  21.2 9.2 %collective-permute-start.6 = (bf16[256,128]{1,0:T(8,128)(2,1)S(1)}, bf16[256,128]{1,0:T(8,128)(2,1)S(1)}, u32[]{:S(2)}, u32[]{:S(2)}) collective-permute-start(bf16[256,128]{1,0:T(8,128)(2,1)S(1)} %get-tuple-element.40), channel_id=1, source_target_pairs={{0,2},{1,3},{2,0},{3,1},{4,6},{5,7},{6,4},{7,5},{8,10},{9,11},{10,... | collective-permute-start | bytes 196616 | tf_op jit(solution)/shard_map/ppermute | solution.py:266
  24.2 6.2 %collective-permute-start.7 = (bf16[256,128]{1,0:T(8,128)(2,1)S(1)}, bf16[256,128]{1,0:T(8,128)(2,1)S(1)}, u32[]{:S(2)}, u32[]{:S(2)}) collective-permute-start(bf16[256,128]{1,0:T(8,128)(2,1)S(1)} %get-tuple-element.41), channel_id=1, source_target_pairs={{0,4},{1,5},{2,6},{3,7},{4,0},{5,1},{6,2},{7,3},{8,12},{9,13},{10,... | collective-permute-start | bytes 196616 | tf_op jit(solution)/shard_map/ppermute | solution.py:266
  25.4 5.9 %collective-permute-start.8 = (bf16[256,128]{1,0:T(8,128)(2,1)S(1)}, bf16[256,128]{1,0:T(8,128)(2,1)S(1)}, u32[]{:S(2)}, u32[]{:S(2)}) collective-permute-start(bf16[256,128]{1,0:T(8,128)(2,1)S(1)} %get-tuple-element.42), channel_id=1, source_target_pairs={{0,6},{1,7},{2,4},{3,5},{4,2},{5,3},{6,0},{7,1},{8,14},{9,15},{10,... | collective-permute-start | bytes 196616 | tf_op jit(solution)/shard_map/ppermute | solution.py:266
  25.7 5.6 %collective-permute-start.9 = (bf16[256,128]{1,0:T(8,128)(2,1)S(1)}, bf16[256,128]{1,0:T(8,128)(2,1)S(1)}, u32[]{:S(2)}, u32[]{:S(2)}) collective-permute-start(bf16[256,128]{1,0:T(8,128)(2,1)S(1)} %get-tuple-element.43), channel_id=1, source_target_pairs={{0,8},{1,9},{2,10},{3,11},{4,12},{5,13},{6,14},{7,15},{8,0},{9,1},... | collective-permute-start | bytes 196616 | tf_op jit(solution)/shard_map/ppermute | solution.py:266
  28.8 7.3 %collective-permute-start.4 = (bf16[832,128]{1,0:T(8,128)(2,1)S(1)}, bf16[832,128]{1,0:T(8,128)(2,1)S(1)}, u32[]{:S(2)}, u32[]{:S(2)}) collective-permute-start(bf16[832,128]{1,0:T(8,128)(2,1)S(1)} %get-tuple-element.34.b), channel_id=1, source_target_pairs={{0,4},{1,5},{2,6},{3,7},{4,0},{5,1},{6,2},{7,3},{8,12},{9,13},{10,... | collective-permute-start | bytes 638984 | tf_op jit(solution)/shard_map/ppermute | solution.py:266
  30.4 5.7 %collective-permute-start.3 = (bf16[768,128]{1,0:T(8,128)(2,1)S(1)}, bf16[768,128]{1,0:T(8,128)(2,1)S(1)}, u32[]{:S(2)}, u32[]{:S(2)}) collective-permute-start(bf16[768,128]{1,0:T(8,128)(2,1)S(1)} %get-tuple-element.33.a), channel_id=1, source_target_pairs={{0,2},{1,3},{2,0},{3,1},{4,6},{5,7},{6,4},{7,5},{8,10},{9,11},{10,... | collective-permute-start | bytes 589832 | tf_op jit(solution)/shard_map/ppermute | solution.py:266
  30.4 5.7 %collective-permute-start.5 = (bf16[1600,128]{1,0:T(8,128)(2,1)S(1)}, bf16[1600,128]{1,0:T(8,128)(2,1)S(1)}, u32[]{:S(2)}, u32[]{:S(2)}) collective-permute-start(bf16[1600,128]{1,0:T(8,128)(2,1)S(1)} %get-tuple-element.35), channel_id=1, source_target_pairs={{0,1},{1,0},{2,3},{3,2},{4,5},{5,4},{6,7},{7,6},{8,9},{9,8},{10,11... | collective-permute-start | bytes 1228808 | tf_op jit(solution)/shard_map/ppermute | solution.py:266
  31.3 4.9 %copy-start.1 = (bf16[1024,1024]{1,0:T(8,128)(2,1)S(1)}, bf16[1024,1024]{1,0:T(8,128)(2,1)}, u32[]{:S(2)}) copy-start(bf16[1024,1024]{1,0:T(8,128)(2,1)} %refs_14_.1) | copy-start | bytes 6291460
  31.3 7.0 %copy-start = (bf16[1024,1024]{1,0:T(8,128)(2,1)S(1)}, bf16[1024,1024]{1,0:T(8,128)(2,1)}, u32[]{:S(2)}) copy-start(bf16[1024,1024]{1,0:T(8,128)(2,1)} %refs_15_.1) | copy-start | bytes 6291460
  36.1 2.2 %collective-permute-start.13 = (bf16[2624,128]{1,0:T(8,128)(2,1)S(1)}, bf16[2624,128]{1,0:T(8,128)(2,1)S(1)}, u32[]{:S(2)}, u32[]{:S(2)}) collective-permute-start(bf16[2624,128]{1,0:T(8,128)(2,1)S(1)} %shard_map.108), channel_id=1, source_target_pairs={{0,1},{1,0},{2,3},{3,2},{4,5},{5,4},{6,7},{7,6},{8,9},{9,8},{10,11... | collective-permute-start | bytes 2015240 | tf_op jit(solution)/shard_map/ppermute | solution.py:266

commit v11 on v10

--- a/solution.py
+++ b/solution.py
@@ -19,7 +19,9 @@
 Z2, Z1, Y, CORE = 8, 4, 2, 1
 GROUP = 16
 HINT = (0, 8 * 10**9)
-PLACES = tuple(range(0, GROUP, 2))
+SENT = ((0, CORE), (Y, Y | CORE)) + tuple(
+    tuple(z | slot for slot in range(4)) for z in (Z1, Z2 | Z1, Z2)
+)
 HALF_A = ((0, Z2, Z1, Z1 | Z2), (Y, Y | Z2, Y | Z1, Y | Z1 | Z2))
 HALF_B = ((0, Z2, Y, Y | Z2), (Z1, Z1 | Z2, Z1 | Y, Z1 | Y | Z2))
 
@@ -66,7 +68,7 @@
 
 
 def columns_kernel(cotangent, w_second, *refs):
-    outs, (cot, second, turned, back, sems) = refs[: len(PLACES)], refs[len(PLACES) :]
+    outs, (cot, second, turned, back, sems) = refs[: len(SENT)], refs[len(SENT) :]
     width = w_second.shape[0]
     each = width // GROUP
     place = lax.axis_index("grp")
@@ -78,10 +80,10 @@
     for span, copy in zip(spans, copies[1:]):
         copy.wait()
         back[span, :] = nt(second[span, :], cot[0]).astype(BF16)
-    for out, slot in zip(outs, PLACES):
-        for core in range(2):
-            span = pl.ds(pl.multiple_of((place ^ (slot | core)) * each, each), each)
-            at = core * 2 * each
+    for out, slots in zip(outs, SENT):
+        for i, slot in enumerate(slots):
+            span = pl.ds(pl.multiple_of((place ^ slot) * each, each), each)
+            at = i * 2 * each
             out[at : at + each, :] = turned[span, :]
             out[at + each : at + 2 * each, :] = back[span, :]
 
@@ -93,26 +95,48 @@
     return at
 
 
-def split_kernel(piece, came, half_a, half_b):
-    cut = half_a.shape[0] // 2
-    stack(half_a, 0, piece.at[:cut], came.at[:cut])
-    stack(half_b, 0, piece.at[cut:], came.at[cut:])
+def split_kernel(piece, came, columns_y, columns_z, half_a, half_b):
+    cut = (half_a.shape[0] - columns_z.shape[0]) // 2
+    stack(half_a, 0, piece.at[:cut], came.at[:cut], columns_z)
+    stack(half_b, 0, piece.at[cut:], came.at[cut:], columns_y)
 
 
 def join_kernel(half_a, came_a, half_b, came_b, out_a, out_b, both):
-    stack(out_a, 0, half_a, came_a)
-    stack(out_b, 0, half_b, came_b)
-    stack(both, 0, out_a, out_b)
+    size, last = out_b.shape[0] // 2, half_a.shape[0] - (both.shape[0] - out_b.shape[0]) // 2
+    cut = half_a.shape[0] - last
+    stack(out_a, 0, half_a.at[:cut], came_a.at[:cut], came_a.at[cut + last // 2 :])
+    stack(out_b, 0, half_b.at[:size], came_b.at[:size])
+    stack(both, 0, out_a.at[: 2 * cut], out_b)
+
+
+def turn_kernel(one, two, out):
+    half = out.shape[0] // 2
+    stack(out, 0, one.at[half:], two.at[half:])
+
+
+def block_of(slot, rows, own, came_a, came_b, far_a, one, two, turn):
+    ref, at = {
+        0: (own, 0),
+        Y: (came_b, came_b.shape[0] - 2 * rows),
+        Z1: (came_a, came_a.shape[0] - 4 * rows),
+        Z1 | Y: (far_a, far_a.shape[0] - 2 * rows),
+        Z2 | Z1: (one, 0),
+        Z2: (two, 0),
+        Z2 | Z1 | Y: (turn, 0),
+        Z2 | Y: (turn, 2 * rows),
+    }[slot - slot % 2]
+    at += slot % 2 * rows
+    return ref.at[at : at + rows]
 
 
 def other_kernel(*refs):
-    *blocks, out = refs
-    rows = out.shape[0] // len(PLACES)
-    stack(out, 0, *[ref.at[rows:] for ref in blocks])
+    *refs, out = refs
+    rows = out.shape[0] * 2 // GROUP
+    stack(out, 0, *[block_of(slot, rows, *refs) for slot in range(1, GROUP, 2)])
 
 
 def pair_kernel(far_a, far_b, columns, out):
-    stack(out, 0, far_a, far_b, columns)
+    stack(out, 0, far_a.at[: out.shape[0] - far_b.shape[0] - columns.shape[0]], far_b, columns)
 
 
 def place_of(slot):
@@ -172,7 +196,7 @@
 
 
 def step_kernel(own, slots, cut, rest, core, pair, *refs):
-    blocks, refs = refs[: len(PLACES)], refs[len(PLACES) :]
+    blocks, refs = refs[:7], refs[7:]
     early_feat, early_lifted, early_spread, early_adj, early_meta, w_piece = refs[:6]
     w_first, w_second, output, grad_first, grad_second = refs[6:11]
     hidden, spread, feat, adj, meta, dout, dpre, lifted = refs[11:]
@@ -227,7 +251,7 @@
             at = deep + slot // 2 * 2 * each
             source = pair[at : at + 2 * each, :]
         else:
-            source = blocks[slot // 2][: 2 * each, :]
+            source = block_of(slot, 2 * each, *blocks)[...]
         back = nn((source.astype(F32) * mask).astype(BF16), adj[p]) * mask
         dout[:, span] = back[:each].astype(BF16)
         pre = pre_piece[:, span]
@@ -276,27 +300,33 @@
     )
     came = swap(piece, Z2)
     cotangent, _ = lax.optimization_barrier((cotangent, piece))
-    columns = list(call(
+    own_columns, columns_y, columns_z, one, two = call(
         columns_kernel,
         (cotangent, w_second),
-        [((4 * each, rows), BF16)] * len(PLACES),
+        [((len(x) * 2 * each, rows), BF16) for x in SENT],
         [pltpu.VMEM(x.shape, BF16) for x in (cotangent, w_second)]
         + [pltpu.VMEM((width, rows), BF16)] * 2
         + [pltpu.SemaphoreType.DMA((1 + CHUNKS,))],
         stay=True,
-    ))
-    came, columns[0] = lax.optimization_barrier((came, columns[0]))
-    columns = [swap(x, slot) if slot else x for x, slot in zip(columns, PLACES)]
-    a, b = call(split_kernel, (piece, came), [((2 * size, LANES), BF16) for size in (cut, rest)])
+    )
+    one, two = swap(one, Z2 | Z1), swap(two, Z2)
+    a, b = call(
+        split_kernel,
+        (piece, came, columns_y, columns_z),
+        [((2 * cut + 8 * each, LANES), BF16), ((2 * rest + 4 * each, LANES), BF16)],
+    )
     came_a, came_b = swap(a, Z1), swap(b, Y)
     a, b, both = call(
         join_kernel,
         (a, came_a, b, came_b),
-        [((4 * size, LANES), BF16) for size in (cut, rest, cut + rest)],
+        [((4 * cut + 4 * each, LANES), BF16)] + [((4 * size, LANES), BF16) for size in (rest, cut + rest)],
         flops=HINT[0],
     )
     far_a, far_b, core = swap(a, Y), swap(b, Z1), swap(both, CORE)
-    (others,) = call(other_kernel, columns, [((half * 2 * each, rows), BF16)], flops=HINT[1])
+    (turn,) = call(turn_kernel, (one, two), [((8 * each, rows), BF16)], flops=HINT[1])
+    turn = swap(turn, Y)
+    blocks = (own_columns, came_a, came_b, far_a, one, two, turn)
+    (others,) = call(other_kernel, blocks, [((half * 2 * each, rows), BF16)])
     far_a, far_b, core = lax.optimization_barrier((far_a, far_b, core))
     (pair,) = call(
         pair_kernel,
@@ -319,7 +349,7 @@
     )
     return call(
         functools.partial(step_kernel, own, slots, cut, rest),
-        (core, pair, *columns, *early, w_first, w_second),
+        (core, pair, *blocks, *early, w_first, w_second),
         [((1, rows, width), BF16), ((each, width), F32), ((each, width), F32)],
         [
             pltpu.VMEM((GROUP * rows, width), BF16),

time: 46 us -> 43.2 us (0.939)
  starting transfers between devices: 23.8 us -> 14.5 us
  waiting for transfers between devices: 8.87 us -> 15.3 us
    ppermute x14 -> x10, starting transfers between devices: 23.8 us -> 14.5 us  [swap(): return lax.ppermute(x, 'grp', [(i, i ^ slot) for i in range(GROUP)])]
    ppermute x14 -> x10, waiting for transfers between devices: 8.87 us -> 15.3 us  [swap(): return lax.ppermute(x, 'grp', [(i, i ^ slot) for i in range(GROUP)])]
    pallas_call x8 -> x9, Pallas kernels: 12.4 us -> 12.5 us  [call(): pl.pallas_call(kernel, out_shape=tuple((jax.ShapeDtypeStruct(*out) for ou...]
  transfers between devices with their start and end apart: 14 -> 10, of which waited for: 4 -> 7; matrix products, arithmetic and copies ran while one was open for 0% -> 0% of each run, Pallas kernels for 9% -> 9%
where the time goes in v11:
time: 43.2 us; the launch traced here: 43 us
  waiting for transfers between devices  15.3 us (35%)
  starting transfers between devices  14.5 us (34%)
  Pallas kernels  12.5 us (29%)
  between operations  0.74 us (2%)
    ppermute x10, waiting for transfers between devices, swap(): return lax.ppermute(x, 'grp', [(i, i ^ slot) for i in range(GROUP)])  15.3 us
    ppermute x10, starting transfers between devices, swap(): return lax.ppermute(x, 'grp', [(i, i ^ slot) for i in range(GROUP)])  14.5 us
    pallas_call x9, Pallas kernels, call(): pl.pallas_call(kernel, out_shape=tuple((jax.ShapeDtypeStruct(*out) for ou...  12.5 us
  transfers between devices with their start and end apart: 10, of which 7 were waited for; matrix products, arithmetic and copies ran while one was open for 0% of the time, Pallas kernels for 9%

profile of v11, /device:TPU:0, one launch (start us, length us, event | category | flops | bytes accessed | tf_op | source)
XLA Modules:
  0.0 43.0 jit_solution(12468634528340822893)
XLA Ops:
  0.6 0.9 %shard_map.103.piece = bf16[400,128]{1,0:T(8,128)(2,1)S(1)} custom-call(s32[2]{0:T(128)} %counts.1, s32[1,8]{1,0:T(1,128)} %owner.1, s32[1,8]{1,0:T(1,128)} %local.1, bf16[2,16,1024]{2,1,0:T(8,128)(2,1)} %features.1, bf16[1,128,128]{2,1,0:T(8,128)(2,1)} %adjacency.1), custom_call_target="tpu_custom_call" | custom-call | tf_op jit(solution)/shard_map/pallas_call | solution.py:268
  1.6 4.1 %collective-permute-start = (bf16[400,128]{1,0:T(8,128)(2,1)S(1)}, bf16[400,128]{1,0:T(8,128)(2,1)S(1)}, u32[]{:S(2)}, u32[]{:S(2)}) collective-permute-start(bf16[400,128]{1,0:T(8,128)(2,1)S(1)} %shard_map.103.piece), channel_id=1, source_target_pairs={{0,8},{1,9},{2,10},{3,11},{4,12},{5,13},{6,14},{7,15},{8,0},{9,1},... | collective-permute-start | bytes 307208 | tf_op jit(solution)/shard_map/ppermute | solution.py:290
  5.7 2.9 %shard_map.104 = (bf16[256,128]{1,0:T(8,128)(2,1)S(1)}, bf16[256,128]{1,0:T(8,128)(2,1)S(1)}, bf16[512,128]{1,0:T(8,128)(2,1)S(1)}, bf16[512,128]{1,0:T(8,128)(2,1)S(1)}, bf16[512,128]{1,0:T(8,128)(2,1)S(1)}) custom-call(bf16[1,128,1024]{2,1,0:T(8,128)(2,1)} %cotangent, bf16[1024,1024]{1,0:T(8,128)(2,1)} %refs_14_.1), custom_call_target="tpu_custom_call" | custom-call | tf_op jit(solution)/shard_map/pallas_call | solution.py:268
  8.6 2.2 %collective-permute-done.came = bf16[400,128]{1,0:T(8,128)(2,1)S(1)} collective-permute-done((bf16[400,128]{1,0:T(8,128)(2,1)S(1)}, bf16[400,128]{1,0:T(8,128)(2,1)S(1)}, u32[]{:S(2)}, u32[]{:S(2)}) %collective-permute-start) | collective-permute-done | bytes 102432 | tf_op jit(solution)/shard_map/ppermute | solution.py:290
  10.8 0.8 %collective-permute-start.1 = (bf16[896,128]{1,0:T(8,128)(2,1)S(1)}, bf16[896,128]{1,0:T(8,128)(2,1)S(1)}, u32[]{:S(2)}, u32[]{:S(2)}) collective-permute-start(bf16[896,128]{1,0:T(8,128)(2,1)S(1)} %get-tuple-element.26.half_a), channel_id=1, source_target_pairs={{0,4},{1,5},{2,6},{3,7},{4,0},{5,1},{6,2},{7,3},{8,12},{9,13},{10,... | collective-permute-start | bytes 688136 | tf_op jit(solution)/shard_map/ppermute | solution.py:290
  11.6 1.5 %collective-permute-start.2 = (bf16[672,128]{1,0:T(8,128)(2,1)S(1)}, bf16[672,128]{1,0:T(8,128)(2,1)S(1)}, u32[]{:S(2)}, u32[]{:S(2)}) collective-permute-start(bf16[672,128]{1,0:T(8,128)(2,1)S(1)} %get-tuple-element.27.half_b), channel_id=1, source_target_pairs={{0,2},{1,3},{2,0},{3,1},{4,6},{5,7},{6,4},{7,5},{8,10},{9,11},{10,... | collective-permute-start | bytes 516104 | tf_op jit(solution)/shard_map/ppermute | solution.py:290
  13.1 2.9 %collective-permute-start.6 = (bf16[512,128]{1,0:T(8,128)(2,1)S(1)}, bf16[512,128]{1,0:T(8,128)(2,1)S(1)}, u32[]{:S(2)}, u32[]{:S(2)}) collective-permute-start(bf16[512,128]{1,0:T(8,128)(2,1)S(1)} %get-tuple-element.35), channel_id=1, source_target_pairs={{0,12},{1,13},{2,14},{3,15},{4,8},{5,9},{6,10},{7,11},{8,4},{9,5},... | collective-permute-start | bytes 393224 | tf_op jit(solution)/shard_map/ppermute | solution.py:290
  16.0 0.5 %collective-permute-start.7 = (bf16[512,128]{1,0:T(8,128)(2,1)S(1)}, bf16[512,128]{1,0:T(8,128)(2,1)S(1)}, u32[]{:S(2)}, u32[]{:S(2)}) collective-permute-start(bf16[512,128]{1,0:T(8,128)(2,1)S(1)} %get-tuple-element.36), channel_id=1, source_target_pairs={{0,8},{1,9},{2,10},{3,11},{4,12},{5,13},{6,14},{7,15},{8,0},{9,1},... | collective-permute-start | bytes 393224 | tf_op jit(solution)/shard_map/ppermute | solution.py:290
  16.5 1.1 %collective-permute-done.2.came_b.refs_2_ = bf16[672,128]{1,0:T(8,128)(2,1)S(1)} collective-permute-done((bf16[672,128]{1,0:T(8,128)(2,1)S(1)}, bf16[672,128]{1,0:T(8,128)(2,1)S(1)}, u32[]{:S(2)}, u32[]{:S(2)}) %collective-permute-start.2) | collective-permute-done | bytes 172064 | tf_op jit(solution)/shard_map/ppermute | solution.py:290
  17.6 0.1 collective-permute-done.1.came_a.refs_1_
  17.6 0.1 shard_map.106
  17.7 2.2 %collective-permute-start.4 = (bf16[832,128]{1,0:T(8,128)(2,1)S(1)}, bf16[832,128]{1,0:T(8,128)(2,1)S(1)}, u32[]{:S(2)}, u32[]{:S(2)}) collective-permute-start(bf16[832,128]{1,0:T(8,128)(2,1)S(1)} %get-tuple-element.29.b), channel_id=1, source_target_pairs={{0,4},{1,5},{2,6},{3,7},{4,0},{5,1},{6,2},{7,3},{8,12},{9,13},{10,... | collective-permute-start | bytes 638984 | tf_op jit(solution)/shard_map/ppermute | solution.py:290
  19.9 1.7 %collective-permute-start.3 = (bf16[1024,128]{1,0:T(8,128)(2,1)S(1)}, bf16[1024,128]{1,0:T(8,128)(2,1)S(1)}, u32[]{:S(2)}, u32[]{:S(2)}) collective-permute-start(bf16[1024,128]{1,0:T(8,128)(2,1)S(1)} %get-tuple-element.28.a), channel_id=1, source_target_pairs={{0,2},{1,3},{2,0},{3,1},{4,6},{5,7},{6,4},{7,5},{8,10},{9,11},{10,... | collective-permute-start | bytes 786440 | tf_op jit(solution)/shard_map/ppermute | solution.py:290
  21.7 0.0 collective-permute-start.5
  21.7 2.0 %collective-permute-done.6.one.refs_4_ = bf16[512,128]{1,0:T(8,128)(2,1)S(1)} collective-permute-done((bf16[512,128]{1,0:T(8,128)(2,1)S(1)}, bf16[512,128]{1,0:T(8,128)(2,1)S(1)}, u32[]{:S(2)}, u32[]{:S(2)}) %collective-permute-start.6) | collective-permute-done | bytes 131104 | tf_op jit(solution)/shard_map/ppermute | solution.py:290
  23.7 4.4 %collective-permute-done.7.two.refs_5_ = bf16[512,128]{1,0:T(8,128)(2,1)S(1)} collective-permute-done((bf16[512,128]{1,0:T(8,128)(2,1)S(1)}, bf16[512,128]{1,0:T(8,128)(2,1)S(1)}, u32[]{:S(2)}, u32[]{:S(2)}) %collective-permute-start.7) | collective-permute-done | bytes 131104 | tf_op jit(solution)/shard_map/ppermute | solution.py:290
  28.1 0.0 copy-start.1
  28.1 0.6 %collective-permute-start.8 = (bf16[512,128]{1,0:T(8,128)(2,1)S(1)}, bf16[512,128]{1,0:T(8,128)(2,1)S(1)}, u32[]{:S(2)}, u32[]{:S(2)}) collective-permute-start(bf16[512,128]{1,0:T(8,128)(2,1)S(1)} %shard_map.107), channel_id=1, source_target_pairs={{0,2},{1,3},{2,0},{3,1},{4,6},{5,7},{6,4},{7,5},{8,10},{9,11},{10,... | collective-permute-start | bytes 393224 | tf_op jit(solution)/shard_map/ppermute | solution.py:290
  28.8 4.4 %collective-permute-done.8.refs_6_ = bf16[512,128]{1,0:T(8,128)(2,1)S(1)} collective-permute-done((bf16[512,128]{1,0:T(8,128)(2,1)S(1)}, bf16[512,128]{1,0:T(8,128)(2,1)S(1)}, u32[]{:S(2)}, u32[]{:S(2)}) %collective-permute-start.8) | collective-permute-done | bytes 131104 | tf_op jit(solution)/shard_map/ppermute | solution.py:290
  33.2 0.0 collective-permute-done.3.refs_3_.far_a
  33.2 0.0 copy-start
  33.2 0.0 collective-permute-done.4.far_b
  33.2 0.0 collective-permute-done.5.core
  33.3 0.1 collective-permute-start.9
  33.4 0.0 copy-done.1
  33.4 1.0 %shard_map.110 = (bf16[256,1024]{1,0:T(8,128)(2,1)S(1)}, bf16[256,1024]{1,0:T(8,128)(2,1)S(1)}, bf16[1024,512]{1,0:T(8,128)(2,1)S(1)}, bf16[8,128,128]{2,1,0:T(8...) custom-call(bf16[1024,128]{1,0:T(8,128)(2,1)S(1)} %get-tuple-element.28.a, ...), custom_call_target="tpu_custom_call" | custom-call | tf_op jit(solution)/shard_map/pallas_call | solution.py:268
  34.4 1.1 %collective-permute-done.9.pair = bf16[2624,128]{1,0:T(8,128)(2,1)S(1)} collective-permute-done((bf16[2624,128]{1,0:T(8,128)(2,1)S(1)}, bf16[2624,128]{1,0:T(8,128)(2,1)S(1)}, u32[]{:S(2)}, u32[]{:S(2)}) %collective-permute-start.9) | collective-permute-done | bytes 671776 | tf_op jit(solution)/shard_map/ppermute | solution.py:290
  35.5 0.0 copy-done
  35.5 7.6 %shard_map.111 = (bf16[1,128,1024]{2,1,0:T(8,128)(2,1)}, f32[64,1024]{1,0:T(8,128)}, f32[64,1024]{1,0:T(8,128)}) custom-call(bf16[1600,128]{1,0:T(8,128)(2,1)S(1)} %collective-permute-done.5.core, bf16[2624,128]{1,0:T(8,128)(2,1)S(1)} %collective-permute-done.9.pair, bf16[256,128]{1,0:T(8,128)(2,1)S(1)} %get-tuple-element.34.refs_0_, ...), custom_call_target="tpu_custom_call" | custom-call | tf_op jit(solution)/shard_map/pallas_call | solution.py:268
  (4 shorter events, 0.1 us)
Async XLA Ops:
  1.6 9.2 %collective-permute-start = (bf16[400,128]{1,0:T(8,128)(2,1)S(1)}, bf16[400,128]{1,0:T(8,128)(2,1)S(1)}, u32[]{:S(2)}, u32[]{:S(2)}) collective-permute-start(bf16[400,128]{1,0:T(8,128)(2,1)S(1)} %shard_map.103.piece), channel_id=1, source_target_pairs={{0,8},{1,9},{2,10},{3,11},{4,12},{5,13},{6,14},{7,15},{8,0},{9,1},... | collective-permute-start | bytes 307208 | tf_op jit(solution)/shard_map/ppermute | solution.py:290
  10.8 6.9 %collective-permute-start.1 = (bf16[896,128]{1,0:T(8,128)(2,1)S(1)}, bf16[896,128]{1,0:T(8,128)(2,1)S(1)}, u32[]{:S(2)}, u32[]{:S(2)}) collective-permute-start(bf16[896,128]{1,0:T(8,128)(2,1)S(1)} %get-tuple-element.26.half_a), channel_id=1, source_target_pairs={{0,4},{1,5},{2,6},{3,7},{4,0},{5,1},{6,2},{7,3},{8,12},{9,13},{10,... | collective-permute-start | bytes 688136 | tf_op jit(solution)/shard_map/ppermute | solution.py:290
  11.6 6.0 %collective-permute-start.2 = (bf16[672,128]{1,0:T(8,128)(2,1)S(1)}, bf16[672,128]{1,0:T(8,128)(2,1)S(1)}, u32[]{:S(2)}, u32[]{:S(2)}) collective-permute-start(bf16[672,128]{1,0:T(8,128)(2,1)S(1)} %get-tuple-element.27.half_b), channel_id=1, source_target_pairs={{0,2},{1,3},{2,0},{3,1},{4,6},{5,7},{6,4},{7,5},{8,10},{9,11},{10,... | collective-permute-start | bytes 516104 | tf_op jit(solution)/shard_map/ppermute | solution.py:290
  13.1 10.6 %collective-permute-start.6 = (bf16[512,128]{1,0:T(8,128)(2,1)S(1)}, bf16[512,128]{1,0:T(8,128)(2,1)S(1)}, u32[]{:S(2)}, u32[]{:S(2)}) collective-permute-start(bf16[512,128]{1,0:T(8,128)(2,1)S(1)} %get-tuple-element.35), channel_id=1, source_target_pairs={{0,12},{1,13},{2,14},{3,15},{4,8},{5,9},{6,10},{7,11},{8,4},{9,5},... | collective-permute-start | bytes 393224 | tf_op jit(solution)/shard_map/ppermute | solution.py:290
  16.0 12.1 %collective-permute-start.7 = (bf16[512,128]{1,0:T(8,128)(2,1)S(1)}, bf16[512,128]{1,0:T(8,128)(2,1)S(1)}, u32[]{:S(2)}, u32[]{:S(2)}) collective-permute-start(bf16[512,128]{1,0:T(8,128)(2,1)S(1)} %get-tuple-element.36), channel_id=1, source_target_pairs={{0,8},{1,9},{2,10},{3,11},{4,12},{5,13},{6,14},{7,15},{8,0},{9,1},... | collective-permute-start | bytes 393224 | tf_op jit(solution)/shard_map/ppermute | solution.py:290
  17.7 15.5 %collective-permute-start.4 = (bf16[832,128]{1,0:T(8,128)(2,1)S(1)}, bf16[832,128]{1,0:T(8,128)(2,1)S(1)}, u32[]{:S(2)}, u32[]{:S(2)}) collective-permute-start(bf16[832,128]{1,0:T(8,128)(2,1)S(1)} %get-tuple-element.29.b), channel_id=1, source_target_pairs={{0,4},{1,5},{2,6},{3,7},{4,0},{5,1},{6,2},{7,3},{8,12},{9,13},{10,... | collective-permute-start | bytes 638984 | tf_op jit(solution)/shard_map/ppermute | solution.py:290
  19.9 13.2 %collective-permute-start.3 = (bf16[1024,128]{1,0:T(8,128)(2,1)S(1)}, bf16[1024,128]{1,0:T(8,128)(2,1)S(1)}, u32[]{:S(2)}, u32[]{:S(2)}) collective-permute-start(bf16[1024,128]{1,0:T(8,128)(2,1)S(1)} %get-tuple-element.28.a), channel_id=1, source_target_pairs={{0,2},{1,3},{2,0},{3,1},{4,6},{5,7},{6,4},{7,5},{8,10},{9,11},{10,... | collective-permute-start | bytes 786440 | tf_op jit(solution)/shard_map/ppermute | solution.py:290
  21.7 11.5 %collective-permute-start.5 = (bf16[1600,128]{1,0:T(8,128)(2,1)S(1)}, bf16[1600,128]{1,0:T(8,128)(2,1)S(1)}, u32[]{:S(2)}, u32[]{:S(2)}) collective-permute-start(bf16[1600,128]{1,0:T(8,128)(2,1)S(1)} %get-tuple-element.30), channel_id=1, source_target_pairs={{0,1},{1,0},{2,3},{3,2},{4,5},{5,4},{6,7},{7,6},{8,9},{9,8},{10,11... | collective-permute-start | bytes 1228808 | tf_op jit(solution)/shard_map/ppermute | solution.py:290
  28.1 5.2 %copy-start.1 = (bf16[1024,1024]{1,0:T(8,128)(2,1)S(1)}, bf16[1024,1024]{1,0:T(8,128)(2,1)}, u32[]{:S(2)}) copy-start(bf16[1024,1024]{1,0:T(8,128)(2,1)} %refs_13_.1) | copy-start | bytes 6291460
  28.1 5.0 %collective-permute-start.8 = (bf16[512,128]{1,0:T(8,128)(2,1)S(1)}, bf16[512,128]{1,0:T(8,128)(2,1)S(1)}, u32[]{:S(2)}, u32[]{:S(2)}) collective-permute-start(bf16[512,128]{1,0:T(8,128)(2,1)S(1)} %shard_map.107), channel_id=1, source_target_pairs={{0,2},{1,3},{2,0},{3,1},{4,6},{5,7},{6,4},{7,5},{8,10},{9,11},{10,... | collective-permute-start | bytes 393224 | tf_op jit(solution)/shard_map/ppermute | solution.py:290
  33.2 2.3 %copy-start = (bf16[1024,1024]{1,0:T(8,128)(2,1)S(1)}, bf16[1024,1024]{1,0:T(8,128)(2,1)}, u32[]{:S(2)}) copy-start(bf16[1024,1024]{1,0:T(8,128)(2,1)} %refs_14_.1) | copy-start | bytes 6291460
  33.3 2.2 %collective-permute-start.9 = (bf16[2624,128]{1,0:T(8,128)(2,1)S(1)}, bf16[2624,128]{1,0:T(8,128)(2,1)S(1)}, u32[]{:S(2)}, u32[]{:S(2)}) collective-permute-start(bf16[2624,128]{1,0:T(8,128)(2,1)S(1)} %shard_map.109), channel_id=1, source_target_pairs={{0,1},{1,0},{2,3},{3,2},{4,5},{5,4},{6,7},{7,6},{8,9},{9,8},{10,11... | collective-permute-start | bytes 2015240 | tf_op jit(solution)/shard_map/ppermute | solution.py:290

commit v12 on v11

--- a/solution.py
+++ b/solution.py
@@ -199,7 +199,7 @@
     blocks, refs = refs[:7], refs[7:]
     early_feat, early_lifted, early_spread, early_adj, early_meta, w_piece = refs[:6]
     w_first, w_second, output, grad_first, grad_second = refs[6:11]
-    hidden, spread, feat, adj, meta, dout, dpre, lifted = refs[11:]
+    hidden, spread, feat, adj, meta, dout, dpre, lifted, result, grads, second, sems = refs[11:]
     width = w_first.shape[0]
     held = own * slots
     rows = adj.shape[1]
@@ -229,19 +229,11 @@
 
     late = slice(first * held, GROUP * held)
     lifted[late, :] = nn(feat[late, :], w_first[...]).astype(BF16)
-    lifted_piece = nt(w_piece[...], feat[...]).astype(BF16)
     for p in range(first, GROUP):
         span = slice(p * rows, (p + 1) * rows)
         spread[span, :] = spread_of(place, held, slots, adj[p], picks[p : p + 1])
-    step = min(width, 2 * LANES)
-    for c in range(0, width, step):
-        half = 0.5 * nn(spread[...], lifted[:, c : c + step])
-        hidden[:, c : c + step] = (half + half * jnp.tanh(half)).astype(BF16)
+    lifted_piece = nt(w_piece[...], feat[...]).astype(BF16)
     pre_piece = nt(lifted_piece, spread[...])
-    live = jnp.broadcast_to(masks[0:1], (rows, LANES)).T[:, :1]
-    agg = nn(adj[0], (hidden[:rows, :].astype(F32) * live).astype(BF16)).astype(BF16)
-    output[0] = (nn(agg, w_second[...]) * live).astype(BF16)
-
     each = grad_first.shape[0]
     for slot in range(GROUP):
         p = place_of(slot)
@@ -257,19 +249,40 @@
         pre = pre_piece[:, span]
         sig = 0.5 + 0.5 * jnp.tanh(0.5 * pre)
         dpre[:, span] = (back[each:] * sig * (1.0 + pre * (1.0 - sig))).astype(BF16)
-    grad_second[...] = nn(dout[...], hidden[...])
-    moved = nn(dpre[...], spread[...])
-    grad_first[...] = nn(moved.astype(BF16), feat[...])
-
-
-def call(kernel, ins, outs, scratch=(), limit=SMALL, stay=False, flops=0):
+
+    chunk = min(width, 2 * LANES)
+    for c in range(0, width, chunk):
+        span = slice(c, c + chunk)
+        half = 0.5 * nn(spread[...], lifted[:, span])
+        hidden[:, span] = (half + half * jnp.tanh(half)).astype(BF16)
+        if c:
+            done = slice(c - chunk, c)
+            second[:, done] = nn(dout[...], hidden[:, done])
+        else:
+            moved = nn(dpre[...], spread[...])
+            grads[...] = nn(moved.astype(BF16), feat[...])
+            first_out = pltpu.make_async_copy(grads, grad_first, sems.at[0])
+            first_out.start()
+    live = jnp.broadcast_to(masks[0:1], (rows, LANES)).T[:, :1]
+    agg = nn(adj[0], (hidden[:rows, :].astype(F32) * live).astype(BF16)).astype(BF16)
+    result[0] = (nn(agg, w_second[...]) * live).astype(BF16)
+    output_out = pltpu.make_async_copy(result, output, sems.at[1])
+    output_out.start()
+    second[:, span] = nn(dout[...], hidden[:, span])
+    second_out = pltpu.make_async_copy(second, grad_second, sems.at[2])
+    second_out.start()
+    for copy in (first_out, output_out, second_out):
+        copy.wait()
+
+
+def call(kernel, ins, outs, scratch=(), limit=SMALL, stay=False, leave=False, flops=0):
     if stay:
         ins = [pltpu.with_memory_space_constraint(x, pltpu.HBM) for x in ins]
     return pl.pallas_call(
         kernel,
         out_shape=tuple(jax.ShapeDtypeStruct(*out) for out in outs),
         in_specs=[HBM if stay else VMEM] * len(ins),
-        out_specs=(VMEM,) * len(outs),
+        out_specs=(HBM if leave else VMEM,) * len(outs),
         scratch_shapes=list(scratch),
         compiler_params=pltpu.CompilerParams(vmem_limit_bytes=limit),
         cost_estimate=pl.CostEstimate(flops=flops, bytes_accessed=0, transcendentals=0),
@@ -282,7 +295,7 @@
     held = own * slots
     each = width // GROUP
     total = GROUP * held
-    cut = held * (width // LANES * 3 // 4)
+    cut = held * (width // LANES // 2)
     rest = held * (width // LANES) + rows + META - cut
     half = GROUP // 2
 
@@ -322,7 +335,7 @@
         [((4 * cut + 4 * each, LANES), BF16)] + [((4 * size, LANES), BF16) for size in (rest, cut + rest)],
         flops=HINT[0],
     )
-    far_a, far_b, core = swap(a, Y), swap(b, Z1), swap(both, CORE)
+    far_b, far_a, core = swap(b, Z1), swap(a, Y), swap(both, CORE)
     (turn,) = call(turn_kernel, (one, two), [((8 * each, rows), BF16)], flops=HINT[1])
     turn = swap(turn, Y)
     blocks = (own_columns, came_a, came_b, far_a, one, two, turn)
@@ -360,8 +373,13 @@
             pltpu.VMEM((each, GROUP * rows), BF16),
             pltpu.VMEM((each, GROUP * rows), BF16),
             pltpu.VMEM((total, width), BF16),
+            pltpu.VMEM((1, rows, width), BF16),
+            pltpu.VMEM((each, width), F32),
+            pltpu.VMEM((each, width), F32),
+            pltpu.SemaphoreType.DMA((3,)),
         ],
         LIMIT,
+        leave=True,
     )
 
 

time: 43.2 us -> 42.8 us (level)
  starting transfers between devices: 14.5 us -> 13.5 us
  waiting for transfers between devices: 15.3 us -> 16.3 us
    ppermute x10, waiting for transfers between devices: 15.3 us -> 16.3 us  [swap(): return lax.ppermute(x, 'grp', [(i, i ^ slot) for i in range(GROUP)])]
    ppermute x10, starting transfers between devices: 14.5 us -> 13.5 us  [swap(): return lax.ppermute(x, 'grp', [(i, i ^ slot) for i in range(GROUP)])]
  transfers between devices with their start and end apart: 10 -> 10, of which waited for: 7 -> 6; matrix products, arithmetic and copies ran while one was open for 0% -> 0% of each run, Pallas kernels for 9% -> 9%
where the time goes in v12:
time: 42.8 us; the launch traced here: 42.7 us
  waiting for transfers between devices  16.3 us (38%)
  starting transfers between devices  13.5 us (32%)
  Pallas kernels  12.2 us (29%)
  between operations  0.74 us (2%)
    ppermute x10, waiting for transfers between devices, swap(): return lax.ppermute(x, 'grp', [(i, i ^ slot) for i in range(GROUP)])  16.3 us
    ppermute x10, starting transfers between devices, swap(): return lax.ppermute(x, 'grp', [(i, i ^ slot) for i in range(GROUP)])  13.5 us
    pallas_call x9, Pallas kernels, call(): pl.pallas_call(kernel, out_shape=tuple((jax.ShapeDtypeStruct(*out) for ou...  12.2 us
  transfers between devices with their start and end apart: 10, of which 6 were waited for; matrix products, arithmetic and copies ran while one was open for 0% of the time, Pallas kernels for 9%

profile of v12, /device:TPU:0, one launch (start us, length us, event | category | flops | bytes accessed | tf_op | source)
XLA Modules:
  0.0 42.7 jit_solution(10277948920816013934)
XLA Ops:
  0.6 0.9 %shard_map.103.piece = bf16[400,128]{1,0:T(8,128)(2,1)S(1)} custom-call(s32[2]{0:T(128)} %counts.1, s32[1,8]{1,0:T(1,128)} %owner.1, s32[1,8]{1,0:T(1,128)} %local.1, bf16[2,16,1024]{2,1,0:T(8,128)(2,1)} %features.1, bf16[1,128,128]{2,1,0:T(8,128)(2,1)} %adjacency.1), custom_call_target="tpu_custom_call" | custom-call | tf_op jit(solution)/shard_map/pallas_call | solution.py:281
  1.6 4.1 %collective-permute-start = (bf16[400,128]{1,0:T(8,128)(2,1)S(1)}, bf16[400,128]{1,0:T(8,128)(2,1)S(1)}, u32[]{:S(2)}, u32[]{:S(2)}) collective-permute-start(bf16[400,128]{1,0:T(8,128)(2,1)S(1)} %shard_map.103.piece), channel_id=1, source_target_pairs={{0,8},{1,9},{2,10},{3,11},{4,12},{5,13},{6,14},{7,15},{8,0},{9,1},... | collective-permute-start | bytes 307208 | tf_op jit(solution)/shard_map/ppermute | solution.py:303
  5.7 2.9 %shard_map.104 = (bf16[256,128]{1,0:T(8,128)(2,1)S(1)}, bf16[256,128]{1,0:T(8,128)(2,1)S(1)}, bf16[512,128]{1,0:T(8,128)(2,1)S(1)}, bf16[512,128]{1,0:T(8,128)(2,1)S(1)}, bf16[512,128]{1,0:T(8,128)(2,1)S(1)}) custom-call(bf16[1,128,1024]{2,1,0:T(8,128)(2,1)} %cotangent, bf16[1024,1024]{1,0:T(8,128)(2,1)} %refs_14_.1), custom_call_target="tpu_custom_call" | custom-call | tf_op jit(solution)/shard_map/pallas_call | solution.py:281
  8.6 2.2 %collective-permute-done.came = bf16[400,128]{1,0:T(8,128)(2,1)S(1)} collective-permute-done((bf16[400,128]{1,0:T(8,128)(2,1)S(1)}, bf16[400,128]{1,0:T(8,128)(2,1)S(1)}, u32[]{:S(2)}, u32[]{:S(2)}) %collective-permute-start) | collective-permute-done | bytes 102432 | tf_op jit(solution)/shard_map/ppermute | solution.py:303
  10.8 1.6 %collective-permute-start.2 = (bf16[800,128]{1,0:T(8,128)(2,1)S(1)}, bf16[800,128]{1,0:T(8,128)(2,1)S(1)}, u32[]{:S(2)}, u32[]{:S(2)}) collective-permute-start(bf16[800,128]{1,0:T(8,128)(2,1)S(1)} %get-tuple-element.27.half_b), channel_id=1, source_target_pairs={{0,2},{1,3},{2,0},{3,1},{4,6},{5,7},{6,4},{7,5},{8,10},{9,11},{10,... | collective-permute-start | bytes 614408 | tf_op jit(solution)/shard_map/ppermute | solution.py:303
  12.4 0.7 %collective-permute-start.1 = (bf16[768,128]{1,0:T(8,128)(2,1)S(1)}, bf16[768,128]{1,0:T(8,128)(2,1)S(1)}, u32[]{:S(2)}, u32[]{:S(2)}) collective-permute-start(bf16[768,128]{1,0:T(8,128)(2,1)S(1)} %get-tuple-element.26.half_a), channel_id=1, source_target_pairs={{0,4},{1,5},{2,6},{3,7},{4,0},{5,1},{6,2},{7,3},{8,12},{9,13},{10,... | collective-permute-start | bytes 589832 | tf_op jit(solution)/shard_map/ppermute | solution.py:303
  13.1 2.8 %collective-permute-start.6 = (bf16[512,128]{1,0:T(8,128)(2,1)S(1)}, bf16[512,128]{1,0:T(8,128)(2,1)S(1)}, u32[]{:S(2)}, u32[]{:S(2)}) collective-permute-start(bf16[512,128]{1,0:T(8,128)(2,1)S(1)} %get-tuple-element.35), channel_id=1, source_target_pairs={{0,12},{1,13},{2,14},{3,15},{4,8},{5,9},{6,10},{7,11},{8,4},{9,5},... | collective-permute-start | bytes 393224 | tf_op jit(solution)/shard_map/ppermute | solution.py:303
  15.9 0.6 %collective-permute-start.7 = (bf16[512,128]{1,0:T(8,128)(2,1)S(1)}, bf16[512,128]{1,0:T(8,128)(2,1)S(1)}, u32[]{:S(2)}, u32[]{:S(2)}) collective-permute-start(bf16[512,128]{1,0:T(8,128)(2,1)S(1)} %get-tuple-element.36), channel_id=1, source_target_pairs={{0,8},{1,9},{2,10},{3,11},{4,12},{5,13},{6,14},{7,15},{8,0},{9,1},... | collective-permute-start | bytes 393224 | tf_op jit(solution)/shard_map/ppermute | solution.py:303
  16.5 1.9 %collective-permute-done.1.came_a.refs_1_ = bf16[768,128]{1,0:T(8,128)(2,1)S(1)} collective-permute-done((bf16[768,128]{1,0:T(8,128)(2,1)S(1)}, bf16[768,128]{1,0:T(8,128)(2,1)S(1)}, u32[]{:S(2)}, u32[]{:S(2)}) %collective-permute-start.1) | collective-permute-done | bytes 196640 | tf_op jit(solution)/shard_map/ppermute | solution.py:303
  18.4 0.0 collective-permute-done.2.came_b.refs_2_
  18.4 0.1 shard_map.106
  18.5 0.6 %collective-permute-start.3 = (bf16[768,128]{1,0:T(8,128)(2,1)S(1)}, bf16[768,128]{1,0:T(8,128)(2,1)S(1)}, u32[]{:S(2)}, u32[]{:S(2)}) collective-permute-start(bf16[768,128]{1,0:T(8,128)(2,1)S(1)} %get-tuple-element.28.a), channel_id=1, source_target_pairs={{0,2},{1,3},{2,0},{3,1},{4,6},{5,7},{6,4},{7,5},{8,10},{9,11},{10,... | collective-permute-start | bytes 589832 | tf_op jit(solution)/shard_map/ppermute | solution.py:303
  19.1 2.5 %collective-permute-start.4 = (bf16[1088,128]{1,0:T(8,128)(2,1)S(1)}, bf16[1088,128]{1,0:T(8,128)(2,1)S(1)}, u32[]{:S(2)}, u32[]{:S(2)}) collective-permute-start(bf16[1088,128]{1,0:T(8,128)(2,1)S(1)} %get-tuple-element.29.b), channel_id=1, source_target_pairs={{0,4},{1,5},{2,6},{3,7},{4,0},{5,1},{6,2},{7,3},{8,12},{9,13},{10,... | collective-permute-start | bytes 835592 | tf_op jit(solution)/shard_map/ppermute | solution.py:303
  21.5 0.0 collective-permute-start.5
  21.5 3.0 %collective-permute-done.6.one.refs_4_ = bf16[512,128]{1,0:T(8,128)(2,1)S(1)} collective-permute-done((bf16[512,128]{1,0:T(8,128)(2,1)S(1)}, bf16[512,128]{1,0:T(8,128)(2,1)S(1)}, u32[]{:S(2)}, u32[]{:S(2)}) %collective-permute-start.6) | collective-permute-done | bytes 131104 | tf_op jit(solution)/shard_map/ppermute | solution.py:303
  24.6 3.6 %collective-permute-done.7.two.refs_5_ = bf16[512,128]{1,0:T(8,128)(2,1)S(1)} collective-permute-done((bf16[512,128]{1,0:T(8,128)(2,1)S(1)}, bf16[512,128]{1,0:T(8,128)(2,1)S(1)}, u32[]{:S(2)}, u32[]{:S(2)}) %collective-permute-start.7) | collective-permute-done | bytes 131104 | tf_op jit(solution)/shard_map/ppermute | solution.py:303
  28.1 0.0 copy-start.1
  28.1 0.6 %collective-permute-start.8 = (bf16[512,128]{1,0:T(8,128)(2,1)S(1)}, bf16[512,128]{1,0:T(8,128)(2,1)S(1)}, u32[]{:S(2)}, u32[]{:S(2)}) collective-permute-start(bf16[512,128]{1,0:T(8,128)(2,1)S(1)} %shard_map.107), channel_id=1, source_target_pairs={{0,2},{1,3},{2,0},{3,1},{4,6},{5,7},{6,4},{7,5},{8,10},{9,11},{10,... | collective-permute-start | bytes 393224 | tf_op jit(solution)/shard_map/ppermute | solution.py:303
  28.7 4.5 %collective-permute-done.8.refs_6_ = bf16[512,128]{1,0:T(8,128)(2,1)S(1)} collective-permute-done((bf16[512,128]{1,0:T(8,128)(2,1)S(1)}, bf16[512,128]{1,0:T(8,128)(2,1)S(1)}, u32[]{:S(2)}, u32[]{:S(2)}) %collective-permute-start.8) | collective-permute-done | bytes 131104 | tf_op jit(solution)/shard_map/ppermute | solution.py:303
  33.2 0.0 collective-permute-done.3.refs_3_.far_a
  33.2 0.0 copy-start
  33.2 0.0 collective-permute-done.4.far_b
  33.2 0.0 collective-permute-done.5.core
  33.3 0.1 collective-permute-start.9
  33.4 0.0 copy-done.1
  33.4 1.0 %shard_map.110 = (bf16[256,1024]{1,0:T(8,128)(2,1)S(1)}, bf16[256,1024]{1,0:T(8,128)(2,1)S(1)}, bf16[1024,512]{1,0:T(8,128)(2,1)S(1)}, bf16[8,128,128]{2,1,0:T(8...) custom-call(bf16[768,128]{1,0:T(8,128)(2,1)S(1)} %get-tuple-element.28.a, ...), custom_call_target="tpu_custom_call" | custom-call | tf_op jit(solution)/shard_map/pallas_call | solution.py:281
  34.4 1.1 %collective-permute-done.9.pair = bf16[2624,128]{1,0:T(8,128)(2,1)S(1)} collective-permute-done((bf16[2624,128]{1,0:T(8,128)(2,1)S(1)}, bf16[2624,128]{1,0:T(8,128)(2,1)S(1)}, u32[]{:S(2)}, u32[]{:S(2)}) %collective-permute-start.9) | collective-permute-done | bytes 671776 | tf_op jit(solution)/shard_map/ppermute | solution.py:303
  35.5 0.0 copy-done
  35.5 7.2 %shard_map.111 = (bf16[1,128,1024]{2,1,0:T(8,128)(2,1)}, f32[64,1024]{1,0:T(8,128)}, f32[64,1024]{1,0:T(8,128)}) custom-call(bf16[1600,128]{1,0:T(8,128)(2,1)S(1)} %collective-permute-done.5.core, bf16[2624,128]{1,0:T(8,128)(2,1)S(1)} %collective-permute-done.9.pair, bf16[256,128]{1,0:T(8,128)(2,1)S(1)} %get-tuple-element.34.refs_0_, ...), custom_call_target="tpu_custom_call" | custom-call | tf_op jit(solution)/shard_map/pallas_call | solution.py:281
  (4 shorter events, 0.1 us)
Async XLA Ops:
  1.6 9.2 %collective-permute-start = (bf16[400,128]{1,0:T(8,128)(2,1)S(1)}, bf16[400,128]{1,0:T(8,128)(2,1)S(1)}, u32[]{:S(2)}, u32[]{:S(2)}) collective-permute-start(bf16[400,128]{1,0:T(8,128)(2,1)S(1)} %shard_map.103.piece), channel_id=1, source_target_pairs={{0,8},{1,9},{2,10},{3,11},{4,12},{5,13},{6,14},{7,15},{8,0},{9,1},... | collective-permute-start | bytes 307208 | tf_op jit(solution)/shard_map/ppermute | solution.py:303
  10.8 7.6 %collective-permute-start.2 = (bf16[800,128]{1,0:T(8,128)(2,1)S(1)}, bf16[800,128]{1,0:T(8,128)(2,1)S(1)}, u32[]{:S(2)}, u32[]{:S(2)}) collective-permute-start(bf16[800,128]{1,0:T(8,128)(2,1)S(1)} %get-tuple-element.27.half_b), channel_id=1, source_target_pairs={{0,2},{1,3},{2,0},{3,1},{4,6},{5,7},{6,4},{7,5},{8,10},{9,11},{10,... | collective-permute-start | bytes 614408 | tf_op jit(solution)/shard_map/ppermute | solution.py:303
  12.4 6.0 %collective-permute-start.1 = (bf16[768,128]{1,0:T(8,128)(2,1)S(1)}, bf16[768,128]{1,0:T(8,128)(2,1)S(1)}, u32[]{:S(2)}, u32[]{:S(2)}) collective-permute-start(bf16[768,128]{1,0:T(8,128)(2,1)S(1)} %get-tuple-element.26.half_a), channel_id=1, source_target_pairs={{0,4},{1,5},{2,6},{3,7},{4,0},{5,1},{6,2},{7,3},{8,12},{9,13},{10,... | collective-permute-start | bytes 589832 | tf_op jit(solution)/shard_map/ppermute | solution.py:303
  13.1 11.5 %collective-permute-start.6 = (bf16[512,128]{1,0:T(8,128)(2,1)S(1)}, bf16[512,128]{1,0:T(8,128)(2,1)S(1)}, u32[]{:S(2)}, u32[]{:S(2)}) collective-permute-start(bf16[512,128]{1,0:T(8,128)(2,1)S(1)} %get-tuple-element.35), channel_id=1, source_target_pairs={{0,12},{1,13},{2,14},{3,15},{4,8},{5,9},{6,10},{7,11},{8,4},{9,5},... | collective-permute-start | bytes 393224 | tf_op jit(solution)/shard_map/ppermute | solution.py:303
  15.9 12.2 %collective-permute-start.7 = (bf16[512,128]{1,0:T(8,128)(2,1)S(1)}, bf16[512,128]{1,0:T(8,128)(2,1)S(1)}, u32[]{:S(2)}, u32[]{:S(2)}) collective-permute-start(bf16[512,128]{1,0:T(8,128)(2,1)S(1)} %get-tuple-element.36), channel_id=1, source_target_pairs={{0,8},{1,9},{2,10},{3,11},{4,12},{5,13},{6,14},{7,15},{8,0},{9,1},... | collective-permute-start | bytes 393224 | tf_op jit(solution)/shard_map/ppermute | solution.py:303
  18.5 14.7 %collective-permute-start.3 = (bf16[768,128]{1,0:T(8,128)(2,1)S(1)}, bf16[768,128]{1,0:T(8,128)(2,1)S(1)}, u32[]{:S(2)}, u32[]{:S(2)}) collective-permute-start(bf16[768,128]{1,0:T(8,128)(2,1)S(1)} %get-tuple-element.28.a), channel_id=1, source_target_pairs={{0,2},{1,3},{2,0},{3,1},{4,6},{5,7},{6,4},{7,5},{8,10},{9,11},{10,... | collective-permute-start | bytes 589832 | tf_op jit(solution)/shard_map/ppermute | solution.py:303
  19.1 14.2 %collective-permute-start.4 = (bf16[1088,128]{1,0:T(8,128)(2,1)S(1)}, bf16[1088,128]{1,0:T(8,128)(2,1)S(1)}, u32[]{:S(2)}, u32[]{:S(2)}) collective-permute-start(bf16[1088,128]{1,0:T(8,128)(2,1)S(1)} %get-tuple-element.29.b), channel_id=1, source_target_pairs={{0,4},{1,5},{2,6},{3,7},{4,0},{5,1},{6,2},{7,3},{8,12},{9,13},{10,... | collective-permute-start | bytes 835592 | tf_op jit(solution)/shard_map/ppermute | solution.py:303
  21.5 11.7 %collective-permute-start.5 = (bf16[1600,128]{1,0:T(8,128)(2,1)S(1)}, bf16[1600,128]{1,0:T(8,128)(2,1)S(1)}, u32[]{:S(2)}, u32[]{:S(2)}) collective-permute-start(bf16[1600,128]{1,0:T(8,128)(2,1)S(1)} %get-tuple-element.30), channel_id=1, source_target_pairs={{0,1},{1,0},{2,3},{3,2},{4,5},{5,4},{6,7},{7,6},{8,9},{9,8},{10,11... | collective-permute-start | bytes 1228808 | tf_op jit(solution)/shard_map/ppermute | solution.py:303
  28.1 5.2 %copy-start.1 = (bf16[1024,1024]{1,0:T(8,128)(2,1)S(1)}, bf16[1024,1024]{1,0:T(8,128)(2,1)}, u32[]{:S(2)}) copy-start(bf16[1024,1024]{1,0:T(8,128)(2,1)} %refs_13_.1) | copy-start | bytes 6291460
  28.1 5.0 %collective-permute-start.8 = (bf16[512,128]{1,0:T(8,128)(2,1)S(1)}, bf16[512,128]{1,0:T(8,128)(2,1)S(1)}, u32[]{:S(2)}, u32[]{:S(2)}) collective-permute-start(bf16[512,128]{1,0:T(8,128)(2,1)S(1)} %shard_map.107), channel_id=1, source_target_pairs={{0,2},{1,3},{2,0},{3,1},{4,6},{5,7},{6,4},{7,5},{8,10},{9,11},{10,... | collective-permute-start | bytes 393224 | tf_op jit(solution)/shard_map/ppermute | solution.py:303
  33.2 2.3 %copy-start = (bf16[1024,1024]{1,0:T(8,128)(2,1)S(1)}, bf16[1024,1024]{1,0:T(8,128)(2,1)}, u32[]{:S(2)}) copy-start(bf16[1024,1024]{1,0:T(8,128)(2,1)} %refs_14_.1) | copy-start | bytes 6291460
  33.3 2.2 %collective-permute-start.9 = (bf16[2624,128]{1,0:T(8,128)(2,1)S(1)}, bf16[2624,128]{1,0:T(8,128)(2,1)S(1)}, u32[]{:S(2)}, u32[]{:S(2)}) collective-permute-start(bf16[2624,128]{1,0:T(8,128)(2,1)S(1)} %shard_map.109), channel_id=1, source_target_pairs={{0,1},{1,0},{2,3},{3,2},{4,5},{5,4},{6,7},{7,6},{8,9},{9,8},{10,11... | collective-permute-start | bytes 2015240 | tf_op jit(solution)/shard_map/ppermute | solution.py:303

commit v13 on v12

--- a/solution.py
+++ b/solution.py
@@ -19,8 +19,10 @@
 Z2, Z1, Y, CORE = 8, 4, 2, 1
 GROUP = 16
 HINT = (0, 8 * 10**9)
-SENT = ((0, CORE), (Y, Y | CORE)) + tuple(
-    tuple(z | slot for slot in range(4)) for z in (Z1, Z2 | Z1, Z2)
+SENT = (
+    ((0, CORE), (Y, Y | CORE), (Z1, Z1 | CORE, Z1 | Y, Z1 | Y | CORE))
+    + tuple((z, z | CORE) for z in (Z2 | Z1, Z2))
+    + tuple((z | Y, z | Y | CORE) for z in (Z2 | Z1, Z2))
 )
 HALF_A = ((0, Z2, Z1, Z1 | Z2), (Y, Y | Z2, Y | Z1, Y | Z1 | Z2))
 HALF_B = ((0, Z2, Y, Y | Z2), (Z1, Z1 | Z2, Z1 | Y, Z1 | Y | Z2))
@@ -95,7 +97,10 @@
     return at
 
 
-def split_kernel(piece, came, columns_y, columns_z, half_a, half_b):
+def split_kernel(piece, came, columns_y, columns_z, *refs):
+    near_one, near_two, across_one, across_two, half_a, half_b, one, two = refs
+    stack(one, 0, near_one, across_one)
+    stack(two, 0, near_two, across_two)
     cut = (half_a.shape[0] - columns_z.shape[0]) // 2
     stack(half_a, 0, piece.at[:cut], came.at[:cut], columns_z)
     stack(half_b, 0, piece.at[cut:], came.at[cut:], columns_y)
@@ -109,12 +114,7 @@
     stack(both, 0, out_a.at[: 2 * cut], out_b)
 
 
-def turn_kernel(one, two, out):
-    half = out.shape[0] // 2
-    stack(out, 0, one.at[half:], two.at[half:])
-
-
-def block_of(slot, rows, own, came_a, came_b, far_a, one, two, turn):
+def block_of(slot, rows, own, came_a, came_b, far_a, one, two):
     ref, at = {
         0: (own, 0),
         Y: (came_b, came_b.shape[0] - 2 * rows),
@@ -122,17 +122,23 @@
         Z1 | Y: (far_a, far_a.shape[0] - 2 * rows),
         Z2 | Z1: (one, 0),
         Z2: (two, 0),
-        Z2 | Z1 | Y: (turn, 0),
-        Z2 | Y: (turn, 2 * rows),
+        Z2 | Z1 | Y: (one, 2 * rows),
+        Z2 | Y: (two, 2 * rows),
     }[slot - slot % 2]
     at += slot % 2 * rows
     return ref.at[at : at + rows]
 
 
-def other_kernel(*refs):
-    *refs, out = refs
-    rows = out.shape[0] * 2 // GROUP
-    stack(out, 0, *[block_of(slot, rows, *refs) for slot in range(1, GROUP, 2)])
+def far_kernel(one, two, out):
+    rows = out.shape[0] // 4
+    odd = [slice(k * rows, (k + 1) * rows) for k in (1, 3)]
+    stack(out, 0, *[ref.at[span] for ref in (two, one) for span in odd])
+
+
+def other_kernel(own, came_a, came_b, far_a, late, out):
+    rows = late.shape[0] // 4
+    near = [block_of(slot, rows, own, came_a, came_b, far_a, None, None) for slot in range(1, Z2, 2)]
+    stack(out, 0, *near, late)
 
 
 def pair_kernel(far_a, far_b, columns, out):
@@ -196,7 +202,7 @@
 
 
 def step_kernel(own, slots, cut, rest, core, pair, *refs):
-    blocks, refs = refs[:7], refs[7:]
+    blocks, refs = refs[:6], refs[6:]
     early_feat, early_lifted, early_spread, early_adj, early_meta, w_piece = refs[:6]
     w_first, w_second, output, grad_first, grad_second = refs[6:11]
     hidden, spread, feat, adj, meta, dout, dpre, lifted, result, grads, second, sems = refs[11:]
@@ -313,7 +319,7 @@
     )
     came = swap(piece, Z2)
     cotangent, _ = lax.optimization_barrier((cotangent, piece))
-    own_columns, columns_y, columns_z, one, two = call(
+    own_columns, columns_y, columns_z, *parts = call(
         columns_kernel,
         (cotangent, w_second),
         [((len(x) * 2 * each, rows), BF16) for x in SENT],
@@ -322,12 +328,14 @@
         + [pltpu.SemaphoreType.DMA((1 + CHUNKS,))],
         stay=True,
     )
+    parts[2:] = [swap(x, Y) for x in parts[2:]]
+    a, b, one, two = call(
+        split_kernel,
+        (piece, came, columns_y, columns_z, *parts),
+        [((2 * cut + 8 * each, LANES), BF16), ((2 * rest + 4 * each, LANES), BF16)]
+        + [((8 * each, rows), BF16)] * 2,
+    )
     one, two = swap(one, Z2 | Z1), swap(two, Z2)
-    a, b = call(
-        split_kernel,
-        (piece, came, columns_y, columns_z),
-        [((2 * cut + 8 * each, LANES), BF16), ((2 * rest + 4 * each, LANES), BF16)],
-    )
     came_a, came_b = swap(a, Z1), swap(b, Y)
     a, b, both = call(
         join_kernel,
@@ -336,10 +344,9 @@
         flops=HINT[0],
     )
     far_b, far_a, core = swap(b, Z1), swap(a, Y), swap(both, CORE)
-    (turn,) = call(turn_kernel, (one, two), [((8 * each, rows), BF16)], flops=HINT[1])
-    turn = swap(turn, Y)
-    blocks = (own_columns, came_a, came_b, far_a, one, two, turn)
-    (others,) = call(other_kernel, blocks, [((half * 2 * each, rows), BF16)])
+    blocks = (own_columns, came_a, came_b, far_a, one, two)
+    (late,) = call(far_kernel, (one, two), [((8 * each, rows), BF16)], flops=HINT[1])
+    (others,) = call(other_kernel, (*blocks[:4], late), [((half * 2 * each, rows), BF16)])
     far_a, far_b, core = lax.optimization_barrier((far_a, far_b, core))
     (pair,) = call(
         pair_kernel,

time: 42.8 us -> 44.1 us (1.030)
  waiting for transfers between devices: 16.3 us -> 18.9 us
  starting transfers between devices: 13.5 us -> 12.2 us
    ppermute x10 -> x11, waiting for transfers between devices: 16.3 us -> 18.9 us  [swap(): return lax.ppermute(x, 'grp', [(i, i ^ slot) for i in range(GROUP)])]
    ppermute x10 -> x11, starting transfers between devices: 13.5 us -> 12.2 us  [swap(): return lax.ppermute(x, 'grp', [(i, i ^ slot) for i in range(GROUP)])]
  transfers between devices with their start and end apart: 10 -> 11, of which waited for: 6 -> 7; matrix products, arithmetic and copies ran while one was open for 0% -> 0% of each run, Pallas kernels for 9% -> 9%
where the time goes in v13:
time: 44.1 us; the launch traced here: 43.9 us
  waiting for transfers between devices  18.9 us (43%)
  starting transfers between devices  12.2 us (28%)
  Pallas kernels  12.1 us (27%)
  between operations  0.72 us (2%)
    ppermute x11, waiting for transfers between devices, swap(): return lax.ppermute(x, 'grp', [(i, i ^ slot) for i in range(GROUP)])  18.9 us
    ppermute x11, starting transfers between devices, swap(): return lax.ppermute(x, 'grp', [(i, i ^ slot) for i in range(GROUP)])  12.2 us
    pallas_call x9, Pallas kernels, call(): pl.pallas_call(kernel, out_shape=tuple((jax.ShapeDtypeStruct(*out) for ou...  12.1 us
  transfers between devices with their start and end apart: 11, of which 7 were waited for; matrix products, arithmetic and copies ran while one was open for 0% of the time, Pallas kernels for 9%

profile of v13, /device:TPU:0, one launch (start us, length us, event | category | flops | bytes accessed | tf_op | source)
XLA Modules:
  0.0 43.9 jit_solution(4766020153719299753)
XLA Ops:
  0.6 0.9 %shard_map.103.piece = bf16[400,128]{1,0:T(8,128)(2,1)S(1)} custom-call(s32[2]{0:T(128)} %counts.1, s32[1,8]{1,0:T(1,128)} %owner.1, s32[1,8]{1,0:T(1,128)} %local.1, bf16[2,16,1024]{2,1,0:T(8,128)(2,1)} %features.1, bf16[1,128,128]{2,1,0:T(8,128)(2,1)} %adjacency.1), custom_call_target="tpu_custom_call" | custom-call | tf_op jit(solution)/shard_map/pallas_call | solution.py:287
  1.6 4.1 %collective-permute-start = (bf16[400,128]{1,0:T(8,128)(2,1)S(1)}, bf16[400,128]{1,0:T(8,128)(2,1)S(1)}, u32[]{:S(2)}, u32[]{:S(2)}) collective-permute-start(bf16[400,128]{1,0:T(8,128)(2,1)S(1)} %shard_map.103.piece), channel_id=1, source_target_pairs={{0,8},{1,9},{2,10},{3,11},{4,12},{5,13},{6,14},{7,15},{8,0},{9,1},... | collective-permute-start | bytes 307208 | tf_op jit(solution)/shard_map/ppermute | solution.py:309
  5.7 2.9 %shard_map.104 = (bf16[256,128]{1,0:T(8,128)(2,1)S(1)}, bf16[256,128]{1,0:T(8,128)(2,1)S(1)}, bf16[512,128]{1,0:T(8,128)(2,1)S(1)}, bf16[256,128]{1,0:T(8,128)(2...) custom-call(bf16[1,128,1024]{2,1,0:T(8,128)(2,1)} %cotangent, ...), custom_call_target="tpu_custom_call" | custom-call | tf_op jit(solution)/shard_map/pallas_call | solution.py:287
  8.6 1.6 %collective-permute-start.1 = (bf16[256,128]{1,0:T(8,128)(2,1)S(1)}, bf16[256,128]{1,0:T(8,128)(2,1)S(1)}, u32[]{:S(2)}, u32[]{:S(2)}) collective-permute-start(bf16[256,128]{1,0:T(8,128)(2,1)S(1)} %get-tuple-element.32), channel_id=1, source_target_pairs={{0,2},{1,3},{2,0},{3,1},{4,6},{5,7},{6,4},{7,5},{8,10},{9,11},{10,... | collective-permute-start | bytes 196616 | tf_op jit(solution)/shard_map/ppermute | solution.py:309
  10.1 0.5 %collective-permute-start.2 = (bf16[256,128]{1,0:T(8,128)(2,1)S(1)}, bf16[256,128]{1,0:T(8,128)(2,1)S(1)}, u32[]{:S(2)}, u32[]{:S(2)}) collective-permute-start(bf16[256,128]{1,0:T(8,128)(2,1)S(1)} %get-tuple-element.33), channel_id=1, source_target_pairs={{0,2},{1,3},{2,0},{3,1},{4,6},{5,7},{6,4},{7,5},{8,10},{9,11},{10,... | collective-permute-start | bytes 196616 | tf_op jit(solution)/shard_map/ppermute | solution.py:309
  10.6 2.8 %collective-permute-done.1.refs_2_ = bf16[256,128]{1,0:T(8,128)(2,1)S(1)} collective-permute-done((bf16[256,128]{1,0:T(8,128)(2,1)S(1)}, bf16[256,128]{1,0:T(8,128)(2,1)S(1)}, u32[]{:S(2)}, u32[]{:S(2)}) %collective-permute-start.1) | collective-permute-done | bytes 65568 | tf_op jit(solution)/shard_map/ppermute | solution.py:309
  13.4 1.0 %collective-permute-done.2.refs_3_ = bf16[256,128]{1,0:T(8,128)(2,1)S(1)} collective-permute-done((bf16[256,128]{1,0:T(8,128)(2,1)S(1)}, bf16[256,128]{1,0:T(8,128)(2,1)S(1)}, u32[]{:S(2)}, u32[]{:S(2)}) %collective-permute-start.2) | collective-permute-done | bytes 65568 | tf_op jit(solution)/shard_map/ppermute | solution.py:309
  14.4 0.0 collective-permute-done.came
  14.5 0.8 %collective-permute-start.4 = (bf16[800,128]{1,0:T(8,128)(2,1)S(1)}, bf16[800,128]{1,0:T(8,128)(2,1)S(1)}, u32[]{:S(2)}, u32[]{:S(2)}) collective-permute-start(bf16[800,128]{1,0:T(8,128)(2,1)S(1)} %get-tuple-element.35.half_b), channel_id=1, source_target_pairs={{0,2},{1,3},{2,0},{3,1},{4,6},{5,7},{6,4},{7,5},{8,10},{9,11},{10,... | collective-permute-start | bytes 614408 | tf_op jit(solution)/shard_map/ppermute | solution.py:309
  15.2 1.6 %collective-permute-start.3 = (bf16[768,128]{1,0:T(8,128)(2,1)S(1)}, bf16[768,128]{1,0:T(8,128)(2,1)S(1)}, u32[]{:S(2)}, u32[]{:S(2)}) collective-permute-start(bf16[768,128]{1,0:T(8,128)(2,1)S(1)} %get-tuple-element.34.half_a), channel_id=1, source_target_pairs={{0,4},{1,5},{2,6},{3,7},{4,0},{5,1},{6,2},{7,3},{8,12},{9,13},{10,... | collective-permute-start | bytes 589832 | tf_op jit(solution)/shard_map/ppermute | solution.py:309
  16.8 0.2 collective-permute-start.8
  17.0 1.7 %collective-permute-start.9 = (bf16[512,128]{1,0:T(8,128)(2,1)S(1)}, bf16[512,128]{1,0:T(8,128)(2,1)S(1)}, u32[]{:S(2)}, u32[]{:S(2)}) collective-permute-start(bf16[512,128]{1,0:T(8,128)(2,1)S(1)} %get-tuple-element.44), channel_id=1, source_target_pairs={{0,8},{1,9},{2,10},{3,11},{4,12},{5,13},{6,14},{7,15},{8,0},{9,1},... | collective-permute-start | bytes 393224 | tf_op jit(solution)/shard_map/ppermute | solution.py:309
  18.7 7.6 %collective-permute-done.3.came_a.refs_1_ = bf16[768,128]{1,0:T(8,128)(2,1)S(1)} collective-permute-done((bf16[768,128]{1,0:T(8,128)(2,1)S(1)}, bf16[768,128]{1,0:T(8,128)(2,1)S(1)}, u32[]{:S(2)}, u32[]{:S(2)}) %collective-permute-start.3) | collective-permute-done | bytes 196640 | tf_op jit(solution)/shard_map/ppermute | solution.py:309
  26.3 0.0 collective-permute-done.4.came_b.refs_2_
  26.3 0.1 shard_map.106
  26.4 1.6 %collective-permute-start.5 = (bf16[768,128]{1,0:T(8,128)(2,1)S(1)}, bf16[768,128]{1,0:T(8,128)(2,1)S(1)}, u32[]{:S(2)}, u32[]{:S(2)}) collective-permute-start(bf16[768,128]{1,0:T(8,128)(2,1)S(1)} %get-tuple-element.36.a), channel_id=1, source_target_pairs={{0,2},{1,3},{2,0},{3,1},{4,6},{5,7},{6,4},{7,5},{8,10},{9,11},{10,... | collective-permute-start | bytes 589832 | tf_op jit(solution)/shard_map/ppermute | solution.py:309
  28.0 0.0 collective-permute-start.6
  28.0 0.0 collective-permute-start.7
  28.0 0.0 collective-permute-done.8.one.refs_4_
  28.0 0.9 %collective-permute-done.9.two.refs_5_ = bf16[512,128]{1,0:T(8,128)(2,1)S(1)} collective-permute-done((bf16[512,128]{1,0:T(8,128)(2,1)S(1)}, bf16[512,128]{1,0:T(8,128)(2,1)S(1)}, u32[]{:S(2)}, u32[]{:S(2)}) %collective-permute-start.9) | collective-permute-done | bytes 131104 | tf_op jit(solution)/shard_map/ppermute | solution.py:309
  28.9 0.0 copy-start.1
  28.9 3.2 %collective-permute-done.5.far_a.refs_3_ = bf16[768,128]{1,0:T(8,128)(2,1)S(1)} collective-permute-done((bf16[768,128]{1,0:T(8,128)(2,1)S(1)}, bf16[768,128]{1,0:T(8,128)(2,1)S(1)}, u32[]{:S(2)}, u32[]{:S(2)}) %collective-permute-start.5) | collective-permute-done | bytes 196640 | tf_op jit(solution)/shard_map/ppermute | solution.py:309
  32.1 0.0 copy-start
  32.1 2.4 %collective-permute-done.6.far_b = bf16[1088,128]{1,0:T(8,128)(2,1)S(1)} collective-permute-done((bf16[1088,128]{1,0:T(8,128)(2,1)S(1)}, bf16[1088,128]{1,0:T(8,128)(2,1)S(1)}, u32[]{:S(2)}, u32[]{:S(2)}) %collective-permute-start.6) | collective-permute-done | bytes 278560 | tf_op jit(solution)/shard_map/ppermute | solution.py:309
  34.5 0.0 collective-permute-done.7.core
  34.6 0.1 collective-permute-start.10
  34.7 0.0 copy-done.1
  34.7 1.0 %shard_map.110 = (bf16[256,1024]{1,0:T(8,128)(2,1)S(1)}, bf16[256,1024]{1,0:T(8,128)(2,1)S(1)}, bf16[1024,512]{1,0:T(8,128)(2,1)S(1)}, bf16[8,128,128]{2,1,0:T(8...) custom-call(bf16[768,128]{1,0:T(8,128)(2,1)S(1)} %get-tuple-element.36.a, ...), custom_call_target="tpu_custom_call" | custom-call | tf_op jit(solution)/shard_map/pallas_call | solution.py:287
  35.7 1.1 %collective-permute-done.10.pair = bf16[2624,128]{1,0:T(8,128)(2,1)S(1)} collective-permute-done((bf16[2624,128]{1,0:T(8,128)(2,1)S(1)}, bf16[2624,128]{1,0:T(8,128)(2,1)S(1)}, u32[]{:S(2)}, u32[]{:S(2)}) %collective-permute-start.10) | collective-permute-done | bytes 671776 | tf_op jit(solution)/shard_map/ppermute | solution.py:309
  36.8 0.0 copy-done
  36.8 7.1 %shard_map.111 = (bf16[1,128,1024]{2,1,0:T(8,128)(2,1)}, f32[64,1024]{1,0:T(8,128)}, f32[64,1024]{1,0:T(8,128)}) custom-call(bf16[1600,128]{1,0:T(8,128)(2,1)S(1)} %collective-permute-done.7.core, bf16[2624,128]{1,0:T(8,128)(2,1)S(1)} %collective-permute-done.10.pair, bf16[256,128]{1,0:T(8,128)(2,1)S(1)} %get-tuple-element.42.own.refs_0_, ...), custom_call_target="tpu_custom_call" | custom-call | tf_op jit(solution)/shard_map/pallas_call | solution.py:287
  (4 shorter events, 0.1 us)
Async XLA Ops:
  1.6 12.8 %collective-permute-start = (bf16[400,128]{1,0:T(8,128)(2,1)S(1)}, bf16[400,128]{1,0:T(8,128)(2,1)S(1)}, u32[]{:S(2)}, u32[]{:S(2)}) collective-permute-start(bf16[400,128]{1,0:T(8,128)(2,1)S(1)} %shard_map.103.piece), channel_id=1, source_target_pairs={{0,8},{1,9},{2,10},{3,11},{4,12},{5,13},{6,14},{7,15},{8,0},{9,1},... | collective-permute-start | bytes 307208 | tf_op jit(solution)/shard_map/ppermute | solution.py:309
  8.6 4.9 %collective-permute-start.1 = (bf16[256,128]{1,0:T(8,128)(2,1)S(1)}, bf16[256,128]{1,0:T(8,128)(2,1)S(1)}, u32[]{:S(2)}, u32[]{:S(2)}) collective-permute-start(bf16[256,128]{1,0:T(8,128)(2,1)S(1)} %get-tuple-element.32), channel_id=1, source_target_pairs={{0,2},{1,3},{2,0},{3,1},{4,6},{5,7},{6,4},{7,5},{8,10},{9,11},{10,... | collective-permute-start | bytes 196616 | tf_op jit(solution)/shard_map/ppermute | solution.py:309
  10.1 4.3 %collective-permute-start.2 = (bf16[256,128]{1,0:T(8,128)(2,1)S(1)}, bf16[256,128]{1,0:T(8,128)(2,1)S(1)}, u32[]{:S(2)}, u32[]{:S(2)}) collective-permute-start(bf16[256,128]{1,0:T(8,128)(2,1)S(1)} %get-tuple-element.33), channel_id=1, source_target_pairs={{0,2},{1,3},{2,0},{3,1},{4,6},{5,7},{6,4},{7,5},{8,10},{9,11},{10,... | collective-permute-start | bytes 196616 | tf_op jit(solution)/shard_map/ppermute | solution.py:309
  14.5 11.8 %collective-permute-start.4 = (bf16[800,128]{1,0:T(8,128)(2,1)S(1)}, bf16[800,128]{1,0:T(8,128)(2,1)S(1)}, u32[]{:S(2)}, u32[]{:S(2)}) collective-permute-start(bf16[800,128]{1,0:T(8,128)(2,1)S(1)} %get-tuple-element.35.half_b), channel_id=1, source_target_pairs={{0,2},{1,3},{2,0},{3,1},{4,6},{5,7},{6,4},{7,5},{8,10},{9,11},{10,... | collective-permute-start | bytes 614408 | tf_op jit(solution)/shard_map/ppermute | solution.py:309
  15.2 11.1 %collective-permute-start.3 = (bf16[768,128]{1,0:T(8,128)(2,1)S(1)}, bf16[768,128]{1,0:T(8,128)(2,1)S(1)}, u32[]{:S(2)}, u32[]{:S(2)}) collective-permute-start(bf16[768,128]{1,0:T(8,128)(2,1)S(1)} %get-tuple-element.34.half_a), channel_id=1, source_target_pairs={{0,4},{1,5},{2,6},{3,7},{4,0},{5,1},{6,2},{7,3},{8,12},{9,13},{10,... | collective-permute-start | bytes 589832 | tf_op jit(solution)/shard_map/ppermute | solution.py:309
  16.8 11.2 %collective-permute-start.8 = (bf16[512,128]{1,0:T(8,128)(2,1)S(1)}, bf16[512,128]{1,0:T(8,128)(2,1)S(1)}, u32[]{:S(2)}, u32[]{:S(2)}) collective-permute-start(bf16[512,128]{1,0:T(8,128)(2,1)S(1)} %get-tuple-element.43), channel_id=1, source_target_pairs={{0,12},{1,13},{2,14},{3,15},{4,8},{5,9},{6,10},{7,11},{8,4},{9,5},... | collective-permute-start | bytes 393224 | tf_op jit(solution)/shard_map/ppermute | solution.py:309
  17.0 11.8 %collective-permute-start.9 = (bf16[512,128]{1,0:T(8,128)(2,1)S(1)}, bf16[512,128]{1,0:T(8,128)(2,1)S(1)}, u32[]{:S(2)}, u32[]{:S(2)}) collective-permute-start(bf16[512,128]{1,0:T(8,128)(2,1)S(1)} %get-tuple-element.44), channel_id=1, source_target_pairs={{0,8},{1,9},{2,10},{3,11},{4,12},{5,13},{6,14},{7,15},{8,0},{9,1},... | collective-permute-start | bytes 393224 | tf_op jit(solution)/shard_map/ppermute | solution.py:309
  26.4 5.7 %collective-permute-start.5 = (bf16[768,128]{1,0:T(8,128)(2,1)S(1)}, bf16[768,128]{1,0:T(8,128)(2,1)S(1)}, u32[]{:S(2)}, u32[]{:S(2)}) collective-permute-start(bf16[768,128]{1,0:T(8,128)(2,1)S(1)} %get-tuple-element.36.a), channel_id=1, source_target_pairs={{0,2},{1,3},{2,0},{3,1},{4,6},{5,7},{6,4},{7,5},{8,10},{9,11},{10,... | collective-permute-start | bytes 589832 | tf_op jit(solution)/shard_map/ppermute | solution.py:309
  28.0 6.5 %collective-permute-start.6 = (bf16[1088,128]{1,0:T(8,128)(2,1)S(1)}, bf16[1088,128]{1,0:T(8,128)(2,1)S(1)}, u32[]{:S(2)}, u32[]{:S(2)}) collective-permute-start(bf16[1088,128]{1,0:T(8,128)(2,1)S(1)} %get-tuple-element.37.b), channel_id=1, source_target_pairs={{0,4},{1,5},{2,6},{3,7},{4,0},{5,1},{6,2},{7,3},{8,12},{9,13},{10,... | collective-permute-start | bytes 835592 | tf_op jit(solution)/shard_map/ppermute | solution.py:309
  28.0 6.5 %collective-permute-start.7 = (bf16[1600,128]{1,0:T(8,128)(2,1)S(1)}, bf16[1600,128]{1,0:T(8,128)(2,1)S(1)}, u32[]{:S(2)}, u32[]{:S(2)}) collective-permute-start(bf16[1600,128]{1,0:T(8,128)(2,1)S(1)} %get-tuple-element.38), channel_id=1, source_target_pairs={{0,1},{1,0},{2,3},{3,2},{4,5},{5,4},{6,7},{7,6},{8,9},{9,8},{10,11... | collective-permute-start | bytes 1228808 | tf_op jit(solution)/shard_map/ppermute | solution.py:309
  28.9 5.8 %copy-start.1 = (bf16[1024,1024]{1,0:T(8,128)(2,1)S(1)}, bf16[1024,1024]{1,0:T(8,128)(2,1)}, u32[]{:S(2)}) copy-start(bf16[1024,1024]{1,0:T(8,128)(2,1)} %refs_12_.1) | copy-start | bytes 6291460
  32.1 4.7 %copy-start = (bf16[1024,1024]{1,0:T(8,128)(2,1)S(1)}, bf16[1024,1024]{1,0:T(8,128)(2,1)}, u32[]{:S(2)}) copy-start(bf16[1024,1024]{1,0:T(8,128)(2,1)} %refs_13_.1) | copy-start | bytes 6291460
  34.6 2.2 %collective-permute-start.10 = (bf16[2624,128]{1,0:T(8,128)(2,1)S(1)}, bf16[2624,128]{1,0:T(8,128)(2,1)S(1)}, u32[]{:S(2)}, u32[]{:S(2)}) collective-permute-start(bf16[2624,128]{1,0:T(8,128)(2,1)S(1)} %shard_map.109), channel_id=1, source_target_pairs={{0,1},{1,0},{2,3},{3,2},{4,5},{5,4},{6,7},{7,6},{8,9},{9,8},{10,11... | collective-permute-start | bytes 2015240 | tf_op jit(solution)/shard_map/ppermute | solution.py:309

commit v14 on v7

--- a/solution.py
+++ b/solution.py
@@ -13,7 +13,6 @@
 HBM = pl.BlockSpec(memory_space=pltpu.HBM)
 LANES = 128
 META = 16
-CHUNKS = 4
 LIMIT = 24 * 2**20
 SMALL = 8 * 2**20
 Z2, Z1, Y, CORE = 8, 4, 2, 1
@@ -31,28 +30,24 @@
     return lax.dot_general(a, b, (((1,), (1,)), ((), ())), preferred_element_type=F32)
 
 
-def prepare_kernel(counts, owner, local, features, adjacency, cotangent, w_second, *refs):
-    piece, near, across, count, own_by, own_at, feat, adj, cot, second, turned, back, sems = refs
-    own, slots, width = features.shape
-    rows = adjacency.shape[1]
-    each = width // GROUP
-    place = lax.axis_index("grp")
-    moves = [(features, feat), (adjacency, adj), (counts, count), (owner, own_by), (local, own_at)]
-    moves.append((cotangent, cot))
-    some = width // CHUNKS
-    for c in range(CHUNKS):
-        span = slice(c * some, (c + 1) * some)
-        moves.append((w_second.at[span], second.at[span]))
+def start_all(moves, sems):
     copies = [pltpu.make_async_copy(a, b, sems.at[i]) for i, (a, b) in enumerate(moves)]
     for copy in copies:
         copy.start()
-
+    return copies
+
+
+def pack_kernel(counts, owner, local, features, adjacency, piece, *scratch):
+    count, own_by, own_at, feat, adj, sems = scratch
+    own, slots, width = features.shape
+    rows = adjacency.shape[1]
     held = own * slots
+    copies = start_all(zip((features, adjacency, counts, owner, local), (feat, adj, count, own_by, own_at)), sems)
     slot = lax.broadcasted_iota(jnp.int32, (slots, LANES), 0)
     line = lax.broadcasted_iota(jnp.int32, (META, LANES), 0)
     pick = lax.broadcasted_iota(jnp.int32, (META, LANES), 1) // slots
     meta = jnp.zeros((META, LANES), jnp.int32)
-    for copy in copies[:5]:
+    for copy in copies:
         copy.wait()
     for i in range(own):
         live = slot < count[i]
@@ -67,12 +62,13 @@
     piece[at : at + rows, :] = adj[0]
     piece[at + rows : at + rows + META, :] = meta.astype(F32).astype(BF16)
 
-    copies[5].wait()
-    turned[...] = cot[0].astype(F32).T.astype(BF16)
-    for c in range(CHUNKS):
-        copies[6 + c].wait()
-        span = slice(c * some, (c + 1) * some)
-        back[span, :] = nt(second[span, :], cot[0]).astype(BF16)
+
+def product_kernel(cotangent, w_second, near, across, turned, back):
+    each = w_second.shape[0] // GROUP
+    place = lax.axis_index("grp")
+    cot = cotangent[0]
+    turned[...] = cot.astype(F32).T.astype(BF16)
+    back[...] = nt(w_second[...], cot).astype(BF16)
     for h, out in enumerate((near, across)):
         for i in range(out.shape[0] // (2 * each)):
             to = 4 * (i // 2) + 2 * h + i % 2
@@ -182,7 +178,7 @@
     sent, refs = dict(zip(FAR, refs)), refs[len(FAR) :]
     early_feat, early_lifted, early_spread, early_adj, early_meta, w_piece = refs[:6]
     w_first, w_second, output, grad_first, grad_second = refs[6:11]
-    hidden, spread, feat, adj, meta, dout, dpre, lifted = refs[11:]
+    hidden, spread, feat, adj, meta, dout, dpre, lifted, result, grads, second, sems = refs[11:]
     width = w_first.shape[0]
     held = own * slots
     rows = adj.shape[1]
@@ -212,19 +208,11 @@
 
     late = slice(first * held, GROUP * held)
     lifted[late, :] = nn(feat[late, :], w_first[...]).astype(BF16)
-    lifted_piece = nt(w_piece[...], feat[...]).astype(BF16)
     for p in range(first, GROUP):
         span = slice(p * rows, (p + 1) * rows)
         spread[span, :] = spread_of(place, held, slots, adj[p], picks[p : p + 1])
-    step = min(width, 2 * LANES)
-    for c in range(0, width, step):
-        half = 0.5 * nn(spread[...], lifted[:, c : c + step])
-        hidden[:, c : c + step] = (half + half * jnp.tanh(half)).astype(BF16)
+    lifted_piece = nt(w_piece[...], feat[...]).astype(BF16)
     pre_piece = nt(lifted_piece, spread[...])
-    live = jnp.broadcast_to(masks[0:1], (rows, LANES)).T[:, :1]
-    agg = nn(adj[0], (hidden[:rows, :].astype(F32) * live).astype(BF16)).astype(BF16)
-    output[0] = (nn(agg, w_second[...]) * live).astype(BF16)
-
     each = grad_first.shape[0]
     size = sent[0].shape[0]
     sent[Z1] = came.at[came.shape[0] - size :]
@@ -232,30 +220,51 @@
         p = place_of(slot)
         mask = masks[p : p + 1]
         span = slice(p * rows, (p + 1) * rows)
-        s, h = slot // 4, slot // 2 % 2
         if slot % 2:
-            at = deep + (2 * s + h) * 2 * each
+            at = deep + slot // 2 * 2 * each
             source = pair[at : at + 2 * each, :]
         else:
-            source = sent[4 * s][h * size // 2 : h * size // 2 + 2 * each, :]
+            at = slot // 2 % 2 * size // 2
+            source = sent[slot - slot % 4][at : at + 2 * each, :]
         back = nn((source.astype(F32) * mask).astype(BF16), adj[p]) * mask
         dout[:, span] = back[:each].astype(BF16)
         pre = pre_piece[:, span]
         sig = 0.5 + 0.5 * jnp.tanh(0.5 * pre)
         dpre[:, span] = (back[each:] * sig * (1.0 + pre * (1.0 - sig))).astype(BF16)
-    grad_second[...] = nn(dout[...], hidden[...])
-    moved = nn(dpre[...], spread[...])
-    grad_first[...] = nn(moved.astype(BF16), feat[...])
-
-
-def call(kernel, ins, outs, scratch=(), limit=SMALL, stay=False, flops=0):
+
+    chunk = min(width, 2 * LANES)
+    for c in range(0, width, chunk):
+        span = slice(c, c + chunk)
+        half = 0.5 * nn(spread[...], lifted[:, span])
+        hidden[:, span] = (half + half * jnp.tanh(half)).astype(BF16)
+        if c:
+            done = slice(c - chunk, c)
+            second[:, done] = nn(dout[...], hidden[:, done])
+        else:
+            moved = nn(dpre[...], spread[...])
+            grads[...] = nn(moved.astype(BF16), feat[...])
+            first_out = pltpu.make_async_copy(grads, grad_first, sems.at[0])
+            first_out.start()
+    live = jnp.broadcast_to(masks[0:1], (rows, LANES)).T[:, :1]
+    agg = nn(adj[0], (hidden[:rows, :].astype(F32) * live).astype(BF16)).astype(BF16)
+    result[0] = (nn(agg, w_second[...]) * live).astype(BF16)
+    output_out = pltpu.make_async_copy(result, output, sems.at[1])
+    output_out.start()
+    second[:, span] = nn(dout[...], hidden[:, span])
+    second_out = pltpu.make_async_copy(second, grad_second, sems.at[2])
+    second_out.start()
+    for copy in (first_out, output_out, second_out):
+        copy.wait()
+
+
+def call(kernel, ins, outs, scratch=(), limit=SMALL, stay=False, leave=False, flops=0):
     if stay:
         ins = [pltpu.with_memory_space_constraint(x, pltpu.HBM) for x in ins]
     return pl.pallas_call(
         kernel,
         out_shape=tuple(jax.ShapeDtypeStruct(*out) for out in outs),
         in_specs=[HBM if stay else VMEM] * len(ins),
-        out_specs=(VMEM,) * len(outs),
+        out_specs=(HBM if leave else VMEM,) * len(outs),
         scratch_shapes=list(scratch),
         compiler_params=pltpu.CompilerParams(vmem_limit_bytes=limit),
         cost_estimate=pl.CostEstimate(flops=flops, bytes_accessed=0, transcendentals=0),
@@ -275,15 +284,22 @@
     def swap(x, slot):
         return lax.ppermute(x, "grp", [(i, i ^ slot) for i in range(GROUP)])
 
-    piece, near, across = call(
-        prepare_kernel,
-        (counts, pick_owner, pick_local, features, adjacency, cotangent, w_second),
-        [((cut + rest, LANES), BF16)] + [((GROUP * each, rows), BF16)] * 2,
+    (piece,) = call(
+        pack_kernel,
+        (counts, pick_owner, pick_local, features, adjacency),
+        [((cut + rest, LANES), BF16)],
         [pltpu.SMEM(x.shape, jnp.int32) for x in (counts, pick_owner, pick_local)]
-        + [pltpu.VMEM(x.shape, BF16) for x in (features, adjacency, cotangent, w_second)]
-        + [pltpu.VMEM((width, rows), BF16)] * 2
-        + [pltpu.SemaphoreType.DMA((6 + CHUNKS,))],
+        + [pltpu.VMEM(x.shape, BF16) for x in (features, adjacency)]
+        + [pltpu.SemaphoreType.DMA((5,))],
         stay=True,
+        flops=10**10,
+    )
+    cotangent, _ = lax.optimization_barrier((cotangent, piece))
+    near, across = call(
+        product_kernel,
+        (cotangent, w_second),
+        [((GROUP * each, rows), BF16)] * 2,
+        [pltpu.VMEM((width, rows), BF16)] * 2,
     )
     came = swap(piece, Z2)
     across = swap(across, Y)
@@ -337,8 +353,13 @@
             pltpu.VMEM((each, GROUP * rows), BF16),
             pltpu.VMEM((each, GROUP * rows), BF16),
             pltpu.VMEM((total, width), BF16),
+            pltpu.VMEM((1, rows, width), BF16),
+            pltpu.VMEM((each, width), F32),
+            pltpu.VMEM((each, width), F32),
+            pltpu.SemaphoreType.DMA((3,)),
         ],
         LIMIT,
+        leave=True,
     )
 
 

time: 42.5 us -> 41.5 us (0.976)
  Pallas kernels: 11.6 us -> 10 us
  local copies, waits for them, and re-layouts: 0.01 us -> 0.62 us
    pallas_call x7 -> x8, Pallas kernels: 11.6 us -> 10 us  [call(): pl.pallas_call(kernel, out_shape=tuple((jax.ShapeDtypeStruct(*out) for ou...]
    unnamed x4 -> x6, local copies, waits for them, and re-layouts: 0.01 us -> 0.62 us
where the time goes in v14:
time: 41.5 us; the launch traced here: 40.9 us
  waiting for transfers between devices  16.3 us (39%)
  starting transfers between devices  13.2 us (32%)
  Pallas kernels  10 us (24%)
  between operations  0.73 us (2%)
  local copies, waits for them, and re-layouts  0.62 us (1%)
    ppermute x10, waiting for transfers between devices, swap(): return lax.ppermute(x, 'grp', [(i, i ^ slot) for i in range(GROUP)])  16.3 us
    ppermute x10, starting transfers between devices, swap(): return lax.ppermute(x, 'grp', [(i, i ^ slot) for i in range(GROUP)])  13.2 us
    pallas_call x8, Pallas kernels, call(): pl.pallas_call(kernel, out_shape=tuple((jax.ShapeDtypeStruct(*out) for ou...  10 us
  transfers between devices with their start and end apart: 10, of which 7 were waited for; matrix products, arithmetic and copies ran while one was open for 0% of the time, Pallas kernels for 3%

profile of v14, /device:TPU:0, one launch (start us, length us, event | category | flops | bytes accessed | tf_op | source)
XLA Modules:
  0.0 40.9 jit_solution(6392580191721893072)
XLA Ops:
  0.6 0.0 copy-start.2
  0.6 0.0 copy-start
  0.7 1.1 %shard_map.103.piece = bf16[400,128]{1,0:T(8,128)(2,1)S(1)} custom-call(s32[2]{0:T(128)} %counts.1, s32[1,8]{1,0:T(1,128)} %owner.1, s32[1,8]{1,0:T(1,128)} %local.1, bf16[2,16,1024]{2,1,0:T(8,128)(2,1)} %features.1, bf16[1,128,128]{2,1,0:T(8,128)(2,1)} %adjacency.1), custom_call_target="tpu_custom_call" | custom-call | flops 10000000000 | tf_op jit(solution)/shard_map/pallas_call | solution.py:263
  1.8 0.0 copy-done.2
  1.8 0.6 %copy-done = bf16[1024,1024]{1,0:T(8,128)(2,1)S(1)} copy-done((bf16[1024,1024]{1,0:T(8,128)(2,1)S(1)}, bf16[1024,1024]{1,0:T(8,128)(2,1)}, u32[]{:S(2)}) %copy-start) | copy-done | bytes 2097176
  2.4 0.7 %shard_map.104 = (bf16[1024,128]{1,0:T(8,128)(2,1)S(1)}, bf16[1024,128]{1,0:T(8,128)(2,1)S(1)}) custom-call(bf16[1,128,1024]{2,1,0:T(8,128)(2,1)S(1)} %copy-done.2, bf16[1024,1024]{1,0:T(8,128)(2,1)S(1)} %copy-done), custom_call_target="tpu_custom_call" | custom-call | tf_op jit(solution)/shard_map/pallas_call | solution.py:263
  3.1 3.0 %collective-permute-start.1 = (bf16[1024,128]{1,0:T(8,128)(2,1)S(1)}, bf16[1024,128]{1,0:T(8,128)(2,1)S(1)}, u32[]{:S(2)}, u32[]{:S(2)}) collective-permute-start(bf16[1024,128]{1,0:T(8,128)(2,1)S(1)} %get-tuple-element.25), channel_id=1, source_target_pairs={{0,2},{1,3},{2,0},{3,1},{4,6},{5,7},{6,4},{7,5},{8,10},{9,11},{10,... | collective-permute-start | bytes 786440 | tf_op jit(solution)/shard_map/ppermute | solution.py:285
  6.1 2.6 %collective-permute-start = (bf16[400,128]{1,0:T(8,128)(2,1)S(1)}, bf16[400,128]{1,0:T(8,128)(2,1)S(1)}, u32[]{:S(2)}, u32[]{:S(2)}) collective-permute-start(bf16[400,128]{1,0:T(8,128)(2,1)S(1)} %shard_map.103.piece), channel_id=1, source_target_pairs={{0,8},{1,9},{2,10},{3,11},{4,12},{5,13},{6,14},{7,15},{8,0},{9,1},... | collective-permute-start | bytes 307208 | tf_op jit(solution)/shard_map/ppermute | solution.py:285
  8.7 4.8 %collective-permute-done.came = bf16[400,128]{1,0:T(8,128)(2,1)S(1)} collective-permute-done((bf16[400,128]{1,0:T(8,128)(2,1)S(1)}, bf16[400,128]{1,0:T(8,128)(2,1)S(1)}, u32[]{:S(2)}, u32[]{:S(2)}) %collective-permute-start) | collective-permute-done | bytes 102432 | tf_op jit(solution)/shard_map/ppermute | solution.py:285
  13.6 0.0 collective-permute-done.1.across
  13.6 0.7 %collective-permute-start.2 = (bf16[896,128]{1,0:T(8,128)(2,1)S(1)}, bf16[896,128]{1,0:T(8,128)(2,1)S(1)}, u32[]{:S(2)}, u32[]{:S(2)}) collective-permute-start(bf16[896,128]{1,0:T(8,128)(2,1)S(1)} %get-tuple-element.26.beside), channel_id=1, source_target_pairs={{0,4},{1,5},{2,6},{3,7},{4,0},{5,1},{6,2},{7,3},{8,12},{9,13},{10,... | collective-permute-start | bytes 688136 | tf_op jit(solution)/shard_map/ppermute | solution.py:285
  14.4 2.9 %collective-permute-start.7 = (bf16[512,128]{1,0:T(8,128)(2,1)S(1)}, bf16[512,128]{1,0:T(8,128)(2,1)S(1)}, u32[]{:S(2)}, u32[]{:S(2)}) collective-permute-start(bf16[512,128]{1,0:T(8,128)(2,1)S(1)} %get-tuple-element.34), channel_id=1, source_target_pairs={{0,12},{1,13},{2,14},{3,15},{4,8},{5,9},{6,10},{7,11},{8,4},{9,5},... | collective-permute-start | bytes 393224 | tf_op jit(solution)/shard_map/ppermute | solution.py:285
  17.3 0.5 %collective-permute-start.8 = (bf16[512,128]{1,0:T(8,128)(2,1)S(1)}, bf16[512,128]{1,0:T(8,128)(2,1)S(1)}, u32[]{:S(2)}, u32[]{:S(2)}) collective-permute-start(bf16[512,128]{1,0:T(8,128)(2,1)S(1)} %get-tuple-element.35), channel_id=1, source_target_pairs={{0,8},{1,9},{2,10},{3,11},{4,12},{5,13},{6,14},{7,15},{8,0},{9,1},... | collective-permute-start | bytes 393224 | tf_op jit(solution)/shard_map/ppermute | solution.py:285
  17.7 0.7 %collective-permute-start.3 = (bf16[416,128]{1,0:T(8,128)(2,1)S(1)}, bf16[416,128]{1,0:T(8,128)(2,1)S(1)}, u32[]{:S(2)}, u32[]{:S(2)}) collective-permute-start(bf16[416,128]{1,0:T(8,128)(2,1)S(1)} %get-tuple-element.27.half_b), channel_id=1, source_target_pairs={{0,2},{1,3},{2,0},{3,1},{4,6},{5,7},{6,4},{7,5},{8,10},{9,11},{10,... | collective-permute-start | bytes 319496 | tf_op jit(solution)/shard_map/ppermute | solution.py:285
  18.5 4.0 %collective-permute-done.3.came_b = bf16[416,128]{1,0:T(8,128)(2,1)S(1)} collective-permute-done((bf16[416,128]{1,0:T(8,128)(2,1)S(1)}, bf16[416,128]{1,0:T(8,128)(2,1)S(1)}, u32[]{:S(2)}, u32[]{:S(2)}) %collective-permute-start.3) | collective-permute-done | bytes 106528 | tf_op jit(solution)/shard_map/ppermute | solution.py:285
  22.5 0.0 collective-permute-done.2.came
  22.5 0.1 shard_map.106
  22.5 0.1 collective-permute-start.6
  22.6 1.1 %collective-permute-start.5 = (bf16[832,128]{1,0:T(8,128)(2,1)S(1)}, bf16[832,128]{1,0:T(8,128)(2,1)S(1)}, u32[]{:S(2)}, u32[]{:S(2)}) collective-permute-start(bf16[832,128]{1,0:T(8,128)(2,1)S(1)} %get-tuple-element.29.b), channel_id=1, source_target_pairs={{0,4},{1,5},{2,6},{3,7},{4,0},{5,1},{6,2},{7,3},{8,12},{9,13},{10,... | collective-permute-start | bytes 638984 | tf_op jit(solution)/shard_map/ppermute | solution.py:285
  23.7 1.5 %collective-permute-start.4 = (bf16[768,128]{1,0:T(8,128)(2,1)S(1)}, bf16[768,128]{1,0:T(8,128)(2,1)S(1)}, u32[]{:S(2)}, u32[]{:S(2)}) collective-permute-start(bf16[768,128]{1,0:T(8,128)(2,1)S(1)} %get-tuple-element.28.a), channel_id=1, source_target_pairs={{0,2},{1,3},{2,0},{3,1},{4,6},{5,7},{6,4},{7,5},{8,10},{9,11},{10,... | collective-permute-start | bytes 589832 | tf_op jit(solution)/shard_map/ppermute | solution.py:285
  25.2 1.4 %collective-permute-done.7.refs_0_ = bf16[512,128]{1,0:T(8,128)(2,1)S(1)} collective-permute-done((bf16[512,128]{1,0:T(8,128)(2,1)S(1)}, bf16[512,128]{1,0:T(8,128)(2,1)S(1)}, u32[]{:S(2)}, u32[]{:S(2)}) %collective-permute-start.7) | collective-permute-done | bytes 131104 | tf_op jit(solution)/shard_map/ppermute | solution.py:285
  26.5 2.9 %collective-permute-done.8.refs_1_ = bf16[512,128]{1,0:T(8,128)(2,1)S(1)} collective-permute-done((bf16[512,128]{1,0:T(8,128)(2,1)S(1)}, bf16[512,128]{1,0:T(8,128)(2,1)S(1)}, u32[]{:S(2)}, u32[]{:S(2)}) %collective-permute-start.8) | collective-permute-done | bytes 131104 | tf_op jit(solution)/shard_map/ppermute | solution.py:285
  29.5 0.0 copy-start.1
  29.5 1.2 %collective-permute-done.4.far_a = bf16[768,128]{1,0:T(8,128)(2,1)S(1)} collective-permute-done((bf16[768,128]{1,0:T(8,128)(2,1)S(1)}, bf16[768,128]{1,0:T(8,128)(2,1)S(1)}, u32[]{:S(2)}, u32[]{:S(2)}) %collective-permute-start.4) | collective-permute-done | bytes 196640 | tf_op jit(solution)/shard_map/ppermute | solution.py:285
  30.6 0.9 %collective-permute-done.5.far_b = bf16[832,128]{1,0:T(8,128)(2,1)S(1)} collective-permute-done((bf16[832,128]{1,0:T(8,128)(2,1)S(1)}, bf16[832,128]{1,0:T(8,128)(2,1)S(1)}, u32[]{:S(2)}, u32[]{:S(2)}) %collective-permute-start.5) | collective-permute-done | bytes 213024 | tf_op jit(solution)/shard_map/ppermute | solution.py:285
  31.6 0.0 collective-permute-done.6.core
  31.6 0.1 collective-permute-start.9
  31.7 0.0 copy-done.1
  31.7 1.0 %shard_map.109 = (bf16[256,1024]{1,0:T(8,128)(2,1)S(1)}, bf16[256,1024]{1,0:T(8,128)(2,1)S(1)}, bf16[1024,512]{1,0:T(8,128)(2,1)S(1)}, bf16[8,128,128]{2,1,0:T(8...) custom-call(bf16[768,128]{1,0:T(8,128)(2,1)S(1)} %get-tuple-element.28.a, ...), custom_call_target="tpu_custom_call" | custom-call | tf_op jit(solution)/shard_map/pallas_call | solution.py:263
  32.7 1.1 %collective-permute-done.9.pair = bf16[2624,128]{1,0:T(8,128)(2,1)S(1)} collective-permute-done((bf16[2624,128]{1,0:T(8,128)(2,1)S(1)}, bf16[2624,128]{1,0:T(8,128)(2,1)S(1)}, u32[]{:S(2)}, u32[]{:S(2)}) %collective-permute-start.9) | collective-permute-done | bytes 671776 | tf_op jit(solution)/shard_map/ppermute | solution.py:285
  33.8 7.1 %shard_map.110 = (bf16[1,128,1024]{2,1,0:T(8,128)(2,1)}, f32[64,1024]{1,0:T(8,128)}, f32[64,1024]{1,0:T(8,128)}) custom-call(bf16[1600,128]{1,0:T(8,128)(2,1)S(1)} %collective-permute-done.6.core, bf16[2624,128]{1,0:T(8,128)(2,1)S(1)} %collective-permute-done.9.pair, bf16[896,128]{1,0:T(8,128)(2,1)S(1)} %collective-permute-done.2.came, ...), custom_call_target="tpu_custom_call" | custom-call | tf_op jit(solution)/shard_map/pallas_call | solution.py:263
  (3 shorter events, 0.1 us)
Async XLA Ops:
  0.6 1.1 %copy-start.2 = (bf16[1,128,1024]{2,1,0:T(8,128)(2,1)S(1)}, bf16[1,128,1024]{2,1,0:T(8,128)(2,1)}, u32[]{:S(2)}) copy-start(bf16[1,128,1024]{2,1,0:T(8,128)(2,1)} %cotangent) | copy-start | bytes 786436
  0.6 1.7 %copy-start = (bf16[1024,1024]{1,0:T(8,128)(2,1)S(1)}, bf16[1024,1024]{1,0:T(8,128)(2,1)}, u32[]{:S(2)}) copy-start(bf16[1024,1024]{1,0:T(8,128)(2,1)} %refs_10_.1) | copy-start | bytes 6291460
  3.1 10.5 %collective-permute-start.1 = (bf16[1024,128]{1,0:T(8,128)(2,1)S(1)}, bf16[1024,128]{1,0:T(8,128)(2,1)S(1)}, u32[]{:S(2)}, u32[]{:S(2)}) collective-permute-start(bf16[1024,128]{1,0:T(8,128)(2,1)S(1)} %get-tuple-element.25), channel_id=1, source_target_pairs={{0,2},{1,3},{2,0},{3,1},{4,6},{5,7},{6,4},{7,5},{8,10},{9,11},{10,... | collective-permute-start | bytes 786440 | tf_op jit(solution)/shard_map/ppermute | solution.py:285
  6.1 7.4 %collective-permute-start = (bf16[400,128]{1,0:T(8,128)(2,1)S(1)}, bf16[400,128]{1,0:T(8,128)(2,1)S(1)}, u32[]{:S(2)}, u32[]{:S(2)}) collective-permute-start(bf16[400,128]{1,0:T(8,128)(2,1)S(1)} %shard_map.103.piece), channel_id=1, source_target_pairs={{0,8},{1,9},{2,10},{3,11},{4,12},{5,13},{6,14},{7,15},{8,0},{9,1},... | collective-permute-start | bytes 307208 | tf_op jit(solution)/shard_map/ppermute | solution.py:285
  13.6 8.8 %collective-permute-start.2 = (bf16[896,128]{1,0:T(8,128)(2,1)S(1)}, bf16[896,128]{1,0:T(8,128)(2,1)S(1)}, u32[]{:S(2)}, u32[]{:S(2)}) collective-permute-start(bf16[896,128]{1,0:T(8,128)(2,1)S(1)} %get-tuple-element.26.beside), channel_id=1, source_target_pairs={{0,4},{1,5},{2,6},{3,7},{4,0},{5,1},{6,2},{7,3},{8,12},{9,13},{10,... | collective-permute-start | bytes 688136 | tf_op jit(solution)/shard_map/ppermute | solution.py:285
  14.4 12.2 %collective-permute-start.7 = (bf16[512,128]{1,0:T(8,128)(2,1)S(1)}, bf16[512,128]{1,0:T(8,128)(2,1)S(1)}, u32[]{:S(2)}, u32[]{:S(2)}) collective-permute-start(bf16[512,128]{1,0:T(8,128)(2,1)S(1)} %get-tuple-element.34), channel_id=1, source_target_pairs={{0,12},{1,13},{2,14},{3,15},{4,8},{5,9},{6,10},{7,11},{8,4},{9,5},... | collective-permute-start | bytes 393224 | tf_op jit(solution)/shard_map/ppermute | solution.py:285
  17.3 12.2 %collective-permute-start.8 = (bf16[512,128]{1,0:T(8,128)(2,1)S(1)}, bf16[512,128]{1,0:T(8,128)(2,1)S(1)}, u32[]{:S(2)}, u32[]{:S(2)}) collective-permute-start(bf16[512,128]{1,0:T(8,128)(2,1)S(1)} %get-tuple-element.35), channel_id=1, source_target_pairs={{0,8},{1,9},{2,10},{3,11},{4,12},{5,13},{6,14},{7,15},{8,0},{9,1},... | collective-permute-start | bytes 393224 | tf_op jit(solution)/shard_map/ppermute | solution.py:285
  17.7 4.7 %collective-permute-start.3 = (bf16[416,128]{1,0:T(8,128)(2,1)S(1)}, bf16[416,128]{1,0:T(8,128)(2,1)S(1)}, u32[]{:S(2)}, u32[]{:S(2)}) collective-permute-start(bf16[416,128]{1,0:T(8,128)(2,1)S(1)} %get-tuple-element.27.half_b), channel_id=1, source_target_pairs={{0,2},{1,3},{2,0},{3,1},{4,6},{5,7},{6,4},{7,5},{8,10},{9,11},{10,... | collective-permute-start | bytes 319496 | tf_op jit(solution)/shard_map/ppermute | solution.py:285
  22.5 9.1 %collective-permute-start.6 = (bf16[1600,128]{1,0:T(8,128)(2,1)S(1)}, bf16[1600,128]{1,0:T(8,128)(2,1)S(1)}, u32[]{:S(2)}, u32[]{:S(2)}) collective-permute-start(bf16[1600,128]{1,0:T(8,128)(2,1)S(1)} %get-tuple-element.30), channel_id=1, source_target_pairs={{0,1},{1,0},{2,3},{3,2},{4,5},{5,4},{6,7},{7,6},{8,9},{9,8},{10,11... | collective-permute-start | bytes 1228808 | tf_op jit(solution)/shard_map/ppermute | solution.py:285
  22.6 9.0 %collective-permute-start.5 = (bf16[832,128]{1,0:T(8,128)(2,1)S(1)}, bf16[832,128]{1,0:T(8,128)(2,1)S(1)}, u32[]{:S(2)}, u32[]{:S(2)}) collective-permute-start(bf16[832,128]{1,0:T(8,128)(2,1)S(1)} %get-tuple-element.29.b), channel_id=1, source_target_pairs={{0,4},{1,5},{2,6},{3,7},{4,0},{5,1},{6,2},{7,3},{8,12},{9,13},{10,... | collective-permute-start | bytes 638984 | tf_op jit(solution)/shard_map/ppermute | solution.py:285
  23.7 7.0 %collective-permute-start.4 = (bf16[768,128]{1,0:T(8,128)(2,1)S(1)}, bf16[768,128]{1,0:T(8,128)(2,1)S(1)}, u32[]{:S(2)}, u32[]{:S(2)}) collective-permute-start(bf16[768,128]{1,0:T(8,128)(2,1)S(1)} %get-tuple-element.28.a), channel_id=1, source_target_pairs={{0,2},{1,3},{2,0},{3,1},{4,6},{5,7},{6,4},{7,5},{8,10},{9,11},{10,... | collective-permute-start | bytes 589832 | tf_op jit(solution)/shard_map/ppermute | solution.py:285
  29.5 2.2 %copy-start.1 = (bf16[1024,1024]{1,0:T(8,128)(2,1)S(1)}, bf16[1024,1024]{1,0:T(8,128)(2,1)}, u32[]{:S(2)}) copy-start(bf16[1024,1024]{1,0:T(8,128)(2,1)} %refs_9_.1) | copy-start | bytes 6291460
  31.6 2.2 %collective-permute-start.9 = (bf16[2624,128]{1,0:T(8,128)(2,1)S(1)}, bf16[2624,128]{1,0:T(8,128)(2,1)S(1)}, u32[]{:S(2)}, u32[]{:S(2)}) collective-permute-start(bf16[2624,128]{1,0:T(8,128)(2,1)S(1)} %shard_map.108), channel_id=1, source_target_pairs={{0,1},{1,0},{2,3},{3,2},{4,5},{5,4},{6,7},{7,6},{8,9},{9,8},{10,11... | collective-permute-start | bytes 2015240 | tf_op jit(solution)/shard_map/ppermute | solution.py:285

commit v15 on v14

--- a/solution.py
+++ b/solution.py
@@ -277,7 +277,7 @@
     held = own * slots
     each = width // GROUP
     total = GROUP * held
-    cut = held * (width // LANES * 3 // 4)
+    cut = held * (width // LANES)
     rest = held * (width // LANES) + rows + META - cut
     half = GROUP // 2
 
@@ -316,7 +316,7 @@
         (beside, came, b, came_b),
         [((4 * size, LANES), BF16) for size in (cut, rest, cut + rest)],
     )
-    far_a, far_b, core = swap(a, Y), swap(b, Z1), swap(both, CORE)
+    core, far_b, far_a = swap(both, CORE), swap(b, Z1), swap(a, Y)
     (columns,) = call(
         columns_kernel, (came, *sent), [((half * 2 * each, rows), BF16)], flops=8 * 10**9
     )

time: 41.5 us -> 42.7 us (1.029)
  the two profiles are of different devices: /device:TPU:0 before, /device:TPU:25 now
where the time goes in v15:
time: 42.7 us; the launch traced here: 42.5 us
  waiting for transfers between devices  23.5 us (55%)
  Pallas kernels  10 us (23%)
  starting transfers between devices  7.63 us (18%)
  between operations  0.72 us (2%)
  local copies, waits for them, and re-layouts  0.62 us (1%)
    ppermute x10, waiting for transfers between devices, swap(): return lax.ppermute(x, 'grp', [(i, i ^ slot) for i in range(GROUP)])  23.5 us
    pallas_call x8, Pallas kernels, call(): pl.pallas_call(kernel, out_shape=tuple((jax.ShapeDtypeStruct(*out) for ou...  10 us
    ppermute x10, starting transfers between devices, swap(): return lax.ppermute(x, 'grp', [(i, i ^ slot) for i in range(GROUP)])  7.63 us
  transfers between devices with their start and end apart: 10, of which 7 were waited for; matrix products, arithmetic and copies ran while one was open for 0% of the time, Pallas kernels for 3%

profile of v15, /device:TPU:25, one launch (start us, length us, event | category | flops | bytes accessed | tf_op | source)
XLA Modules:
  0.0 42.5 jit_solution(1867745369455111529)
XLA Ops:
  0.6 0.0 copy-start.2
  0.6 0.0 copy-start
  0.7 1.1 %shard_map.103.piece = bf16[400,128]{1,0:T(8,128)(2,1)S(1)} custom-call(s32[2]{0:T(128)} %counts.1, s32[1,8]{1,0:T(1,128)} %owner.1, s32[1,8]{1,0:T(1,128)} %local.1, bf16[2,16,1024]{2,1,0:T(8,128)(2,1)} %features.1, bf16[1,128,128]{2,1,0:T(8,128)(2,1)} %adjacency.1), custom_call_target="tpu_custom_call" | custom-call | flops 10000000000 | tf_op jit(solution)/shard_map/pallas_call | solution.py:263
  1.8 0.0 copy-done.2
  1.8 0.6 %copy-done = bf16[1024,1024]{1,0:T(8,128)(2,1)S(1)} copy-done((bf16[1024,1024]{1,0:T(8,128)(2,1)S(1)}, bf16[1024,1024]{1,0:T(8,128)(2,1)}, u32[]{:S(2)}) %copy-start) | copy-done | bytes 2097176
  2.4 0.7 %shard_map.104 = (bf16[1024,128]{1,0:T(8,128)(2,1)S(1)}, bf16[1024,128]{1,0:T(8,128)(2,1)S(1)}) custom-call(bf16[1,128,1024]{2,1,0:T(8,128)(2,1)S(1)} %copy-done.2, bf16[1024,1024]{1,0:T(8,128)(2,1)S(1)} %copy-done), custom_call_target="tpu_custom_call" | custom-call | tf_op jit(solution)/shard_map/pallas_call | solution.py:263
  3.1 1.3 %collective-permute-start.1 = (bf16[1024,128]{1,0:T(8,128)(2,1)S(1)}, bf16[1024,128]{1,0:T(8,128)(2,1)S(1)}, u32[]{:S(2)}, u32[]{:S(2)}) collective-permute-start(bf16[1024,128]{1,0:T(8,128)(2,1)S(1)} %get-tuple-element.25), channel_id=1, source_target_pairs={{0,2},{1,3},{2,0},{3,1},{4,6},{5,7},{6,4},{7,5},{8,10},{9,11},{10,... | collective-permute-start | bytes 786440 | tf_op jit(solution)/shard_map/ppermute | solution.py:285
  4.4 0.0 collective-permute-start
  4.5 7.5 %collective-permute-done.came = bf16[400,128]{1,0:T(8,128)(2,1)S(1)} collective-permute-done((bf16[400,128]{1,0:T(8,128)(2,1)S(1)}, bf16[400,128]{1,0:T(8,128)(2,1)S(1)}, u32[]{:S(2)}, u32[]{:S(2)}) %collective-permute-start) | collective-permute-done | bytes 102432 | tf_op jit(solution)/shard_map/ppermute | solution.py:285
  12.0 0.0 collective-permute-done.1.across
  12.0 0.1 shard_map.105
  12.0 0.1 collective-permute-start.2
  12.1 0.4 %collective-permute-start.7 = (bf16[512,128]{1,0:T(8,128)(2,1)S(1)}, bf16[512,128]{1,0:T(8,128)(2,1)S(1)}, u32[]{:S(2)}, u32[]{:S(2)}) collective-permute-start(bf16[512,128]{1,0:T(8,128)(2,1)S(1)} %get-tuple-element.34), channel_id=1, source_target_pairs={{0,12},{1,13},{2,14},{3,15},{4,8},{5,9},{6,10},{7,11},{8,4},{9,5},... | collective-permute-start | bytes 393224 | tf_op jit(solution)/shard_map/ppermute | solution.py:285
  12.5 2.2 %collective-permute-start.8 = (bf16[512,128]{1,0:T(8,128)(2,1)S(1)}, bf16[512,128]{1,0:T(8,128)(2,1)S(1)}, u32[]{:S(2)}, u32[]{:S(2)}) collective-permute-start(bf16[512,128]{1,0:T(8,128)(2,1)S(1)} %get-tuple-element.35), channel_id=1, source_target_pairs={{0,8},{1,9},{2,10},{3,11},{4,12},{5,13},{6,14},{7,15},{8,0},{9,1},... | collective-permute-start | bytes 393224 | tf_op jit(solution)/shard_map/ppermute | solution.py:285
  14.7 0.2 collective-permute-start.3
  15.0 3.3 %collective-permute-done.3.came_b = bf16[288,128]{1,0:T(8,128)(2,1)S(1)} collective-permute-done((bf16[288,128]{1,0:T(8,128)(2,1)S(1)}, bf16[288,128]{1,0:T(8,128)(2,1)S(1)}, u32[]{:S(2)}, u32[]{:S(2)}) %collective-permute-start.3) | collective-permute-done | bytes 73760 | tf_op jit(solution)/shard_map/ppermute | solution.py:285
  18.2 4.5 %collective-permute-done.2.came = bf16[1024,128]{1,0:T(8,128)(2,1)S(1)} collective-permute-done((bf16[1024,128]{1,0:T(8,128)(2,1)S(1)}, bf16[1024,128]{1,0:T(8,128)(2,1)S(1)}, u32[]{:S(2)}, u32[]{:S(2)}) %collective-permute-start.2) | collective-permute-done | bytes 262176 | tf_op jit(solution)/shard_map/ppermute | solution.py:285
  22.8 0.1 shard_map.106
  22.8 2.0 %collective-permute-start.6 = (bf16[1600,128]{1,0:T(8,128)(2,1)S(1)}, bf16[1600,128]{1,0:T(8,128)(2,1)S(1)}, u32[]{:S(2)}, u32[]{:S(2)}) collective-permute-start(bf16[1600,128]{1,0:T(8,128)(2,1)S(1)} %get-tuple-element.30), channel_id=1, source_target_pairs={{0,1},{1,0},{2,3},{3,2},{4,5},{5,4},{6,7},{7,6},{8,9},{9,8},{10,11... | collective-permute-start | bytes 1228808 | tf_op jit(solution)/shard_map/ppermute | solution.py:285
  24.9 0.4 collective-permute-start.4
  25.3 0.0 collective-permute-start.5
  25.3 0.0 collective-permute-done.7.refs_0_
  25.3 0.2 collective-permute-done.8.refs_1_
  25.4 0.0 copy-start.1
  25.4 4.9 %collective-permute-done.5.far_b = bf16[576,128]{1,0:T(8,128)(2,1)S(1)} collective-permute-done((bf16[576,128]{1,0:T(8,128)(2,1)S(1)}, bf16[576,128]{1,0:T(8,128)(2,1)S(1)}, u32[]{:S(2)}, u32[]{:S(2)}) %collective-permute-start.5) | collective-permute-done | bytes 147488 | tf_op jit(solution)/shard_map/ppermute | solution.py:285
  30.3 2.4 %collective-permute-done.4.far_a = bf16[1024,128]{1,0:T(8,128)(2,1)S(1)} collective-permute-done((bf16[1024,128]{1,0:T(8,128)(2,1)S(1)}, bf16[1024,128]{1,0:T(8,128)(2,1)S(1)}, u32[]{:S(2)}, u32[]{:S(2)}) %collective-permute-start.4) | collective-permute-done | bytes 262176 | tf_op jit(solution)/shard_map/ppermute | solution.py:285
  32.7 0.0 collective-permute-done.6.core
  32.8 0.9 %collective-permute-start.9 = (bf16[2624,128]{1,0:T(8,128)(2,1)S(1)}, bf16[2624,128]{1,0:T(8,128)(2,1)S(1)}, u32[]{:S(2)}, u32[]{:S(2)}) collective-permute-start(bf16[2624,128]{1,0:T(8,128)(2,1)S(1)} %shard_map.108), channel_id=1, source_target_pairs={{0,1},{1,0},{2,3},{3,2},{4,5},{5,4},{6,7},{7,6},{8,9},{9,8},{10,11... | collective-permute-start | bytes 2015240 | tf_op jit(solution)/shard_map/ppermute | solution.py:285
  33.7 0.0 copy-done.1
  33.7 1.0 %shard_map.109 = (bf16[256,1024]{1,0:T(8,128)(2,1)S(1)}, bf16[256,1024]{1,0:T(8,128)(2,1)S(1)}, bf16[1024,512]{1,0:T(8,128)(2,1)S(1)}, bf16[8,128,128]{2,1,0:T(8...) custom-call(bf16[1024,128]{1,0:T(8,128)(2,1)S(1)} %get-tuple-element.28.a, ...), custom_call_target="tpu_custom_call" | custom-call | tf_op jit(solution)/shard_map/pallas_call | solution.py:263
  34.7 0.7 %collective-permute-done.9.pair = bf16[2624,128]{1,0:T(8,128)(2,1)S(1)} collective-permute-done((bf16[2624,128]{1,0:T(8,128)(2,1)S(1)}, bf16[2624,128]{1,0:T(8,128)(2,1)S(1)}, u32[]{:S(2)}, u32[]{:S(2)}) %collective-permute-start.9) | collective-permute-done | bytes 671776 | tf_op jit(solution)/shard_map/ppermute | solution.py:285
  35.5 7.1 %shard_map.110 = (bf16[1,128,1024]{2,1,0:T(8,128)(2,1)}, f32[64,1024]{1,0:T(8,128)}, f32[64,1024]{1,0:T(8,128)}) custom-call(bf16[1600,128]{1,0:T(8,128)(2,1)S(1)} %collective-permute-done.6.core, bf16[2624,128]{1,0:T(8,128)(2,1)S(1)} %collective-permute-done.9.pair, bf16[1024,128]{1,0:T(8,128)(2,1)S(1)} %collective-permute-done.2.came, ...), custom_call_target="tpu_custom_call" | custom-call | tf_op jit(solution)/shard_map/pallas_call | solution.py:263
  (2 shorter events, 0.1 us)
Async XLA Ops:
  0.6 1.1 %copy-start.2 = (bf16[1,128,1024]{2,1,0:T(8,128)(2,1)S(1)}, bf16[1,128,1024]{2,1,0:T(8,128)(2,1)}, u32[]{:S(2)}) copy-start(bf16[1,128,1024]{2,1,0:T(8,128)(2,1)} %cotangent) | copy-start | bytes 786436
  0.6 1.7 %copy-start = (bf16[1024,1024]{1,0:T(8,128)(2,1)S(1)}, bf16[1024,1024]{1,0:T(8,128)(2,1)}, u32[]{:S(2)}) copy-start(bf16[1024,1024]{1,0:T(8,128)(2,1)} %refs_10_.1) | copy-start | bytes 6291460
  3.1 8.9 %collective-permute-start.1 = (bf16[1024,128]{1,0:T(8,128)(2,1)S(1)}, bf16[1024,128]{1,0:T(8,128)(2,1)S(1)}, u32[]{:S(2)}, u32[]{:S(2)}) collective-permute-start(bf16[1024,128]{1,0:T(8,128)(2,1)S(1)} %get-tuple-element.25), channel_id=1, source_target_pairs={{0,2},{1,3},{2,0},{3,1},{4,6},{5,7},{6,4},{7,5},{8,10},{9,11},{10,... | collective-permute-start | bytes 786440 | tf_op jit(solution)/shard_map/ppermute | solution.py:285
  4.4 7.6 %collective-permute-start = (bf16[400,128]{1,0:T(8,128)(2,1)S(1)}, bf16[400,128]{1,0:T(8,128)(2,1)S(1)}, u32[]{:S(2)}, u32[]{:S(2)}) collective-permute-start(bf16[400,128]{1,0:T(8,128)(2,1)S(1)} %shard_map.103.piece), channel_id=1, source_target_pairs={{0,8},{1,9},{2,10},{3,11},{4,12},{5,13},{6,14},{7,15},{8,0},{9,1},... | collective-permute-start | bytes 307208 | tf_op jit(solution)/shard_map/ppermute | solution.py:285
  12.0 10.7 %collective-permute-start.2 = (bf16[1024,128]{1,0:T(8,128)(2,1)S(1)}, bf16[1024,128]{1,0:T(8,128)(2,1)S(1)}, u32[]{:S(2)}, u32[]{:S(2)}) collective-permute-start(bf16[1024,128]{1,0:T(8,128)(2,1)S(1)} %get-tuple-element.26.beside), channel_id=1, source_target_pairs={{0,4},{1,5},{2,6},{3,7},{4,0},{5,1},{6,2},{7,3},{8,12},{9,13},{10,... | collective-permute-start | bytes 786440 | tf_op jit(solution)/shard_map/ppermute | solution.py:285
  12.1 13.2 %collective-permute-start.7 = (bf16[512,128]{1,0:T(8,128)(2,1)S(1)}, bf16[512,128]{1,0:T(8,128)(2,1)S(1)}, u32[]{:S(2)}, u32[]{:S(2)}) collective-permute-start(bf16[512,128]{1,0:T(8,128)(2,1)S(1)} %get-tuple-element.34), channel_id=1, source_target_pairs={{0,12},{1,13},{2,14},{3,15},{4,8},{5,9},{6,10},{7,11},{8,4},{9,5},... | collective-permute-start | bytes 393224 | tf_op jit(solution)/shard_map/ppermute | solution.py:285
  12.5 12.9 %collective-permute-start.8 = (bf16[512,128]{1,0:T(8,128)(2,1)S(1)}, bf16[512,128]{1,0:T(8,128)(2,1)S(1)}, u32[]{:S(2)}, u32[]{:S(2)}) collective-permute-start(bf16[512,128]{1,0:T(8,128)(2,1)S(1)} %get-tuple-element.35), channel_id=1, source_target_pairs={{0,8},{1,9},{2,10},{3,11},{4,12},{5,13},{6,14},{7,15},{8,0},{9,1},... | collective-permute-start | bytes 393224 | tf_op jit(solution)/shard_map/ppermute | solution.py:285
  14.7 3.5 %collective-permute-start.3 = (bf16[288,128]{1,0:T(8,128)(2,1)S(1)}, bf16[288,128]{1,0:T(8,128)(2,1)S(1)}, u32[]{:S(2)}, u32[]{:S(2)}) collective-permute-start(bf16[288,128]{1,0:T(8,128)(2,1)S(1)} %get-tuple-element.27.half_b), channel_id=1, source_target_pairs={{0,2},{1,3},{2,0},{3,1},{4,6},{5,7},{6,4},{7,5},{8,10},{9,11},{10,... | collective-permute-start | bytes 221192 | tf_op jit(solution)/shard_map/ppermute | solution.py:285
  22.8 9.9 %collective-permute-start.6 = (bf16[1600,128]{1,0:T(8,128)(2,1)S(1)}, bf16[1600,128]{1,0:T(8,128)(2,1)S(1)}, u32[]{:S(2)}, u32[]{:S(2)}) collective-permute-start(bf16[1600,128]{1,0:T(8,128)(2,1)S(1)} %get-tuple-element.30), channel_id=1, source_target_pairs={{0,1},{1,0},{2,3},{3,2},{4,5},{5,4},{6,7},{7,6},{8,9},{9,8},{10,11... | collective-permute-start | bytes 1228808 | tf_op jit(solution)/shard_map/ppermute | solution.py:285
  24.9 7.9 %collective-permute-start.4 = (bf16[1024,128]{1,0:T(8,128)(2,1)S(1)}, bf16[1024,128]{1,0:T(8,128)(2,1)S(1)}, u32[]{:S(2)}, u32[]{:S(2)}) collective-permute-start(bf16[1024,128]{1,0:T(8,128)(2,1)S(1)} %get-tuple-element.28.a), channel_id=1, source_target_pairs={{0,2},{1,3},{2,0},{3,1},{4,6},{5,7},{6,4},{7,5},{8,10},{9,11},{10,... | collective-permute-start | bytes 786440 | tf_op jit(solution)/shard_map/ppermute | solution.py:285
  25.3 5.1 %collective-permute-start.5 = (bf16[576,128]{1,0:T(8,128)(2,1)S(1)}, bf16[576,128]{1,0:T(8,128)(2,1)S(1)}, u32[]{:S(2)}, u32[]{:S(2)}) collective-permute-start(bf16[576,128]{1,0:T(8,128)(2,1)S(1)} %get-tuple-element.29.b), channel_id=1, source_target_pairs={{0,4},{1,5},{2,6},{3,7},{4,0},{5,1},{6,2},{7,3},{8,12},{9,13},{10,... | collective-permute-start | bytes 442376 | tf_op jit(solution)/shard_map/ppermute | solution.py:285
  25.4 8.3 %copy-start.1 = (bf16[1024,1024]{1,0:T(8,128)(2,1)S(1)}, bf16[1024,1024]{1,0:T(8,128)(2,1)}, u32[]{:S(2)}) copy-start(bf16[1024,1024]{1,0:T(8,128)(2,1)} %refs_9_.1) | copy-start | bytes 6291460
  32.8 2.7 %collective-permute-start.9 = (bf16[2624,128]{1,0:T(8,128)(2,1)S(1)}, bf16[2624,128]{1,0:T(8,128)(2,1)S(1)}, u32[]{:S(2)}, u32[]{:S(2)}) collective-permute-start(bf16[2624,128]{1,0:T(8,128)(2,1)S(1)} %shard_map.108), channel_id=1, source_target_pairs={{0,1},{1,0},{2,3},{3,2},{4,5},{5,4},{6,7},{7,6},{8,9},{9,8},{10,11... | collective-permute-start | bytes 2015240 | tf_op jit(solution)/shard_map/ppermute | solution.py:285

commit v16 on v15

--- a/solution.py
+++ b/solution.py
@@ -17,7 +17,10 @@
 SMALL = 8 * 2**20
 Z2, Z1, Y, CORE = 8, 4, 2, 1
 GROUP = 16
-FAR = (Z2 | Z1, Z2, 0)
+FAR = (Z2 | Z1, Z2)
+NEAR = tuple(z | c for z in (0, *FAR) for c in (0, CORE))
+ACROSS = tuple(Y | slot for slot in NEAR)
+BESIDE = (Z1, Z1 | CORE, Z1 | Y, Z1 | Y | CORE)
 HALF_A = ((0, Z2, Z1, Z1 | Z2), (Y, Y | Z2, Y | Z1, Y | Z1 | Z2))
 HALF_B = ((0, Z2, Y, Y | Z2), (Z1, Z1 | Z2, Z1 | Y, Z1 | Y | Z2))
 
@@ -63,16 +66,15 @@
     piece[at + rows : at + rows + META, :] = meta.astype(F32).astype(BF16)
 
 
-def product_kernel(cotangent, w_second, near, across, turned, back):
+def product_kernel(cotangent, w_second, near, across, beside, turned, back):
     each = w_second.shape[0] // GROUP
     place = lax.axis_index("grp")
     cot = cotangent[0]
     turned[...] = cot.astype(F32).T.astype(BF16)
     back[...] = nt(w_second[...], cot).astype(BF16)
-    for h, out in enumerate((near, across)):
-        for i in range(out.shape[0] // (2 * each)):
-            to = 4 * (i // 2) + 2 * h + i % 2
-            span = pl.ds(pl.multiple_of((place ^ to) * each, each), each)
+    for out, slots in ((near, NEAR), (across, ACROSS), (beside, BESIDE)):
+        for i, slot in enumerate(slots):
+            span = pl.ds(pl.multiple_of((place ^ slot) * each, each), each)
             at = i * 2 * each
             out[at : at + each, :] = turned[span, :]
             out[at + each : at + 2 * each, :] = back[span, :]
@@ -85,33 +87,44 @@
     return at
 
 
-def split_kernel(piece, came, near, across, beside, half_b, *sent):
-    cut = beside.shape[0] - sent[0].shape[0]
-    stack(half_b, 0, piece.at[cut // 2 :], came.at[cut // 2 :])
-    at = stack(beside, 0, piece.at[: cut // 2], came.at[: cut // 2])
-    size = sent[0].shape[0] // 2
-    for slot, (out, at) in {Z1: (beside, at), **{slot: (out, 0) for slot, out in zip(FAR, sent)}}.items():
-        span = slice(slot // 4 * size, (slot // 4 + 1) * size)
-        stack(out, at, near.at[span], across.at[span])
-
-
-def join_kernel(beside, came, half_b, came_b, out_a, out_b, both):
-    cut = out_a.shape[0] // 2
-    stack(out_a, 0, beside.at[:cut], came.at[:cut])
-    stack(out_b, 0, half_b, came_b)
+def split_kernel(piece, came, near, across, beside, half_a, turn, keep, *sent):
+    cut = half_a.shape[0] // 2
+    stack(half_a, 0, piece.at[:cut], came.at[:cut])
+    two = beside.shape[0] // 2
+    stack(turn, 0, piece.at[cut:], came.at[cut:], beside.at[two:])
+    stack(keep, 0, near.at[:two], across.at[:two], beside.at[:two])
+    for i, out in enumerate(sent, 1):
+        span = slice(i * two, (i + 1) * two)
+        stack(out, 0, near.at[span], across.at[span])
+
+
+def join_kernel(half_a, came_a, turn, came_b, out_a, out_b, both):
+    size = out_b.shape[0] // 2
+    stack(out_a, 0, half_a, came_a)
+    stack(out_b, 0, turn.at[:size], came_b.at[:size])
     stack(both, 0, out_a, out_b)
 
 
-def columns_kernel(came, *refs):
-    *sent, out = refs
-    size = sent[0].shape[0]
-    blocks = dict(zip(FAR, sent))
-    blocks[Z1] = came.at[came.shape[0] - size :]
-    rows = size // 4
+def block_of(slot, rows, keep, came, *sent):
+    z, h, b = slot - slot % 4, slot // 2 % 2, slot % 2
+    if z in FAR:
+        ref, at = sent[FAR.index(z)], 2 * h + b
+    elif z == 0 or h == 0:
+        ref, at = keep, (4 if z else 2 * h) + b
+    else:
+        ref, at = came, b
+    at *= rows
+    if ref is came:
+        at += came.shape[0] - 2 * rows
+    return ref.at[at : at + rows]
+
+
+def columns_kernel(*refs):
+    *refs, out = refs
+    rows = out.shape[0] * 2 // GROUP
     at = 0
-    for slot in range(0, GROUP, 4):
-        for h in range(2):
-            at = stack(out, at, blocks[slot].at[(2 * h + 1) * rows : (2 * h + 2) * rows])
+    for slot in range(1, GROUP, 2):
+        at = stack(out, at, block_of(slot, rows, *refs))
 
 
 def pair_kernel(far_a, far_b, columns, out):
@@ -174,8 +187,8 @@
     w_piece[...] = part.astype(BF16)
 
 
-def step_kernel(own, slots, cut, rest, core, pair, came, *refs):
-    sent, refs = dict(zip(FAR, refs)), refs[len(FAR) :]
+def step_kernel(own, slots, cut, rest, core, pair, *refs):
+    blocks, refs = refs[: 2 + len(FAR)], refs[2 + len(FAR) :]
     early_feat, early_lifted, early_spread, early_adj, early_meta, w_piece = refs[:6]
     w_first, w_second, output, grad_first, grad_second = refs[6:11]
     hidden, spread, feat, adj, meta, dout, dpre, lifted, result, grads, second, sems = refs[11:]
@@ -214,8 +227,6 @@
     lifted_piece = nt(w_piece[...], feat[...]).astype(BF16)
     pre_piece = nt(lifted_piece, spread[...])
     each = grad_first.shape[0]
-    size = sent[0].shape[0]
-    sent[Z1] = came.at[came.shape[0] - size :]
     for slot in range(GROUP):
         p = place_of(slot)
         mask = masks[p : p + 1]
@@ -224,8 +235,7 @@
             at = deep + slot // 2 * 2 * each
             source = pair[at : at + 2 * each, :]
         else:
-            at = slot // 2 % 2 * size // 2
-            source = sent[slot - slot % 4][at : at + 2 * each, :]
+            source = block_of(slot, 2 * each, *blocks)[...]
         back = nn((source.astype(F32) * mask).astype(BF16), adj[p]) * mask
         dout[:, span] = back[:each].astype(BF16)
         pre = pre_piece[:, span]
@@ -295,30 +305,29 @@
         flops=10**10,
     )
     cotangent, _ = lax.optimization_barrier((cotangent, piece))
-    near, across = call(
+    near, across, beside = call(
         product_kernel,
         (cotangent, w_second),
-        [((GROUP * each, rows), BF16)] * 2,
+        [((len(x) * 2 * each, rows), BF16) for x in (NEAR, ACROSS, BESIDE)],
         [pltpu.VMEM((width, rows), BF16)] * 2,
     )
-    came = swap(piece, Z2)
-    across = swap(across, Y)
-    beside, b, *sent = call(
+    came, across, beside = swap(piece, Z2), swap(across, Y), swap(beside, Z1)
+    a, turn, keep, *sent = call(
         split_kernel,
-        (piece, came, near, across),
-        [((2 * cut + 8 * each, LANES), BF16), ((2 * rest, LANES), BF16)]
+        (piece, came, near, across, beside),
+        [((x, LANES), BF16) for x in (2 * cut, 2 * rest + 4 * each, 12 * each)]
         + [((8 * each, rows), BF16)] * len(FAR),
     )
-    came, came_b = swap(beside, Z1), swap(b, Y)
-    sent = [swap(x, slot) if slot else x for x, slot in zip(sent, FAR)]
+    came_a, came_b = swap(a, Z1), swap(turn, Y)
+    sent = [swap(x, slot) for x, slot in zip(sent, FAR)]
     a, b, both = call(
         join_kernel,
-        (beside, came, b, came_b),
+        (a, came_a, turn, came_b),
         [((4 * size, LANES), BF16) for size in (cut, rest, cut + rest)],
     )
     core, far_b, far_a = swap(both, CORE), swap(b, Z1), swap(a, Y)
     (columns,) = call(
-        columns_kernel, (came, *sent), [((half * 2 * each, rows), BF16)], flops=8 * 10**9
+        columns_kernel, (keep, came_b, *sent), [((half * 2 * each, rows), BF16)], flops=8 * 10**9
     )
     far_a, far_b, core = lax.optimization_barrier((far_a, far_b, core))
     (pair,) = call(
@@ -342,7 +351,7 @@
     )
     return call(
         functools.partial(step_kernel, own, slots, cut, rest),
-        (core, pair, came, *sent, *early, w_first, w_second),
+        (core, pair, keep, came_b, *sent, *early, w_first, w_second),
         [((1, rows, width), BF16), ((each, width), F32), ((each, width), F32)],
         [
             pltpu.VMEM((GROUP * rows, width), BF16),

time: 42.7 us -> 40.7 us (0.953)
  the two profiles are of different devices: /device:TPU:25 before, /device:TPU:0 now
where the time goes in v16:
time: 40.7 us; the launch traced here: 40.5 us
  starting transfers between devices  14.7 us (36%)
  waiting for transfers between devices  14.3 us (35%)
  Pallas kernels  10.2 us (25%)
  between operations  0.73 us (2%)
  local copies, waits for them, and re-layouts  0.62 us (2%)
    ppermute x11, starting transfers between devices, swap(): return lax.ppermute(x, 'grp', [(i, i ^ slot) for i in range(GROUP)])  14.7 us
    ppermute x11, waiting for transfers between devices, swap(): return lax.ppermute(x, 'grp', [(i, i ^ slot) for i in range(GROUP)])  14.3 us
    pallas_call x8, Pallas kernels, call(): pl.pallas_call(kernel, out_shape=tuple((jax.ShapeDtypeStruct(*out) for ou...  10.2 us
  transfers between devices with their start and end apart: 11, of which 5 were waited for; matrix products, arithmetic and copies ran while one was open for 0% of the time, Pallas kernels for 3%

profile of v16, /device:TPU:0, one launch (start us, length us, event | category | flops | bytes accessed | tf_op | source)
XLA Modules:
  0.0 40.5 jit_solution(6913926459388581087)
XLA Ops:
  0.6 0.0 copy-start.2
  0.6 0.0 copy-start
  0.7 1.1 %shard_map.103.piece = bf16[400,128]{1,0:T(8,128)(2,1)S(1)} custom-call(s32[2]{0:T(128)} %counts.1, s32[1,8]{1,0:T(1,128)} %owner.1, s32[1,8]{1,0:T(1,128)} %local.1, bf16[2,16,1024]{2,1,0:T(8,128)(2,1)} %features.1, bf16[1,128,128]{2,1,0:T(8,128)(2,1)} %adjacency.1), custom_call_target="tpu_custom_call" | custom-call | flops 10000000000 | tf_op jit(solution)/shard_map/pallas_call | solution.py:273
  1.8 0.0 copy-done.2
  1.8 0.6 %copy-done = bf16[1024,1024]{1,0:T(8,128)(2,1)S(1)} copy-done((bf16[1024,1024]{1,0:T(8,128)(2,1)S(1)}, bf16[1024,1024]{1,0:T(8,128)(2,1)}, u32[]{:S(2)}) %copy-start) | copy-done | bytes 2097176
  2.4 0.7 %shard_map.104 = (bf16[768,128]{1,0:T(8,128)(2,1)S(1)}, bf16[768,128]{1,0:T(8,128)(2,1)S(1)}, bf16[512,128]{1,0:T(8,128)(2,1)S(1)}) custom-call(bf16[1,128,1024]{2,1,0:T(8,128)(2,1)S(1)} %copy-done.2, bf16[1024,1024]{1,0:T(8,128)(2,1)S(1)} %copy-done), custom_call_target="tpu_custom_call" | custom-call | tf_op jit(solution)/shard_map/pallas_call | solution.py:273
  3.1 3.0 %collective-permute-start.1 = (bf16[768,128]{1,0:T(8,128)(2,1)S(1)}, bf16[768,128]{1,0:T(8,128)(2,1)S(1)}, u32[]{:S(2)}, u32[]{:S(2)}) collective-permute-start(bf16[768,128]{1,0:T(8,128)(2,1)S(1)} %get-tuple-element.26), channel_id=1, source_target_pairs={{0,2},{1,3},{2,0},{3,1},{4,6},{5,7},{6,4},{7,5},{8,10},{9,11},{10,... | collective-permute-start | bytes 589832 | tf_op jit(solution)/shard_map/ppermute | solution.py:295
  6.1 1.6 %collective-permute-start.2 = (bf16[512,128]{1,0:T(8,128)(2,1)S(1)}, bf16[512,128]{1,0:T(8,128)(2,1)S(1)}, u32[]{:S(2)}, u32[]{:S(2)}) collective-permute-start(bf16[512,128]{1,0:T(8,128)(2,1)S(1)} %get-tuple-element.27), channel_id=1, source_target_pairs={{0,4},{1,5},{2,6},{3,7},{4,0},{5,1},{6,2},{7,3},{8,12},{9,13},{10,... | collective-permute-start | bytes 393224 | tf_op jit(solution)/shard_map/ppermute | solution.py:295
  7.7 2.6 %collective-permute-start = (bf16[400,128]{1,0:T(8,128)(2,1)S(1)}, bf16[400,128]{1,0:T(8,128)(2,1)S(1)}, u32[]{:S(2)}, u32[]{:S(2)}) collective-permute-start(bf16[400,128]{1,0:T(8,128)(2,1)S(1)} %shard_map.103.piece), channel_id=1, source_target_pairs={{0,8},{1,9},{2,10},{3,11},{4,12},{5,13},{6,14},{7,15},{8,0},{9,1},... | collective-permute-start | bytes 307208 | tf_op jit(solution)/shard_map/ppermute | solution.py:295
  10.3 3.8 %collective-permute-done.came = bf16[400,128]{1,0:T(8,128)(2,1)S(1)} collective-permute-done((bf16[400,128]{1,0:T(8,128)(2,1)S(1)}, bf16[400,128]{1,0:T(8,128)(2,1)S(1)}, u32[]{:S(2)}, u32[]{:S(2)}) %collective-permute-start) | collective-permute-done | bytes 102432 | tf_op jit(solution)/shard_map/ppermute | solution.py:295
  14.1 0.0 collective-permute-done.2.beside
  14.1 0.0 collective-permute-done.1.across
  14.2 0.6 %collective-permute-start.4 = (bf16[544,128]{1,0:T(8,128)(2,1)S(1)}, bf16[544,128]{1,0:T(8,128)(2,1)S(1)}, u32[]{:S(2)}, u32[]{:S(2)}) collective-permute-start(bf16[544,128]{1,0:T(8,128)(2,1)S(1)} %get-tuple-element.29.turn), channel_id=1, source_target_pairs={{0,2},{1,3},{2,0},{3,1},{4,6},{5,7},{6,4},{7,5},{8,10},{9,11},{10,... | collective-permute-start | bytes 417800 | tf_op jit(solution)/shard_map/ppermute | solution.py:295
  14.7 1.8 %collective-permute-start.3 = (bf16[512,128]{1,0:T(8,128)(2,1)S(1)}, bf16[512,128]{1,0:T(8,128)(2,1)S(1)}, u32[]{:S(2)}, u32[]{:S(2)}) collective-permute-start(bf16[512,128]{1,0:T(8,128)(2,1)S(1)} %get-tuple-element.28.half_a), channel_id=1, source_target_pairs={{0,4},{1,5},{2,6},{3,7},{4,0},{5,1},{6,2},{7,3},{8,12},{9,13},{10,... | collective-permute-start | bytes 393224 | tf_op jit(solution)/shard_map/ppermute | solution.py:295
  16.5 1.7 %collective-permute-start.8 = (bf16[512,128]{1,0:T(8,128)(2,1)S(1)}, bf16[512,128]{1,0:T(8,128)(2,1)S(1)}, u32[]{:S(2)}, u32[]{:S(2)}) collective-permute-start(bf16[512,128]{1,0:T(8,128)(2,1)S(1)} %get-tuple-element.37), channel_id=1, source_target_pairs={{0,12},{1,13},{2,14},{3,15},{4,8},{5,9},{6,10},{7,11},{8,4},{9,5},... | collective-permute-start | bytes 393224 | tf_op jit(solution)/shard_map/ppermute | solution.py:295
  18.2 0.6 %collective-permute-start.9 = (bf16[512,128]{1,0:T(8,128)(2,1)S(1)}, bf16[512,128]{1,0:T(8,128)(2,1)S(1)}, u32[]{:S(2)}, u32[]{:S(2)}) collective-permute-start(bf16[512,128]{1,0:T(8,128)(2,1)S(1)} %get-tuple-element.38), channel_id=1, source_target_pairs={{0,8},{1,9},{2,10},{3,11},{4,12},{5,13},{6,14},{7,15},{8,0},{9,1},... | collective-permute-start | bytes 393224 | tf_op jit(solution)/shard_map/ppermute | solution.py:295
  18.8 2.9 %collective-permute-done.3.came_a = bf16[512,128]{1,0:T(8,128)(2,1)S(1)} collective-permute-done((bf16[512,128]{1,0:T(8,128)(2,1)S(1)}, bf16[512,128]{1,0:T(8,128)(2,1)S(1)}, u32[]{:S(2)}, u32[]{:S(2)}) %collective-permute-start.3) | collective-permute-done | bytes 131104 | tf_op jit(solution)/shard_map/ppermute | solution.py:295
  21.7 0.0 collective-permute-done.4.came_b.refs_1_
  21.7 0.1 shard_map.106
  21.8 0.1 collective-permute-start.7
  21.8 1.6 %collective-permute-start.5 = (bf16[1024,128]{1,0:T(8,128)(2,1)S(1)}, bf16[1024,128]{1,0:T(8,128)(2,1)S(1)}, u32[]{:S(2)}, u32[]{:S(2)}) collective-permute-start(bf16[1024,128]{1,0:T(8,128)(2,1)S(1)} %get-tuple-element.30.a), channel_id=1, source_target_pairs={{0,2},{1,3},{2,0},{3,1},{4,6},{5,7},{6,4},{7,5},{8,10},{9,11},{10,... | collective-permute-start | bytes 786440 | tf_op jit(solution)/shard_map/ppermute | solution.py:295
  23.4 1.2 %collective-permute-start.6 = (bf16[576,128]{1,0:T(8,128)(2,1)S(1)}, bf16[576,128]{1,0:T(8,128)(2,1)S(1)}, u32[]{:S(2)}, u32[]{:S(2)}) collective-permute-start(bf16[576,128]{1,0:T(8,128)(2,1)S(1)} %get-tuple-element.31.b), channel_id=1, source_target_pairs={{0,4},{1,5},{2,6},{3,7},{4,0},{5,1},{6,2},{7,3},{8,12},{9,13},{10,... | collective-permute-start | bytes 442376 | tf_op jit(solution)/shard_map/ppermute | solution.py:295
  24.6 0.0 collective-permute-done.8.refs_2_
  24.6 4.1 %collective-permute-done.9.refs_3_ = bf16[512,128]{1,0:T(8,128)(2,1)S(1)} collective-permute-done((bf16[512,128]{1,0:T(8,128)(2,1)S(1)}, bf16[512,128]{1,0:T(8,128)(2,1)S(1)}, u32[]{:S(2)}, u32[]{:S(2)}) %collective-permute-start.9) | collective-permute-done | bytes 131104 | tf_op jit(solution)/shard_map/ppermute | solution.py:295
  28.7 0.0 copy-start.1
  28.7 2.4 %collective-permute-done.6.far_b = bf16[576,128]{1,0:T(8,128)(2,1)S(1)} collective-permute-done((bf16[576,128]{1,0:T(8,128)(2,1)S(1)}, bf16[576,128]{1,0:T(8,128)(2,1)S(1)}, u32[]{:S(2)}, u32[]{:S(2)}) %collective-permute-start.6) | collective-permute-done | bytes 147488 | tf_op jit(solution)/shard_map/ppermute | solution.py:295
  31.1 0.0 collective-permute-done.5.far_a
  31.1 0.0 collective-permute-done.7.core
  31.2 0.1 collective-permute-start.10
  31.2 0.0 copy-done.1
  31.3 1.0 %shard_map.109 = (bf16[256,1024]{1,0:T(8,128)(2,1)S(1)}, bf16[256,1024]{1,0:T(8,128)(2,1)S(1)}, bf16[1024,512]{1,0:T(8,128)(2,1)S(1)}, bf16[8,128,128]{2,1,0:T(8...) custom-call(bf16[1024,128]{1,0:T(8,128)(2,1)S(1)} %get-tuple-element.30.a, ...), custom_call_target="tpu_custom_call" | custom-call | tf_op jit(solution)/shard_map/pallas_call | solution.py:273
  32.3 1.1 %collective-permute-done.10.pair = bf16[2624,128]{1,0:T(8,128)(2,1)S(1)} collective-permute-done((bf16[2624,128]{1,0:T(8,128)(2,1)S(1)}, bf16[2624,128]{1,0:T(8,128)(2,1)S(1)}, u32[]{:S(2)}, u32[]{:S(2)}) %collective-permute-start.10) | collective-permute-done | bytes 671776 | tf_op jit(solution)/shard_map/ppermute | solution.py:295
  33.4 7.2 %shard_map.110 = (bf16[1,128,1024]{2,1,0:T(8,128)(2,1)}, f32[64,1024]{1,0:T(8,128)}, f32[64,1024]{1,0:T(8,128)}) custom-call(bf16[1600,128]{1,0:T(8,128)(2,1)S(1)} %collective-permute-done.7.core, bf16[2624,128]{1,0:T(8,128)(2,1)S(1)} %collective-permute-done.10.pair, bf16[768,128]{1,0:T(8,128)(2,1)S(1)} %get-tuple-element.36.refs_0_, ...), custom_call_target="tpu_custom_call" | custom-call | tf_op jit(solution)/shard_map/pallas_call | solution.py:273
  (3 shorter events, 0.1 us)
Async XLA Ops:
  0.6 1.1 %copy-start.2 = (bf16[1,128,1024]{2,1,0:T(8,128)(2,1)S(1)}, bf16[1,128,1024]{2,1,0:T(8,128)(2,1)}, u32[]{:S(2)}) copy-start(bf16[1,128,1024]{2,1,0:T(8,128)(2,1)} %cotangent) | copy-start | bytes 786436
  0.6 1.7 %copy-start = (bf16[1024,1024]{1,0:T(8,128)(2,1)S(1)}, bf16[1024,1024]{1,0:T(8,128)(2,1)}, u32[]{:S(2)}) copy-start(bf16[1024,1024]{1,0:T(8,128)(2,1)} %refs_11_.1) | copy-start | bytes 6291460
  3.1 11.0 %collective-permute-start.1 = (bf16[768,128]{1,0:T(8,128)(2,1)S(1)}, bf16[768,128]{1,0:T(8,128)(2,1)S(1)}, u32[]{:S(2)}, u32[]{:S(2)}) collective-permute-start(bf16[768,128]{1,0:T(8,128)(2,1)S(1)} %get-tuple-element.26), channel_id=1, source_target_pairs={{0,2},{1,3},{2,0},{3,1},{4,6},{5,7},{6,4},{7,5},{8,10},{9,11},{10,... | collective-permute-start | bytes 589832 | tf_op jit(solution)/shard_map/ppermute | solution.py:295
  6.1 8.0 %collective-permute-start.2 = (bf16[512,128]{1,0:T(8,128)(2,1)S(1)}, bf16[512,128]{1,0:T(8,128)(2,1)S(1)}, u32[]{:S(2)}, u32[]{:S(2)}) collective-permute-start(bf16[512,128]{1,0:T(8,128)(2,1)S(1)} %get-tuple-element.27), channel_id=1, source_target_pairs={{0,4},{1,5},{2,6},{3,7},{4,0},{5,1},{6,2},{7,3},{8,12},{9,13},{10,... | collective-permute-start | bytes 393224 | tf_op jit(solution)/shard_map/ppermute | solution.py:295
  7.7 6.4 %collective-permute-start = (bf16[400,128]{1,0:T(8,128)(2,1)S(1)}, bf16[400,128]{1,0:T(8,128)(2,1)S(1)}, u32[]{:S(2)}, u32[]{:S(2)}) collective-permute-start(bf16[400,128]{1,0:T(8,128)(2,1)S(1)} %shard_map.103.piece), channel_id=1, source_target_pairs={{0,8},{1,9},{2,10},{3,11},{4,12},{5,13},{6,14},{7,15},{8,0},{9,1},... | collective-permute-start | bytes 307208 | tf_op jit(solution)/shard_map/ppermute | solution.py:295
  14.2 7.5 %collective-permute-start.4 = (bf16[544,128]{1,0:T(8,128)(2,1)S(1)}, bf16[544,128]{1,0:T(8,128)(2,1)S(1)}, u32[]{:S(2)}, u32[]{:S(2)}) collective-permute-start(bf16[544,128]{1,0:T(8,128)(2,1)S(1)} %get-tuple-element.29.turn), channel_id=1, source_target_pairs={{0,2},{1,3},{2,0},{3,1},{4,6},{5,7},{6,4},{7,5},{8,10},{9,11},{10,... | collective-permute-start | bytes 417800 | tf_op jit(solution)/shard_map/ppermute | solution.py:295
  14.7 6.9 %collective-permute-start.3 = (bf16[512,128]{1,0:T(8,128)(2,1)S(1)}, bf16[512,128]{1,0:T(8,128)(2,1)S(1)}, u32[]{:S(2)}, u32[]{:S(2)}) collective-permute-start(bf16[512,128]{1,0:T(8,128)(2,1)S(1)} %get-tuple-element.28.half_a), channel_id=1, source_target_pairs={{0,4},{1,5},{2,6},{3,7},{4,0},{5,1},{6,2},{7,3},{8,12},{9,13},{10,... | collective-permute-start | bytes 393224 | tf_op jit(solution)/shard_map/ppermute | solution.py:295
  16.5 8.1 %collective-permute-start.8 = (bf16[512,128]{1,0:T(8,128)(2,1)S(1)}, bf16[512,128]{1,0:T(8,128)(2,1)S(1)}, u32[]{:S(2)}, u32[]{:S(2)}) collective-permute-start(bf16[512,128]{1,0:T(8,128)(2,1)S(1)} %get-tuple-element.37), channel_id=1, source_target_pairs={{0,12},{1,13},{2,14},{3,15},{4,8},{5,9},{6,10},{7,11},{8,4},{9,5},... | collective-permute-start | bytes 393224 | tf_op jit(solution)/shard_map/ppermute | solution.py:295
  18.2 10.4 %collective-permute-start.9 = (bf16[512,128]{1,0:T(8,128)(2,1)S(1)}, bf16[512,128]{1,0:T(8,128)(2,1)S(1)}, u32[]{:S(2)}, u32[]{:S(2)}) collective-permute-start(bf16[512,128]{1,0:T(8,128)(2,1)S(1)} %get-tuple-element.38), channel_id=1, source_target_pairs={{0,8},{1,9},{2,10},{3,11},{4,12},{5,13},{6,14},{7,15},{8,0},{9,1},... | collective-permute-start | bytes 393224 | tf_op jit(solution)/shard_map/ppermute | solution.py:295
  21.8 9.4 %collective-permute-start.7 = (bf16[1600,128]{1,0:T(8,128)(2,1)S(1)}, bf16[1600,128]{1,0:T(8,128)(2,1)S(1)}, u32[]{:S(2)}, u32[]{:S(2)}) collective-permute-start(bf16[1600,128]{1,0:T(8,128)(2,1)S(1)} %get-tuple-element.32), channel_id=1, source_target_pairs={{0,1},{1,0},{2,3},{3,2},{4,5},{5,4},{6,7},{7,6},{8,9},{9,8},{10,11... | collective-permute-start | bytes 1228808 | tf_op jit(solution)/shard_map/ppermute | solution.py:295
  21.8 9.3 %collective-permute-start.5 = (bf16[1024,128]{1,0:T(8,128)(2,1)S(1)}, bf16[1024,128]{1,0:T(8,128)(2,1)S(1)}, u32[]{:S(2)}, u32[]{:S(2)}) collective-permute-start(bf16[1024,128]{1,0:T(8,128)(2,1)S(1)} %get-tuple-element.30.a), channel_id=1, source_target_pairs={{0,2},{1,3},{2,0},{3,1},{4,6},{5,7},{6,4},{7,5},{8,10},{9,11},{10,... | collective-permute-start | bytes 786440 | tf_op jit(solution)/shard_map/ppermute | solution.py:295
  23.4 7.7 %collective-permute-start.6 = (bf16[576,128]{1,0:T(8,128)(2,1)S(1)}, bf16[576,128]{1,0:T(8,128)(2,1)S(1)}, u32[]{:S(2)}, u32[]{:S(2)}) collective-permute-start(bf16[576,128]{1,0:T(8,128)(2,1)S(1)} %get-tuple-element.31.b), channel_id=1, source_target_pairs={{0,4},{1,5},{2,6},{3,7},{4,0},{5,1},{6,2},{7,3},{8,12},{9,13},{10,... | collective-permute-start | bytes 442376 | tf_op jit(solution)/shard_map/ppermute | solution.py:295
  28.7 2.6 %copy-start.1 = (bf16[1024,1024]{1,0:T(8,128)(2,1)S(1)}, bf16[1024,1024]{1,0:T(8,128)(2,1)}, u32[]{:S(2)}) copy-start(bf16[1024,1024]{1,0:T(8,128)(2,1)} %refs_10_.1) | copy-start | bytes 6291460
  31.2 2.2 %collective-permute-start.10 = (bf16[2624,128]{1,0:T(8,128)(2,1)S(1)}, bf16[2624,128]{1,0:T(8,128)(2,1)S(1)}, u32[]{:S(2)}, u32[]{:S(2)}) collective-permute-start(bf16[2624,128]{1,0:T(8,128)(2,1)S(1)} %shard_map.108), channel_id=1, source_target_pairs={{0,1},{1,0},{2,3},{3,2},{4,5},{5,4},{6,7},{7,6},{8,9},{9,8},{10,11... | collective-permute-start | bytes 2015240 | tf_op jit(solution)/shard_map/ppermute | solution.py:295

commit v17 on v16

--- a/solution.py
+++ b/solution.py
@@ -21,6 +21,7 @@
 NEAR = tuple(z | c for z in (0, *FAR) for c in (0, CORE))
 ACROSS = tuple(Y | slot for slot in NEAR)
 BESIDE = (Z1, Z1 | CORE, Z1 | Y, Z1 | Y | CORE)
+PARTS = (ACROSS[:3], ACROSS[3:], BESIDE[:2], BESIDE[2:])
 HALF_A = ((0, Z2, Z1, Z1 | Z2), (Y, Y | Z2, Y | Z1, Y | Z1 | Z2))
 HALF_B = ((0, Z2, Y, Y | Z2), (Z1, Z1 | Z2, Z1 | Y, Z1 | Y | Z2))
 
@@ -66,13 +67,14 @@
     piece[at + rows : at + rows + META, :] = meta.astype(F32).astype(BF16)
 
 
-def product_kernel(cotangent, w_second, near, across, beside, turned, back):
+def product_kernel(cotangent, w_second, near, *refs):
+    *parts, turned, back = refs
     each = w_second.shape[0] // GROUP
     place = lax.axis_index("grp")
     cot = cotangent[0]
     turned[...] = cot.astype(F32).T.astype(BF16)
     back[...] = nt(w_second[...], cot).astype(BF16)
-    for out, slots in ((near, NEAR), (across, ACROSS), (beside, BESIDE)):
+    for out, slots in zip((near, *parts), (NEAR, *PARTS)):
         for i, slot in enumerate(slots):
             span = pl.ds(pl.multiple_of((place ^ slot) * each, each), each)
             at = i * 2 * each
@@ -87,15 +89,14 @@
     return at
 
 
-def split_kernel(piece, came, near, across, beside, half_a, turn, keep, *sent):
+def split_kernel(piece, came, near, across, further, beside, turned, half_a, turn, keep, one, two):
     cut = half_a.shape[0] // 2
     stack(half_a, 0, piece.at[:cut], came.at[:cut])
-    two = beside.shape[0] // 2
-    stack(turn, 0, piece.at[cut:], came.at[cut:], beside.at[two:])
-    stack(keep, 0, near.at[:two], across.at[:two], beside.at[:two])
-    for i, out in enumerate(sent, 1):
-        span = slice(i * two, (i + 1) * two)
-        stack(out, 0, near.at[span], across.at[span])
+    rows = near.shape[0] // len(NEAR)
+    stack(turn, 0, piece.at[cut:], came.at[cut:], turned)
+    stack(keep, 0, near.at[: 2 * rows], across.at[: 2 * rows], beside)
+    stack(one, 0, near.at[2 * rows : 4 * rows], across.at[2 * rows :], further.at[:rows])
+    stack(two, 0, near.at[4 * rows :], further.at[rows:])
 
 
 def join_kernel(half_a, came_a, turn, came_b, out_a, out_b, both):
@@ -305,16 +306,17 @@
         flops=10**10,
     )
     cotangent, _ = lax.optimization_barrier((cotangent, piece))
-    near, across, beside = call(
+    near, *columns = call(
         product_kernel,
         (cotangent, w_second),
-        [((len(x) * 2 * each, rows), BF16) for x in (NEAR, ACROSS, BESIDE)],
+        [((len(x) * 2 * each, rows), BF16) for x in (NEAR, *PARTS)],
         [pltpu.VMEM((width, rows), BF16)] * 2,
     )
-    came, across, beside = swap(piece, Z2), swap(across, Y), swap(beside, Z1)
+    came = swap(piece, Z2)
+    columns = [swap(x, slot) for x, slot in zip(columns, (Y, Y, Z1, Z1))]
     a, turn, keep, *sent = call(
         split_kernel,
-        (piece, came, near, across, beside),
+        (piece, came, near, *columns),
         [((x, LANES), BF16) for x in (2 * cut, 2 * rest + 4 * each, 12 * each)]
         + [((8 * each, rows), BF16)] * len(FAR),
     )

time: 40.7 us -> 41 us (level)
    ppermute x11 -> x13, waiting for transfers between devices: 14.3 us -> 14.5 us  [swap(): return lax.ppermute(x, 'grp', [(i, i ^ slot) for i in range(GROUP)])]
    ppermute x11 -> x13, starting transfers between devices: 14.7 us -> 14.6 us  [swap(): return lax.ppermute(x, 'grp', [(i, i ^ slot) for i in range(GROUP)])]
  transfers between devices with their start and end apart: 11 -> 13, of which waited for: 5 -> 7; matrix products, arithmetic and copies ran while one was open for 0% -> 0% of each run, Pallas kernels for 3% -> 4%
where the time goes in v17:
time: 41 us; the launch traced here: 40.8 us
  starting transfers between devices  14.6 us (36%)
  waiting for transfers between devices  14.5 us (35%)
  Pallas kernels  10.2 us (25%)
  local copies, waits for them, and re-layouts  0.82 us (2%)
  between operations  0.73 us (2%)
    ppermute x13, starting transfers between devices, swap(): return lax.ppermute(x, 'grp', [(i, i ^ slot) for i in range(GROUP)])  14.6 us
    ppermute x13, waiting for transfers between devices, swap(): return lax.ppermute(x, 'grp', [(i, i ^ slot) for i in range(GROUP)])  14.5 us
    pallas_call x8, Pallas kernels, call(): pl.pallas_call(kernel, out_shape=tuple((jax.ShapeDtypeStruct(*out) for ou...  10.2 us
    unnamed x6, local copies, waits for them, and re-layouts  0.82 us
  transfers between devices with their start and end apart: 13, of which 7 were waited for; matrix products, arithmetic and copies ran while one was open for 0% of the time, Pallas kernels for 4%

profile of v17, /device:TPU:0, one launch (start us, length us, event | category | flops | bytes accessed | tf_op | source)
XLA Modules:
  0.0 40.8 jit_solution(4360712670840459905)
XLA Ops:
  0.6 0.0 copy-start.2
  0.6 0.0 copy-start
  0.7 1.1 %shard_map.103.piece = bf16[400,128]{1,0:T(8,128)(2,1)S(1)} custom-call(s32[2]{0:T(128)} %counts.1, s32[1,8]{1,0:T(1,128)} %owner.1, s32[1,8]{1,0:T(1,128)} %local.1, bf16[2,16,1024]{2,1,0:T(8,128)(2,1)} %features.1, bf16[1,128,128]{2,1,0:T(8,128)(2,1)} %adjacency.1), custom_call_target="tpu_custom_call" | custom-call | flops 10000000000 | tf_op jit(solution)/shard_map/pallas_call | solution.py:274
  1.8 4.1 %collective-permute-start = (bf16[400,128]{1,0:T(8,128)(2,1)S(1)}, bf16[400,128]{1,0:T(8,128)(2,1)S(1)}, u32[]{:S(2)}, u32[]{:S(2)}) collective-permute-start(bf16[400,128]{1,0:T(8,128)(2,1)S(1)} %shard_map.103.piece), channel_id=1, source_target_pairs={{0,8},{1,9},{2,10},{3,11},{4,12},{5,13},{6,14},{7,15},{8,0},{9,1},... | collective-permute-start | bytes 307208 | tf_op jit(solution)/shard_map/ppermute | solution.py:296
  5.9 0.0 copy-done.2
  5.9 0.0 copy-done
  5.9 0.7 %shard_map.104 = (bf16[768,128]{1,0:T(8,128)(2,1)S(1)}, bf16[384,128]{1,0:T(8,128)(2,1)S(1)}, bf16[384,128]{1,0:T(8,128)(2,1)S(1)}, bf16[256,128]{1,0:T(8,128)(2,1)S(1)}, bf16[256,128]{1,0:T(8,128)(2,1)S(1)}) custom-call(bf16[1,128,1024]{2,1,0:T(8,128)(2,1)S(1)} %copy-done.2, bf16[1024,1024]{1,0:T(8,128)(2,1)S(1)} %copy-done), custom_call_target="tpu_custom_call" | custom-call | tf_op jit(solution)/shard_map/pallas_call | solution.py:274
  6.6 1.6 %collective-permute-start.1 = (bf16[384,128]{1,0:T(8,128)(2,1)S(1)}, bf16[384,128]{1,0:T(8,128)(2,1)S(1)}, u32[]{:S(2)}, u32[]{:S(2)}) collective-permute-start(bf16[384,128]{1,0:T(8,128)(2,1)S(1)} %get-tuple-element.28), channel_id=1, source_target_pairs={{0,2},{1,3},{2,0},{3,1},{4,6},{5,7},{6,4},{7,5},{8,10},{9,11},{10,... | collective-permute-start | bytes 294920 | tf_op jit(solution)/shard_map/ppermute | solution.py:296
  8.2 0.5 %collective-permute-start.2 = (bf16[384,128]{1,0:T(8,128)(2,1)S(1)}, bf16[384,128]{1,0:T(8,128)(2,1)S(1)}, u32[]{:S(2)}, u32[]{:S(2)}) collective-permute-start(bf16[384,128]{1,0:T(8,128)(2,1)S(1)} %get-tuple-element.29), channel_id=1, source_target_pairs={{0,2},{1,3},{2,0},{3,1},{4,6},{5,7},{6,4},{7,5},{8,10},{9,11},{10,... | collective-permute-start | bytes 294920 | tf_op jit(solution)/shard_map/ppermute | solution.py:296
  8.7 1.6 %collective-permute-start.3 = (bf16[256,128]{1,0:T(8,128)(2,1)S(1)}, bf16[256,128]{1,0:T(8,128)(2,1)S(1)}, u32[]{:S(2)}, u32[]{:S(2)}) collective-permute-start(bf16[256,128]{1,0:T(8,128)(2,1)S(1)} %get-tuple-element.30), channel_id=1, source_target_pairs={{0,4},{1,5},{2,6},{3,7},{4,0},{5,1},{6,2},{7,3},{8,12},{9,13},{10,... | collective-permute-start | bytes 196616 | tf_op jit(solution)/shard_map/ppermute | solution.py:296
  10.3 0.5 %collective-permute-start.4 = (bf16[256,128]{1,0:T(8,128)(2,1)S(1)}, bf16[256,128]{1,0:T(8,128)(2,1)S(1)}, u32[]{:S(2)}, u32[]{:S(2)}) collective-permute-start(bf16[256,128]{1,0:T(8,128)(2,1)S(1)} %get-tuple-element.31), channel_id=1, source_target_pairs={{0,4},{1,5},{2,6},{3,7},{4,0},{5,1},{6,2},{7,3},{8,12},{9,13},{10,... | collective-permute-start | bytes 196616 | tf_op jit(solution)/shard_map/ppermute | solution.py:296
  10.7 2.3 %collective-permute-done.3.beside = bf16[256,128]{1,0:T(8,128)(2,1)S(1)} collective-permute-done((bf16[256,128]{1,0:T(8,128)(2,1)S(1)}, bf16[256,128]{1,0:T(8,128)(2,1)S(1)}, u32[]{:S(2)}, u32[]{:S(2)}) %collective-permute-start.3) | collective-permute-done | bytes 65568 | tf_op jit(solution)/shard_map/ppermute | solution.py:296
  13.0 1.5 %collective-permute-done.4.turned = bf16[256,128]{1,0:T(8,128)(2,1)S(1)} collective-permute-done((bf16[256,128]{1,0:T(8,128)(2,1)S(1)}, bf16[256,128]{1,0:T(8,128)(2,1)S(1)}, u32[]{:S(2)}, u32[]{:S(2)}) %collective-permute-start.4) | collective-permute-done | bytes 65568 | tf_op jit(solution)/shard_map/ppermute | solution.py:296
  14.5 0.0 collective-permute-done.1.across
  14.5 0.0 collective-permute-done.2.further
  14.5 0.0 collective-permute-done.came
  14.5 0.1 shard_map.105
  14.6 1.6 %collective-permute-start.6 = (bf16[544,128]{1,0:T(8,128)(2,1)S(1)}, bf16[544,128]{1,0:T(8,128)(2,1)S(1)}, u32[]{:S(2)}, u32[]{:S(2)}) collective-permute-start(bf16[544,128]{1,0:T(8,128)(2,1)S(1)} %get-tuple-element.33.turn), channel_id=1, source_target_pairs={{0,2},{1,3},{2,0},{3,1},{4,6},{5,7},{6,4},{7,5},{8,10},{9,11},{10,... | collective-permute-start | bytes 417800 | tf_op jit(solution)/shard_map/ppermute | solution.py:296
  16.2 0.7 %collective-permute-start.5 = (bf16[512,128]{1,0:T(8,128)(2,1)S(1)}, bf16[512,128]{1,0:T(8,128)(2,1)S(1)}, u32[]{:S(2)}, u32[]{:S(2)}) collective-permute-start(bf16[512,128]{1,0:T(8,128)(2,1)S(1)} %get-tuple-element.32.half_a), channel_id=1, source_target_pairs={{0,4},{1,5},{2,6},{3,7},{4,0},{5,1},{6,2},{7,3},{8,12},{9,13},{10,... | collective-permute-start | bytes 393224 | tf_op jit(solution)/shard_map/ppermute | solution.py:296
  16.9 1.8 %collective-permute-start.10 = (bf16[512,128]{1,0:T(8,128)(2,1)S(1)}, bf16[512,128]{1,0:T(8,128)(2,1)S(1)}, u32[]{:S(2)}, u32[]{:S(2)}) collective-permute-start(bf16[512,128]{1,0:T(8,128)(2,1)S(1)} %get-tuple-element.41), channel_id=1, source_target_pairs={{0,12},{1,13},{2,14},{3,15},{4,8},{5,9},{6,10},{7,11},{8,4},{9,5},... | collective-permute-start | bytes 393224 | tf_op jit(solution)/shard_map/ppermute | solution.py:296
  18.7 1.0 %collective-permute-start.11 = (bf16[512,128]{1,0:T(8,128)(2,1)S(1)}, bf16[512,128]{1,0:T(8,128)(2,1)S(1)}, u32[]{:S(2)}, u32[]{:S(2)}) collective-permute-start(bf16[512,128]{1,0:T(8,128)(2,1)S(1)} %get-tuple-element.42), channel_id=1, source_target_pairs={{0,8},{1,9},{2,10},{3,11},{4,12},{5,13},{6,14},{7,15},{8,0},{9,1},... | collective-permute-start | bytes 393224 | tf_op jit(solution)/shard_map/ppermute | solution.py:296
  19.7 2.7 %collective-permute-done.5.came_a = bf16[512,128]{1,0:T(8,128)(2,1)S(1)} collective-permute-done((bf16[512,128]{1,0:T(8,128)(2,1)S(1)}, bf16[512,128]{1,0:T(8,128)(2,1)S(1)}, u32[]{:S(2)}, u32[]{:S(2)}) %collective-permute-start.5) | collective-permute-done | bytes 131104 | tf_op jit(solution)/shard_map/ppermute | solution.py:296
  22.4 0.0 collective-permute-done.6.came_b.refs_1_
  22.4 0.1 shard_map.106
  22.5 0.1 collective-permute-start.9
  22.5 0.6 %collective-permute-start.7 = (bf16[1024,128]{1,0:T(8,128)(2,1)S(1)}, bf16[1024,128]{1,0:T(8,128)(2,1)S(1)}, u32[]{:S(2)}, u32[]{:S(2)}) collective-permute-start(bf16[1024,128]{1,0:T(8,128)(2,1)S(1)} %get-tuple-element.34.a), channel_id=1, source_target_pairs={{0,2},{1,3},{2,0},{3,1},{4,6},{5,7},{6,4},{7,5},{8,10},{9,11},{10,... | collective-permute-start | bytes 786440 | tf_op jit(solution)/shard_map/ppermute | solution.py:296
  23.1 0.6 %collective-permute-start.8 = (bf16[576,128]{1,0:T(8,128)(2,1)S(1)}, bf16[576,128]{1,0:T(8,128)(2,1)S(1)}, u32[]{:S(2)}, u32[]{:S(2)}) collective-permute-start(bf16[576,128]{1,0:T(8,128)(2,1)S(1)} %get-tuple-element.35.b), channel_id=1, source_target_pairs={{0,4},{1,5},{2,6},{3,7},{4,0},{5,1},{6,2},{7,3},{8,12},{9,13},{10,... | collective-permute-start | bytes 442376 | tf_op jit(solution)/shard_map/ppermute | solution.py:296
  23.7 2.2 %collective-permute-done.10.refs_2_ = bf16[512,128]{1,0:T(8,128)(2,1)S(1)} collective-permute-done((bf16[512,128]{1,0:T(8,128)(2,1)S(1)}, bf16[512,128]{1,0:T(8,128)(2,1)S(1)}, u32[]{:S(2)}, u32[]{:S(2)}) %collective-permute-start.10) | collective-permute-done | bytes 131104 | tf_op jit(solution)/shard_map/ppermute | solution.py:296
  26.0 4.8 %collective-permute-done.11.refs_3_ = bf16[512,128]{1,0:T(8,128)(2,1)S(1)} collective-permute-done((bf16[512,128]{1,0:T(8,128)(2,1)S(1)}, bf16[512,128]{1,0:T(8,128)(2,1)S(1)}, u32[]{:S(2)}, u32[]{:S(2)}) %collective-permute-start.11) | collective-permute-done | bytes 131104 | tf_op jit(solution)/shard_map/ppermute | solution.py:296
  30.8 0.0 copy-start.1
  30.8 0.6 %collective-permute-done.8.far_b = bf16[576,128]{1,0:T(8,128)(2,1)S(1)} collective-permute-done((bf16[576,128]{1,0:T(8,128)(2,1)S(1)}, bf16[576,128]{1,0:T(8,128)(2,1)S(1)}, u32[]{:S(2)}, u32[]{:S(2)}) %collective-permute-start.8) | collective-permute-done | bytes 147488 | tf_op jit(solution)/shard_map/ppermute | solution.py:296
  31.4 0.0 collective-permute-done.7.far_a
  31.4 0.0 collective-permute-done.9.core
  31.5 0.1 collective-permute-start.12
  31.5 0.8 %copy-done.1 = bf16[1024,1024]{1,0:T(8,128)(2,1)S(1)} copy-done((bf16[1024,1024]{1,0:T(8,128)(2,1)S(1)}, bf16[1024,1024]{1,0:T(8,128)(2,1)}, u32[]{:S(2)}) %copy-start.1) | copy-done | bytes 2097176
  32.4 1.0 %shard_map.109 = (bf16[256,1024]{1,0:T(8,128)(2,1)S(1)}, bf16[256,1024]{1,0:T(8,128)(2,1)S(1)}, bf16[1024,512]{1,0:T(8,128)(2,1)S(1)}, bf16[8,128,128]{2,1,0:T(8...) custom-call(bf16[1024,128]{1,0:T(8,128)(2,1)S(1)} %get-tuple-element.34.a, ...), custom_call_target="tpu_custom_call" | custom-call | tf_op jit(solution)/shard_map/pallas_call | solution.py:274
  33.4 0.3 collective-permute-done.12.pair
  33.7 7.2 %shard_map.110 = (bf16[1,128,1024]{2,1,0:T(8,128)(2,1)}, f32[64,1024]{1,0:T(8,128)}, f32[64,1024]{1,0:T(8,128)}) custom-call(bf16[1600,128]{1,0:T(8,128)(2,1)S(1)} %collective-permute-done.9.core, bf16[2624,128]{1,0:T(8,128)(2,1)S(1)} %collective-permute-done.12.pair, bf16[768,128]{1,0:T(8,128)(2,1)S(1)} %get-tuple-element.40.refs_0_, ...), custom_call_target="tpu_custom_call" | custom-call | tf_op jit(solution)/shard_map/pallas_call | solution.py:274
  (2 shorter events, 0.1 us)
Async XLA Ops:
  0.6 5.2 %copy-start.2 = (bf16[1,128,1024]{2,1,0:T(8,128)(2,1)S(1)}, bf16[1,128,1024]{2,1,0:T(8,128)(2,1)}, u32[]{:S(2)}) copy-start(bf16[1,128,1024]{2,1,0:T(8,128)(2,1)} %cotangent) | copy-start | bytes 786436
  0.6 5.2 %copy-start = (bf16[1024,1024]{1,0:T(8,128)(2,1)S(1)}, bf16[1024,1024]{1,0:T(8,128)(2,1)}, u32[]{:S(2)}) copy-start(bf16[1024,1024]{1,0:T(8,128)(2,1)} %refs_11_.1) | copy-start | bytes 6291460
  1.8 12.8 %collective-permute-start = (bf16[400,128]{1,0:T(8,128)(2,1)S(1)}, bf16[400,128]{1,0:T(8,128)(2,1)S(1)}, u32[]{:S(2)}, u32[]{:S(2)}) collective-permute-start(bf16[400,128]{1,0:T(8,128)(2,1)S(1)} %shard_map.103.piece), channel_id=1, source_target_pairs={{0,8},{1,9},{2,10},{3,11},{4,12},{5,13},{6,14},{7,15},{8,0},{9,1},... | collective-permute-start | bytes 307208 | tf_op jit(solution)/shard_map/ppermute | solution.py:296
  6.6 7.9 %collective-permute-start.1 = (bf16[384,128]{1,0:T(8,128)(2,1)S(1)}, bf16[384,128]{1,0:T(8,128)(2,1)S(1)}, u32[]{:S(2)}, u32[]{:S(2)}) collective-permute-start(bf16[384,128]{1,0:T(8,128)(2,1)S(1)} %get-tuple-element.28), channel_id=1, source_target_pairs={{0,2},{1,3},{2,0},{3,1},{4,6},{5,7},{6,4},{7,5},{8,10},{9,11},{10,... | collective-permute-start | bytes 294920 | tf_op jit(solution)/shard_map/ppermute | solution.py:296
  8.2 6.4 %collective-permute-start.2 = (bf16[384,128]{1,0:T(8,128)(2,1)S(1)}, bf16[384,128]{1,0:T(8,128)(2,1)S(1)}, u32[]{:S(2)}, u32[]{:S(2)}) collective-permute-start(bf16[384,128]{1,0:T(8,128)(2,1)S(1)} %get-tuple-element.29), channel_id=1, source_target_pairs={{0,2},{1,3},{2,0},{3,1},{4,6},{5,7},{6,4},{7,5},{8,10},{9,11},{10,... | collective-permute-start | bytes 294920 | tf_op jit(solution)/shard_map/ppermute | solution.py:296
  8.7 4.3 %collective-permute-start.3 = (bf16[256,128]{1,0:T(8,128)(2,1)S(1)}, bf16[256,128]{1,0:T(8,128)(2,1)S(1)}, u32[]{:S(2)}, u32[]{:S(2)}) collective-permute-start(bf16[256,128]{1,0:T(8,128)(2,1)S(1)} %get-tuple-element.30), channel_id=1, source_target_pairs={{0,4},{1,5},{2,6},{3,7},{4,0},{5,1},{6,2},{7,3},{8,12},{9,13},{10,... | collective-permute-start | bytes 196616 | tf_op jit(solution)/shard_map/ppermute | solution.py:296
  10.3 4.3 %collective-permute-start.4 = (bf16[256,128]{1,0:T(8,128)(2,1)S(1)}, bf16[256,128]{1,0:T(8,128)(2,1)S(1)}, u32[]{:S(2)}, u32[]{:S(2)}) collective-permute-start(bf16[256,128]{1,0:T(8,128)(2,1)S(1)} %get-tuple-element.31), channel_id=1, source_target_pairs={{0,4},{1,5},{2,6},{3,7},{4,0},{5,1},{6,2},{7,3},{8,12},{9,13},{10,... | collective-permute-start | bytes 196616 | tf_op jit(solution)/shard_map/ppermute | solution.py:296
  14.6 7.8 %collective-permute-start.6 = (bf16[544,128]{1,0:T(8,128)(2,1)S(1)}, bf16[544,128]{1,0:T(8,128)(2,1)S(1)}, u32[]{:S(2)}, u32[]{:S(2)}) collective-permute-start(bf16[544,128]{1,0:T(8,128)(2,1)S(1)} %get-tuple-element.33.turn), channel_id=1, source_target_pairs={{0,2},{1,3},{2,0},{3,1},{4,6},{5,7},{6,4},{7,5},{8,10},{9,11},{10,... | collective-permute-start | bytes 417800 | tf_op jit(solution)/shard_map/ppermute | solution.py:296
  16.2 6.2 %collective-permute-start.5 = (bf16[512,128]{1,0:T(8,128)(2,1)S(1)}, bf16[512,128]{1,0:T(8,128)(2,1)S(1)}, u32[]{:S(2)}, u32[]{:S(2)}) collective-permute-start(bf16[512,128]{1,0:T(8,128)(2,1)S(1)} %get-tuple-element.32.half_a), channel_id=1, source_target_pairs={{0,4},{1,5},{2,6},{3,7},{4,0},{5,1},{6,2},{7,3},{8,12},{9,13},{10,... | collective-permute-start | bytes 393224 | tf_op jit(solution)/shard_map/ppermute | solution.py:296
  16.9 9.1 %collective-permute-start.10 = (bf16[512,128]{1,0:T(8,128)(2,1)S(1)}, bf16[512,128]{1,0:T(8,128)(2,1)S(1)}, u32[]{:S(2)}, u32[]{:S(2)}) collective-permute-start(bf16[512,128]{1,0:T(8,128)(2,1)S(1)} %get-tuple-element.41), channel_id=1, source_target_pairs={{0,12},{1,13},{2,14},{3,15},{4,8},{5,9},{6,10},{7,11},{8,4},{9,5},... | collective-permute-start | bytes 393224 | tf_op jit(solution)/shard_map/ppermute | solution.py:296
  18.7 12.1 %collective-permute-start.11 = (bf16[512,128]{1,0:T(8,128)(2,1)S(1)}, bf16[512,128]{1,0:T(8,128)(2,1)S(1)}, u32[]{:S(2)}, u32[]{:S(2)}) collective-permute-start(bf16[512,128]{1,0:T(8,128)(2,1)S(1)} %get-tuple-element.42), channel_id=1, source_target_pairs={{0,8},{1,9},{2,10},{3,11},{4,12},{5,13},{6,14},{7,15},{8,0},{9,1},... | collective-permute-start | bytes 393224 | tf_op jit(solution)/shard_map/ppermute | solution.py:296
  22.5 9.0 %collective-permute-start.9 = (bf16[1600,128]{1,0:T(8,128)(2,1)S(1)}, bf16[1600,128]{1,0:T(8,128)(2,1)S(1)}, u32[]{:S(2)}, u32[]{:S(2)}) collective-permute-start(bf16[1600,128]{1,0:T(8,128)(2,1)S(1)} %get-tuple-element.36), channel_id=1, source_target_pairs={{0,1},{1,0},{2,3},{3,2},{4,5},{5,4},{6,7},{7,6},{8,9},{9,8},{10,11... | collective-permute-start | bytes 1228808 | tf_op jit(solution)/shard_map/ppermute | solution.py:296
  22.5 8.9 %collective-permute-start.7 = (bf16[1024,128]{1,0:T(8,128)(2,1)S(1)}, bf16[1024,128]{1,0:T(8,128)(2,1)S(1)}, u32[]{:S(2)}, u32[]{:S(2)}) collective-permute-start(bf16[1024,128]{1,0:T(8,128)(2,1)S(1)} %get-tuple-element.34.a), channel_id=1, source_target_pairs={{0,2},{1,3},{2,0},{3,1},{4,6},{5,7},{6,4},{7,5},{8,10},{9,11},{10,... | collective-permute-start | bytes 786440 | tf_op jit(solution)/shard_map/ppermute | solution.py:296
  23.1 8.3 %collective-permute-start.8 = (bf16[576,128]{1,0:T(8,128)(2,1)S(1)}, bf16[576,128]{1,0:T(8,128)(2,1)S(1)}, u32[]{:S(2)}, u32[]{:S(2)}) collective-permute-start(bf16[576,128]{1,0:T(8,128)(2,1)S(1)} %get-tuple-element.35.b), channel_id=1, source_target_pairs={{0,4},{1,5},{2,6},{3,7},{4,0},{5,1},{6,2},{7,3},{8,12},{9,13},{10,... | collective-permute-start | bytes 442376 | tf_op jit(solution)/shard_map/ppermute | solution.py:296
  30.8 1.6 %copy-start.1 = (bf16[1024,1024]{1,0:T(8,128)(2,1)S(1)}, bf16[1024,1024]{1,0:T(8,128)(2,1)}, u32[]{:S(2)}) copy-start(bf16[1024,1024]{1,0:T(8,128)(2,1)} %refs_10_.1) | copy-start | bytes 6291460
  31.5 2.2 %collective-permute-start.12 = (bf16[2624,128]{1,0:T(8,128)(2,1)S(1)}, bf16[2624,128]{1,0:T(8,128)(2,1)S(1)}, u32[]{:S(2)}, u32[]{:S(2)}) collective-permute-start(bf16[2624,128]{1,0:T(8,128)(2,1)S(1)} %shard_map.108), channel_id=1, source_target_pairs={{0,1},{1,0},{2,3},{3,2},{4,5},{5,4},{6,7},{7,6},{8,9},{9,8},{10,11... | collective-permute-start | bytes 2015240 | tf_op jit(solution)/shard_map/ppermute | solution.py:296

commit v18 on v16

--- a/solution.py
+++ b/solution.py
@@ -166,7 +166,7 @@
     return nt(adj, chosen).astype(BF16)
 
 
-def early_kernel(own, slots, cut, a, far_a, b, far_b, w_first, feat, lifted, spread, adj, meta, w_piece):
+def early_kernel(own, slots, cut, a, far_a, b, far_b, w_first, feat, lifted, spread, adj, meta, w_piece, partial):
     held = own * slots
     rows = adj.shape[1]
     place = lax.axis_index("grp")
@@ -176,6 +176,9 @@
     for p in range(GROUP // 2):
         picks = meta[p, 0:1, :].astype(F32).astype(jnp.int32)
         spread[p * rows : (p + 1) * rows, :] = spread_of(place, held, slots, adj[p], picks)
+    chunk = min(w_first.shape[1], 2 * LANES)
+    for c in range(0, w_first.shape[1], chunk):
+        partial[:, c : c + chunk] = nn(spread[:, : feat.shape[0]], lifted[:, c : c + chunk])
     each = w_piece.shape[0]
     wide = max(each, LANES)
     per = wide // each
@@ -190,8 +193,8 @@
 def step_kernel(own, slots, cut, rest, core, pair, *refs):
     blocks, refs = refs[: 2 + len(FAR)], refs[2 + len(FAR) :]
     early_feat, early_lifted, early_spread, early_adj, early_meta, w_piece = refs[:6]
-    w_first, w_second, output, grad_first, grad_second = refs[6:11]
-    hidden, spread, feat, adj, meta, dout, dpre, lifted, result, grads, second, sems = refs[11:]
+    partial, w_first, w_second, output, grad_first, grad_second = refs[6:12]
+    hidden, spread, feat, adj, meta, dout, dpre, lifted, result, grads, second, sems = refs[12:]
     width = w_first.shape[0]
     held = own * slots
     rows = adj.shape[1]
@@ -245,8 +248,11 @@
     chunk = min(width, 2 * LANES)
     for c in range(0, width, chunk):
         span = slice(c, c + chunk)
-        half = 0.5 * nn(spread[...], lifted[:, span])
-        hidden[:, span] = (half + half * jnp.tanh(half)).astype(BF16)
+        here = first * rows
+        half = 0.5 * (partial[:, span] + nn(spread[:here, first * held :], lifted[late, span]))
+        hidden[:here, span] = (half + half * jnp.tanh(half)).astype(BF16)
+        half = 0.5 * nn(spread[here:, :], lifted[:, span])
+        hidden[here:, span] = (half + half * jnp.tanh(half)).astype(BF16)
         if c:
             done = slice(c - chunk, c)
             second[:, done] = nn(dout[...], hidden[:, done])
@@ -346,6 +352,7 @@
             ((half, rows, rows), BF16),
             ((half, META, LANES), BF16),
             ((each, width), BF16),
+            ((half * rows, width), F32),
         ],
         limit=LIMIT,
     )

time: 40.7 us -> 40.6 us (level)
  waiting for transfers between devices: 14.3 us -> 13.8 us
    ppermute x11, waiting for transfers between devices: 14.3 us -> 13.8 us  [swap(): return lax.ppermute(x, 'grp', [(i, i ^ slot) for i in range(GROUP)])]
    pallas_call x8, Pallas kernels: 10.2 us -> 10.6 us  [call(): pl.pallas_call(kernel, out_shape=tuple((jax.ShapeDtypeStruct(*out) for ou...]
  transfers between devices with their start and end apart: 11 -> 11, of which waited for: 5 -> 5; matrix products, arithmetic and copies ran while one was open for 0% -> 0% of each run, Pallas kernels for 3% -> 4%
where the time goes in v18:
time: 40.6 us; the launch traced here: 40.5 us
  starting transfers between devices  14.7 us (36%)
  waiting for transfers between devices  13.8 us (34%)
  Pallas kernels  10.6 us (26%)
  between operations  0.73 us (2%)
  local copies, waits for them, and re-layouts  0.62 us (2%)
    ppermute x11, starting transfers between devices, swap(): return lax.ppermute(x, 'grp', [(i, i ^ slot) for i in range(GROUP)])  14.7 us
    ppermute x11, waiting for transfers between devices, swap(): return lax.ppermute(x, 'grp', [(i, i ^ slot) for i in range(GROUP)])  13.8 us
    pallas_call x8, Pallas kernels, call(): pl.pallas_call(kernel, out_shape=tuple((jax.ShapeDtypeStruct(*out) for ou...  10.6 us
  transfers between devices with their start and end apart: 11, of which 5 were waited for; matrix products, arithmetic and copies ran while one was open for 0% of the time, Pallas kernels for 4%

profile of v18, /device:TPU:0, one launch (start us, length us, event | category | flops | bytes accessed | tf_op | source)
XLA Modules:
  0.0 40.5 jit_solution(11317192638364413823)
XLA Ops:
  0.6 0.0 copy-start.2
  0.6 0.0 copy-start
  0.7 1.1 %shard_map.103.piece = bf16[400,128]{1,0:T(8,128)(2,1)S(1)} custom-call(s32[2]{0:T(128)} %counts.1, s32[1,8]{1,0:T(1,128)} %owner.1, s32[1,8]{1,0:T(1,128)} %local.1, bf16[2,16,1024]{2,1,0:T(8,128)(2,1)} %features.1, bf16[1,128,128]{2,1,0:T(8,128)(2,1)} %adjacency.1), custom_call_target="tpu_custom_call" | custom-call | flops 10000000000 | tf_op jit(solution)/shard_map/pallas_call | solution.py:279
  1.8 0.0 copy-done.2
  1.8 0.6 %copy-done = bf16[1024,1024]{1,0:T(8,128)(2,1)S(1)} copy-done((bf16[1024,1024]{1,0:T(8,128)(2,1)S(1)}, bf16[1024,1024]{1,0:T(8,128)(2,1)}, u32[]{:S(2)}) %copy-start) | copy-done | bytes 2097176
  2.4 0.7 %shard_map.104 = (bf16[768,128]{1,0:T(8,128)(2,1)S(1)}, bf16[768,128]{1,0:T(8,128)(2,1)S(1)}, bf16[512,128]{1,0:T(8,128)(2,1)S(1)}) custom-call(bf16[1,128,1024]{2,1,0:T(8,128)(2,1)S(1)} %copy-done.2, bf16[1024,1024]{1,0:T(8,128)(2,1)S(1)} %copy-done), custom_call_target="tpu_custom_call" | custom-call | tf_op jit(solution)/shard_map/pallas_call | solution.py:279
  3.1 3.0 %collective-permute-start.1 = (bf16[768,128]{1,0:T(8,128)(2,1)S(1)}, bf16[768,128]{1,0:T(8,128)(2,1)S(1)}, u32[]{:S(2)}, u32[]{:S(2)}) collective-permute-start(bf16[768,128]{1,0:T(8,128)(2,1)S(1)} %get-tuple-element.27), channel_id=1, source_target_pairs={{0,2},{1,3},{2,0},{3,1},{4,6},{5,7},{6,4},{7,5},{8,10},{9,11},{10,... | collective-permute-start | bytes 589832 | tf_op jit(solution)/shard_map/ppermute | solution.py:301
  6.1 1.6 %collective-permute-start.2 = (bf16[512,128]{1,0:T(8,128)(2,1)S(1)}, bf16[512,128]{1,0:T(8,128)(2,1)S(1)}, u32[]{:S(2)}, u32[]{:S(2)}) collective-permute-start(bf16[512,128]{1,0:T(8,128)(2,1)S(1)} %get-tuple-element.28), channel_id=1, source_target_pairs={{0,4},{1,5},{2,6},{3,7},{4,0},{5,1},{6,2},{7,3},{8,12},{9,13},{10,... | collective-permute-start | bytes 393224 | tf_op jit(solution)/shard_map/ppermute | solution.py:301
  7.7 2.6 %collective-permute-start = (bf16[400,128]{1,0:T(8,128)(2,1)S(1)}, bf16[400,128]{1,0:T(8,128)(2,1)S(1)}, u32[]{:S(2)}, u32[]{:S(2)}) collective-permute-start(bf16[400,128]{1,0:T(8,128)(2,1)S(1)} %shard_map.103.piece), channel_id=1, source_target_pairs={{0,8},{1,9},{2,10},{3,11},{4,12},{5,13},{6,14},{7,15},{8,0},{9,1},... | collective-permute-start | bytes 307208 | tf_op jit(solution)/shard_map/ppermute | solution.py:301
  10.3 3.8 %collective-permute-done.came = bf16[400,128]{1,0:T(8,128)(2,1)S(1)} collective-permute-done((bf16[400,128]{1,0:T(8,128)(2,1)S(1)}, bf16[400,128]{1,0:T(8,128)(2,1)S(1)}, u32[]{:S(2)}, u32[]{:S(2)}) %collective-permute-start) | collective-permute-done | bytes 102432 | tf_op jit(solution)/shard_map/ppermute | solution.py:301
  14.1 0.0 collective-permute-done.2.beside
  14.1 0.0 collective-permute-done.1.across
  14.2 0.6 %collective-permute-start.4 = (bf16[544,128]{1,0:T(8,128)(2,1)S(1)}, bf16[544,128]{1,0:T(8,128)(2,1)S(1)}, u32[]{:S(2)}, u32[]{:S(2)}) collective-permute-start(bf16[544,128]{1,0:T(8,128)(2,1)S(1)} %get-tuple-element.30.turn), channel_id=1, source_target_pairs={{0,2},{1,3},{2,0},{3,1},{4,6},{5,7},{6,4},{7,5},{8,10},{9,11},{10,... | collective-permute-start | bytes 417800 | tf_op jit(solution)/shard_map/ppermute | solution.py:301
  14.7 1.8 %collective-permute-start.3 = (bf16[512,128]{1,0:T(8,128)(2,1)S(1)}, bf16[512,128]{1,0:T(8,128)(2,1)S(1)}, u32[]{:S(2)}, u32[]{:S(2)}) collective-permute-start(bf16[512,128]{1,0:T(8,128)(2,1)S(1)} %get-tuple-element.29.half_a), channel_id=1, source_target_pairs={{0,4},{1,5},{2,6},{3,7},{4,0},{5,1},{6,2},{7,3},{8,12},{9,13},{10,... | collective-permute-start | bytes 393224 | tf_op jit(solution)/shard_map/ppermute | solution.py:301
  16.5 1.7 %collective-permute-start.8 = (bf16[512,128]{1,0:T(8,128)(2,1)S(1)}, bf16[512,128]{1,0:T(8,128)(2,1)S(1)}, u32[]{:S(2)}, u32[]{:S(2)}) collective-permute-start(bf16[512,128]{1,0:T(8,128)(2,1)S(1)} %get-tuple-element.38), channel_id=1, source_target_pairs={{0,12},{1,13},{2,14},{3,15},{4,8},{5,9},{6,10},{7,11},{8,4},{9,5},... | collective-permute-start | bytes 393224 | tf_op jit(solution)/shard_map/ppermute | solution.py:301
  18.2 0.6 %collective-permute-start.9 = (bf16[512,128]{1,0:T(8,128)(2,1)S(1)}, bf16[512,128]{1,0:T(8,128)(2,1)S(1)}, u32[]{:S(2)}, u32[]{:S(2)}) collective-permute-start(bf16[512,128]{1,0:T(8,128)(2,1)S(1)} %get-tuple-element.39), channel_id=1, source_target_pairs={{0,8},{1,9},{2,10},{3,11},{4,12},{5,13},{6,14},{7,15},{8,0},{9,1},... | collective-permute-start | bytes 393224 | tf_op jit(solution)/shard_map/ppermute | solution.py:301
  18.8 2.9 %collective-permute-done.3.came_a = bf16[512,128]{1,0:T(8,128)(2,1)S(1)} collective-permute-done((bf16[512,128]{1,0:T(8,128)(2,1)S(1)}, bf16[512,128]{1,0:T(8,128)(2,1)S(1)}, u32[]{:S(2)}, u32[]{:S(2)}) %collective-permute-start.3) | collective-permute-done | bytes 131104 | tf_op jit(solution)/shard_map/ppermute | solution.py:301
  21.7 0.0 collective-permute-done.4.came_b.refs_1_
  21.7 0.1 shard_map.106
  21.8 0.1 collective-permute-start.7
  21.8 1.6 %collective-permute-start.5 = (bf16[1024,128]{1,0:T(8,128)(2,1)S(1)}, bf16[1024,128]{1,0:T(8,128)(2,1)S(1)}, u32[]{:S(2)}, u32[]{:S(2)}) collective-permute-start(bf16[1024,128]{1,0:T(8,128)(2,1)S(1)} %get-tuple-element.31.a), channel_id=1, source_target_pairs={{0,2},{1,3},{2,0},{3,1},{4,6},{5,7},{6,4},{7,5},{8,10},{9,11},{10,... | collective-permute-start | bytes 786440 | tf_op jit(solution)/shard_map/ppermute | solution.py:301
  23.4 1.2 %collective-permute-start.6 = (bf16[576,128]{1,0:T(8,128)(2,1)S(1)}, bf16[576,128]{1,0:T(8,128)(2,1)S(1)}, u32[]{:S(2)}, u32[]{:S(2)}) collective-permute-start(bf16[576,128]{1,0:T(8,128)(2,1)S(1)} %get-tuple-element.32.b), channel_id=1, source_target_pairs={{0,4},{1,5},{2,6},{3,7},{4,0},{5,1},{6,2},{7,3},{8,12},{9,13},{10,... | collective-permute-start | bytes 442376 | tf_op jit(solution)/shard_map/ppermute | solution.py:301
  24.6 0.0 collective-permute-done.8.refs_2_
  24.6 4.1 %collective-permute-done.9.refs_3_ = bf16[512,128]{1,0:T(8,128)(2,1)S(1)} collective-permute-done((bf16[512,128]{1,0:T(8,128)(2,1)S(1)}, bf16[512,128]{1,0:T(8,128)(2,1)S(1)}, u32[]{:S(2)}, u32[]{:S(2)}) %collective-permute-start.9) | collective-permute-done | bytes 131104 | tf_op jit(solution)/shard_map/ppermute | solution.py:301
  28.7 0.0 copy-start.1
  28.7 2.4 %collective-permute-done.6.far_b = bf16[576,128]{1,0:T(8,128)(2,1)S(1)} collective-permute-done((bf16[576,128]{1,0:T(8,128)(2,1)S(1)}, bf16[576,128]{1,0:T(8,128)(2,1)S(1)}, u32[]{:S(2)}, u32[]{:S(2)}) %collective-permute-start.6) | collective-permute-done | bytes 147488 | tf_op jit(solution)/shard_map/ppermute | solution.py:301
  31.1 0.0 collective-permute-done.5.far_a
  31.1 0.0 collective-permute-done.7.core
  31.2 0.1 collective-permute-start.10
  31.2 0.0 copy-done.1
  31.3 1.6 %shard_map.109 = (bf16[256,1024]{1,0:T(8,128)(2,1)S(1)}, bf16[256,1024]{1,0:T(8,128)(2,1)S(1)}, bf16[1024,512]{1,0:T(8,128)(2,1)S(1)}, bf16[8,128,128]{2,1,0:T(8...) custom-call(bf16[1024,128]{1,0:T(8,128)(2,1)S(1)} %get-tuple-element.31.a, ...), custom_call_target="tpu_custom_call" | custom-call | tf_op jit(solution)/shard_map/pallas_call | solution.py:279
  32.8 0.5 %collective-permute-done.10.pair = bf16[2624,128]{1,0:T(8,128)(2,1)S(1)} collective-permute-done((bf16[2624,128]{1,0:T(8,128)(2,1)S(1)}, bf16[2624,128]{1,0:T(8,128)(2,1)S(1)}, u32[]{:S(2)}, u32[]{:S(2)}) %collective-permute-start.10) | collective-permute-done | bytes 671776 | tf_op jit(solution)/shard_map/ppermute | solution.py:301
  33.4 7.1 %shard_map.110 = (bf16[1,128,1024]{2,1,0:T(8,128)(2,1)}, f32[64,1024]{1,0:T(8,128)}, f32[64,1024]{1,0:T(8,128)}) custom-call(bf16[1600,128]{1,0:T(8,128)(2,1)S(1)} %collective-permute-done.7.core, bf16[2624,128]{1,0:T(8,128)(2,1)S(1)} %collective-permute-done.10.pair, bf16[768,128]{1,0:T(8,128)(2,1)S(1)} %get-tuple-element.37.refs_0_, ...), custom_call_target="tpu_custom_call" | custom-call | tf_op jit(solution)/shard_map/pallas_call | solution.py:279
  (3 shorter events, 0.1 us)
Async XLA Ops:
  0.6 1.1 %copy-start.2 = (bf16[1,128,1024]{2,1,0:T(8,128)(2,1)S(1)}, bf16[1,128,1024]{2,1,0:T(8,128)(2,1)}, u32[]{:S(2)}) copy-start(bf16[1,128,1024]{2,1,0:T(8,128)(2,1)} %cotangent) | copy-start | bytes 786436
  0.6 1.7 %copy-start = (bf16[1024,1024]{1,0:T(8,128)(2,1)S(1)}, bf16[1024,1024]{1,0:T(8,128)(2,1)}, u32[]{:S(2)}) copy-start(bf16[1024,1024]{1,0:T(8,128)(2,1)} %refs_12_.1) | copy-start | bytes 6291460
  3.1 11.0 %collective-permute-start.1 = (bf16[768,128]{1,0:T(8,128)(2,1)S(1)}, bf16[768,128]{1,0:T(8,128)(2,1)S(1)}, u32[]{:S(2)}, u32[]{:S(2)}) collective-permute-start(bf16[768,128]{1,0:T(8,128)(2,1)S(1)} %get-tuple-element.27), channel_id=1, source_target_pairs={{0,2},{1,3},{2,0},{3,1},{4,6},{5,7},{6,4},{7,5},{8,10},{9,11},{10,... | collective-permute-start | bytes 589832 | tf_op jit(solution)/shard_map/ppermute | solution.py:301
  6.1 8.0 %collective-permute-start.2 = (bf16[512,128]{1,0:T(8,128)(2,1)S(1)}, bf16[512,128]{1,0:T(8,128)(2,1)S(1)}, u32[]{:S(2)}, u32[]{:S(2)}) collective-permute-start(bf16[512,128]{1,0:T(8,128)(2,1)S(1)} %get-tuple-element.28), channel_id=1, source_target_pairs={{0,4},{1,5},{2,6},{3,7},{4,0},{5,1},{6,2},{7,3},{8,12},{9,13},{10,... | collective-permute-start | bytes 393224 | tf_op jit(solution)/shard_map/ppermute | solution.py:301
  7.7 6.4 %collective-permute-start = (bf16[400,128]{1,0:T(8,128)(2,1)S(1)}, bf16[400,128]{1,0:T(8,128)(2,1)S(1)}, u32[]{:S(2)}, u32[]{:S(2)}) collective-permute-start(bf16[400,128]{1,0:T(8,128)(2,1)S(1)} %shard_map.103.piece), channel_id=1, source_target_pairs={{0,8},{1,9},{2,10},{3,11},{4,12},{5,13},{6,14},{7,15},{8,0},{9,1},... | collective-permute-start | bytes 307208 | tf_op jit(solution)/shard_map/ppermute | solution.py:301
  14.2 7.5 %collective-permute-start.4 = (bf16[544,128]{1,0:T(8,128)(2,1)S(1)}, bf16[544,128]{1,0:T(8,128)(2,1)S(1)}, u32[]{:S(2)}, u32[]{:S(2)}) collective-permute-start(bf16[544,128]{1,0:T(8,128)(2,1)S(1)} %get-tuple-element.30.turn), channel_id=1, source_target_pairs={{0,2},{1,3},{2,0},{3,1},{4,6},{5,7},{6,4},{7,5},{8,10},{9,11},{10,... | collective-permute-start | bytes 417800 | tf_op jit(solution)/shard_map/ppermute | solution.py:301
  14.7 6.9 %collective-permute-start.3 = (bf16[512,128]{1,0:T(8,128)(2,1)S(1)}, bf16[512,128]{1,0:T(8,128)(2,1)S(1)}, u32[]{:S(2)}, u32[]{:S(2)}) collective-permute-start(bf16[512,128]{1,0:T(8,128)(2,1)S(1)} %get-tuple-element.29.half_a), channel_id=1, source_target_pairs={{0,4},{1,5},{2,6},{3,7},{4,0},{5,1},{6,2},{7,3},{8,12},{9,13},{10,... | collective-permute-start | bytes 393224 | tf_op jit(solution)/shard_map/ppermute | solution.py:301
  16.5 8.1 %collective-permute-start.8 = (bf16[512,128]{1,0:T(8,128)(2,1)S(1)}, bf16[512,128]{1,0:T(8,128)(2,1)S(1)}, u32[]{:S(2)}, u32[]{:S(2)}) collective-permute-start(bf16[512,128]{1,0:T(8,128)(2,1)S(1)} %get-tuple-element.38), channel_id=1, source_target_pairs={{0,12},{1,13},{2,14},{3,15},{4,8},{5,9},{6,10},{7,11},{8,4},{9,5},... | collective-permute-start | bytes 393224 | tf_op jit(solution)/shard_map/ppermute | solution.py:301
  18.2 10.4 %collective-permute-start.9 = (bf16[512,128]{1,0:T(8,128)(2,1)S(1)}, bf16[512,128]{1,0:T(8,128)(2,1)S(1)}, u32[]{:S(2)}, u32[]{:S(2)}) collective-permute-start(bf16[512,128]{1,0:T(8,128)(2,1)S(1)} %get-tuple-element.39), channel_id=1, source_target_pairs={{0,8},{1,9},{2,10},{3,11},{4,12},{5,13},{6,14},{7,15},{8,0},{9,1},... | collective-permute-start | bytes 393224 | tf_op jit(solution)/shard_map/ppermute | solution.py:301
  21.8 9.4 %collective-permute-start.7 = (bf16[1600,128]{1,0:T(8,128)(2,1)S(1)}, bf16[1600,128]{1,0:T(8,128)(2,1)S(1)}, u32[]{:S(2)}, u32[]{:S(2)}) collective-permute-start(bf16[1600,128]{1,0:T(8,128)(2,1)S(1)} %get-tuple-element.33), channel_id=1, source_target_pairs={{0,1},{1,0},{2,3},{3,2},{4,5},{5,4},{6,7},{7,6},{8,9},{9,8},{10,11... | collective-permute-start | bytes 1228808 | tf_op jit(solution)/shard_map/ppermute | solution.py:301
  21.8 9.3 %collective-permute-start.5 = (bf16[1024,128]{1,0:T(8,128)(2,1)S(1)}, bf16[1024,128]{1,0:T(8,128)(2,1)S(1)}, u32[]{:S(2)}, u32[]{:S(2)}) collective-permute-start(bf16[1024,128]{1,0:T(8,128)(2,1)S(1)} %get-tuple-element.31.a), channel_id=1, source_target_pairs={{0,2},{1,3},{2,0},{3,1},{4,6},{5,7},{6,4},{7,5},{8,10},{9,11},{10,... | collective-permute-start | bytes 786440 | tf_op jit(solution)/shard_map/ppermute | solution.py:301
  23.4 7.7 %collective-permute-start.6 = (bf16[576,128]{1,0:T(8,128)(2,1)S(1)}, bf16[576,128]{1,0:T(8,128)(2,1)S(1)}, u32[]{:S(2)}, u32[]{:S(2)}) collective-permute-start(bf16[576,128]{1,0:T(8,128)(2,1)S(1)} %get-tuple-element.32.b), channel_id=1, source_target_pairs={{0,4},{1,5},{2,6},{3,7},{4,0},{5,1},{6,2},{7,3},{8,12},{9,13},{10,... | collective-permute-start | bytes 442376 | tf_op jit(solution)/shard_map/ppermute | solution.py:301
  28.7 2.6 %copy-start.1 = (bf16[1024,1024]{1,0:T(8,128)(2,1)S(1)}, bf16[1024,1024]{1,0:T(8,128)(2,1)}, u32[]{:S(2)}) copy-start(bf16[1024,1024]{1,0:T(8,128)(2,1)} %refs_11_.1) | copy-start | bytes 6291460
  31.2 2.2 %collective-permute-start.10 = (bf16[2624,128]{1,0:T(8,128)(2,1)S(1)}, bf16[2624,128]{1,0:T(8,128)(2,1)S(1)}, u32[]{:S(2)}, u32[]{:S(2)}) collective-permute-start(bf16[2624,128]{1,0:T(8,128)(2,1)S(1)} %shard_map.108), channel_id=1, source_target_pairs={{0,1},{1,0},{2,3},{3,2},{4,5},{5,4},{6,7},{7,6},{8,9},{9,8},{10,11... | collective-permute-start | bytes 2015240 | tf_op jit(solution)/shard_map/ppermute | solution.py:301

commit v19 on v18

--- a/solution.py
+++ b/solution.py
@@ -172,7 +172,7 @@
     place = lax.axis_index("grp")
     arrays = list(zip((a, far_a, b, far_b), HALF_A + HALF_B))
     lay_out([(ref, 0, at) for ref, at in arrays], held, cut, feat, adj, meta)
-    lifted[...] = nn(feat[...], w_first[...]).astype(BF16)
+    lifted[...] = (0.5 * nn(feat[...], w_first[...])).astype(BF16)
     for p in range(GROUP // 2):
         picks = meta[p, 0:1, :].astype(F32).astype(jnp.int32)
         spread[p * rows : (p + 1) * rows, :] = spread_of(place, held, slots, adj[p], picks)
@@ -223,7 +223,7 @@
     masks = (lane < count).astype(F32)
 
     late = slice(first * held, GROUP * held)
-    lifted[late, :] = nn(feat[late, :], w_first[...]).astype(BF16)
+    lifted[late, :] = (0.5 * nn(feat[late, :], w_first[...])).astype(BF16)
     for p in range(first, GROUP):
         span = slice(p * rows, (p + 1) * rows)
         spread[span, :] = spread_of(place, held, slots, adj[p], picks[p : p + 1])
@@ -249,9 +249,9 @@
     for c in range(0, width, chunk):
         span = slice(c, c + chunk)
         here = first * rows
-        half = 0.5 * (partial[:, span] + nn(spread[:here, first * held :], lifted[late, span]))
+        half = partial[:, span] + nn(spread[:here, first * held :], lifted[late, span])
         hidden[:here, span] = (half + half * jnp.tanh(half)).astype(BF16)
-        half = 0.5 * nn(spread[here:, :], lifted[:, span])
+        half = nn(spread[here:, :], lifted[:, span])
         hidden[here:, span] = (half + half * jnp.tanh(half)).astype(BF16)
         if c:
             done = slice(c - chunk, c)

time: 40.6 us -> 40.2 us (level)
  no operation moved by 1% of the time
where the time goes in v19:
time: 40.2 us; the launch traced here: 40.1 us
  starting transfers between devices  14.7 us (37%)
  waiting for transfers between devices  13.8 us (34%)
  Pallas kernels  10.2 us (25%)
  between operations  0.73 us (2%)
  local copies, waits for them, and re-layouts  0.62 us (2%)
    ppermute x11, starting transfers between devices, swap(): return lax.ppermute(x, 'grp', [(i, i ^ slot) for i in range(GROUP)])  14.7 us
    ppermute x11, waiting for transfers between devices, swap(): return lax.ppermute(x, 'grp', [(i, i ^ slot) for i in range(GROUP)])  13.8 us
    pallas_call x8, Pallas kernels, call(): pl.pallas_call(kernel, out_shape=tuple((jax.ShapeDtypeStruct(*out) for ou...  10.2 us
  transfers between devices with their start and end apart: 11, of which 5 were waited for; matrix products, arithmetic and copies ran while one was open for 0% of the time, Pallas kernels for 4%

profile of v19, /device:TPU:0, one launch (start us, length us, event | category | flops | bytes accessed | tf_op | source)
XLA Modules:
  0.0 40.1 jit_solution(203774122090217293)
XLA Ops:
  0.6 0.0 copy-start.2
  0.6 0.0 copy-start
  0.7 1.1 %shard_map.103.piece = bf16[400,128]{1,0:T(8,128)(2,1)S(1)} custom-call(s32[2]{0:T(128)} %counts.1, s32[1,8]{1,0:T(1,128)} %owner.1, s32[1,8]{1,0:T(1,128)} %local.1, bf16[2,16,1024]{2,1,0:T(8,128)(2,1)} %features.1, bf16[1,128,128]{2,1,0:T(8,128)(2,1)} %adjacency.1), custom_call_target="tpu_custom_call" | custom-call | flops 10000000000 | tf_op jit(solution)/shard_map/pallas_call | solution.py:279
  1.8 0.0 copy-done.2
  1.8 0.6 %copy-done = bf16[1024,1024]{1,0:T(8,128)(2,1)S(1)} copy-done((bf16[1024,1024]{1,0:T(8,128)(2,1)S(1)}, bf16[1024,1024]{1,0:T(8,128)(2,1)}, u32[]{:S(2)}) %copy-start) | copy-done | bytes 2097176
  2.4 0.7 %shard_map.104 = (bf16[768,128]{1,0:T(8,128)(2,1)S(1)}, bf16[768,128]{1,0:T(8,128)(2,1)S(1)}, bf16[512,128]{1,0:T(8,128)(2,1)S(1)}) custom-call(bf16[1,128,1024]{2,1,0:T(8,128)(2,1)S(1)} %copy-done.2, bf16[1024,1024]{1,0:T(8,128)(2,1)S(1)} %copy-done), custom_call_target="tpu_custom_call" | custom-call | tf_op jit(solution)/shard_map/pallas_call | solution.py:279
  3.1 3.0 %collective-permute-start.1 = (bf16[768,128]{1,0:T(8,128)(2,1)S(1)}, bf16[768,128]{1,0:T(8,128)(2,1)S(1)}, u32[]{:S(2)}, u32[]{:S(2)}) collective-permute-start(bf16[768,128]{1,0:T(8,128)(2,1)S(1)} %get-tuple-element.27), channel_id=1, source_target_pairs={{0,2},{1,3},{2,0},{3,1},{4,6},{5,7},{6,4},{7,5},{8,10},{9,11},{10,... | collective-permute-start | bytes 589832 | tf_op jit(solution)/shard_map/ppermute | solution.py:301
  6.1 1.6 %collective-permute-start.2 = (bf16[512,128]{1,0:T(8,128)(2,1)S(1)}, bf16[512,128]{1,0:T(8,128)(2,1)S(1)}, u32[]{:S(2)}, u32[]{:S(2)}) collective-permute-start(bf16[512,128]{1,0:T(8,128)(2,1)S(1)} %get-tuple-element.28), channel_id=1, source_target_pairs={{0,4},{1,5},{2,6},{3,7},{4,0},{5,1},{6,2},{7,3},{8,12},{9,13},{10,... | collective-permute-start | bytes 393224 | tf_op jit(solution)/shard_map/ppermute | solution.py:301
  7.7 2.6 %collective-permute-start = (bf16[400,128]{1,0:T(8,128)(2,1)S(1)}, bf16[400,128]{1,0:T(8,128)(2,1)S(1)}, u32[]{:S(2)}, u32[]{:S(2)}) collective-permute-start(bf16[400,128]{1,0:T(8,128)(2,1)S(1)} %shard_map.103.piece), channel_id=1, source_target_pairs={{0,8},{1,9},{2,10},{3,11},{4,12},{5,13},{6,14},{7,15},{8,0},{9,1},... | collective-permute-start | bytes 307208 | tf_op jit(solution)/shard_map/ppermute | solution.py:301
  10.3 3.8 %collective-permute-done.came = bf16[400,128]{1,0:T(8,128)(2,1)S(1)} collective-permute-done((bf16[400,128]{1,0:T(8,128)(2,1)S(1)}, bf16[400,128]{1,0:T(8,128)(2,1)S(1)}, u32[]{:S(2)}, u32[]{:S(2)}) %collective-permute-start) | collective-permute-done | bytes 102432 | tf_op jit(solution)/shard_map/ppermute | solution.py:301
  14.1 0.0 collective-permute-done.2.beside
  14.1 0.0 collective-permute-done.1.across
  14.2 0.6 %collective-permute-start.4 = (bf16[544,128]{1,0:T(8,128)(2,1)S(1)}, bf16[544,128]{1,0:T(8,128)(2,1)S(1)}, u32[]{:S(2)}, u32[]{:S(2)}) collective-permute-start(bf16[544,128]{1,0:T(8,128)(2,1)S(1)} %get-tuple-element.30.turn), channel_id=1, source_target_pairs={{0,2},{1,3},{2,0},{3,1},{4,6},{5,7},{6,4},{7,5},{8,10},{9,11},{10,... | collective-permute-start | bytes 417800 | tf_op jit(solution)/shard_map/ppermute | solution.py:301
  14.7 1.8 %collective-permute-start.3 = (bf16[512,128]{1,0:T(8,128)(2,1)S(1)}, bf16[512,128]{1,0:T(8,128)(2,1)S(1)}, u32[]{:S(2)}, u32[]{:S(2)}) collective-permute-start(bf16[512,128]{1,0:T(8,128)(2,1)S(1)} %get-tuple-element.29.half_a), channel_id=1, source_target_pairs={{0,4},{1,5},{2,6},{3,7},{4,0},{5,1},{6,2},{7,3},{8,12},{9,13},{10,... | collective-permute-start | bytes 393224 | tf_op jit(solution)/shard_map/ppermute | solution.py:301
  16.5 1.7 %collective-permute-start.8 = (bf16[512,128]{1,0:T(8,128)(2,1)S(1)}, bf16[512,128]{1,0:T(8,128)(2,1)S(1)}, u32[]{:S(2)}, u32[]{:S(2)}) collective-permute-start(bf16[512,128]{1,0:T(8,128)(2,1)S(1)} %get-tuple-element.38), channel_id=1, source_target_pairs={{0,12},{1,13},{2,14},{3,15},{4,8},{5,9},{6,10},{7,11},{8,4},{9,5},... | collective-permute-start | bytes 393224 | tf_op jit(solution)/shard_map/ppermute | solution.py:301
  18.2 0.6 %collective-permute-start.9 = (bf16[512,128]{1,0:T(8,128)(2,1)S(1)}, bf16[512,128]{1,0:T(8,128)(2,1)S(1)}, u32[]{:S(2)}, u32[]{:S(2)}) collective-permute-start(bf16[512,128]{1,0:T(8,128)(2,1)S(1)} %get-tuple-element.39), channel_id=1, source_target_pairs={{0,8},{1,9},{2,10},{3,11},{4,12},{5,13},{6,14},{7,15},{8,0},{9,1},... | collective-permute-start | bytes 393224 | tf_op jit(solution)/shard_map/ppermute | solution.py:301
  18.8 2.9 %collective-permute-done.3.came_a = bf16[512,128]{1,0:T(8,128)(2,1)S(1)} collective-permute-done((bf16[512,128]{1,0:T(8,128)(2,1)S(1)}, bf16[512,128]{1,0:T(8,128)(2,1)S(1)}, u32[]{:S(2)}, u32[]{:S(2)}) %collective-permute-start.3) | collective-permute-done | bytes 131104 | tf_op jit(solution)/shard_map/ppermute | solution.py:301
  21.7 0.0 collective-permute-done.4.came_b.refs_1_
  21.7 0.1 shard_map.106
  21.8 0.1 collective-permute-start.7
  21.8 1.6 %collective-permute-start.5 = (bf16[1024,128]{1,0:T(8,128)(2,1)S(1)}, bf16[1024,128]{1,0:T(8,128)(2,1)S(1)}, u32[]{:S(2)}, u32[]{:S(2)}) collective-permute-start(bf16[1024,128]{1,0:T(8,128)(2,1)S(1)} %get-tuple-element.31.a), channel_id=1, source_target_pairs={{0,2},{1,3},{2,0},{3,1},{4,6},{5,7},{6,4},{7,5},{8,10},{9,11},{10,... | collective-permute-start | bytes 786440 | tf_op jit(solution)/shard_map/ppermute | solution.py:301
  23.4 1.2 %collective-permute-start.6 = (bf16[576,128]{1,0:T(8,128)(2,1)S(1)}, bf16[576,128]{1,0:T(8,128)(2,1)S(1)}, u32[]{:S(2)}, u32[]{:S(2)}) collective-permute-start(bf16[576,128]{1,0:T(8,128)(2,1)S(1)} %get-tuple-element.32.b), channel_id=1, source_target_pairs={{0,4},{1,5},{2,6},{3,7},{4,0},{5,1},{6,2},{7,3},{8,12},{9,13},{10,... | collective-permute-start | bytes 442376 | tf_op jit(solution)/shard_map/ppermute | solution.py:301
  24.6 0.0 collective-permute-done.8.refs_2_
  24.6 4.1 %collective-permute-done.9.refs_3_ = bf16[512,128]{1,0:T(8,128)(2,1)S(1)} collective-permute-done((bf16[512,128]{1,0:T(8,128)(2,1)S(1)}, bf16[512,128]{1,0:T(8,128)(2,1)S(1)}, u32[]{:S(2)}, u32[]{:S(2)}) %collective-permute-start.9) | collective-permute-done | bytes 131104 | tf_op jit(solution)/shard_map/ppermute | solution.py:301
  28.7 0.0 copy-start.1
  28.7 2.4 %collective-permute-done.6.far_b = bf16[576,128]{1,0:T(8,128)(2,1)S(1)} collective-permute-done((bf16[576,128]{1,0:T(8,128)(2,1)S(1)}, bf16[576,128]{1,0:T(8,128)(2,1)S(1)}, u32[]{:S(2)}, u32[]{:S(2)}) %collective-permute-start.6) | collective-permute-done | bytes 147488 | tf_op jit(solution)/shard_map/ppermute | solution.py:301
  31.1 0.0 collective-permute-done.5.far_a
  31.1 0.0 collective-permute-done.7.core
  31.2 0.1 collective-permute-start.10
  31.2 0.0 copy-done.1
  31.3 1.6 %shard_map.109 = (bf16[256,1024]{1,0:T(8,128)(2,1)S(1)}, bf16[256,1024]{1,0:T(8,128)(2,1)S(1)}, bf16[1024,512]{1,0:T(8,128)(2,1)S(1)}, bf16[8,128,128]{2,1,0:T(8...) custom-call(bf16[1024,128]{1,0:T(8,128)(2,1)S(1)} %get-tuple-element.31.a, ...), custom_call_target="tpu_custom_call" | custom-call | tf_op jit(solution)/shard_map/pallas_call | solution.py:279
  32.8 0.5 %collective-permute-done.10.pair = bf16[2624,128]{1,0:T(8,128)(2,1)S(1)} collective-permute-done((bf16[2624,128]{1,0:T(8,128)(2,1)S(1)}, bf16[2624,128]{1,0:T(8,128)(2,1)S(1)}, u32[]{:S(2)}, u32[]{:S(2)}) %collective-permute-start.10) | collective-permute-done | bytes 671776 | tf_op jit(solution)/shard_map/ppermute | solution.py:301
  33.4 6.7 %shard_map.110 = (bf16[1,128,1024]{2,1,0:T(8,128)(2,1)}, f32[64,1024]{1,0:T(8,128)}, f32[64,1024]{1,0:T(8,128)}) custom-call(bf16[1600,128]{1,0:T(8,128)(2,1)S(1)} %collective-permute-done.7.core, bf16[2624,128]{1,0:T(8,128)(2,1)S(1)} %collective-permute-done.10.pair, bf16[768,128]{1,0:T(8,128)(2,1)S(1)} %get-tuple-element.37.refs_0_, ...), custom_call_target="tpu_custom_call" | custom-call | tf_op jit(solution)/shard_map/pallas_call | solution.py:279
  (3 shorter events, 0.1 us)
Async XLA Ops:
  0.6 1.1 %copy-start.2 = (bf16[1,128,1024]{2,1,0:T(8,128)(2,1)S(1)}, bf16[1,128,1024]{2,1,0:T(8,128)(2,1)}, u32[]{:S(2)}) copy-start(bf16[1,128,1024]{2,1,0:T(8,128)(2,1)} %cotangent) | copy-start | bytes 786436
  0.6 1.7 %copy-start = (bf16[1024,1024]{1,0:T(8,128)(2,1)S(1)}, bf16[1024,1024]{1,0:T(8,128)(2,1)}, u32[]{:S(2)}) copy-start(bf16[1024,1024]{1,0:T(8,128)(2,1)} %refs_12_.1) | copy-start | bytes 6291460
  3.1 11.0 %collective-permute-start.1 = (bf16[768,128]{1,0:T(8,128)(2,1)S(1)}, bf16[768,128]{1,0:T(8,128)(2,1)S(1)}, u32[]{:S(2)}, u32[]{:S(2)}) collective-permute-start(bf16[768,128]{1,0:T(8,128)(2,1)S(1)} %get-tuple-element.27), channel_id=1, source_target_pairs={{0,2},{1,3},{2,0},{3,1},{4,6},{5,7},{6,4},{7,5},{8,10},{9,11},{10,... | collective-permute-start | bytes 589832 | tf_op jit(solution)/shard_map/ppermute | solution.py:301
  6.1 8.0 %collective-permute-start.2 = (bf16[512,128]{1,0:T(8,128)(2,1)S(1)}, bf16[512,128]{1,0:T(8,128)(2,1)S(1)}, u32[]{:S(2)}, u32[]{:S(2)}) collective-permute-start(bf16[512,128]{1,0:T(8,128)(2,1)S(1)} %get-tuple-element.28), channel_id=1, source_target_pairs={{0,4},{1,5},{2,6},{3,7},{4,0},{5,1},{6,2},{7,3},{8,12},{9,13},{10,... | collective-permute-start | bytes 393224 | tf_op jit(solution)/shard_map/ppermute | solution.py:301
  7.7 6.4 %collective-permute-start = (bf16[400,128]{1,0:T(8,128)(2,1)S(1)}, bf16[400,128]{1,0:T(8,128)(2,1)S(1)}, u32[]{:S(2)}, u32[]{:S(2)}) collective-permute-start(bf16[400,128]{1,0:T(8,128)(2,1)S(1)} %shard_map.103.piece), channel_id=1, source_target_pairs={{0,8},{1,9},{2,10},{3,11},{4,12},{5,13},{6,14},{7,15},{8,0},{9,1},... | collective-permute-start | bytes 307208 | tf_op jit(solution)/shard_map/ppermute | solution.py:301
  14.2 7.5 %collective-permute-start.4 = (bf16[544,128]{1,0:T(8,128)(2,1)S(1)}, bf16[544,128]{1,0:T(8,128)(2,1)S(1)}, u32[]{:S(2)}, u32[]{:S(2)}) collective-permute-start(bf16[544,128]{1,0:T(8,128)(2,1)S(1)} %get-tuple-element.30.turn), channel_id=1, source_target_pairs={{0,2},{1,3},{2,0},{3,1},{4,6},{5,7},{6,4},{7,5},{8,10},{9,11},{10,... | collective-permute-start | bytes 417800 | tf_op jit(solution)/shard_map/ppermute | solution.py:301
  14.7 6.9 %collective-permute-start.3 = (bf16[512,128]{1,0:T(8,128)(2,1)S(1)}, bf16[512,128]{1,0:T(8,128)(2,1)S(1)}, u32[]{:S(2)}, u32[]{:S(2)}) collective-permute-start(bf16[512,128]{1,0:T(8,128)(2,1)S(1)} %get-tuple-element.29.half_a), channel_id=1, source_target_pairs={{0,4},{1,5},{2,6},{3,7},{4,0},{5,1},{6,2},{7,3},{8,12},{9,13},{10,... | collective-permute-start | bytes 393224 | tf_op jit(solution)/shard_map/ppermute | solution.py:301
  16.5 8.1 %collective-permute-start.8 = (bf16[512,128]{1,0:T(8,128)(2,1)S(1)}, bf16[512,128]{1,0:T(8,128)(2,1)S(1)}, u32[]{:S(2)}, u32[]{:S(2)}) collective-permute-start(bf16[512,128]{1,0:T(8,128)(2,1)S(1)} %get-tuple-element.38), channel_id=1, source_target_pairs={{0,12},{1,13},{2,14},{3,15},{4,8},{5,9},{6,10},{7,11},{8,4},{9,5},... | collective-permute-start | bytes 393224 | tf_op jit(solution)/shard_map/ppermute | solution.py:301
  18.2 10.4 %collective-permute-start.9 = (bf16[512,128]{1,0:T(8,128)(2,1)S(1)}, bf16[512,128]{1,0:T(8,128)(2,1)S(1)}, u32[]{:S(2)}, u32[]{:S(2)}) collective-permute-start(bf16[512,128]{1,0:T(8,128)(2,1)S(1)} %get-tuple-element.39), channel_id=1, source_target_pairs={{0,8},{1,9},{2,10},{3,11},{4,12},{5,13},{6,14},{7,15},{8,0},{9,1},... | collective-permute-start | bytes 393224 | tf_op jit(solution)/shard_map/ppermute | solution.py:301
  21.8 9.4 %collective-permute-start.7 = (bf16[1600,128]{1,0:T(8,128)(2,1)S(1)}, bf16[1600,128]{1,0:T(8,128)(2,1)S(1)}, u32[]{:S(2)}, u32[]{:S(2)}) collective-permute-start(bf16[1600,128]{1,0:T(8,128)(2,1)S(1)} %get-tuple-element.33), channel_id=1, source_target_pairs={{0,1},{1,0},{2,3},{3,2},{4,5},{5,4},{6,7},{7,6},{8,9},{9,8},{10,11... | collective-permute-start | bytes 1228808 | tf_op jit(solution)/shard_map/ppermute | solution.py:301
  21.8 9.3 %collective-permute-start.5 = (bf16[1024,128]{1,0:T(8,128)(2,1)S(1)}, bf16[1024,128]{1,0:T(8,128)(2,1)S(1)}, u32[]{:S(2)}, u32[]{:S(2)}) collective-permute-start(bf16[1024,128]{1,0:T(8,128)(2,1)S(1)} %get-tuple-element.31.a), channel_id=1, source_target_pairs={{0,2},{1,3},{2,0},{3,1},{4,6},{5,7},{6,4},{7,5},{8,10},{9,11},{10,... | collective-permute-start | bytes 786440 | tf_op jit(solution)/shard_map/ppermute | solution.py:301
  23.4 7.7 %collective-permute-start.6 = (bf16[576,128]{1,0:T(8,128)(2,1)S(1)}, bf16[576,128]{1,0:T(8,128)(2,1)S(1)}, u32[]{:S(2)}, u32[]{:S(2)}) collective-permute-start(bf16[576,128]{1,0:T(8,128)(2,1)S(1)} %get-tuple-element.32.b), channel_id=1, source_target_pairs={{0,4},{1,5},{2,6},{3,7},{4,0},{5,1},{6,2},{7,3},{8,12},{9,13},{10,... | collective-permute-start | bytes 442376 | tf_op jit(solution)/shard_map/ppermute | solution.py:301
  28.7 2.6 %copy-start.1 = (bf16[1024,1024]{1,0:T(8,128)(2,1)S(1)}, bf16[1024,1024]{1,0:T(8,128)(2,1)}, u32[]{:S(2)}) copy-start(bf16[1024,1024]{1,0:T(8,128)(2,1)} %refs_11_.1) | copy-start | bytes 6291460
  31.2 2.2 %collective-permute-start.10 = (bf16[2624,128]{1,0:T(8,128)(2,1)S(1)}, bf16[2624,128]{1,0:T(8,128)(2,1)S(1)}, u32[]{:S(2)}, u32[]{:S(2)}) collective-permute-start(bf16[2624,128]{1,0:T(8,128)(2,1)S(1)} %shard_map.108), channel_id=1, source_target_pairs={{0,1},{1,0},{2,3},{3,2},{4,5},{5,4},{6,7},{7,6},{8,9},{9,8},{10,11... | collective-permute-start | bytes 2015240 | tf_op jit(solution)/shard_map/ppermute | solution.py:301

commit v20 on v19

--- a/solution.py
+++ b/solution.py
@@ -245,7 +245,7 @@
         sig = 0.5 + 0.5 * jnp.tanh(0.5 * pre)
         dpre[:, span] = (back[each:] * sig * (1.0 + pre * (1.0 - sig))).astype(BF16)
 
-    chunk = min(width, 2 * LANES)
+    chunk = min(width, 4 * LANES)
     for c in range(0, width, chunk):
         span = slice(c, c + chunk)
         here = first * rows

time: 40.2 us -> 40.3 us (level)
  no operation moved by 1% of the time
where the time goes in v20:
time: 40.3 us; the launch traced here: 40.1 us
  starting transfers between devices  14.7 us (36%)
  waiting for transfers between devices  13.8 us (34%)
  Pallas kernels  10.3 us (26%)
  between operations  0.73 us (2%)
  local copies, waits for them, and re-layouts  0.62 us (2%)
    ppermute x11, starting transfers between devices, swap(): return lax.ppermute(x, 'grp', [(i, i ^ slot) for i in range(GROUP)])  14.7 us
    ppermute x11, waiting for transfers between devices, swap(): return lax.ppermute(x, 'grp', [(i, i ^ slot) for i in range(GROUP)])  13.8 us
    pallas_call x8, Pallas kernels, call(): pl.pallas_call(kernel, out_shape=tuple((jax.ShapeDtypeStruct(*out) for ou...  10.3 us
  transfers between devices with their start and end apart: 11, of which 5 were waited for; matrix products, arithmetic and copies ran while one was open for 0% of the time, Pallas kernels for 4%

profile of v20, /device:TPU:0, one launch (start us, length us, event | category | flops | bytes accessed | tf_op | source)
XLA Modules:
  0.0 40.1 jit_solution(6868337114971838209)
XLA Ops:
  0.6 0.0 copy-start.2
  0.6 0.0 copy-start
  0.7 1.1 %shard_map.103.piece = bf16[400,128]{1,0:T(8,128)(2,1)S(1)} custom-call(s32[2]{0:T(128)} %counts.1, s32[1,8]{1,0:T(1,128)} %owner.1, s32[1,8]{1,0:T(1,128)} %local.1, bf16[2,16,1024]{2,1,0:T(8,128)(2,1)} %features.1, bf16[1,128,128]{2,1,0:T(8,128)(2,1)} %adjacency.1), custom_call_target="tpu_custom_call" | custom-call | flops 10000000000 | tf_op jit(solution)/shard_map/pallas_call | solution.py:279
  1.8 0.0 copy-done.2
  1.8 0.6 %copy-done = bf16[1024,1024]{1,0:T(8,128)(2,1)S(1)} copy-done((bf16[1024,1024]{1,0:T(8,128)(2,1)S(1)}, bf16[1024,1024]{1,0:T(8,128)(2,1)}, u32[]{:S(2)}) %copy-start) | copy-done | bytes 2097176
  2.4 0.7 %shard_map.104 = (bf16[768,128]{1,0:T(8,128)(2,1)S(1)}, bf16[768,128]{1,0:T(8,128)(2,1)S(1)}, bf16[512,128]{1,0:T(8,128)(2,1)S(1)}) custom-call(bf16[1,128,1024]{2,1,0:T(8,128)(2,1)S(1)} %copy-done.2, bf16[1024,1024]{1,0:T(8,128)(2,1)S(1)} %copy-done), custom_call_target="tpu_custom_call" | custom-call | tf_op jit(solution)/shard_map/pallas_call | solution.py:279
  3.1 3.0 %collective-permute-start.1 = (bf16[768,128]{1,0:T(8,128)(2,1)S(1)}, bf16[768,128]{1,0:T(8,128)(2,1)S(1)}, u32[]{:S(2)}, u32[]{:S(2)}) collective-permute-start(bf16[768,128]{1,0:T(8,128)(2,1)S(1)} %get-tuple-element.27), channel_id=1, source_target_pairs={{0,2},{1,3},{2,0},{3,1},{4,6},{5,7},{6,4},{7,5},{8,10},{9,11},{10,... | collective-permute-start | bytes 589832 | tf_op jit(solution)/shard_map/ppermute | solution.py:301
  6.1 1.6 %collective-permute-start.2 = (bf16[512,128]{1,0:T(8,128)(2,1)S(1)}, bf16[512,128]{1,0:T(8,128)(2,1)S(1)}, u32[]{:S(2)}, u32[]{:S(2)}) collective-permute-start(bf16[512,128]{1,0:T(8,128)(2,1)S(1)} %get-tuple-element.28), channel_id=1, source_target_pairs={{0,4},{1,5},{2,6},{3,7},{4,0},{5,1},{6,2},{7,3},{8,12},{9,13},{10,... | collective-permute-start | bytes 393224 | tf_op jit(solution)/shard_map/ppermute | solution.py:301
  7.7 2.6 %collective-permute-start = (bf16[400,128]{1,0:T(8,128)(2,1)S(1)}, bf16[400,128]{1,0:T(8,128)(2,1)S(1)}, u32[]{:S(2)}, u32[]{:S(2)}) collective-permute-start(bf16[400,128]{1,0:T(8,128)(2,1)S(1)} %shard_map.103.piece), channel_id=1, source_target_pairs={{0,8},{1,9},{2,10},{3,11},{4,12},{5,13},{6,14},{7,15},{8,0},{9,1},... | collective-permute-start | bytes 307208 | tf_op jit(solution)/shard_map/ppermute | solution.py:301
  10.3 3.8 %collective-permute-done.came = bf16[400,128]{1,0:T(8,128)(2,1)S(1)} collective-permute-done((bf16[400,128]{1,0:T(8,128)(2,1)S(1)}, bf16[400,128]{1,0:T(8,128)(2,1)S(1)}, u32[]{:S(2)}, u32[]{:S(2)}) %collective-permute-start) | collective-permute-done | bytes 102432 | tf_op jit(solution)/shard_map/ppermute | solution.py:301
  14.1 0.0 collective-permute-done.2.beside
  14.1 0.0 collective-permute-done.1.across
  14.2 0.6 %collective-permute-start.4 = (bf16[544,128]{1,0:T(8,128)(2,1)S(1)}, bf16[544,128]{1,0:T(8,128)(2,1)S(1)}, u32[]{:S(2)}, u32[]{:S(2)}) collective-permute-start(bf16[544,128]{1,0:T(8,128)(2,1)S(1)} %get-tuple-element.30.turn), channel_id=1, source_target_pairs={{0,2},{1,3},{2,0},{3,1},{4,6},{5,7},{6,4},{7,5},{8,10},{9,11},{10,... | collective-permute-start | bytes 417800 | tf_op jit(solution)/shard_map/ppermute | solution.py:301
  14.7 1.8 %collective-permute-start.3 = (bf16[512,128]{1,0:T(8,128)(2,1)S(1)}, bf16[512,128]{1,0:T(8,128)(2,1)S(1)}, u32[]{:S(2)}, u32[]{:S(2)}) collective-permute-start(bf16[512,128]{1,0:T(8,128)(2,1)S(1)} %get-tuple-element.29.half_a), channel_id=1, source_target_pairs={{0,4},{1,5},{2,6},{3,7},{4,0},{5,1},{6,2},{7,3},{8,12},{9,13},{10,... | collective-permute-start | bytes 393224 | tf_op jit(solution)/shard_map/ppermute | solution.py:301
  16.5 1.7 %collective-permute-start.8 = (bf16[512,128]{1,0:T(8,128)(2,1)S(1)}, bf16[512,128]{1,0:T(8,128)(2,1)S(1)}, u32[]{:S(2)}, u32[]{:S(2)}) collective-permute-start(bf16[512,128]{1,0:T(8,128)(2,1)S(1)} %get-tuple-element.38), channel_id=1, source_target_pairs={{0,12},{1,13},{2,14},{3,15},{4,8},{5,9},{6,10},{7,11},{8,4},{9,5},... | collective-permute-start | bytes 393224 | tf_op jit(solution)/shard_map/ppermute | solution.py:301
  18.2 0.6 %collective-permute-start.9 = (bf16[512,128]{1,0:T(8,128)(2,1)S(1)}, bf16[512,128]{1,0:T(8,128)(2,1)S(1)}, u32[]{:S(2)}, u32[]{:S(2)}) collective-permute-start(bf16[512,128]{1,0:T(8,128)(2,1)S(1)} %get-tuple-element.39), channel_id=1, source_target_pairs={{0,8},{1,9},{2,10},{3,11},{4,12},{5,13},{6,14},{7,15},{8,0},{9,1},... | collective-permute-start | bytes 393224 | tf_op jit(solution)/shard_map/ppermute | solution.py:301
  18.8 2.9 %collective-permute-done.3.came_a = bf16[512,128]{1,0:T(8,128)(2,1)S(1)} collective-permute-done((bf16[512,128]{1,0:T(8,128)(2,1)S(1)}, bf16[512,128]{1,0:T(8,128)(2,1)S(1)}, u32[]{:S(2)}, u32[]{:S(2)}) %collective-permute-start.3) | collective-permute-done | bytes 131104 | tf_op jit(solution)/shard_map/ppermute | solution.py:301
  21.7 0.0 collective-permute-done.4.came_b.refs_1_
  21.7 0.1 shard_map.106
  21.8 0.1 collective-permute-start.7
  21.8 1.6 %collective-permute-start.5 = (bf16[1024,128]{1,0:T(8,128)(2,1)S(1)}, bf16[1024,128]{1,0:T(8,128)(2,1)S(1)}, u32[]{:S(2)}, u32[]{:S(2)}) collective-permute-start(bf16[1024,128]{1,0:T(8,128)(2,1)S(1)} %get-tuple-element.31.a), channel_id=1, source_target_pairs={{0,2},{1,3},{2,0},{3,1},{4,6},{5,7},{6,4},{7,5},{8,10},{9,11},{10,... | collective-permute-start | bytes 786440 | tf_op jit(solution)/shard_map/ppermute | solution.py:301
  23.4 1.2 %collective-permute-start.6 = (bf16[576,128]{1,0:T(8,128)(2,1)S(1)}, bf16[576,128]{1,0:T(8,128)(2,1)S(1)}, u32[]{:S(2)}, u32[]{:S(2)}) collective-permute-start(bf16[576,128]{1,0:T(8,128)(2,1)S(1)} %get-tuple-element.32.b), channel_id=1, source_target_pairs={{0,4},{1,5},{2,6},{3,7},{4,0},{5,1},{6,2},{7,3},{8,12},{9,13},{10,... | collective-permute-start | bytes 442376 | tf_op jit(solution)/shard_map/ppermute | solution.py:301
  24.6 0.0 collective-permute-done.8.refs_2_
  24.6 4.1 %collective-permute-done.9.refs_3_ = bf16[512,128]{1,0:T(8,128)(2,1)S(1)} collective-permute-done((bf16[512,128]{1,0:T(8,128)(2,1)S(1)}, bf16[512,128]{1,0:T(8,128)(2,1)S(1)}, u32[]{:S(2)}, u32[]{:S(2)}) %collective-permute-start.9) | collective-permute-done | bytes 131104 | tf_op jit(solution)/shard_map/ppermute | solution.py:301
  28.7 0.0 copy-start.1
  28.7 2.4 %collective-permute-done.6.far_b = bf16[576,128]{1,0:T(8,128)(2,1)S(1)} collective-permute-done((bf16[576,128]{1,0:T(8,128)(2,1)S(1)}, bf16[576,128]{1,0:T(8,128)(2,1)S(1)}, u32[]{:S(2)}, u32[]{:S(2)}) %collective-permute-start.6) | collective-permute-done | bytes 147488 | tf_op jit(solution)/shard_map/ppermute | solution.py:301
  31.1 0.0 collective-permute-done.5.far_a
  31.1 0.0 collective-permute-done.7.core
  31.2 0.1 collective-permute-start.10
  31.2 0.0 copy-done.1
  31.3 1.6 %shard_map.109 = (bf16[256,1024]{1,0:T(8,128)(2,1)S(1)}, bf16[256,1024]{1,0:T(8,128)(2,1)S(1)}, bf16[1024,512]{1,0:T(8,128)(2,1)S(1)}, bf16[8,128,128]{2,1,0:T(8...) custom-call(bf16[1024,128]{1,0:T(8,128)(2,1)S(1)} %get-tuple-element.31.a, ...), custom_call_target="tpu_custom_call" | custom-call | tf_op jit(solution)/shard_map/pallas_call | solution.py:279
  32.8 0.5 %collective-permute-done.10.pair = bf16[2624,128]{1,0:T(8,128)(2,1)S(1)} collective-permute-done((bf16[2624,128]{1,0:T(8,128)(2,1)S(1)}, bf16[2624,128]{1,0:T(8,128)(2,1)S(1)}, u32[]{:S(2)}, u32[]{:S(2)}) %collective-permute-start.10) | collective-permute-done | bytes 671776 | tf_op jit(solution)/shard_map/ppermute | solution.py:301
  33.4 6.8 %shard_map.110 = (bf16[1,128,1024]{2,1,0:T(8,128)(2,1)}, f32[64,1024]{1,0:T(8,128)}, f32[64,1024]{1,0:T(8,128)}) custom-call(bf16[1600,128]{1,0:T(8,128)(2,1)S(1)} %collective-permute-done.7.core, bf16[2624,128]{1,0:T(8,128)(2,1)S(1)} %collective-permute-done.10.pair, bf16[768,128]{1,0:T(8,128)(2,1)S(1)} %get-tuple-element.37.refs_0_, ...), custom_call_target="tpu_custom_call" | custom-call | tf_op jit(solution)/shard_map/pallas_call | solution.py:279
  (3 shorter events, 0.1 us)
Async XLA Ops:
  0.6 1.1 %copy-start.2 = (bf16[1,128,1024]{2,1,0:T(8,128)(2,1)S(1)}, bf16[1,128,1024]{2,1,0:T(8,128)(2,1)}, u32[]{:S(2)}) copy-start(bf16[1,128,1024]{2,1,0:T(8,128)(2,1)} %cotangent) | copy-start | bytes 786436
  0.6 1.7 %copy-start = (bf16[1024,1024]{1,0:T(8,128)(2,1)S(1)}, bf16[1024,1024]{1,0:T(8,128)(2,1)}, u32[]{:S(2)}) copy-start(bf16[1024,1024]{1,0:T(8,128)(2,1)} %refs_12_.1) | copy-start | bytes 6291460
  3.1 11.0 %collective-permute-start.1 = (bf16[768,128]{1,0:T(8,128)(2,1)S(1)}, bf16[768,128]{1,0:T(8,128)(2,1)S(1)}, u32[]{:S(2)}, u32[]{:S(2)}) collective-permute-start(bf16[768,128]{1,0:T(8,128)(2,1)S(1)} %get-tuple-element.27), channel_id=1, source_target_pairs={{0,2},{1,3},{2,0},{3,1},{4,6},{5,7},{6,4},{7,5},{8,10},{9,11},{10,... | collective-permute-start | bytes 589832 | tf_op jit(solution)/shard_map/ppermute | solution.py:301
  6.1 8.0 %collective-permute-start.2 = (bf16[512,128]{1,0:T(8,128)(2,1)S(1)}, bf16[512,128]{1,0:T(8,128)(2,1)S(1)}, u32[]{:S(2)}, u32[]{:S(2)}) collective-permute-start(bf16[512,128]{1,0:T(8,128)(2,1)S(1)} %get-tuple-element.28), channel_id=1, source_target_pairs={{0,4},{1,5},{2,6},{3,7},{4,0},{5,1},{6,2},{7,3},{8,12},{9,13},{10,... | collective-permute-start | bytes 393224 | tf_op jit(solution)/shard_map/ppermute | solution.py:301
  7.7 6.4 %collective-permute-start = (bf16[400,128]{1,0:T(8,128)(2,1)S(1)}, bf16[400,128]{1,0:T(8,128)(2,1)S(1)}, u32[]{:S(2)}, u32[]{:S(2)}) collective-permute-start(bf16[400,128]{1,0:T(8,128)(2,1)S(1)} %shard_map.103.piece), channel_id=1, source_target_pairs={{0,8},{1,9},{2,10},{3,11},{4,12},{5,13},{6,14},{7,15},{8,0},{9,1},... | collective-permute-start | bytes 307208 | tf_op jit(solution)/shard_map/ppermute | solution.py:301
  14.2 7.5 %collective-permute-start.4 = (bf16[544,128]{1,0:T(8,128)(2,1)S(1)}, bf16[544,128]{1,0:T(8,128)(2,1)S(1)}, u32[]{:S(2)}, u32[]{:S(2)}) collective-permute-start(bf16[544,128]{1,0:T(8,128)(2,1)S(1)} %get-tuple-element.30.turn), channel_id=1, source_target_pairs={{0,2},{1,3},{2,0},{3,1},{4,6},{5,7},{6,4},{7,5},{8,10},{9,11},{10,... | collective-permute-start | bytes 417800 | tf_op jit(solution)/shard_map/ppermute | solution.py:301
  14.7 6.9 %collective-permute-start.3 = (bf16[512,128]{1,0:T(8,128)(2,1)S(1)}, bf16[512,128]{1,0:T(8,128)(2,1)S(1)}, u32[]{:S(2)}, u32[]{:S(2)}) collective-permute-start(bf16[512,128]{1,0:T(8,128)(2,1)S(1)} %get-tuple-element.29.half_a), channel_id=1, source_target_pairs={{0,4},{1,5},{2,6},{3,7},{4,0},{5,1},{6,2},{7,3},{8,12},{9,13},{10,... | collective-permute-start | bytes 393224 | tf_op jit(solution)/shard_map/ppermute | solution.py:301
  16.5 8.1 %collective-permute-start.8 = (bf16[512,128]{1,0:T(8,128)(2,1)S(1)}, bf16[512,128]{1,0:T(8,128)(2,1)S(1)}, u32[]{:S(2)}, u32[]{:S(2)}) collective-permute-start(bf16[512,128]{1,0:T(8,128)(2,1)S(1)} %get-tuple-element.38), channel_id=1, source_target_pairs={{0,12},{1,13},{2,14},{3,15},{4,8},{5,9},{6,10},{7,11},{8,4},{9,5},... | collective-permute-start | bytes 393224 | tf_op jit(solution)/shard_map/ppermute | solution.py:301
  18.2 10.4 %collective-permute-start.9 = (bf16[512,128]{1,0:T(8,128)(2,1)S(1)}, bf16[512,128]{1,0:T(8,128)(2,1)S(1)}, u32[]{:S(2)}, u32[]{:S(2)}) collective-permute-start(bf16[512,128]{1,0:T(8,128)(2,1)S(1)} %get-tuple-element.39), channel_id=1, source_target_pairs={{0,8},{1,9},{2,10},{3,11},{4,12},{5,13},{6,14},{7,15},{8,0},{9,1},... | collective-permute-start | bytes 393224 | tf_op jit(solution)/shard_map/ppermute | solution.py:301
  21.8 9.4 %collective-permute-start.7 = (bf16[1600,128]{1,0:T(8,128)(2,1)S(1)}, bf16[1600,128]{1,0:T(8,128)(2,1)S(1)}, u32[]{:S(2)}, u32[]{:S(2)}) collective-permute-start(bf16[1600,128]{1,0:T(8,128)(2,1)S(1)} %get-tuple-element.33), channel_id=1, source_target_pairs={{0,1},{1,0},{2,3},{3,2},{4,5},{5,4},{6,7},{7,6},{8,9},{9,8},{10,11... | collective-permute-start | bytes 1228808 | tf_op jit(solution)/shard_map/ppermute | solution.py:301
  21.8 9.3 %collective-permute-start.5 = (bf16[1024,128]{1,0:T(8,128)(2,1)S(1)}, bf16[1024,128]{1,0:T(8,128)(2,1)S(1)}, u32[]{:S(2)}, u32[]{:S(2)}) collective-permute-start(bf16[1024,128]{1,0:T(8,128)(2,1)S(1)} %get-tuple-element.31.a), channel_id=1, source_target_pairs={{0,2},{1,3},{2,0},{3,1},{4,6},{5,7},{6,4},{7,5},{8,10},{9,11},{10,... | collective-permute-start | bytes 786440 | tf_op jit(solution)/shard_map/ppermute | solution.py:301
  23.4 7.7 %collective-permute-start.6 = (bf16[576,128]{1,0:T(8,128)(2,1)S(1)}, bf16[576,128]{1,0:T(8,128)(2,1)S(1)}, u32[]{:S(2)}, u32[]{:S(2)}) collective-permute-start(bf16[576,128]{1,0:T(8,128)(2,1)S(1)} %get-tuple-element.32.b), channel_id=1, source_target_pairs={{0,4},{1,5},{2,6},{3,7},{4,0},{5,1},{6,2},{7,3},{8,12},{9,13},{10,... | collective-permute-start | bytes 442376 | tf_op jit(solution)/shard_map/ppermute | solution.py:301
  28.7 2.6 %copy-start.1 = (bf16[1024,1024]{1,0:T(8,128)(2,1)S(1)}, bf16[1024,1024]{1,0:T(8,128)(2,1)}, u32[]{:S(2)}) copy-start(bf16[1024,1024]{1,0:T(8,128)(2,1)} %refs_11_.1) | copy-start | bytes 6291460
  31.2 2.2 %collective-permute-start.10 = (bf16[2624,128]{1,0:T(8,128)(2,1)S(1)}, bf16[2624,128]{1,0:T(8,128)(2,1)S(1)}, u32[]{:S(2)}, u32[]{:S(2)}) collective-permute-start(bf16[2624,128]{1,0:T(8,128)(2,1)S(1)} %shard_map.108), channel_id=1, source_target_pairs={{0,1},{1,0},{2,3},{3,2},{4,5},{5,4},{6,7},{7,6},{8,9},{9,8},{10,11... | collective-permute-start | bytes 2015240 | tf_op jit(solution)/shard_map/ppermute | solution.py:301
